TPU v7x, 32 devices: a whole 2x2x4 slice. The times are simulated.
32 devices in a mesh: groups: 2 (over y), src: 4 (over z), dst: 4 (over x, core).
Axes of the slice: x: 2, y: 2, z: 4, core: 2. Of those that a mesh axis runs over, the one named last changes fastest.
Arguments:
- node_state: bfloat16 [2, 1024, 128], P(None, ('groups', 'src', 'dst')), parts along dimension 1, may hold values from -6 to 6
- forcing: bfloat16 [2, 1024, 128], P(None, ('groups', 'src', 'dst')), parts along dimension 1, may hold values from -6 to 6
- edge_attr: bfloat16 [2, 8, 4, 512, 128], P(None, ('groups', 'src'), 'dst'), parts along dimension 1, may hold values from -6 to 6
- src_index: int32 [8, 4, 512], P(('groups', 'src'), 'dst'), parts along dimension 0, may hold values from 0 to 127
- dst_index: int32 [8, 4, 512], P(('groups', 'src'), 'dst'), parts along dimension 0, may hold values from 0 to 127
- edge_count: int32 [8, 4], P(('groups', 'src'), 'dst'), parts along dimension 0, may hold values from 128 to 512, as said below
- cotangent: bfloat16 [2, 1024, 256], P(None, ('groups', 'src', 'dst')), parts along dimension 1, may hold values from -6 to 6
- edge_w1: bfloat16 [384, 512], replicated, may hold values from -0.3125 to 0.3125
- edge_w2: bfloat16 [512, 256], replicated, may hold values from -0.25 to 0.25
- node_w1: bfloat16 [512, 256], replicated, may hold values from -0.25 to 0.25
Outputs:
- grad_state: float32 [2, 1024, 128], P(None, ('groups', 'src', 'dst')), parts along dimension 1
- grad_forcing: float32 [2, 1024, 128], P(None, ('groups', 'src', 'dst')), parts along dimension 1
- grad_edges: float32 [2, 8, 4, 512, 128], P(None, ('groups', 'src'), 'dst'), parts along dimension 1
- grad_edge_w1: float32 [768, 512], P('groups'), parts along dimension 0
- grad_edge_w2: float32 [1024, 256], P('groups'), parts along dimension 0
- grad_node_w1: float32 [1024, 256], P('groups'), parts along dimension 0
There are 2 independent parts, one for each index of `groups`. A program takes and returns all parts, laid end to end along the dimension named above; an argument that names none is the same for every part. Nothing has to cross between parts.
Inputs may be any that keep to these rules, and one draw needn't show every extreme that they name: The live slots of a tile are its first edge_count ones; every draw has a tile with all 512 slots live.
All inputs are finite; a program needn't handle non-finite values.
Results may differ from a plain program's by a relative error of at most 0.006.
Values may be sent and summed in bfloat16 or wider, within the bound.
No kernel may reach another device: no remote copies, remote signals or barrier semaphores. Data moves between devices by JAX's collectives and lax.ppermute only.
A program may use at most 64 MiB of HBM per device.

v0:
```python
import jax
import jax.numpy as jnp
from jax import lax
from jax.sharding import PartitionSpec as P

T_STEPS = 2


def silu_slope(value):
    sigma = jax.nn.sigmoid(value)
    return sigma * (1.0 + value * (1.0 - sigma))


def local(
    node_state,
    forcing,
    edge_attr,
    src_index,
    dst_index,
    edge_count,
    cotangent,
    edge_w1,
    edge_w2,
    node_w1,
):
    node_rows = node_state.shape[1]
    width_x = node_state.shape[2]
    width_m = edge_w2.shape[1]
    src_rows = node_rows * lax.axis_size("dst")
    dst_rows = node_rows * lax.axis_size("src")
    sources = lax.all_gather(node_state, "dst", axis=1, tiled=True)
    targets, forcing_block, cotangent_block = (
        lax.all_gather(node_state, "src", axis=1, tiled=True),
        lax.all_gather(forcing, "src", axis=1, tiled=True),
        lax.all_gather(cotangent, "src", axis=1, tiled=True),
    )
    src_local = src_index[0, 0]
    dst_local = dst_index[0, 0]
    alive = lax.iota(jnp.int32, src_local.shape[0]) < edge_count[0, 0]
    alive_float = alive.astype(jnp.float32)[:, None]
    alive_half = alive.astype(jnp.bfloat16)[:, None]
    own_start = lax.axis_index("src") * node_rows
    grad_first = jnp.zeros(edge_w1.shape, jnp.float32)
    grad_second = jnp.zeros(edge_w2.shape, jnp.float32)
    grad_node = jnp.zeros(node_w1.shape, jnp.float32)
    state_out, forcing_out, edge_out = ([], [], [])
    for moment in range(T_STEPS):
        edge_in = jnp.concatenate(
            [sources[moment][src_local], targets[moment][dst_local], edge_attr[moment, 0, 0]],
            axis=1,
        )
        pre_edge = jnp.dot(edge_in, edge_w1, preferred_element_type=jnp.float32)
        hidden = jax.nn.silu(pre_edge).astype(jnp.bfloat16)
        message = jnp.dot(hidden, edge_w2, preferred_element_type=jnp.float32) * alive_float
        partial_value = jax.ops.segment_sum(message, dst_local, num_segments=dst_rows)
        agg_block = lax.psum(partial_value, "src")
        node_in = jnp.concatenate(
            [targets[moment], agg_block.astype(jnp.bfloat16), forcing_block[moment]], axis=1
        )
        pre_node = jnp.dot(node_in, node_w1, preferred_element_type=jnp.float32)
        grad_pre_node = (cotangent_block[moment].astype(jnp.float32) * silu_slope(pre_node)).astype(
            jnp.bfloat16
        )
        grad_node_in = jnp.dot(grad_pre_node, node_w1.T, preferred_element_type=jnp.float32)
        own_in = lax.dynamic_slice_in_dim(node_in, own_start, node_rows, 0)
        own_pre = lax.dynamic_slice_in_dim(grad_pre_node, own_start, node_rows, 0)
        grad_node = grad_node + jnp.dot(own_in.T, own_pre, preferred_element_type=jnp.float32)
        own_grad = lax.dynamic_slice_in_dim(grad_node_in, own_start, node_rows, 0)
        grad_agg = grad_node_in[:, width_x : width_x + width_m].astype(jnp.bfloat16)
        grad_message = grad_agg[dst_local] * alive_half
        grad_second = grad_second + jnp.dot(
            hidden.T, grad_message, preferred_element_type=jnp.float32
        )
        grad_hidden = jnp.dot(grad_message, edge_w2.T, preferred_element_type=jnp.float32)
        grad_pre_edge = (grad_hidden * silu_slope(pre_edge)).astype(jnp.bfloat16)
        grad_first = grad_first + jnp.dot(
            edge_in.T, grad_pre_edge, preferred_element_type=jnp.float32
        )
        grad_edge_in = jnp.dot(grad_pre_edge, edge_w1.T, preferred_element_type=jnp.float32)
        source_part = jax.ops.segment_sum(
            grad_edge_in[:, :width_x], src_local, num_segments=src_rows
        )
        target_part = jax.ops.segment_sum(
            grad_edge_in[:, width_x : 2 * width_x], dst_local, num_segments=dst_rows
        )
        from_sources = lax.psum_scatter(source_part, "dst", scatter_dimension=0, tiled=True)
        from_targets = lax.psum_scatter(target_part, "src", scatter_dimension=0, tiled=True)
        state_out.append(own_grad[:, :width_x] + from_sources + from_targets)
        forcing_out.append(own_grad[:, width_x + width_m :])
        edge_out.append(grad_edge_in[:, 2 * width_x :])
    grad_first, grad_second, grad_node = lax.psum(
        (grad_first, grad_second, grad_node), ("src", "dst")
    )
    return (
        jnp.stack(state_out),
        jnp.stack(forcing_out),
        jnp.stack(edge_out)[:, None, None],
        grad_first,
        grad_second,
        grad_node,
    )


def solution(mesh):
    in_specs = (
        P(None, ("groups", "src", "dst"), None),
        P(None, ("groups", "src", "dst"), None),
        P(None, ("groups", "src"), "dst", None, None),
        P(("groups", "src"), "dst", None),
        P(("groups", "src"), "dst", None),
        P(("groups", "src"), "dst"),
        P(None, ("groups", "src", "dst"), None),
        P(),
        P(),
        P(),
    )
    out_specs = (
        P(None, ("groups", "src", "dst"), None),
        P(None, ("groups", "src", "dst"), None),
        P(None, ("groups", "src"), "dst", None, None),
        P("groups", None),
        P("groups", None),
        P("groups", None),
    )
    return jax.shard_map(local, mesh=mesh, in_specs=in_specs, out_specs=out_specs, check_vma=False)
```

profile of v0, /device:TPU:0, one launch (start us, length us, event | category | flops | bytes accessed | tf_op | source)
XLA Modules:
  0.0 241.1 jit_solution(16488376678973169801)
XLA Ops:
  8.1 6.6 %all_gather.14 = bf16[2,128,128]{2,1,0:T(8,128)(2,1)S(1)} all-gather(bf16[2,32,128]{2,1,0:T(8,128)(2,1)} %param.10), channel_id=1, replica_groups=mesh['groups'=2,'src'=4,'dst'=4] {'dst'}, dimensions={1}, use_global_device_ids=true | all-gather | bytes 81920 | tf_op jit(solution)/shard_map/all_gather | solution.py:31
  14.6 13.8 %all_gather.13 = bf16[2,128,128]{2,1,0:T(8,128)(2,1)S(1)} all-gather(bf16[2,32,128]{2,1,0:T(8,128)(2,1)S(1)} %copy-done.30), channel_id=1, replica_groups=mesh['groups'=2,'src'=4,'dst'=4] {'src'}, dimensions={1}, use_global_device_ids=true | all-gather | bytes 81920 | tf_op jit(solution)/shard_map/all_gather | solution.py:33
  30.4 13.1 %all_gather.15 = bf16[2,128,128]{2,1,0:T(8,128)(2,1)S(1)} all-gather(bf16[2,32,128]{2,1,0:T(8,128)(2,1)S(1)} %copy-done.34), channel_id=1, replica_groups=mesh['groups'=2,'src'=4,'dst'=4] {'src'}, dimensions={1}, use_global_device_ids=true | all-gather | bytes 81920 | tf_op jit(solution)/shard_map/all_gather | solution.py:34
  43.6 1.3 gather_fusion
  49.0 14.2 %all_gather.12 = bf16[2,128,256]{2,1,0:T(8,128)(2,1)} all-gather(bf16[2,32,256]{2,1,0:T(8,128)(2,1)S(1)} %copy-done.33), channel_id=1, replica_groups=mesh['groups'=2,'src'=4,'dst'=4] {'src'}, dimensions={1}, use_global_device_ids=true | all-gather | bytes 163840 | tf_op jit(solution)/shard_map/all_gather | solution.py:35
  64.7 3.3 %scatter_custom_fusion.3 = f32[128,256]{1,0:T(8,128)S(1)} fusion(s32[512]{0:T(512)S(1)} %bitcast.77, f32[512,256]{1,0:T(8,128)S(1)} %convolution_multiply_fusion.2, f32[]{:T(128)} %constant.8.clone.1), kind=kCustom, calls=%fused_computation.62 | custom fusion | flops 131072 | bytes 131076 | tf_op jit(solution)/shard_map/scatter-add | solution.py:55
  68.1 1.5 multiply_convert_fusion.1
  70.3 3.3 %scatter_custom_fusion = f32[128,256]{1,0:T(8,128)S(1)} fusion(s32[512]{0:T(512)S(1)} %bitcast.78, f32[512,256]{1,0:T(8,128)S(1)} %convolution_multiply_fusion.3, f32[]{:T(128)} %constant.8.clone.1), kind=kCustom, calls=%fused_computation.64 | custom fusion | flops 131072 | bytes 131076 | tf_op jit(solution)/shard_map/scatter-add | solution.py:55
  73.7 24.8 %all-reduce.6 = (bf16[128,256]{1,0:T(8,128)(2,1)S(1)}, bf16[128,256]{1,0:T(8,128)(2,1)}) all-reduce(f32[128,256]{1,0:T(8,128)S(1)} %scatter_custom_fusion.3, f32[128,256]{1,0:T(8,128)S(1)} %scatter_custom_fusion), channel_id=1, replica_groups=mesh['groups'=2,'src'=4,'dst'=4] {'src'}, use_global_device_ids=true, to_apply=%region_7.8 | all-reduce | flops 65536 | bytes 393216 | tf_op jit(solution)/shard_map/psum | solution.py:56
  100.4 1.9 gather_fusion.5
  104.1 2.8 %scatter_custom_fusion.5 = f32[128,128]{1,0:T(8,128)} fusion(s32[512]{0:T(512)S(1)} %bitcast.79, f32[512,384]{1,0:T(8,128)S(1)} %fusion.54, f32[]{:T(128)} %constant.8.clone.1), kind=kCustom, calls=%fused_computation.30 | custom fusion | flops 65536 | bytes 327684 | tf_op jit(solution)/shard_map/scatter-add | solution.py:83
  107.0 2.8 %scatter_custom_fusion.4 = f32[128,128]{1,0:T(8,128)} fusion(s32[512]{0:T(512)S(1)} %bitcast.75, f32[512,384]{1,0:T(8,128)S(1)} %fusion.54, f32[]{:T(128)} %constant.8.clone.1), kind=kCustom, calls=%fused_computation.32 | custom fusion | flops 65536 | bytes 327684 | tf_op jit(solution)/shard_map/scatter-add | solution.py:80
  111.6 2.0 gather_fusion.2
  114.3 1.8 fusion
  117.3 2.8 %scatter_custom_fusion.1 = f32[128,128]{1,0:T(8,128)} fusion(s32[512]{0:T(512)S(1)} %bitcast.76, f32[512,384]{1,0:T(8,128)S(1)} %fusion.52, f32[]{:T(128)} %constant.8.clone.1), kind=kCustom, calls=%fused_computation.36 | custom fusion | flops 65536 | bytes 327684 | tf_op jit(solution)/shard_map/scatter-add | solution.py:80
  120.2 2.8 %scatter_custom_fusion.2 = f32[128,128]{1,0:T(8,128)} fusion(s32[512]{0:T(512)S(1)} %bitcast.80, f32[512,384]{1,0:T(8,128)S(1)} %fusion.52, f32[]{:T(128)} %constant.8.clone.1), kind=kCustom, calls=%fused_computation.34 | custom fusion | flops 65536 | bytes 327684 | tf_op jit(solution)/shard_map/scatter-add | solution.py:83
  123.1 1.7 pad_maximum_fusion.6
  127.4 2.7 %convolution_add_fusion.2 = f32[512,256]{1,0:T(8,128)} fusion(f32[512,256]{1,0:T(8,128)} %fusion.12, bf16[512,256]{1,0:T(8,128)(2,1)S(1)} %copy-done.17, bf16[512]{0:T(512)(128)(2,1)S(1)} %copy-done.37, f32[512,512]{1,0:T(8,128)} %copy-done.1), kind=kOutput, calls=%fused_computation.18 | convolution fusion | flops 135790592 | bytes 2360320 | tf_op jit(solution)/shard_map/dot_general | solution.py:71
  132.4 1.8 convolution_add_fusion.1
  135.1 9.8 %reduce-scatter.9.cloned.1.call-done = f32[32,128]{1,0:T(8,128)} async-done(((f32[128,128]{1,0:T(8,128)}), f32[32,128]{1,0:T(8,128)}) %reduce-scatter.9.cloned.1.call-update) | async-done | bytes 16400 | tf_op jit(solution)/shard_map/reduce_scatter | solution.py:86
  145.7 21.1 %reduce-scatter.5.cloned.1.call-done = f32[32,128]{1,0:T(8,128)} async-done(((f32[128,128]{1,0:T(8,128)}), f32[32,128]{1,0:T(8,128)}) %reduce-scatter.5.cloned.1.call-update) | async-done | bytes 16400 | tf_op jit(solution)/shard_map/reduce_scatter | solution.py:86
  166.8 21.4 %reduce-scatter.7.cloned.1.call-done = f32[32,128]{1,0:T(8,128)} async-done(((f32[128,128]{1,0:T(8,128)}), f32[32,128]{1,0:T(8,128)}) %reduce-scatter.7.cloned.1.call-update) | async-done | bytes 16400 | tf_op jit(solution)/shard_map/reduce_scatter | solution.py:87
  189.5 40.3 %all-reduce.5.cloned.1.call-done = (f32[384,512]{1,0:T(8,128)}, f32[512,256]{1,0:T(8,128)}, f32[512,256]{1,0:T(8,128)}) async-done(((f32[384,512]{1,0:T(8,128)}, f32[512,256]{1,0:T(8,128)}, f32[512,256]{1,0:T(8,128)}), (f32[384,512]{1,0:T(8,128)}, f32[512,256]{1,0:T(8,128)}, f32[512,256]{1,0:T(8,128)})) %all-reduce.5.cloned.1.call-update) | async-done | bytes 1835024 | tf_op jit(solution)/shard_map/psum | solution.py:91
  229.8 2.1 copy.26
  (123 shorter events, 24.9 us)
Async XLA Ops:
  8.0 55.3 %copy-start = (bf16[384,512]{1,0:T(8,128)(2,1)S(1)}, bf16[384,512]{1,0:T(8,128)(2,1)}, u32[]{:S(2)}) copy-start(bf16[384,512]{1,0:T(8,128)(2,1)} %param.17) | copy-start | bytes 1179652
  8.0 6.6 %copy-start.30 = (bf16[2,32,128]{2,1,0:T(8,128)(2,1)S(1)}, bf16[2,32,128]{2,1,0:T(8,128)(2,1)}, u32[]{:S(2)}) copy-start(bf16[2,32,128]{2,1,0:T(8,128)(2,1)} %param.10) | copy-start | bytes 49156
  8.0 127.1 %reduce-scatter.11.cloned.1.call-start = ((), (), s32[]{:S(2)}) async-start(), calls=%async_computation.7 | async-start | bytes 81920 | tf_op jit(solution)/shard_map/reduce_scatter | solution.py:87
  44.9 23.1 %copy-start.20 = (bf16[512,128]{1,0:T(8,128)(2,1)}, bf16[512,128]{1,0:T(8,128)(2,1)S(1)}, u32[]{:S(2)}) copy-start(bf16[512,128]{1,0:T(8,128)(2,1)S(1)} %gather_fusion) | copy-start | bytes 393220
  47.6 20.4 %copy-start.22 = (bf16[512,128]{1,0:T(8,128)(2,1)}, bf16[512,128]{1,0:T(8,128)(2,1)S(1)}, u32[]{:S(2)}) copy-start(bf16[512,128]{1,0:T(8,128)(2,1)S(1)} %gather_fusion.1) | copy-start | bytes 393220
  47.6 1.4 copy-start.33
  47.7 15.6 %copy-start.15 = (bf16[2,1,1,512,128]{4,3,2,1,0:T(8,128)(2,1)S(1)}, bf16[2,1,1,512,128]{4,3,2,1,0:T(8,128)(2,1)}, u32[]{:S(2)}) copy-start(bf16[2,1,1,512,128]{4,3,2,1,0:T(8,128)(2,1)} %param.12) | copy-start | bytes 786436
  63.2 4.8 %copy-start.26 = (bf16[512,128]{1,0:T(8,128)(2,1)}, bf16[512,128]{1,0:T(8,128)(2,1)S(1)}, u32[]{:S(2)}) copy-start(bf16[512,128]{1,0:T(8,128)(2,1)S(1)} %get-tuple-element.27) | copy-start | bytes 393220
  64.3 38.1 %copy-start.1 = (f32[512,512]{1,0:T(8,128)}, f32[512,512]{1,0:T(8,128)S(1)}, u32[]{:S(2)}) copy-start(f32[512,512]{1,0:T(8,128)S(1)} %fusion.15) | copy-start | bytes 3145732
  70.3 28.1 %copy-start.2 = (bf16[512,256]{1,0:T(8,128)(2,1)S(1)}, bf16[512,256]{1,0:T(8,128)(2,1)}, u32[]{:S(2)}) copy-start(bf16[512,256]{1,0:T(8,128)(2,1)} %param.19) | copy-start | bytes 786436
  73.7 24.8 %copy-start.24 = (bf16[2,128,256]{2,1,0:T(8,128)(2,1)S(1)}, bf16[2,128,256]{2,1,0:T(8,128)(2,1)}, u32[]{:S(2)}) copy-start(bf16[2,128,256]{2,1,0:T(8,128)(2,1)} %all_gather.12) | copy-start | bytes 393220
  100.4 2.7 %copy-start.13 = (bf16[512,256]{1,0:T(8,128)(2,1)S(1)}, bf16[512,256]{1,0:T(8,128)(2,1)}, u32[]{:S(2)}) copy-start(bf16[512,256]{1,0:T(8,128)(2,1)} %param.18) | copy-start | bytes 786436
  100.4 2.7 %copy-start.37 = (bf16[512]{0:T(512)(128)(2,1)S(1)}, bf16[512]{0:T(512)(128)(2,1)}, u32[]{:S(2)}) copy-start(bf16[512]{0:T(512)(128)(2,1)} %fusion.41) | copy-start | bytes 3076
  107.0 37.9 %reduce-scatter.9.cloned.1.call-start = ((), (), s32[]{:S(2)}) async-start(), calls=%async_computation.6 | async-start | bytes 81920 | tf_op jit(solution)/shard_map/reduce_scatter | solution.py:86
  107.0 2.9 %copy-start.25 = (bf16[2,128,256]{2,1,0:T(8,128)(2,1)S(1)}, bf16[2,128,256]{2,1,0:T(8,128)(2,1)}, u32[]{:S(2)}) copy-start(bf16[2,128,256]{2,1,0:T(8,128)(2,1)} %all_gather.12) | copy-start | bytes 393220
  109.9 56.9 %reduce-scatter.5.cloned.1.call-start = ((), (), s32[]{:S(2)}) async-start(), calls=%async_computation.4 | async-start | bytes 81920 | tf_op jit(solution)/shard_map/reduce_scatter | solution.py:86
  111.6 2.0 copy-start.11
  111.6 2.7 %copy-start.14 = (bf16[512,256]{1,0:T(8,128)(2,1)S(1)}, bf16[512,256]{1,0:T(8,128)(2,1)}, u32[]{:S(2)}) copy-start(bf16[512,256]{1,0:T(8,128)(2,1)} %param.18) | copy-start | bytes 786436
  120.1 4.7 %copy-start.5 = (bf16[512,512]{1,0:T(8,128)(2,1)S(1)}, bf16[512,512]{1,0:T(8,128)(2,1)}, u32[]{:S(2)}) copy-start(bf16[512,512]{1,0:T(8,128)(2,1)} %copy-done.4) | copy-start | bytes 1572868
  120.2 68.0 %reduce-scatter.7.cloned.1.call-start = ((), (), s32[]{:S(2)}) async-start(), calls=%async_computation.5 | async-start | bytes 81920 | tf_op jit(solution)/shard_map/reduce_scatter | solution.py:87
  123.1 106.8 %all-reduce.5.cloned.1.call-start = ((), (), s32[]{:S(2)}) async-start(), calls=%async_computation.8 | async-start | bytes 3670016 | tf_op jit(solution)/shard_map/psum | solution.py:91
  123.1 1.7 copy-start.19
  127.4 2.7 %copy-start.3 = (f32[384,512]{1,0:T(8,128)S(1)}, f32[384,512]{1,0:T(8,128)}, u32[]{:S(2)}) copy-start(f32[384,512]{1,0:T(8,128)} %fusion.16) | copy-start | bytes 2359300
  229.8 2.1 copy-start.7
  (19 other events, 18.2 us)
Sparse Core Ops, SparseCore 0:
  107.1 17.4 reduce-scatter.10
  127.2 17.6 reduce-scatter.8
  147.3 19.4 reduce-scatter.4
  169.0 19.1 reduce-scatter.6
Sparse Core Ops, SparseCore 1:
  134.3 95.5 all-reduce.4
where the time goes:
time: 242 us; the launch traced here: 241 us
  waiting for transfers between devices  92.6 us (38%)
  blocking collectives  72.5 us (30%)
  other arithmetic  23.3 us (10%)
  local copies, waits for them, and re-layouts  20.2 us (8%)
  between operations  16.4 us (7%)
  matrix products  16 us (7%)
    psum x1, waiting for transfers between devices, local(): lax.psum((grad_first, grad_second, grad_node), ('src', 'dst'))  40.3 us
    reduce_scatter x2, waiting for transfers between devices, local(): lax.psum_scatter(source_part, 'dst', scatter_dimension=0, tiled=True)  30.9 us
    psum x1, blocking collectives, local(): agg_block = lax.psum(partial_value, 'src')  24.8 us
    reduce_scatter x2, waiting for transfers between devices, local(): lax.psum_scatter(target_part, 'src', scatter_dimension=0, tiled=True)  21.4 us
    all_gather x1, blocking collectives, local(): lax.all_gather(cotangent, 'src', axis=1, tiled=True)  14.2 us
    all_gather x1, blocking collectives, local(): lax.all_gather(node_state, 'src', axis=1, tiled=True)  13.8 us
    all_gather x1, blocking collectives, local(): lax.all_gather(forcing, 'src', axis=1, tiled=True)  13.1 us
    unnamed x79, local copies, waits for them, and re-layouts  10.8 us
  transfers between devices with their start and end apart: 5, of which 4 were waited for; matrix products, arithmetic and copies ran while one was open for 11% of the time, Pallas kernels for 0%

commit v1 on v0

--- a/solution.py
+++ b/solution.py
@@ -1,9 +1,331 @@
+import functools
+
 import jax
 import jax.numpy as jnp
 from jax import lax
+from jax.experimental import pallas as pl
+from jax.experimental.pallas import tpu as pltpu
 from jax.sharding import PartitionSpec as P
 
 T_STEPS = 2
+WAYS = 4
+LANES = 128
+BF = jnp.bfloat16
+F32 = jnp.float32
+
+
+def sigmoid(value):
+    return 0.5 * jnp.tanh(0.5 * value) + 0.5
+
+
+def slope_of(value):
+    sigma = sigmoid(value)
+    return sigma * (1.0 + value * (1.0 - sigma))
+
+
+def mm(a, b):
+    return jnp.dot(a, b, preferred_element_type=F32)
+
+
+def mm_nt(a, b):
+    return lax.dot_general(a, b, (((1,), (1,)), ((), ())), preferred_element_type=F32)
+
+
+def mm_tn(a, b):
+    return lax.dot_general(a, b, (((0,), (0,)), ((), ())), preferred_element_type=F32)
+
+
+def one_hot_t(index, nodes, live=None):
+    hit = lax.broadcasted_iota(jnp.int32, (nodes, index.shape[1]), 0) == index
+    if live is not None:
+        hit = jnp.logical_and(hit, live)
+    return jnp.where(hit, 1.0, 0.0).astype(BF)
+
+
+def stacked(refs, moment):
+    return jnp.concatenate([ref[moment] for ref in refs], axis=0)
+
+
+def summed(refs, moment):
+    rows = refs[0].shape[1] // WAYS
+    return jnp.concatenate(
+        [
+            sum(ref[moment, (j ^ k) * rows : ((j ^ k) + 1) * rows].astype(F32) for k, ref in enumerate(refs))
+            for j in range(WAYS)
+        ],
+        axis=0,
+    )
+
+
+def selectors(place, src_index, dst_index, rows):
+    nodes = rows * WAYS
+    slots = src_index.shape[1]
+    live = lax.broadcasted_iota(jnp.int32, (1, slots), 1) < place[2]
+    src_t = one_hot_t(src_index[...] ^ (place[1] * rows), nodes)
+    dst_t = one_hot_t(dst_index[...] ^ (place[0] * rows), nodes, live)
+    dst_all = one_hot_t(dst_index[...] ^ (place[0] * rows), nodes)
+    return src_t, dst_t, dst_all
+
+
+def forward_kernel(place, *refs):
+    sources, targets = refs[:WAYS], refs[WAYS : 2 * WAYS]
+    attr, src_index, dst_index, w1, w2 = refs[2 * WAYS : 2 * WAYS + 5]
+    message, slope, *pieces, held = refs[2 * WAYS + 5 :]
+    rows, width = sources[0].shape[1], sources[0].shape[2]
+    src_t, dst_t, dst_all = selectors(place, src_index, dst_index, rows)
+    for moment in range(T_STEPS):
+        edge_in = jnp.concatenate(
+            [
+                mm_tn(src_t, stacked(sources, moment)).astype(BF),
+                mm_tn(dst_all, stacked(targets, moment)[:, :width]).astype(BF),
+                attr[moment],
+            ],
+            axis=1,
+        )
+        pre = mm(edge_in, w1[...])
+        sigma = sigmoid(pre)
+        hidden = (pre * sigma).astype(BF)
+        slope[moment] = sigma * (1.0 + pre * (1.0 - sigma))
+        sums = mm(dst_t, hidden).astype(BF)
+        held[moment] = sums
+        message[moment] = mm(sums, w2[...]).astype(BF)
+    block = w1.shape[1] // WAYS
+    for k in range(WAYS):
+        start = pl.multiple_of((place[0] ^ k) * block, block)
+        pieces[k][...] = held[:, :, pl.ds(start, block)]
+
+
+def backward_kernel(place, *refs):
+    n = WAYS
+    sources, targets, messages, pieces = refs[:n], refs[n : 2 * n], refs[2 * n : 3 * n], refs[3 * n : 4 * n]
+    attr, src_index, dst_index, slope, w1, w2, wn = refs[4 * n : 4 * n + 7]
+    outs = refs[4 * n + 7 :]
+    state_own, forcing_own, edges = outs[:3]
+    over_dst, over_src = outs[3 : 3 + n], outs[3 + n : 3 + 2 * n]
+    node_held, pre_held, agg_held, gpe_held, p_held, q_held, first = outs[3 + 2 * n :]
+    rows, width = sources[0].shape[1], sources[0].shape[2]
+    nodes = rows * n
+    slots = attr.shape[1]
+    width_m = w2.shape[1]
+    src_t, dst_t, _ = selectors(place, src_index, dst_index, rows)
+    for moment in range(T_STEPS):
+        at = slice(moment * nodes, (moment + 1) * nodes)
+        block = stacked(targets, moment)
+        state, forcing, cotangent = block[:, :width], block[:, width : 2 * width], block[:, 2 * width :]
+        agg = summed(messages, moment)
+        node_in = jnp.concatenate([state, agg.astype(BF), forcing], axis=1)
+        pre_node = mm(node_in, wn[...])
+        grad_pre = (cotangent.astype(F32) * slope_of(pre_node)).astype(BF)
+        node_held[at] = node_in
+        pre_held[at] = grad_pre
+        grad_in = mm_nt(grad_pre, wn[...])
+        state_own[moment] = grad_in[:rows, :width]
+        forcing_own[moment] = grad_in[:rows, width + width_m :]
+        grad_agg = grad_in[:, width : width + width_m].astype(BF)
+        agg_held[at] = grad_agg
+        grad_message = mm_tn(dst_t, grad_agg).astype(BF)
+        grad_pre_edge = (mm_nt(grad_message, w2[...]) * slope[moment]).astype(BF)
+        gpe_held[moment * slots : (moment + 1) * slots] = grad_pre_edge
+        edges[moment] = mm_nt(grad_pre_edge, w1[2 * width :])
+        from_src = mm(src_t, grad_pre_edge).astype(BF)
+        from_dst = mm(dst_t, grad_pre_edge).astype(BF)
+        p_held[at] = from_src
+        q_held[at] = from_dst
+        to_src = mm_nt(from_src, w1[:width]).astype(BF)
+        to_dst = mm_nt(from_dst, w1[width : 2 * width]).astype(BF)
+        half = rows // 2
+        for k in range(n):
+            for j in range(2):
+                lanes = slice((moment * 2 + j) * width, (moment * 2 + j + 1) * width)
+                spot = slice(k * rows + j * half, k * rows + (j + 1) * half)
+                over_dst[k][-half:, lanes] = to_src[spot]
+                over_src[k][:, lanes] = to_dst[spot]
+    states = jnp.concatenate([stacked(sources, moment) for moment in range(T_STEPS)], axis=0)
+    first[:width] = mm_tn(states, p_held[...])
+    first[width : 2 * width] = mm_tn(node_held[:, :width], q_held[...])
+    first[2 * width :] = mm_tn(attr[...].reshape(T_STEPS * slots, width), gpe_held[...])
+    block = wn.shape[0] // n
+    spot = pl.multiple_of(place[0] * block, block)
+    node_grad = mm_tn(node_held[:, pl.ds(spot, block)], pre_held[...])
+    sums = jnp.concatenate([summed(pieces, moment) for moment in range(T_STEPS)], axis=0).astype(BF)
+    second = mm_tn(sums, agg_held[...])
+    both = jnp.concatenate([second, node_grad], axis=1)
+    part = first.shape[0] // n
+    small = block // n
+
+    for k in range(n):
+        other = place[1] ^ k
+        over_dst[k][:part] = first[pl.ds(pl.multiple_of(other * part, part), part)].astype(BF)
+    for j in range(n):
+        for k in range(n):
+            @pl.when((place[1] ^ k) == j)
+            def _(j=j, k=k):
+                over_dst[k][part : part + small] = both[j * small : (j + 1) * small].astype(BF)
+
+
+def middle_kernel(state_own, *refs):
+    n = WAYS
+    parts, pieces = refs[:n], refs[n : 2 * n]
+    state_sum, own, *sent = refs[2 * n :]
+    total = sum(ref[...].astype(F32) for ref in parts)
+    half = pieces[0].shape[0]
+    width = state_own.shape[2]
+    core = total[:-half]
+    own[...] = core
+    rounded = core.astype(BF)
+    nodes = total[-half:] + pieces[0][...].astype(F32)
+    for moment in range(T_STEPS):
+        for j in range(2):
+            lanes = slice((moment * 2 + j) * width, (moment * 2 + j + 1) * width)
+            spot = slice(j * half, (j + 1) * half)
+            state_sum[moment, spot] = state_own[moment, spot] + nodes[:, lanes]
+    for k in range(1, n):
+        sent[k - 1][:-half] = rounded
+        sent[k - 1][-half:] = pieces[k][...]
+
+
+def gather_kernel(place, state_sum, own, *refs):
+    n = WAYS
+    arrived = refs[: n - 1]
+    state, sent = refs[n - 1 :]
+    width = state_sum.shape[2]
+    half = state_sum.shape[1] // 2
+    wide = own.shape[0]
+    small = (sent.shape[0] - wide) // (n - 1)
+    part = wide - small
+    nodes = sum(ref[wide:].astype(F32) for ref in arrived)
+    for moment in range(T_STEPS):
+        for j in range(2):
+            lanes = slice((moment * 2 + j) * width, (moment * 2 + j + 1) * width)
+            spot = slice(j * half, (j + 1) * half)
+            state[moment, spot] = state_sum[moment, spot] + nodes[:, lanes]
+    first = own[:part] + sum(ref[:part].astype(F32) for ref in arrived)
+    sent[:part] = first.astype(BF)
+    for k in range(n):
+        start = pl.multiple_of(part + (place[0] ^ k) * small, small)
+        sent[pl.ds(start, small)] = own[part:].astype(BF) if k == 0 else arrived[k - 1][part:wide]
+
+
+def final_kernel(place, *refs):
+    n = WAYS
+    arrived = refs[:n]
+    first, second, node = refs[n:]
+    part = first.shape[0] // n
+    small = second.shape[0] // n // n
+    half = second.shape[1]
+    for k in range(n):
+        other = place[1] ^ k
+        first[pl.ds(pl.multiple_of(other * part, part), part)] = arrived[k][:part].astype(F32)
+        for j in range(n):
+            rows = arrived[k][part + j * small : part + (j + 1) * small].astype(F32)
+            start = pl.multiple_of((j * n + other) * small, small)
+            second[pl.ds(start, small)] = rows[:, :half]
+            node[pl.ds(start, small)] = rows[:, half:]
+
+
+def call(kernel, outs, scratch, args, scalars=True):
+    in_specs = [pl.BlockSpec(memory_space=pltpu.SMEM)] if scalars else []
+    in_specs += [pl.BlockSpec(memory_space=pltpu.VMEM)] * (len(args) - len(in_specs))
+    return pl.pallas_call(
+        kernel,
+        out_shape=[jax.ShapeDtypeStruct(shape, dtype) for shape, dtype in outs],
+        in_specs=in_specs,
+        out_specs=[pl.BlockSpec(memory_space=pltpu.VMEM)] * len(outs),
+        scratch_shapes=[pltpu.VMEM(shape, dtype) for shape, dtype in scratch],
+        compiler_params=pltpu.CompilerParams(vmem_limit_bytes=48 << 20),
+    )(*args)
+
+
+def swap(value, axis, k):
+    return lax.ppermute(value, axis, [(i, i ^ k) for i in range(WAYS)])
+
+
+def fan(value, axis):
+    return [value] + [swap(value, axis, k) for k in range(1, WAYS)]
+
+
+def exchange(values, axis):
+    return [values[0]] + [swap(values[k], axis, k) for k in range(1, WAYS)]
+
+
+def local(
+    node_state,
+    forcing,
+    edge_attr,
+    src_index,
+    dst_index,
+    edge_count,
+    cotangent,
+    edge_w1,
+    edge_w2,
+    node_w1,
+):
+    rows, width = node_state.shape[1:]
+    hid, width_m = edge_w2.shape
+    width_in, width_out = node_w1.shape
+    slots = edge_attr.shape[3]
+    nodes = rows * WAYS
+    steps = T_STEPS
+    place = jnp.stack(
+        [lax.axis_index("src"), lax.axis_index("dst"), edge_count[0, 0]]
+    ).astype(jnp.int32)
+    attr = edge_attr[:, 0, 0]
+    src_row, dst_row = src_index[0], dst_index[0]
+    sources = fan(node_state, "dst")
+    targets = fan(jnp.concatenate([node_state, forcing, cotangent], axis=2), "src")
+    block = hid // WAYS
+    message, slope, *pieces = call(
+        forward_kernel,
+        [((steps, nodes, width_m), BF), ((steps, slots, hid), F32)]
+        + [((steps, nodes, block), BF)] * WAYS,
+        [((steps, nodes, hid), BF)],
+        [place, *sources, *targets, attr, src_row, dst_row, edge_w1, edge_w2],
+    )
+    messages = fan(message, "src")
+    pieces = exchange(pieces, "src")
+    part = edge_w1.shape[0] // WAYS
+    small = block // WAYS
+    half = rows // 2
+    wide = part + small
+    state_own, grad_forcing, edges, *sent = call(
+        backward_kernel,
+        [((steps, rows, width), F32), ((steps, rows, width), F32), ((steps, slots, width), F32)]
+        + [((wide + half, hid), BF)] * WAYS
+        + [((half, hid), BF)] * WAYS,
+        [
+            ((steps * nodes, width_in), BF),
+            ((steps * nodes, width_out), BF),
+            ((steps * nodes, width_m), BF),
+            ((steps * slots, hid), BF),
+            ((steps * nodes, hid), BF),
+            ((steps * nodes, hid), BF),
+            (edge_w1.shape, F32),
+        ],
+        [place, *sources, *targets, *messages, *pieces, attr, src_row, dst_row, slope, edge_w1, edge_w2, node_w1],
+    )
+    over_dst, over_src = sent[:WAYS], sent[WAYS:]
+    state_sum, own, *sent = call(
+        middle_kernel,
+        [((steps, rows, width), F32), ((wide, hid), F32)] + [((wide + half, hid), BF)] * (WAYS - 1),
+        [],
+        [state_own, *exchange(over_dst, "dst"), *over_src],
+        scalars=False,
+    )
+    arrived = [swap(sent[k - 1], "src", k) for k in range(1, WAYS)]
+    grad_state, share = call(
+        gather_kernel,
+        [((steps, rows, width), F32), ((wide + (WAYS - 1) * small, hid), BF)],
+        [],
+        [place, state_sum, own, *arrived],
+    )
+    across = swap(share, "dst", 2)
+    grad_first, grad_second, grad_node = call(
+        final_kernel,
+        [(edge_w1.shape, F32), (edge_w2.shape, F32), (node_w1.shape, F32)],
+        [],
+        [place, share, swap(share, "dst", 1), across, swap(across, "dst", 1)],
+    )
+    return grad_state, grad_forcing, edges[:, None, None], grad_first, grad_second, grad_node
 
 
 def silu_slope(value):
@@ -11,7 +333,7 @@
     return sigma * (1.0 + value * (1.0 - sigma))
 
 
-def local(
+def local_any(
     node_state,
     forcing,
     edge_attr,
@@ -122,4 +444,6 @@
         P("groups", None),
         P("groups", None),
     )
-    return jax.shard_map(local, mesh=mesh, in_specs=in_specs, out_specs=out_specs, check_vma=False)
+    square = mesh.shape["src"] == WAYS and mesh.shape["dst"] == WAYS
+    body = local if square else local_any
+    return jax.shard_map(body, mesh=mesh, in_specs=in_specs, out_specs=out_specs, check_vma=False)

time: 242 us -> 84.1 us (0.35)
  blocking collectives: 72.5 us -> 0 us
  waiting for transfers between devices: 92.6 us -> 40.6 us
  other arithmetic: 23.3 us -> 0.08 us
  starting transfers between devices: 0.21 us -> 23.2 us
  matrix products: 16 us -> 0 us
  between operations: 16.4 us -> 1.35 us
  local copies, waits for them, and re-layouts: 20.2 us -> 8.16 us
  Pallas kernels: 0 us -> 9.65 us
    reduce_scatter x4 -> x0, waiting for transfers between devices: 52.2 us -> none  [the longest x2 30.9 us: local(): lax.psum_scatter(source_part, 'dst', scatter_dimension=0, tiled=True)]
    all_gather x4 -> x0, blocking collectives: 47.7 us -> none  [the longest x1 14.2 us: local(): lax.all_gather(cotangent, 'src', axis=1, tiled=True)]
    ppermute x0 -> x21, waiting for transfers between devices: none -> 40.6 us  [swap(): return lax.ppermute(value, axis, [(i, i ^ k) for i in range(WAYS)])]
    psum x1 -> x0, waiting for transfers between devices: 40.3 us -> none  [local(): lax.psum((grad_first, grad_second, grad_node), ('src', 'dst'))]
    psum x1 -> x0, blocking collectives: 24.8 us -> none  [local(): agg_block = lax.psum(partial_value, 'src')]
    ppermute x0 -> x21, starting transfers between devices: none -> 23.2 us  [swap(): return lax.ppermute(value, axis, [(i, i ^ k) for i in range(WAYS)])]
    scatter-add x6 -> x0, other arithmetic: 18.1 us -> none  [the longest x2 6.68 us: local(): jax.ops.segment_sum(message, dst_local, num_segments=dst_rows)]
    dot_general x18 -> x0, matrix products: 16 us -> none  [the longest x2 3.97 us: local(): jnp.dot(hidden.T, grad_message, preferred_element_type=jnp.float32)]
  transfers between devices with their start and end apart: 5 -> 21, of which waited for: 4 -> 10; matrix products, arithmetic and copies ran while one was open for 11% -> 3% of each run, Pallas kernels for 0% -> 0%
where the time goes in v1:
time: 84.1 us; the launch traced here: 83 us
  waiting for transfers between devices  40.6 us (48%)
  starting transfers between devices  23.2 us (28%)
  Pallas kernels  9.65 us (11%)
  local copies, waits for them, and re-layouts  8.16 us (10%)
  between operations  1.35 us (2%)
    ppermute x21, waiting for transfers between devices, swap(): return lax.ppermute(value, axis, [(i, i ^ k) for i in range(WAYS)])  40.6 us
    ppermute x21, starting transfers between devices, swap(): return lax.ppermute(value, axis, [(i, i ^ k) for i in range(WAYS)])  23.2 us
    pallas_call x5, Pallas kernels, call(): pl.pallas_call(kernel, out_shape=[jax.ShapeDtypeStruct(shape, dtype) for...  9.65 us
    unnamed x16, local copies, waits for them, and re-layouts  7.4 us
  transfers between devices with their start and end apart: 21, of which 10 were waited for; matrix products, arithmetic and copies ran while one was open for 3% of the time, Pallas kernels for 0%

profile of v1, /device:TPU:0, one launch (start us, length us, event | category | flops | bytes accessed | tf_op | source)
XLA Modules:
  0.0 83.0 jit_solution(4357357570682561534)
XLA Ops:
  0.6 2.4 %collective-permute-start.2 = (bf16[2,32,128]{2,1,0:T(8,128)(2,1)}, bf16[2,32,128]{2,1,0:T(8,128)(2,1)S(1)}, u32[]{:S(2)}, u32[]{:S(2)}) collective-permute-start(bf16[2,32,128]{2,1,0:T(8,128)(2,1)} %refs_0_.3), channel_id=1, source_target_pairs={{0,3},{1,2},{2,1},{3,0},{4,7},{5,6},{6,5},{7,4},{8,11},{9,10},{10,... | collective-permute-start | bytes 49160 | tf_op jit(solution)/shard_map/ppermute | solution.py:240
  6.0 3.8 %collective-permute-start.5 = (bf16[2,32,512]{2,1,0:T(8,128)(2,1)S(1)}, bf16[2,32,512]{2,1,0:T(8,128)(2,1)S(1)}, u32[]{:S(2)}, u32[]{:S(2)}) collective-permute-start(bf16[2,32,512]{2,1,0:T(8,128)(2,1)S(1)} %constant_dynamic-update-slice_fusion.refs_4_), channel_id=1, source_target_pairs={{0,12},{4,8},{8,4},{12,0},{1,13},{5,9},{9,5},{13,1},{2,14},{6,10},... | collective-permute-start | bytes 196616 | tf_op jit(solution)/shard_map/ppermute | solution.py:240
  11.2 1.3 %collective-permute-done.5.refs_7_ = bf16[2,32,512]{2,1,0:T(8,128)(2,1)S(1)} collective-permute-done((bf16[2,32,512]{2,1,0:T(8,128)(2,1)S(1)}, bf16[2,32,512]{2,1,0:T(8,128)(2,1)S(1)}, u32[]{:S(2)}, u32[]{:S(2)}) %collective-permute-start.5) | collective-permute-done | bytes 65568 | tf_op jit(solution)/shard_map/ppermute | solution.py:240
  12.5 3.3 %collective-permute-done.4.refs_6_ = bf16[2,32,512]{2,1,0:T(8,128)(2,1)S(1)} collective-permute-done((bf16[2,32,512]{2,1,0:T(8,128)(2,1)S(1)}, bf16[2,32,512]{2,1,0:T(8,128)(2,1)S(1)}, u32[]{:S(2)}, u32[]{:S(2)}) %collective-permute-start.4) | collective-permute-done | bytes 65568 | tf_op jit(solution)/shard_map/ppermute | solution.py:240
  21.2 2.6 %shard_map.145 = (bf16[2,128,256]{2,1,0:T(8,128)(2,1)S(1)}, f32[2,512,512]{2,1,0:T(8,128)S(1)}, bf16[2,128,128]{2,1,0:T(8,128)(2,1)S(1)}, bf16[2,128,128]{2,1,0:...) custom-call(s32[3]{0:T(128)S(1)} %pad_add_fusion.place, ...), custom_call_target="tpu_custom_call" | custom-call | tf_op jit(solution)/shard_map/pallas_call | solution.py:229
  24.5 2.3 %collective-permute-start.8 = (bf16[2,128,256]{2,1,0:T(8,128)(2,1)S(1)}, bf16[2,128,256]{2,1,0:T(8,128)(2,1)S(1)}, u32[]{:S(2)}, u32[]{:S(2)}) collective-permute-start(bf16[2,128,256]{2,1,0:T(8,128)(2,1)S(1)} %get-tuple-element.33.refs_8_), channel_id=1, source_target_pairs={{0,12},{4,8},{8,4},{12,0},{1,13},{5,9},{9,5},{13,1},{2,14},{6,10},... | collective-permute-start | bytes 393224 | tf_op jit(solution)/shard_map/ppermute | solution.py:240
  27.3 1.6 %collective-permute-start.6 = (bf16[2,128,256]{2,1,0:T(8,128)(2,1)S(1)}, bf16[2,128,256]{2,1,0:T(8,128)(2,1)S(1)}, u32[]{:S(2)}, u32[]{:S(2)}) collective-permute-start(bf16[2,128,256]{2,1,0:T(8,128)(2,1)S(1)} %get-tuple-element.33.refs_8_), channel_id=1, source_target_pairs={{0,4},{4,0},{8,12},{12,8},{1,5},{5,1},{9,13},{13,9},{2,6},{6,2},{1... | collective-permute-start | bytes 393224 | tf_op jit(solution)/shard_map/ppermute | solution.py:240
  28.9 1.1 %collective-permute-start.10 = (bf16[2,128,128]{2,1,0:T(8,128)(2,1)S(1)}, bf16[2,128,128]{2,1,0:T(8,128)(2,1)S(1)}, u32[]{:S(2)}, u32[]{:S(2)}) collective-permute-start(bf16[2,128,128]{2,1,0:T(8,128)(2,1)S(1)} %get-tuple-element.36), channel_id=1, source_target_pairs={{0,8},{4,12},{8,0},{12,4},{1,9},{5,13},{9,1},{13,5},{2,10},{6,14},... | collective-permute-start | bytes 196616 | tf_op jit(solution)/shard_map/ppermute | solution.py:240
  30.0 1.7 %collective-permute-start.11 = (bf16[2,128,128]{2,1,0:T(8,128)(2,1)S(1)}, bf16[2,128,128]{2,1,0:T(8,128)(2,1)S(1)}, u32[]{:S(2)}, u32[]{:S(2)}) collective-permute-start(bf16[2,128,128]{2,1,0:T(8,128)(2,1)S(1)} %get-tuple-element.37), channel_id=1, source_target_pairs={{0,12},{4,8},{8,4},{12,0},{1,13},{5,9},{9,5},{13,1},{2,14},{6,10},... | collective-permute-start | bytes 196616 | tf_op jit(solution)/shard_map/ppermute | solution.py:240
  31.7 11.4 %collective-permute-done.10.refs_14_ = bf16[2,128,128]{2,1,0:T(8,128)(2,1)S(1)} collective-permute-done((bf16[2,128,128]{2,1,0:T(8,128)(2,1)S(1)}, bf16[2,128,128]{2,1,0:T(8,128)(2,1)S(1)}, u32[]{:S(2)}, u32[]{:S(2)}) %collective-permute-start.10) | collective-permute-done | bytes 65568 | tf_op jit(solution)/shard_map/ppermute | solution.py:240
  44.1 3.9 %shard_map.146 = (f32[2,32,128]{2,1,0:T(8,128)S(1)}, f32[2,32,128]{2,1,0:T(8,128)}, f32[2,512,128]{2,1,0:T(8,128)}, bf16[144,512]{1,0:T(8,128)(2,1)S(1)}, bf16[1...) custom-call(s32[3]{0:T(128)S(1)} %pad_add_fusion.place, ...), custom_call_target="tpu_custom_call" | custom-call | tf_op jit(solution)/shard_map/pallas_call | solution.py:229
  48.0 1.3 %collective-permute-start.13 = (bf16[144,512]{1,0:T(8,128)(2,1)S(1)}, bf16[144,512]{1,0:T(8,128)(2,1)S(1)}, u32[]{:S(2)}, u32[]{:S(2)}) collective-permute-start(bf16[144,512]{1,0:T(8,128)(2,1)S(1)} %get-tuple-element.42), channel_id=1, source_target_pairs={{0,2},{1,3},{2,0},{3,1},{4,6},{5,7},{6,4},{7,5},{8,10},{9,11},{10,... | collective-permute-start | bytes 442376 | tf_op jit(solution)/shard_map/ppermute | solution.py:240
  49.8 4.8 %collective-permute-done.13.refs_2_ = bf16[144,512]{1,0:T(8,128)(2,1)S(1)} collective-permute-done((bf16[144,512]{1,0:T(8,128)(2,1)S(1)}, bf16[144,512]{1,0:T(8,128)(2,1)S(1)}, u32[]{:S(2)}, u32[]{:S(2)}) %collective-permute-start.13) | collective-permute-done | bytes 147488 | tf_op jit(solution)/shard_map/ppermute | solution.py:240
  54.6 2.4 %collective-permute-done.14.refs_3_ = bf16[144,512]{1,0:T(8,128)(2,1)S(1)} collective-permute-done((bf16[144,512]{1,0:T(8,128)(2,1)S(1)}, bf16[144,512]{1,0:T(8,128)(2,1)S(1)}, u32[]{:S(2)}, u32[]{:S(2)}) %collective-permute-start.14) | collective-permute-done | bytes 147488 | tf_op jit(solution)/shard_map/ppermute | solution.py:240
  57.1 1.3 %collective-permute-start.15 = (bf16[144,512]{1,0:T(8,128)(2,1)S(1)}, bf16[144,512]{1,0:T(8,128)(2,1)S(1)}, u32[]{:S(2)}, u32[]{:S(2)}) collective-permute-start(bf16[144,512]{1,0:T(8,128)(2,1)S(1)} %get-tuple-element.50), channel_id=1, source_target_pairs={{0,4},{4,0},{8,12},{12,8},{1,5},{5,1},{9,13},{13,9},{2,6},{6,2},{1... | collective-permute-start | bytes 442376 | tf_op jit(solution)/shard_map/ppermute | solution.py:240
  58.4 1.4 %collective-permute-start.16 = (bf16[144,512]{1,0:T(8,128)(2,1)S(1)}, bf16[144,512]{1,0:T(8,128)(2,1)S(1)}, u32[]{:S(2)}, u32[]{:S(2)}) collective-permute-start(bf16[144,512]{1,0:T(8,128)(2,1)S(1)} %get-tuple-element.51), channel_id=1, source_target_pairs={{0,8},{4,12},{8,0},{12,4},{1,9},{5,13},{9,1},{13,5},{2,10},{6,14},... | collective-permute-start | bytes 442376 | tf_op jit(solution)/shard_map/ppermute | solution.py:240
  59.8 1.8 %collective-permute-start.17 = (bf16[144,512]{1,0:T(8,128)(2,1)S(1)}, bf16[144,512]{1,0:T(8,128)(2,1)S(1)}, u32[]{:S(2)}, u32[]{:S(2)}) collective-permute-start(bf16[144,512]{1,0:T(8,128)(2,1)S(1)} %get-tuple-element.52), channel_id=1, source_target_pairs={{0,12},{4,8},{8,4},{12,0},{1,13},{5,9},{9,5},{13,1},{2,14},{6,10},... | collective-permute-start | bytes 442376 | tf_op jit(solution)/shard_map/ppermute | solution.py:240
  61.6 4.0 %collective-permute-done.15.refs_0_ = bf16[144,512]{1,0:T(8,128)(2,1)S(1)} collective-permute-done((bf16[144,512]{1,0:T(8,128)(2,1)S(1)}, bf16[144,512]{1,0:T(8,128)(2,1)S(1)}, u32[]{:S(2)}, u32[]{:S(2)}) %collective-permute-start.15) | collective-permute-done | bytes 147488 | tf_op jit(solution)/shard_map/ppermute | solution.py:240
  65.5 6.8 %collective-permute-done.16.refs_1_ = bf16[144,512]{1,0:T(8,128)(2,1)S(1)} collective-permute-done((bf16[144,512]{1,0:T(8,128)(2,1)S(1)}, bf16[144,512]{1,0:T(8,128)(2,1)S(1)}, u32[]{:S(2)}, u32[]{:S(2)}) %collective-permute-start.16) | collective-permute-done | bytes 147488 | tf_op jit(solution)/shard_map/ppermute | solution.py:240
  72.4 1.2 %shard_map.148 = (f32[2,32,128]{2,1,0:T(8,128)}, bf16[224,512]{1,0:T(8,128)(2,1)S(1)}) custom-call(s32[3]{0:T(128)S(1)} %pad_add_fusion.place, f32[2,32,128]{2,1,0:T(8,128)S(1)} %get-tuple-element.48.state_sum, f32[128,512]{1,0:T(8,128)S(1)} %get-tuple-element.49.own, bf16[144,512]{1,0:T(8,128)(2,1)S(1)} %collective-permute-done.15.refs_0_, ...), custom_call_target="tpu_custom_call" | custom-call | tf_op jit(solution)/shard_map/pallas_call | solution.py:229
  73.6 1.3 %collective-permute-start.19 = (bf16[224,512]{1,0:T(8,128)(2,1)S(1)}, bf16[224,512]{1,0:T(8,128)(2,1)S(1)}, u32[]{:S(2)}, u32[]{:S(2)}) collective-permute-start(bf16[224,512]{1,0:T(8,128)(2,1)S(1)} %get-tuple-element.56.refs_0_), channel_id=1, source_target_pairs={{0,2},{1,3},{2,0},{3,1},{4,6},{5,7},{6,4},{7,5},{8,10},{9,11},{10,... | collective-permute-start | bytes 688136 | tf_op jit(solution)/shard_map/ppermute | solution.py:240
  74.9 4.7 %collective-permute-done.19.refs_2_ = bf16[224,512]{1,0:T(8,128)(2,1)S(1)} collective-permute-done((bf16[224,512]{1,0:T(8,128)(2,1)S(1)}, bf16[224,512]{1,0:T(8,128)(2,1)S(1)}, u32[]{:S(2)}, u32[]{:S(2)}) %collective-permute-start.19) | collective-permute-done | bytes 229408 | tf_op jit(solution)/shard_map/ppermute | solution.py:240
  79.6 1.5 %collective-permute-done.20.refs_3_ = bf16[224,512]{1,0:T(8,128)(2,1)S(1)} collective-permute-done((bf16[224,512]{1,0:T(8,128)(2,1)S(1)}, bf16[224,512]{1,0:T(8,128)(2,1)S(1)}, u32[]{:S(2)}, u32[]{:S(2)}) %collective-permute-start.20) | collective-permute-done | bytes 229408 | tf_op jit(solution)/shard_map/ppermute | solution.py:240
  81.1 1.9 %shard_map.149 = (f32[384,512]{1,0:T(8,128)}, f32[512,256]{1,0:T(8,128)}, f32[512,256]{1,0:T(8,128)}) custom-call(s32[3]{0:T(128)S(1)} %pad_add_fusion.place, bf16[224,512]{1,0:T(8,128)(2,1)S(1)} %get-tuple-element.56.refs_0_, bf16[224,512]{1,0:T(8,128)(2,1)S(1)} %collective-permute-done.18.refs_1_, bf16[224,512]{1,0:T(8,128)(2,1)S(1)} %collective-permute-done.19.refs_2_, ...), custom_call_target="tpu_custom_call" | custom-call | tf_op jit(solution)/shard_map/pallas_call | solution.py:229
  (41 shorter events, 11.8 us)
Async XLA Ops:
  0.6 9.8 %collective-permute-start.2 = (bf16[2,32,128]{2,1,0:T(8,128)(2,1)}, bf16[2,32,128]{2,1,0:T(8,128)(2,1)S(1)}, u32[]{:S(2)}, u32[]{:S(2)}) collective-permute-start(bf16[2,32,128]{2,1,0:T(8,128)(2,1)} %refs_0_.3), channel_id=1, source_target_pairs={{0,3},{1,2},{2,1},{3,0},{4,7},{5,6},{6,5},{7,4},{8,11},{9,10},{10,... | collective-permute-start | bytes 49160 | tf_op jit(solution)/shard_map/ppermute | solution.py:240
  3.1 8.1 %collective-permute-start.1 = (bf16[2,32,128]{2,1,0:T(8,128)(2,1)}, bf16[2,32,128]{2,1,0:T(8,128)(2,1)S(1)}, u32[]{:S(2)}, u32[]{:S(2)}) collective-permute-start(bf16[2,32,128]{2,1,0:T(8,128)(2,1)} %refs_0_.3), channel_id=1, source_target_pairs={{0,2},{1,3},{2,0},{3,1},{4,6},{5,7},{6,4},{7,5},{8,10},{9,11},{10,... | collective-permute-start | bytes 49160 | tf_op jit(solution)/shard_map/ppermute | solution.py:240
  3.7 7.5 %collective-permute-start = (bf16[2,32,128]{2,1,0:T(8,128)(2,1)}, bf16[2,32,128]{2,1,0:T(8,128)(2,1)S(1)}, u32[]{:S(2)}, u32[]{:S(2)}) collective-permute-start(bf16[2,32,128]{2,1,0:T(8,128)(2,1)} %refs_0_.3), channel_id=1, source_target_pairs={{0,1},{1,0},{2,3},{3,2},{4,5},{5,4},{6,7},{7,6},{8,9},{9,8},{10,11... | collective-permute-start | bytes 49160 | tf_op jit(solution)/shard_map/ppermute | solution.py:240
  6.0 6.5 %collective-permute-start.5 = (bf16[2,32,512]{2,1,0:T(8,128)(2,1)S(1)}, bf16[2,32,512]{2,1,0:T(8,128)(2,1)S(1)}, u32[]{:S(2)}, u32[]{:S(2)}) collective-permute-start(bf16[2,32,512]{2,1,0:T(8,128)(2,1)S(1)} %constant_dynamic-update-slice_fusion.refs_4_), channel_id=1, source_target_pairs={{0,12},{4,8},{8,4},{12,0},{1,13},{5,9},{9,5},{13,1},{2,14},{6,10},... | collective-permute-start | bytes 196616 | tf_op jit(solution)/shard_map/ppermute | solution.py:240
  9.8 6.0 %collective-permute-start.4 = (bf16[2,32,512]{2,1,0:T(8,128)(2,1)S(1)}, bf16[2,32,512]{2,1,0:T(8,128)(2,1)S(1)}, u32[]{:S(2)}, u32[]{:S(2)}) collective-permute-start(bf16[2,32,512]{2,1,0:T(8,128)(2,1)S(1)} %constant_dynamic-update-slice_fusion.refs_4_), channel_id=1, source_target_pairs={{0,8},{4,12},{8,0},{12,4},{1,9},{5,13},{9,1},{13,5},{2,10},{6,14},... | collective-permute-start | bytes 196616 | tf_op jit(solution)/shard_map/ppermute | solution.py:240
  10.5 5.7 %collective-permute-start.3 = (bf16[2,32,512]{2,1,0:T(8,128)(2,1)S(1)}, bf16[2,32,512]{2,1,0:T(8,128)(2,1)S(1)}, u32[]{:S(2)}, u32[]{:S(2)}) collective-permute-start(bf16[2,32,512]{2,1,0:T(8,128)(2,1)S(1)} %constant_dynamic-update-slice_fusion.refs_4_), channel_id=1, source_target_pairs={{0,4},{4,0},{8,12},{12,8},{1,5},{5,1},{9,13},{13,9},{2,6},{6,2},{1... | collective-permute-start | bytes 196616 | tf_op jit(solution)/shard_map/ppermute | solution.py:240
  16.2 1.0 %copy-start = (bf16[384,512]{1,0:T(8,128)(2,1)S(1)}, bf16[384,512]{1,0:T(8,128)(2,1)}, u32[]{:S(2)}) copy-start(bf16[384,512]{1,0:T(8,128)(2,1)} %refs_20_.1) | copy-start | bytes 1179652
  17.2 0.9 %copy-start.1 = (bf16[2,1,1,512,128]{4,3,2,1,0:T(8,128)(2,1)S(1)}, bf16[2,1,1,512,128]{4,3,2,1,0:T(8,128)(2,1)}, u32[]{:S(2)}) copy-start(bf16[2,1,1,512,128]{4,3,2,1,0:T(8,128)(2,1)} %param.12) | copy-start | bytes 786436
  23.8 6.2 %collective-permute-start.9 = (bf16[2,128,128]{2,1,0:T(8,128)(2,1)S(1)}, bf16[2,128,128]{2,1,0:T(8,128)(2,1)S(1)}, u32[]{:S(2)}, u32[]{:S(2)}) collective-permute-start(bf16[2,128,128]{2,1,0:T(8,128)(2,1)S(1)} %get-tuple-element.35), channel_id=1, source_target_pairs={{0,4},{4,0},{8,12},{12,8},{1,5},{5,1},{9,13},{13,9},{2,6},{6,2},{1... | collective-permute-start | bytes 196616 | tf_op jit(solution)/shard_map/ppermute | solution.py:240
  24.5 18.6 %collective-permute-start.8 = (bf16[2,128,256]{2,1,0:T(8,128)(2,1)S(1)}, bf16[2,128,256]{2,1,0:T(8,128)(2,1)S(1)}, u32[]{:S(2)}, u32[]{:S(2)}) collective-permute-start(bf16[2,128,256]{2,1,0:T(8,128)(2,1)S(1)} %get-tuple-element.33.refs_8_), channel_id=1, source_target_pairs={{0,12},{4,8},{8,4},{12,0},{1,13},{5,9},{9,5},{13,1},{2,14},{6,10},... | collective-permute-start | bytes 393224 | tf_op jit(solution)/shard_map/ppermute | solution.py:240
  26.9 16.3 %collective-permute-start.7 = (bf16[2,128,256]{2,1,0:T(8,128)(2,1)S(1)}, bf16[2,128,256]{2,1,0:T(8,128)(2,1)S(1)}, u32[]{:S(2)}, u32[]{:S(2)}) collective-permute-start(bf16[2,128,256]{2,1,0:T(8,128)(2,1)S(1)} %get-tuple-element.33.refs_8_), channel_id=1, source_target_pairs={{0,8},{4,12},{8,0},{12,4},{1,9},{5,13},{9,1},{13,5},{2,10},{6,14},... | collective-permute-start | bytes 393224 | tf_op jit(solution)/shard_map/ppermute | solution.py:240
  27.3 15.8 %collective-permute-start.6 = (bf16[2,128,256]{2,1,0:T(8,128)(2,1)S(1)}, bf16[2,128,256]{2,1,0:T(8,128)(2,1)S(1)}, u32[]{:S(2)}, u32[]{:S(2)}) collective-permute-start(bf16[2,128,256]{2,1,0:T(8,128)(2,1)S(1)} %get-tuple-element.33.refs_8_), channel_id=1, source_target_pairs={{0,4},{4,0},{8,12},{12,8},{1,5},{5,1},{9,13},{13,9},{2,6},{6,2},{1... | collective-permute-start | bytes 393224 | tf_op jit(solution)/shard_map/ppermute | solution.py:240
  28.9 14.2 %collective-permute-start.10 = (bf16[2,128,128]{2,1,0:T(8,128)(2,1)S(1)}, bf16[2,128,128]{2,1,0:T(8,128)(2,1)S(1)}, u32[]{:S(2)}, u32[]{:S(2)}) collective-permute-start(bf16[2,128,128]{2,1,0:T(8,128)(2,1)S(1)} %get-tuple-element.36), channel_id=1, source_target_pairs={{0,8},{4,12},{8,0},{12,4},{1,9},{5,13},{9,1},{13,5},{2,10},{6,14},... | collective-permute-start | bytes 196616 | tf_op jit(solution)/shard_map/ppermute | solution.py:240
  30.0 13.1 %collective-permute-start.11 = (bf16[2,128,128]{2,1,0:T(8,128)(2,1)S(1)}, bf16[2,128,128]{2,1,0:T(8,128)(2,1)S(1)}, u32[]{:S(2)}, u32[]{:S(2)}) collective-permute-start(bf16[2,128,128]{2,1,0:T(8,128)(2,1)S(1)} %get-tuple-element.37), channel_id=1, source_target_pairs={{0,12},{4,8},{8,4},{12,0},{1,13},{5,9},{9,5},{13,1},{2,14},{6,10},... | collective-permute-start | bytes 196616 | tf_op jit(solution)/shard_map/ppermute | solution.py:240
  43.1 1.0 %copy-start.3 = (bf16[512,256]{1,0:T(8,128)(2,1)S(1)}, bf16[512,256]{1,0:T(8,128)(2,1)}, u32[]{:S(2)}) copy-start(bf16[512,256]{1,0:T(8,128)(2,1)} %refs_22_.1) | copy-start | bytes 786436
  48.0 1.9 %collective-permute-start.12 = (bf16[144,512]{1,0:T(8,128)(2,1)S(1)}, bf16[144,512]{1,0:T(8,128)(2,1)S(1)}, u32[]{:S(2)}, u32[]{:S(2)}) collective-permute-start(bf16[144,512]{1,0:T(8,128)(2,1)S(1)} %get-tuple-element.41), channel_id=1, source_target_pairs={{0,1},{1,0},{2,3},{3,2},{4,5},{5,4},{6,7},{7,6},{8,9},{9,8},{10,11... | collective-permute-start | bytes 442376 | tf_op jit(solution)/shard_map/ppermute | solution.py:240
  48.0 6.6 %collective-permute-start.13 = (bf16[144,512]{1,0:T(8,128)(2,1)S(1)}, bf16[144,512]{1,0:T(8,128)(2,1)S(1)}, u32[]{:S(2)}, u32[]{:S(2)}) collective-permute-start(bf16[144,512]{1,0:T(8,128)(2,1)S(1)} %get-tuple-element.42), channel_id=1, source_target_pairs={{0,2},{1,3},{2,0},{3,1},{4,6},{5,7},{6,4},{7,5},{8,10},{9,11},{10,... | collective-permute-start | bytes 442376 | tf_op jit(solution)/shard_map/ppermute | solution.py:240
  49.3 7.7 %collective-permute-start.14 = (bf16[144,512]{1,0:T(8,128)(2,1)S(1)}, bf16[144,512]{1,0:T(8,128)(2,1)S(1)}, u32[]{:S(2)}, u32[]{:S(2)}) collective-permute-start(bf16[144,512]{1,0:T(8,128)(2,1)S(1)} %get-tuple-element.43), channel_id=1, source_target_pairs={{0,3},{1,2},{2,1},{3,0},{4,7},{5,6},{6,5},{7,4},{8,11},{9,10},{10,... | collective-permute-start | bytes 442376 | tf_op jit(solution)/shard_map/ppermute | solution.py:240
  57.1 8.4 %collective-permute-start.15 = (bf16[144,512]{1,0:T(8,128)(2,1)S(1)}, bf16[144,512]{1,0:T(8,128)(2,1)S(1)}, u32[]{:S(2)}, u32[]{:S(2)}) collective-permute-start(bf16[144,512]{1,0:T(8,128)(2,1)S(1)} %get-tuple-element.50), channel_id=1, source_target_pairs={{0,4},{4,0},{8,12},{12,8},{1,5},{5,1},{9,13},{13,9},{2,6},{6,2},{1... | collective-permute-start | bytes 442376 | tf_op jit(solution)/shard_map/ppermute | solution.py:240
  58.4 13.9 %collective-permute-start.16 = (bf16[144,512]{1,0:T(8,128)(2,1)S(1)}, bf16[144,512]{1,0:T(8,128)(2,1)S(1)}, u32[]{:S(2)}, u32[]{:S(2)}) collective-permute-start(bf16[144,512]{1,0:T(8,128)(2,1)S(1)} %get-tuple-element.51), channel_id=1, source_target_pairs={{0,8},{4,12},{8,0},{12,4},{1,9},{5,13},{9,1},{13,5},{2,10},{6,14},... | collective-permute-start | bytes 442376 | tf_op jit(solution)/shard_map/ppermute | solution.py:240
  59.8 12.6 %collective-permute-start.17 = (bf16[144,512]{1,0:T(8,128)(2,1)S(1)}, bf16[144,512]{1,0:T(8,128)(2,1)S(1)}, u32[]{:S(2)}, u32[]{:S(2)}) collective-permute-start(bf16[144,512]{1,0:T(8,128)(2,1)S(1)} %get-tuple-element.52), channel_id=1, source_target_pairs={{0,12},{4,8},{8,4},{12,0},{1,13},{5,9},{9,5},{13,1},{2,14},{6,10},... | collective-permute-start | bytes 442376 | tf_op jit(solution)/shard_map/ppermute | solution.py:240
  73.6 6.0 %collective-permute-start.19 = (bf16[224,512]{1,0:T(8,128)(2,1)S(1)}, bf16[224,512]{1,0:T(8,128)(2,1)S(1)}, u32[]{:S(2)}, u32[]{:S(2)}) collective-permute-start(bf16[224,512]{1,0:T(8,128)(2,1)S(1)} %get-tuple-element.56.refs_0_), channel_id=1, source_target_pairs={{0,2},{1,3},{2,0},{3,1},{4,6},{5,7},{6,4},{7,5},{8,10},{9,11},{10,... | collective-permute-start | bytes 688136 | tf_op jit(solution)/shard_map/ppermute | solution.py:240
  74.9 4.7 %collective-permute-start.18 = (bf16[224,512]{1,0:T(8,128)(2,1)S(1)}, bf16[224,512]{1,0:T(8,128)(2,1)S(1)}, u32[]{:S(2)}, u32[]{:S(2)}) collective-permute-start(bf16[224,512]{1,0:T(8,128)(2,1)S(1)} %get-tuple-element.56.refs_0_), channel_id=1, source_target_pairs={{0,1},{1,0},{2,3},{3,2},{4,5},{5,4},{6,7},{7,6},{8,9},{9,8},{10,11... | collective-permute-start | bytes 688136 | tf_op jit(solution)/shard_map/ppermute | solution.py:240
  79.6 1.5 %collective-permute-start.20 = (bf16[224,512]{1,0:T(8,128)(2,1)S(1)}, bf16[224,512]{1,0:T(8,128)(2,1)S(1)}, u32[]{:S(2)}, u32[]{:S(2)}) collective-permute-start(bf16[224,512]{1,0:T(8,128)(2,1)S(1)} %collective-permute-done.19.refs_2_), channel_id=1, source_target_pairs={{0,1},{1,0},{2,3},{3,2},{4,5},{5,4},{6,7},{7,6},{8,9},{9,8},{10,11... | collective-permute-start | bytes 688136 | tf_op jit(solution)/shard_map/ppermute | solution.py:240
  (4 other events, 3.0 us)

commit v2 on v1

--- a/solution.py
+++ b/solution.py
@@ -57,57 +57,93 @@
     )
 
 
-def selectors(place, src_index, dst_index, rows):
-    nodes = rows * WAYS
-    slots = src_index.shape[1]
-    live = lax.broadcasted_iota(jnp.int32, (1, slots), 1) < place[2]
-    src_t = one_hot_t(src_index[...] ^ (place[1] * rows), nodes)
-    dst_t = one_hot_t(dst_index[...] ^ (place[0] * rows), nodes, live)
-    dst_all = one_hot_t(dst_index[...] ^ (place[0] * rows), nodes)
-    return src_t, dst_t, dst_all
-
-
-def forward_kernel(place, *refs):
+def join_kernel(state, forcing, cotangent, joined, sems):
+    width = state.shape[2]
+    copies = [
+        pltpu.make_async_copy(state, joined.at[:, :, :width], sems.at[0]),
+        pltpu.make_async_copy(forcing, joined.at[:, :, width : 2 * width], sems.at[1]),
+        pltpu.make_async_copy(cotangent, joined.at[:, :, 2 * width :], sems.at[2]),
+    ]
+    for copy in copies:
+        copy.start()
+    for copy in copies:
+        copy.wait()
+
+
+def stage_kernel(count, src_hbm, dst_hbm, state, attr_hbm, w1_hbm, w2_hbm, wn_hbm, *refs):
+    own, attr, w1, w2, wn, src_t, dst_t, base, src_held, dst_held, sems = refs
+    width = state.shape[2]
+    copies = [
+        pltpu.make_async_copy(source, target, sems.at[i])
+        for i, (source, target) in enumerate(
+            [
+                (src_hbm, src_held),
+                (dst_hbm, dst_held),
+                (attr_hbm, attr),
+                (w1_hbm, w1),
+                (state, own),
+                (w2_hbm, w2),
+                (wn_hbm, wn),
+            ]
+        )
+    ]
+    for copy in copies:
+        copy.start()
+    copies[0].wait()
+    copies[1].wait()
+    rows = own.shape[1]
+    nodes, slots = src_t.shape
+    live = lax.broadcasted_iota(jnp.int32, (1, slots), 1) < count[0, 0]
+    src_t[...] = one_hot_t(src_held[...] ^ (lax.axis_index("dst") * rows), nodes)
+    dst_t[...] = one_hot_t(dst_held[...] ^ (lax.axis_index("src") * rows), nodes, live)
+    copies[2].wait()
+    copies[3].wait()
+    for moment in range(T_STEPS):
+        base[moment] = mm(attr[moment], w1[2 * width :])
+    for copy in copies[4:]:
+        copy.wait()
+
+
+def forward_kernel(*refs):
     sources, targets = refs[:WAYS], refs[WAYS : 2 * WAYS]
-    attr, src_index, dst_index, w1, w2 = refs[2 * WAYS : 2 * WAYS + 5]
-    message, slope, *pieces, held = refs[2 * WAYS + 5 :]
-    rows, width = sources[0].shape[1], sources[0].shape[2]
-    src_t, dst_t, dst_all = selectors(place, src_index, dst_index, rows)
+    base, src_t, dst_t, w1, w2 = refs[2 * WAYS : 2 * WAYS + 5]
+    message, message_own, slope, *pieces, held = refs[2 * WAYS + 5 :]
+    width = sources[0].shape[2]
     for moment in range(T_STEPS):
-        edge_in = jnp.concatenate(
+        ends = jnp.concatenate(
             [
-                mm_tn(src_t, stacked(sources, moment)).astype(BF),
-                mm_tn(dst_all, stacked(targets, moment)[:, :width]).astype(BF),
-                attr[moment],
+                mm_tn(src_t[...], stacked(sources, moment)).astype(BF),
+                mm_tn(dst_t[...], stacked(targets, moment)[:, :width]).astype(BF),
             ],
             axis=1,
         )
-        pre = mm(edge_in, w1[...])
+        pre = base[moment] + mm(ends, w1[: 2 * width])
         sigma = sigmoid(pre)
         hidden = (pre * sigma).astype(BF)
         slope[moment] = sigma * (1.0 + pre * (1.0 - sigma))
-        sums = mm(dst_t, hidden).astype(BF)
-        held[moment] = sums
-        message[moment] = mm(sums, w2[...]).astype(BF)
+        sums = mm(dst_t[...], hidden)
+        high = sums.astype(BF)
+        low = (sums - high.astype(F32)).astype(BF)
+        held[moment] = high
+        total = mm(high, w2[...]) + mm(low, w2[...])
+        message_own[moment] = total
+        message[moment] = total.astype(BF)
     block = w1.shape[1] // WAYS
     for k in range(WAYS):
-        start = pl.multiple_of((place[0] ^ k) * block, block)
+        start = pl.multiple_of((lax.axis_index("src") ^ k) * block, block)
         pieces[k][...] = held[:, :, pl.ds(start, block)]
 
 
-def backward_kernel(place, *refs):
+def backward_kernel(*refs):
     n = WAYS
-    sources, targets, messages, pieces = refs[:n], refs[n : 2 * n], refs[2 * n : 3 * n], refs[3 * n : 4 * n]
-    attr, src_index, dst_index, slope, w1, w2, wn = refs[4 * n : 4 * n + 7]
-    outs = refs[4 * n + 7 :]
-    state_own, forcing_own, edges = outs[:3]
-    over_dst, over_src = outs[3 : 3 + n], outs[3 + n : 3 + 2 * n]
-    node_held, pre_held, agg_held, gpe_held, p_held, q_held, first = outs[3 + 2 * n :]
+    sources, targets, messages = refs[:n], refs[n : 2 * n], refs[2 * n : 3 * n]
+    attr, src_t, dst_t, slope, w1, w2, wn = refs[3 * n : 3 * n + 7]
+    state_own, forcing_own, edges, agg_held, node_grad, to_src, to_dst, first = refs[3 * n + 7 : 3 * n + 15]
+    node_held, pre_held, gpe_held, p_held, q_held = refs[3 * n + 15 :]
     rows, width = sources[0].shape[1], sources[0].shape[2]
     nodes = rows * n
     slots = attr.shape[1]
     width_m = w2.shape[1]
-    src_t, dst_t, _ = selectors(place, src_index, dst_index, rows)
     for moment in range(T_STEPS):
         at = slice(moment * nodes, (moment + 1) * nodes)
         block = stacked(targets, moment)
@@ -123,44 +159,49 @@
         forcing_own[moment] = grad_in[:rows, width + width_m :]
         grad_agg = grad_in[:, width : width + width_m].astype(BF)
         agg_held[at] = grad_agg
-        grad_message = mm_tn(dst_t, grad_agg).astype(BF)
+        grad_message = mm_tn(dst_t[...], grad_agg).astype(BF)
         grad_pre_edge = (mm_nt(grad_message, w2[...]) * slope[moment]).astype(BF)
         gpe_held[moment * slots : (moment + 1) * slots] = grad_pre_edge
         edges[moment] = mm_nt(grad_pre_edge, w1[2 * width :])
-        from_src = mm(src_t, grad_pre_edge).astype(BF)
-        from_dst = mm(dst_t, grad_pre_edge).astype(BF)
+        from_src = mm(src_t[...], grad_pre_edge).astype(BF)
+        from_dst = mm(dst_t[...], grad_pre_edge).astype(BF)
         p_held[at] = from_src
         q_held[at] = from_dst
-        to_src = mm_nt(from_src, w1[:width]).astype(BF)
-        to_dst = mm_nt(from_dst, w1[width : 2 * width]).astype(BF)
-        half = rows // 2
-        for k in range(n):
-            for j in range(2):
-                lanes = slice((moment * 2 + j) * width, (moment * 2 + j + 1) * width)
-                spot = slice(k * rows + j * half, k * rows + (j + 1) * half)
-                over_dst[k][-half:, lanes] = to_src[spot]
-                over_src[k][:, lanes] = to_dst[spot]
+        to_src[moment] = mm_nt(from_src, w1[:width]).astype(BF)
+        to_dst[moment] = mm_nt(from_dst, w1[width : 2 * width]).astype(BF)
     states = jnp.concatenate([stacked(sources, moment) for moment in range(T_STEPS)], axis=0)
     first[:width] = mm_tn(states, p_held[...])
     first[width : 2 * width] = mm_tn(node_held[:, :width], q_held[...])
     first[2 * width :] = mm_tn(attr[...].reshape(T_STEPS * slots, width), gpe_held[...])
     block = wn.shape[0] // n
-    spot = pl.multiple_of(place[0] * block, block)
-    node_grad = mm_tn(node_held[:, pl.ds(spot, block)], pre_held[...])
+    spot = pl.multiple_of(lax.axis_index("src") * block, block)
+    node_grad[...] = mm_tn(node_held[:, pl.ds(spot, block)], pre_held[...])
+
+
+def pack_kernel(*refs):
+    n = WAYS
+    pieces, (agg_held, node_grad, to_src, to_dst, first) = refs[:n], refs[n : n + 5]
+    over_dst, over_src = refs[n + 5 : 2 * n + 5], refs[2 * n + 5 : 3 * n + 5]
+    held = refs[3 * n + 5]
+    width = to_src.shape[2]
+    rows = to_src.shape[1] // n
+    half = rows // 2
     sums = jnp.concatenate([summed(pieces, moment) for moment in range(T_STEPS)], axis=0).astype(BF)
     second = mm_tn(sums, agg_held[...])
-    both = jnp.concatenate([second, node_grad], axis=1)
+    held[:, : second.shape[1]] = second
+    held[:, second.shape[1] :] = node_grad[...]
     part = first.shape[0] // n
-    small = block // n
-
+    small = held.shape[0] // n
     for k in range(n):
-        other = place[1] ^ k
+        other = lax.axis_index("dst") ^ k
         over_dst[k][:part] = first[pl.ds(pl.multiple_of(other * part, part), part)].astype(BF)
-    for j in range(n):
-        for k in range(n):
-            @pl.when((place[1] ^ k) == j)
-            def _(j=j, k=k):
-                over_dst[k][part : part + small] = both[j * small : (j + 1) * small].astype(BF)
+        over_dst[k][part : part + small] = held[pl.ds(pl.multiple_of(other * small, small), small)].astype(BF)
+        for moment in range(T_STEPS):
+            for j in range(2):
+                lanes = slice((moment * 2 + j) * width, (moment * 2 + j + 1) * width)
+                spot = slice(k * rows + j * half, k * rows + (j + 1) * half)
+                over_dst[k][-half:, lanes] = to_src[moment, spot]
+                over_src[k][:, lanes] = to_dst[moment, spot]
 
 
 def middle_kernel(state_own, *refs):
@@ -184,7 +225,7 @@
         sent[k - 1][-half:] = pieces[k][...]
 
 
-def gather_kernel(place, state_sum, own, *refs):
+def gather_kernel(state_sum, own, *refs):
     n = WAYS
     arrived = refs[: n - 1]
     state, sent = refs[n - 1 :]
@@ -202,11 +243,11 @@
     first = own[:part] + sum(ref[:part].astype(F32) for ref in arrived)
     sent[:part] = first.astype(BF)
     for k in range(n):
-        start = pl.multiple_of(part + (place[0] ^ k) * small, small)
+        start = pl.multiple_of(part + (lax.axis_index("src") ^ k) * small, small)
         sent[pl.ds(start, small)] = own[part:].astype(BF) if k == 0 else arrived[k - 1][part:wide]
 
 
-def final_kernel(place, *refs):
+def final_kernel(*refs):
     n = WAYS
     arrived = refs[:n]
     first, second, node = refs[n:]
@@ -214,7 +255,7 @@
     small = second.shape[0] // n // n
     half = second.shape[1]
     for k in range(n):
-        other = place[1] ^ k
+        other = lax.axis_index("dst") ^ k
         first[pl.ds(pl.multiple_of(other * part, part), part)] = arrived[k][:part].astype(F32)
         for j in range(n):
             rows = arrived[k][part + j * small : part + (j + 1) * small].astype(F32)
@@ -223,17 +264,21 @@
             node[pl.ds(start, small)] = rows[:, half:]
 
 
-def call(kernel, outs, scratch, args, scalars=True):
-    in_specs = [pl.BlockSpec(memory_space=pltpu.SMEM)] if scalars else []
-    in_specs += [pl.BlockSpec(memory_space=pltpu.VMEM)] * (len(args) - len(in_specs))
+def call(kernel, outs, scratch, args, spaces=None):
     return pl.pallas_call(
         kernel,
         out_shape=[jax.ShapeDtypeStruct(shape, dtype) for shape, dtype in outs],
-        in_specs=in_specs,
+        in_specs=[pl.BlockSpec(memory_space=space) for space in spaces or [pltpu.VMEM] * len(args)],
         out_specs=[pl.BlockSpec(memory_space=pltpu.VMEM)] * len(outs),
-        scratch_shapes=[pltpu.VMEM(shape, dtype) for shape, dtype in scratch],
-        compiler_params=pltpu.CompilerParams(vmem_limit_bytes=48 << 20),
+        scratch_shapes=[
+            pltpu.VMEM(*entry) if isinstance(entry, tuple) else entry for entry in scratch
+        ],
+        compiler_params=pltpu.CompilerParams(vmem_limit_bytes=32 << 20),
     )(*args)
+
+
+def in_hbm(value):
+    return pltpu.with_memory_space_constraint(value, pltpu.HBM)
 
 
 def swap(value, axis, k):
@@ -266,42 +311,74 @@
     slots = edge_attr.shape[3]
     nodes = rows * WAYS
     steps = T_STEPS
-    place = jnp.stack(
-        [lax.axis_index("src"), lax.axis_index("dst"), edge_count[0, 0]]
-    ).astype(jnp.int32)
     attr = edge_attr[:, 0, 0]
-    src_row, dst_row = src_index[0], dst_index[0]
     sources = fan(node_state, "dst")
-    targets = fan(jnp.concatenate([node_state, forcing, cotangent], axis=2), "src")
+    joined = call(
+        join_kernel,
+        [((steps, rows, 2 * width + width_out), BF)],
+        [pltpu.SemaphoreType.DMA((3,))],
+        [in_hbm(value) for value in (node_state, forcing, cotangent)],
+        [pltpu.HBM] * 3,
+    )[0]
+    targets = fan(joined, "src")
+    state_in, attr, w1, w2, wn, src_t, dst_t, base = call(
+        stage_kernel,
+        [
+            (node_state.shape, BF),
+            (attr.shape, BF),
+            (edge_w1.shape, BF),
+            (edge_w2.shape, BF),
+            (node_w1.shape, BF),
+            ((nodes, slots), BF),
+            ((nodes, slots), BF),
+            ((steps, slots, hid), F32),
+        ],
+        [((1, slots), jnp.int32), ((1, slots), jnp.int32), pltpu.SemaphoreType.DMA((7,))],
+        [edge_count]
+        + [in_hbm(value) for value in (src_index[0], dst_index[0], node_state, attr, edge_w1, edge_w2, node_w1)],
+        [pltpu.SMEM] + [pltpu.HBM] * 7,
+    )
+    sources = [state_in] + sources[1:]
     block = hid // WAYS
-    message, slope, *pieces = call(
+    message, message_own, slope, *pieces = call(
         forward_kernel,
-        [((steps, nodes, width_m), BF), ((steps, slots, hid), F32)]
+        [((steps, nodes, width_m), BF), ((steps, nodes, width_m), F32), ((steps, slots, hid), F32)]
         + [((steps, nodes, block), BF)] * WAYS,
         [((steps, nodes, hid), BF)],
-        [place, *sources, *targets, attr, src_row, dst_row, edge_w1, edge_w2],
-    )
-    messages = fan(message, "src")
+        [*sources, *targets, base, src_t, dst_t, w1, w2],
+    )
+    messages = [message_own] + fan(message, "src")[1:]
     pieces = exchange(pieces, "src")
     part = edge_w1.shape[0] // WAYS
     small = block // WAYS
     half = rows // 2
     wide = part + small
-    state_own, grad_forcing, edges, *sent = call(
+    state_own, grad_forcing, edges, *partials = call(
         backward_kernel,
-        [((steps, rows, width), F32), ((steps, rows, width), F32), ((steps, slots, width), F32)]
-        + [((wide + half, hid), BF)] * WAYS
-        + [((half, hid), BF)] * WAYS,
+        [
+            ((steps, rows, width), F32),
+            ((steps, rows, width), F32),
+            ((steps, slots, width), F32),
+            ((steps * nodes, width_m), BF),
+            ((block, width_out), F32),
+            ((steps, nodes, width), BF),
+            ((steps, nodes, width), BF),
+            (edge_w1.shape, F32),
+        ],
         [
             ((steps * nodes, width_in), BF),
             ((steps * nodes, width_out), BF),
-            ((steps * nodes, width_m), BF),
             ((steps * slots, hid), BF),
             ((steps * nodes, hid), BF),
             ((steps * nodes, hid), BF),
-            (edge_w1.shape, F32),
         ],
-        [place, *sources, *targets, *messages, *pieces, attr, src_row, dst_row, slope, edge_w1, edge_w2, node_w1],
+        [*sources, *targets, *messages, attr, src_t, dst_t, slope, w1, w2, wn],
+    )
+    sent = call(
+        pack_kernel,
+        [((wide + half, hid), BF)] * WAYS + [((half, hid), BF)] * WAYS,
+        [((block, hid), F32)],
+        [*pieces, *partials],
     )
     over_dst, over_src = sent[:WAYS], sent[WAYS:]
     state_sum, own, *sent = call(
@@ -309,21 +386,20 @@
         [((steps, rows, width), F32), ((wide, hid), F32)] + [((wide + half, hid), BF)] * (WAYS - 1),
         [],
         [state_own, *exchange(over_dst, "dst"), *over_src],
-        scalars=False,
     )
     arrived = [swap(sent[k - 1], "src", k) for k in range(1, WAYS)]
     grad_state, share = call(
         gather_kernel,
         [((steps, rows, width), F32), ((wide + (WAYS - 1) * small, hid), BF)],
         [],
-        [place, state_sum, own, *arrived],
+        [state_sum, own, *arrived],
     )
     across = swap(share, "dst", 2)
     grad_first, grad_second, grad_node = call(
         final_kernel,
         [(edge_w1.shape, F32), (edge_w2.shape, F32), (node_w1.shape, F32)],
         [],
-        [place, share, swap(share, "dst", 1), across, swap(across, "dst", 1)],
+        [share, swap(share, "dst", 1), across, swap(across, "dst", 1)],
     )
     return grad_state, grad_forcing, edges[:, None, None], grad_first, grad_second, grad_node
 

time: 84.1 us -> 72.5 us (0.86)
  the two profiles are of different devices: /device:TPU:0 before, /device:TPU:9 now
where the time goes in v2:
time: 72.5 us; the launch traced here: 72.3 us
  waiting for transfers between devices  35.4 us (49%)
  starting transfers between devices  26 us (36%)
  Pallas kernels  9.53 us (13%)
  between operations  1.38 us (2%)
    ppermute x21, waiting for transfers between devices, swap(): return lax.ppermute(value, axis, [(i, i ^ k) for i in range(WAYS)])  35.4 us
    ppermute x21, starting transfers between devices, swap(): return lax.ppermute(value, axis, [(i, i ^ k) for i in range(WAYS)])  26 us
    pallas_call x8, Pallas kernels, call(): pl.pallas_call(kernel, out_shape=[jax.ShapeDtypeStruct(shape, dtype) for...  9.53 us
  transfers between devices with their start and end apart: 21, of which 12 were waited for; matrix products, arithmetic and copies ran while one was open for 0% of the time, Pallas kernels for 6%

profile of v2, /device:TPU:9, one launch (start us, length us, event | category | flops | bytes accessed | tf_op | source)
XLA Modules:
  0.0 72.3 jit_solution(10569681441896188851)
XLA Ops:
  1.5 1.4 %collective-permute-start.5 = (bf16[2,32,512]{2,1,0:T(8,128)(2,1)S(1)}, bf16[2,32,512]{2,1,0:T(8,128)(2,1)S(1)}, u32[]{:S(2)}, u32[]{:S(2)}) collective-permute-start(bf16[2,32,512]{2,1,0:T(8,128)(2,1)S(1)} %shard_map.146.refs_4_), channel_id=1, source_target_pairs={{0,12},{4,8},{8,4},{12,0},{1,13},{5,9},{9,5},{13,1},{2,14},{6,10},... | collective-permute-start | bytes 196616 | tf_op jit(solution)/shard_map/ppermute | solution.py:285
  5.0 1.2 %collective-permute-start.1 = (bf16[2,32,128]{2,1,0:T(8,128)(2,1)}, bf16[2,32,128]{2,1,0:T(8,128)(2,1)S(1)}, u32[]{:S(2)}, u32[]{:S(2)}) collective-permute-start(bf16[2,32,128]{2,1,0:T(8,128)(2,1)} %state.3), channel_id=1, source_target_pairs={{0,2},{1,3},{2,0},{3,1},{4,6},{5,7},{6,4},{7,5},{8,10},{9,11},{10,... | collective-permute-start | bytes 49160 | tf_op jit(solution)/shard_map/ppermute | solution.py:285
  6.2 1.5 %collective-permute-start = (bf16[2,32,128]{2,1,0:T(8,128)(2,1)}, bf16[2,32,128]{2,1,0:T(8,128)(2,1)S(1)}, u32[]{:S(2)}, u32[]{:S(2)}) collective-permute-start(bf16[2,32,128]{2,1,0:T(8,128)(2,1)} %state.3), channel_id=1, source_target_pairs={{0,1},{1,0},{2,3},{3,2},{4,5},{5,4},{6,7},{7,6},{8,9},{9,8},{10,11... | collective-permute-start | bytes 49160 | tf_op jit(solution)/shard_map/ppermute | solution.py:285
  8.1 3.2 %collective-permute-start.2 = (bf16[2,32,128]{2,1,0:T(8,128)(2,1)}, bf16[2,32,128]{2,1,0:T(8,128)(2,1)S(1)}, u32[]{:S(2)}, u32[]{:S(2)}) collective-permute-start(bf16[2,32,128]{2,1,0:T(8,128)(2,1)} %state.3), channel_id=1, source_target_pairs={{0,3},{1,2},{2,1},{3,0},{4,7},{5,6},{6,5},{7,4},{8,11},{9,10},{10,... | collective-permute-start | bytes 49160 | tf_op jit(solution)/shard_map/ppermute | solution.py:285
  12.0 1.6 %shard_map.145 = (bf16[2,32,128]{2,1,0:T(8,128)(2,1)S(1)}, bf16[2,512,128]{2,1,0:T(8,128)(2,1)S(1)}, bf16[384,512]{1,0:T(8,128)(2,1)S(1)}, bf16[512,256]{1,0:T(8...) custom-call(s32[1,1]{1,0:T(1,128)S(6)} %copy.17.count, ...), custom_call_target="tpu_custom_call" | custom-call | tf_op jit(solution)/shard_map/pallas_call | solution.py:268
  13.6 1.9 %shard_map.147 = (bf16[2,128,256]{2,1,0:T(8,128)(2,1)S(1)}, f32[2,128,256]{2,1,0:T(8,128)S(1)}, f32[2,512,512]{2,1,0:T(8,128)S(1)}, bf16[2,128,128]{2,1,0:T(8,12...) custom-call(bf16[2,32,128]{2,1,0:T(8,128)(2,1)S(1)} %get-tuple-eleme, ...), custom_call_target="tpu_custom_call" | custom-call | tf_op jit(solution)/shard_map/pallas_call | solution.py:268
  15.5 1.2 %collective-permute-start.8 = (bf16[2,128,256]{2,1,0:T(8,128)(2,1)S(1)}, bf16[2,128,256]{2,1,0:T(8,128)(2,1)S(1)}, u32[]{:S(2)}, u32[]{:S(2)}) collective-permute-start(bf16[2,128,256]{2,1,0:T(8,128)(2,1)S(1)} %get-tuple-element.54), channel_id=1, source_target_pairs={{0,12},{4,8},{8,4},{12,0},{1,13},{5,9},{9,5},{13,1},{2,14},{6,10},... | collective-permute-start | bytes 393224 | tf_op jit(solution)/shard_map/ppermute | solution.py:285
  16.8 1.5 %collective-permute-start.7 = (bf16[2,128,256]{2,1,0:T(8,128)(2,1)S(1)}, bf16[2,128,256]{2,1,0:T(8,128)(2,1)S(1)}, u32[]{:S(2)}, u32[]{:S(2)}) collective-permute-start(bf16[2,128,256]{2,1,0:T(8,128)(2,1)S(1)} %get-tuple-element.54), channel_id=1, source_target_pairs={{0,8},{4,12},{8,0},{12,4},{1,9},{5,13},{9,1},{13,5},{2,10},{6,14},... | collective-permute-start | bytes 393224 | tf_op jit(solution)/shard_map/ppermute | solution.py:285
  19.8 2.0 %collective-permute-start.10 = (bf16[2,128,128]{2,1,0:T(8,128)(2,1)S(1)}, bf16[2,128,128]{2,1,0:T(8,128)(2,1)S(1)}, u32[]{:S(2)}, u32[]{:S(2)}) collective-permute-start(bf16[2,128,128]{2,1,0:T(8,128)(2,1)S(1)} %get-tuple-element.61), channel_id=1, source_target_pairs={{0,8},{4,12},{8,0},{12,4},{1,9},{5,13},{9,1},{13,5},{2,10},{6,14},... | collective-permute-start | bytes 196616 | tf_op jit(solution)/shard_map/ppermute | solution.py:285
  21.8 4.4 %collective-permute-done.8.refs_11_ = bf16[2,128,256]{2,1,0:T(8,128)(2,1)S(1)} collective-permute-done((bf16[2,128,256]{2,1,0:T(8,128)(2,1)S(1)}, bf16[2,128,256]{2,1,0:T(8,128)(2,1)S(1)}, u32[]{:S(2)}, u32[]{:S(2)}) %collective-permute-start.8) | collective-permute-done | bytes 131104 | tf_op jit(solution)/shard_map/ppermute | solution.py:285
  26.2 1.9 %collective-permute-done.7.refs_10_ = bf16[2,128,256]{2,1,0:T(8,128)(2,1)S(1)} collective-permute-done((bf16[2,128,256]{2,1,0:T(8,128)(2,1)S(1)}, bf16[2,128,256]{2,1,0:T(8,128)(2,1)S(1)}, u32[]{:S(2)}, u32[]{:S(2)}) %collective-permute-start.7) | collective-permute-done | bytes 131104 | tf_op jit(solution)/shard_map/ppermute | solution.py:285
  28.6 2.9 %shard_map.148 = (f32[2,32,128]{2,1,0:T(8,128)S(1)}, f32[2,32,128]{2,1,0:T(8,128)}, f32[2,512,128]{2,1,0:T(8,128)}, bf16[256,256]{1,0:T(8,128)(2,1)S(1)}, f32[12...) custom-call(bf16[2,32,128]{2,1,0:T(8,128)(2,1)S(1)} %get-tuple-eleme, ...), custom_call_target="tpu_custom_call" | custom-call | tf_op jit(solution)/shard_map/pallas_call | solution.py:268
  31.5 3.1 %collective-permute-done.11.refs_3_ = bf16[2,128,128]{2,1,0:T(8,128)(2,1)S(1)} collective-permute-done((bf16[2,128,128]{2,1,0:T(8,128)(2,1)S(1)}, bf16[2,128,128]{2,1,0:T(8,128)(2,1)S(1)}, u32[]{:S(2)}, u32[]{:S(2)}) %collective-permute-start.11) | collective-permute-done | bytes 65568 | tf_op jit(solution)/shard_map/ppermute | solution.py:285
  36.1 1.4 %collective-permute-start.14 = (bf16[144,512]{1,0:T(8,128)(2,1)S(1)}, bf16[144,512]{1,0:T(8,128)(2,1)S(1)}, u32[]{:S(2)}, u32[]{:S(2)}) collective-permute-start(bf16[144,512]{1,0:T(8,128)(2,1)S(1)} %get-tuple-element.71), channel_id=1, source_target_pairs={{0,3},{1,2},{2,1},{3,0},{4,7},{5,6},{6,5},{7,4},{8,11},{9,10},{10,... | collective-permute-start | bytes 442376 | tf_op jit(solution)/shard_map/ppermute | solution.py:285
  37.6 3.7 %collective-permute-done.13.refs_2_ = bf16[144,512]{1,0:T(8,128)(2,1)S(1)} collective-permute-done((bf16[144,512]{1,0:T(8,128)(2,1)S(1)}, bf16[144,512]{1,0:T(8,128)(2,1)S(1)}, u32[]{:S(2)}, u32[]{:S(2)}) %collective-permute-start.13) | collective-permute-done | bytes 147488 | tf_op jit(solution)/shard_map/ppermute | solution.py:285
  41.3 3.3 %collective-permute-done.14.refs_3_ = bf16[144,512]{1,0:T(8,128)(2,1)S(1)} collective-permute-done((bf16[144,512]{1,0:T(8,128)(2,1)S(1)}, bf16[144,512]{1,0:T(8,128)(2,1)S(1)}, u32[]{:S(2)}, u32[]{:S(2)}) %collective-permute-start.14) | collective-permute-done | bytes 147488 | tf_op jit(solution)/shard_map/ppermute | solution.py:285
  44.7 1.9 %collective-permute-start.15 = (bf16[144,512]{1,0:T(8,128)(2,1)S(1)}, bf16[144,512]{1,0:T(8,128)(2,1)S(1)}, u32[]{:S(2)}, u32[]{:S(2)}) collective-permute-start(bf16[144,512]{1,0:T(8,128)(2,1)S(1)} %get-tuple-element.78), channel_id=1, source_target_pairs={{0,4},{4,0},{8,12},{12,8},{1,5},{5,1},{9,13},{13,9},{2,6},{6,2},{1... | collective-permute-start | bytes 442376 | tf_op jit(solution)/shard_map/ppermute | solution.py:285
  47.8 4.3 %collective-permute-done.15.refs_0_ = bf16[144,512]{1,0:T(8,128)(2,1)S(1)} collective-permute-done((bf16[144,512]{1,0:T(8,128)(2,1)S(1)}, bf16[144,512]{1,0:T(8,128)(2,1)S(1)}, u32[]{:S(2)}, u32[]{:S(2)}) %collective-permute-start.15) | collective-permute-done | bytes 147488 | tf_op jit(solution)/shard_map/ppermute | solution.py:285
  52.1 2.0 %collective-permute-done.16.refs_1_ = bf16[144,512]{1,0:T(8,128)(2,1)S(1)} collective-permute-done((bf16[144,512]{1,0:T(8,128)(2,1)S(1)}, bf16[144,512]{1,0:T(8,128)(2,1)S(1)}, u32[]{:S(2)}, u32[]{:S(2)}) %collective-permute-start.16) | collective-permute-done | bytes 147488 | tf_op jit(solution)/shard_map/ppermute | solution.py:285
  54.1 7.0 %collective-permute-done.17.refs_2_ = bf16[144,512]{1,0:T(8,128)(2,1)S(1)} collective-permute-done((bf16[144,512]{1,0:T(8,128)(2,1)S(1)}, bf16[144,512]{1,0:T(8,128)(2,1)S(1)}, u32[]{:S(2)}, u32[]{:S(2)}) %collective-permute-start.17) | collective-permute-done | bytes 147488 | tf_op jit(solution)/shard_map/ppermute | solution.py:285
  62.8 1.3 %collective-permute-start.18 = (bf16[224,512]{1,0:T(8,128)(2,1)S(1)}, bf16[224,512]{1,0:T(8,128)(2,1)S(1)}, u32[]{:S(2)}, u32[]{:S(2)}) collective-permute-start(bf16[224,512]{1,0:T(8,128)(2,1)S(1)} %get-tuple-element.84.refs_0_), channel_id=1, source_target_pairs={{0,1},{1,0},{2,3},{3,2},{4,5},{5,4},{6,7},{7,6},{8,9},{9,8},{10,11... | collective-permute-start | bytes 688136 | tf_op jit(solution)/shard_map/ppermute | solution.py:285
  64.1 3.7 %collective-permute-done.19.refs_2_ = bf16[224,512]{1,0:T(8,128)(2,1)S(1)} collective-permute-done((bf16[224,512]{1,0:T(8,128)(2,1)S(1)}, bf16[224,512]{1,0:T(8,128)(2,1)S(1)}, u32[]{:S(2)}, u32[]{:S(2)}) %collective-permute-start.19) | collective-permute-done | bytes 229408 | tf_op jit(solution)/shard_map/ppermute | solution.py:285
  67.8 2.0 %collective-permute-start.20 = (bf16[224,512]{1,0:T(8,128)(2,1)S(1)}, bf16[224,512]{1,0:T(8,128)(2,1)S(1)}, u32[]{:S(2)}, u32[]{:S(2)}) collective-permute-start(bf16[224,512]{1,0:T(8,128)(2,1)S(1)} %collective-permute-done.19.refs_2_), channel_id=1, source_target_pairs={{0,1},{1,0},{2,3},{3,2},{4,5},{5,4},{6,7},{7,6},{8,9},{9,8},{10,11... | collective-permute-start | bytes 688136 | tf_op jit(solution)/shard_map/ppermute | solution.py:285
  70.9 1.4 %shard_map.152 = (f32[384,512]{1,0:T(8,128)}, f32[512,256]{1,0:T(8,128)}, f32[512,256]{1,0:T(8,128)}) custom-call(bf16[224,512]{1,0:T(8,128)(2,1)S(1)} %get-tuple-element.84.refs_0_, bf16[224,512]{1,0:T(8,128)(2,1)S(1)} %collective-permute-done.18.refs_1_, bf16[224,512]{1,0:T(8,128)(2,1)S(1)} %collective-permute-done.19.refs_2_, ...), custom_call_target="tpu_custom_call" | custom-call | tf_op jit(solution)/shard_map/pallas_call | solution.py:268
  (26 shorter events, 11.1 us)
Async XLA Ops:
  1.5 12.1 %collective-permute-start.5 = (bf16[2,32,512]{2,1,0:T(8,128)(2,1)S(1)}, bf16[2,32,512]{2,1,0:T(8,128)(2,1)S(1)}, u32[]{:S(2)}, u32[]{:S(2)}) collective-permute-start(bf16[2,32,512]{2,1,0:T(8,128)(2,1)S(1)} %shard_map.146.refs_4_), channel_id=1, source_target_pairs={{0,12},{4,8},{8,4},{12,0},{1,13},{5,9},{9,5},{13,1},{2,14},{6,10},... | collective-permute-start | bytes 196616 | tf_op jit(solution)/shard_map/ppermute | solution.py:285
  2.8 10.8 %collective-permute-start.4 = (bf16[2,32,512]{2,1,0:T(8,128)(2,1)S(1)}, bf16[2,32,512]{2,1,0:T(8,128)(2,1)S(1)}, u32[]{:S(2)}, u32[]{:S(2)}) collective-permute-start(bf16[2,32,512]{2,1,0:T(8,128)(2,1)S(1)} %shard_map.146.refs_4_), channel_id=1, source_target_pairs={{0,8},{4,12},{8,0},{12,4},{1,9},{5,13},{9,1},{13,5},{2,10},{6,14},... | collective-permute-start | bytes 196616 | tf_op jit(solution)/shard_map/ppermute | solution.py:285
  3.9 9.7 %collective-permute-start.3 = (bf16[2,32,512]{2,1,0:T(8,128)(2,1)S(1)}, bf16[2,32,512]{2,1,0:T(8,128)(2,1)S(1)}, u32[]{:S(2)}, u32[]{:S(2)}) collective-permute-start(bf16[2,32,512]{2,1,0:T(8,128)(2,1)S(1)} %shard_map.146.refs_4_), channel_id=1, source_target_pairs={{0,4},{4,0},{8,12},{12,8},{1,5},{5,1},{9,13},{13,9},{2,6},{6,2},{1... | collective-permute-start | bytes 196616 | tf_op jit(solution)/shard_map/ppermute | solution.py:285
  5.0 3.1 %collective-permute-start.1 = (bf16[2,32,128]{2,1,0:T(8,128)(2,1)}, bf16[2,32,128]{2,1,0:T(8,128)(2,1)S(1)}, u32[]{:S(2)}, u32[]{:S(2)}) collective-permute-start(bf16[2,32,128]{2,1,0:T(8,128)(2,1)} %state.3), channel_id=1, source_target_pairs={{0,2},{1,3},{2,0},{3,1},{4,6},{5,7},{6,4},{7,5},{8,10},{9,11},{10,... | collective-permute-start | bytes 49160 | tf_op jit(solution)/shard_map/ppermute | solution.py:285
  6.2 7.3 %collective-permute-start = (bf16[2,32,128]{2,1,0:T(8,128)(2,1)}, bf16[2,32,128]{2,1,0:T(8,128)(2,1)S(1)}, u32[]{:S(2)}, u32[]{:S(2)}) collective-permute-start(bf16[2,32,128]{2,1,0:T(8,128)(2,1)} %state.3), channel_id=1, source_target_pairs={{0,1},{1,0},{2,3},{3,2},{4,5},{5,4},{6,7},{7,6},{8,9},{9,8},{10,11... | collective-permute-start | bytes 49160 | tf_op jit(solution)/shard_map/ppermute | solution.py:285
  8.1 5.5 %collective-permute-start.2 = (bf16[2,32,128]{2,1,0:T(8,128)(2,1)}, bf16[2,32,128]{2,1,0:T(8,128)(2,1)S(1)}, u32[]{:S(2)}, u32[]{:S(2)}) collective-permute-start(bf16[2,32,128]{2,1,0:T(8,128)(2,1)} %state.3), channel_id=1, source_target_pairs={{0,3},{1,2},{2,1},{3,0},{4,7},{5,6},{6,5},{7,4},{8,11},{9,10},{10,... | collective-permute-start | bytes 49160 | tf_op jit(solution)/shard_map/ppermute | solution.py:285
  15.5 10.6 %collective-permute-start.8 = (bf16[2,128,256]{2,1,0:T(8,128)(2,1)S(1)}, bf16[2,128,256]{2,1,0:T(8,128)(2,1)S(1)}, u32[]{:S(2)}, u32[]{:S(2)}) collective-permute-start(bf16[2,128,256]{2,1,0:T(8,128)(2,1)S(1)} %get-tuple-element.54), channel_id=1, source_target_pairs={{0,12},{4,8},{8,4},{12,0},{1,13},{5,9},{9,5},{13,1},{2,14},{6,10},... | collective-permute-start | bytes 393224 | tf_op jit(solution)/shard_map/ppermute | solution.py:285
  16.8 11.3 %collective-permute-start.7 = (bf16[2,128,256]{2,1,0:T(8,128)(2,1)S(1)}, bf16[2,128,256]{2,1,0:T(8,128)(2,1)S(1)}, u32[]{:S(2)}, u32[]{:S(2)}) collective-permute-start(bf16[2,128,256]{2,1,0:T(8,128)(2,1)S(1)} %get-tuple-element.54), channel_id=1, source_target_pairs={{0,8},{4,12},{8,0},{12,4},{1,9},{5,13},{9,1},{13,5},{2,10},{6,14},... | collective-permute-start | bytes 393224 | tf_op jit(solution)/shard_map/ppermute | solution.py:285
  18.3 10.3 %collective-permute-start.6 = (bf16[2,128,256]{2,1,0:T(8,128)(2,1)S(1)}, bf16[2,128,256]{2,1,0:T(8,128)(2,1)S(1)}, u32[]{:S(2)}, u32[]{:S(2)}) collective-permute-start(bf16[2,128,256]{2,1,0:T(8,128)(2,1)S(1)} %get-tuple-element.54), channel_id=1, source_target_pairs={{0,4},{4,0},{8,12},{12,8},{1,5},{5,1},{9,13},{13,9},{2,6},{6,2},{1... | collective-permute-start | bytes 393224 | tf_op jit(solution)/shard_map/ppermute | solution.py:285
  19.4 12.1 %collective-permute-start.9 = (bf16[2,128,128]{2,1,0:T(8,128)(2,1)S(1)}, bf16[2,128,128]{2,1,0:T(8,128)(2,1)S(1)}, u32[]{:S(2)}, u32[]{:S(2)}) collective-permute-start(bf16[2,128,128]{2,1,0:T(8,128)(2,1)S(1)} %get-tuple-element.60), channel_id=1, source_target_pairs={{0,4},{4,0},{8,12},{12,8},{1,5},{5,1},{9,13},{13,9},{2,6},{6,2},{1... | collective-permute-start | bytes 196616 | tf_op jit(solution)/shard_map/ppermute | solution.py:285
  19.8 11.7 %collective-permute-start.10 = (bf16[2,128,128]{2,1,0:T(8,128)(2,1)S(1)}, bf16[2,128,128]{2,1,0:T(8,128)(2,1)S(1)}, u32[]{:S(2)}, u32[]{:S(2)}) collective-permute-start(bf16[2,128,128]{2,1,0:T(8,128)(2,1)S(1)} %get-tuple-element.61), channel_id=1, source_target_pairs={{0,8},{4,12},{8,0},{12,4},{1,9},{5,13},{9,1},{13,5},{2,10},{6,14},... | collective-permute-start | bytes 196616 | tf_op jit(solution)/shard_map/ppermute | solution.py:285
  26.2 8.4 %collective-permute-start.11 = (bf16[2,128,128]{2,1,0:T(8,128)(2,1)S(1)}, bf16[2,128,128]{2,1,0:T(8,128)(2,1)S(1)}, u32[]{:S(2)}, u32[]{:S(2)}) collective-permute-start(bf16[2,128,128]{2,1,0:T(8,128)(2,1)S(1)} %get-tuple-element.62), channel_id=1, source_target_pairs={{0,12},{4,8},{8,4},{12,0},{1,13},{5,9},{9,5},{13,1},{2,14},{6,10},... | collective-permute-start | bytes 196616 | tf_op jit(solution)/shard_map/ppermute | solution.py:285
  34.8 2.7 %collective-permute-start.12 = (bf16[144,512]{1,0:T(8,128)(2,1)S(1)}, bf16[144,512]{1,0:T(8,128)(2,1)S(1)}, u32[]{:S(2)}, u32[]{:S(2)}) collective-permute-start(bf16[144,512]{1,0:T(8,128)(2,1)S(1)} %get-tuple-element.69), channel_id=1, source_target_pairs={{0,1},{1,0},{2,3},{3,2},{4,5},{5,4},{6,7},{7,6},{8,9},{9,8},{10,11... | collective-permute-start | bytes 442376 | tf_op jit(solution)/shard_map/ppermute | solution.py:285
  35.8 5.4 %collective-permute-start.13 = (bf16[144,512]{1,0:T(8,128)(2,1)S(1)}, bf16[144,512]{1,0:T(8,128)(2,1)S(1)}, u32[]{:S(2)}, u32[]{:S(2)}) collective-permute-start(bf16[144,512]{1,0:T(8,128)(2,1)S(1)} %get-tuple-element.70), channel_id=1, source_target_pairs={{0,2},{1,3},{2,0},{3,1},{4,6},{5,7},{6,4},{7,5},{8,10},{9,11},{10,... | collective-permute-start | bytes 442376 | tf_op jit(solution)/shard_map/ppermute | solution.py:285
  36.1 8.5 %collective-permute-start.14 = (bf16[144,512]{1,0:T(8,128)(2,1)S(1)}, bf16[144,512]{1,0:T(8,128)(2,1)S(1)}, u32[]{:S(2)}, u32[]{:S(2)}) collective-permute-start(bf16[144,512]{1,0:T(8,128)(2,1)S(1)} %get-tuple-element.71), channel_id=1, source_target_pairs={{0,3},{1,2},{2,1},{3,0},{4,7},{5,6},{6,5},{7,4},{8,11},{9,10},{10,... | collective-permute-start | bytes 442376 | tf_op jit(solution)/shard_map/ppermute | solution.py:285
  44.7 7.5 %collective-permute-start.15 = (bf16[144,512]{1,0:T(8,128)(2,1)S(1)}, bf16[144,512]{1,0:T(8,128)(2,1)S(1)}, u32[]{:S(2)}, u32[]{:S(2)}) collective-permute-start(bf16[144,512]{1,0:T(8,128)(2,1)S(1)} %get-tuple-element.78), channel_id=1, source_target_pairs={{0,4},{4,0},{8,12},{12,8},{1,5},{5,1},{9,13},{13,9},{2,6},{6,2},{1... | collective-permute-start | bytes 442376 | tf_op jit(solution)/shard_map/ppermute | solution.py:285
  46.6 7.6 %collective-permute-start.16 = (bf16[144,512]{1,0:T(8,128)(2,1)S(1)}, bf16[144,512]{1,0:T(8,128)(2,1)S(1)}, u32[]{:S(2)}, u32[]{:S(2)}) collective-permute-start(bf16[144,512]{1,0:T(8,128)(2,1)S(1)} %get-tuple-element.79), channel_id=1, source_target_pairs={{0,8},{4,12},{8,0},{12,4},{1,9},{5,13},{9,1},{13,5},{2,10},{6,14},... | collective-permute-start | bytes 442376 | tf_op jit(solution)/shard_map/ppermute | solution.py:285
  47.2 13.9 %collective-permute-start.17 = (bf16[144,512]{1,0:T(8,128)(2,1)S(1)}, bf16[144,512]{1,0:T(8,128)(2,1)S(1)}, u32[]{:S(2)}, u32[]{:S(2)}) collective-permute-start(bf16[144,512]{1,0:T(8,128)(2,1)S(1)} %get-tuple-element.80), channel_id=1, source_target_pairs={{0,12},{4,8},{8,4},{12,0},{1,13},{5,9},{9,5},{13,1},{2,14},{6,10},... | collective-permute-start | bytes 442376 | tf_op jit(solution)/shard_map/ppermute | solution.py:285
  61.8 6.0 %collective-permute-start.19 = (bf16[224,512]{1,0:T(8,128)(2,1)S(1)}, bf16[224,512]{1,0:T(8,128)(2,1)S(1)}, u32[]{:S(2)}, u32[]{:S(2)}) collective-permute-start(bf16[224,512]{1,0:T(8,128)(2,1)S(1)} %get-tuple-element.84.refs_0_), channel_id=1, source_target_pairs={{0,2},{1,3},{2,0},{3,1},{4,6},{5,7},{6,4},{7,5},{8,10},{9,11},{10,... | collective-permute-start | bytes 688136 | tf_op jit(solution)/shard_map/ppermute | solution.py:285
  62.8 7.0 %collective-permute-start.18 = (bf16[224,512]{1,0:T(8,128)(2,1)S(1)}, bf16[224,512]{1,0:T(8,128)(2,1)S(1)}, u32[]{:S(2)}, u32[]{:S(2)}) collective-permute-start(bf16[224,512]{1,0:T(8,128)(2,1)S(1)} %get-tuple-element.84.refs_0_), channel_id=1, source_target_pairs={{0,1},{1,0},{2,3},{3,2},{4,5},{5,4},{6,7},{7,6},{8,9},{9,8},{10,11... | collective-permute-start | bytes 688136 | tf_op jit(solution)/shard_map/ppermute | solution.py:285
  67.8 3.1 %collective-permute-start.20 = (bf16[224,512]{1,0:T(8,128)(2,1)S(1)}, bf16[224,512]{1,0:T(8,128)(2,1)S(1)}, u32[]{:S(2)}, u32[]{:S(2)}) collective-permute-start(bf16[224,512]{1,0:T(8,128)(2,1)S(1)} %collective-permute-done.19.refs_2_), channel_id=1, source_target_pairs={{0,1},{1,0},{2,3},{3,2},{4,5},{5,4},{6,7},{7,6},{8,9},{9,8},{10,11... | collective-permute-start | bytes 688136 | tf_op jit(solution)/shard_map/ppermute | solution.py:285

commit v3 on v0

--- a/solution.py
+++ b/solution.py
@@ -1,9 +1,485 @@
+import functools
+
 import jax
 import jax.numpy as jnp
 from jax import lax
+from jax.experimental import pallas as pl
+from jax.experimental.pallas import tpu as pltpu
 from jax.sharding import PartitionSpec as P
 
 T_STEPS = 2
+WAYS = 4
+ORDER = (3, 1, 2)
+BF = jnp.bfloat16
+F32 = jnp.float32
+
+
+def sigmoid(value):
+    return 0.5 * jnp.tanh(0.5 * value) + 0.5
+
+
+def slope_of(value):
+    sigma = sigmoid(value)
+    return sigma * (1.0 + value * (1.0 - sigma))
+
+
+def mm(a, b):
+    return jnp.dot(a, b, preferred_element_type=F32)
+
+
+def mm_nt(a, b):
+    return lax.dot_general(a, b, (((1,), (1,)), ((), ())), preferred_element_type=F32)
+
+
+def mm_tn(a, b):
+    return lax.dot_general(a, b, (((0,), (0,)), ((), ())), preferred_element_type=F32)
+
+
+def one_hot_t(index, nodes, live=None):
+    hit = lax.broadcasted_iota(jnp.int32, (nodes, index.shape[1]), 0) == index
+    if live is not None:
+        hit = jnp.logical_and(hit, live)
+    return jnp.where(hit, 1.0, 0.0).astype(BF)
+
+
+def stacked(refs, moment):
+    return jnp.concatenate([ref[moment] for ref in refs], axis=0)
+
+
+def turned(value, k):
+    rows = value.shape[0] // WAYS
+    return jnp.concatenate([value[(j ^ k) * rows : ((j ^ k) + 1) * rows] for j in range(WAYS)], axis=0)
+
+
+def join_kernel(near, state, forcing, cotangent, joined, sems):
+    width = state.shape[2]
+    copies = [
+        pltpu.make_async_copy(state, joined.at[:, :, :width], sems.at[0]),
+        pltpu.make_async_copy(forcing, joined.at[:, :, width : 2 * width], sems.at[1]),
+        pltpu.make_async_copy(cotangent, joined.at[:, :, 2 * width :], sems.at[2]),
+    ]
+    for copy in copies:
+        copy.start()
+    for copy in copies:
+        copy.wait()
+
+
+def stage_kernel(count, src_hbm, dst_hbm, attr_hbm, w1_hbm, w2_hbm, wn_hbm, state_hbm, *refs):
+    attr, w1, w2, wn, src_t, dst_t, base, state, src_held, dst_held, sems = refs
+    width = attr.shape[2]
+    copies = [
+        pltpu.make_async_copy(source, target, sems.at[i])
+        for i, (source, target) in enumerate(
+            [
+                (src_hbm, src_held),
+                (dst_hbm, dst_held),
+                (attr_hbm, attr),
+                (w1_hbm, w1),
+                (w2_hbm, w2),
+                (wn_hbm, wn),
+                (state_hbm, state),
+            ]
+        )
+    ]
+    for copy in copies:
+        copy.start()
+    copies[0].wait()
+    copies[1].wait()
+    nodes, slots = src_t.shape
+    rows = nodes // WAYS
+    live = lax.broadcasted_iota(jnp.int32, (1, slots), 1) < count[0, 0]
+    src_t[...] = one_hot_t(src_held[...] ^ (lax.axis_index("dst") * rows), nodes)
+    dst_t[...] = one_hot_t(dst_held[...] ^ (lax.axis_index("src") * rows), nodes, live)
+    copies[2].wait()
+    copies[3].wait()
+    for moment in range(T_STEPS):
+        base[moment] = mm(attr[moment], w1[2 * width :])
+    for copy in copies[4:]:
+        copy.wait()
+
+
+def forward_kernel(moment, *refs):
+    n = WAYS
+    sources, targets, refs = refs[:n], refs[n : 2 * n], refs[2 * n :]
+    base, src_t, dst_t, w1, w2, message, own, slope, sums = refs
+    width = sources[0].shape[2]
+    ends = jnp.concatenate(
+        [
+            mm_tn(src_t[...], stacked(sources, moment)).astype(BF),
+            mm_tn(dst_t[...], stacked(targets, moment)[:, :width]).astype(BF),
+        ],
+        axis=1,
+    )
+    pre = base[moment] + mm(ends, w1[: 2 * width])
+    sigma = sigmoid(pre)
+    hidden = (pre * sigma).astype(BF)
+    slope[...] = sigma * (1.0 + pre * (1.0 - sigma))
+    total = mm(dst_t[...], hidden)
+    high = total.astype(BF)
+    low = (total - high.astype(F32)).astype(BF)
+    sums[...] = high
+    product = mm(high, w2[...]) + mm(low, w2[...])
+    own[...] = product
+    message[...] = product.astype(BF)
+
+
+def first_sum_kernel(own, arrived, total, sent):
+    value = own[...] + turned(arrived[...].astype(F32), 1)
+    total[...] = value
+    sent[...] = value.astype(BF)
+
+
+def backward(moment, sources, targets, total, arrived, attr, src_t, dst_t, slope, sums, w1, w2, wn, node_held):
+    n = WAYS
+    rows, width = targets[0].shape[1], sources[0].shape[2]
+    width_m = w2.shape[1]
+    joined = stacked(targets, moment)
+    state, forcing, cotangent = joined[:, :width], joined[:, width : 2 * width], joined[:, 2 * width :]
+    agg = total[...] + turned(arrived[...].astype(F32), 2)
+    node_in = jnp.concatenate([state, agg.astype(BF), forcing], axis=1)
+    node_held[...] = node_in
+    grad_pre = (cotangent.astype(F32) * slope_of(mm(node_in, wn[...]))).astype(BF)
+    grad_in = mm_nt(grad_pre, wn[...])
+    grad_agg = grad_in[:, width : width + width_m].astype(BF)
+    grad_message = mm_tn(dst_t[...], grad_agg).astype(BF)
+    grad_pre_edge = (mm_nt(grad_message, w2[...]) * slope[...]).astype(BF)
+    edges = mm_nt(grad_pre_edge, w1[2 * width :])
+    from_src = mm(src_t[...], grad_pre_edge).astype(BF)
+    from_dst = mm(dst_t[...], grad_pre_edge).astype(BF)
+    to_src = mm_nt(from_src, w1[:width])
+    to_dst = mm_nt(from_dst, w1[width : 2 * width])
+    first = [
+        mm_tn(stacked(sources, moment), from_src),
+        mm_tn(state, from_dst),
+        mm_tn(attr[moment], grad_pre_edge),
+    ]
+    second = mm_tn(sums[...], grad_agg)
+    block = wn.shape[0] // n
+    spot = pl.multiple_of(lax.axis_index("src") * block, block)
+    node_grad = mm_tn(node_held[:, pl.ds(spot, block)], grad_pre)
+    state_own = grad_in[:rows, :width] + to_dst[:rows]
+    return state_own, grad_in[:rows, width + width_m :], edges, to_src, to_dst, first, second, node_grad
+
+
+def split_refs(refs):
+    n = WAYS
+    return refs[:n], refs[n : 2 * n], refs[2 * n : 2 * n + 10], refs[2 * n + 10 :]
+
+
+def backward_first_kernel(*refs):
+    sources, targets, args, refs = split_refs(refs)
+    *outs, first_out, second_out, node_out, node_held = refs
+    *values, first, second, node_grad = backward(0, sources, targets, *args, node_held)
+    for ref, value in zip(outs, values, strict=True):
+        ref[...] = value
+    width = first[0].shape[0]
+    for i, value in enumerate(first):
+        first_out[i * width : (i + 1) * width] = value
+    second_out[...] = second
+    node_out[...] = node_grad
+
+
+def backward_last_kernel(*refs):
+    n = WAYS
+    sources, targets, args, refs = split_refs(refs)
+    state_0, forcing_0, edges_0, to_src_0, to_dst_0, first_0, second_0, node_0 = refs[:8]
+    state_own, forcing_own, edges, kept_a, core_a, kept_b, core_b, target_kept, target_sent = refs[8:17]
+    first_held, second_held, node_grad_held, node_held = refs[17:]
+    state_1, forcing_1, edges_1, to_src_1, to_dst_1, first, second, node_grad = backward(
+        1, sources, targets, *args, node_held
+    )
+    state_own[0], state_own[1] = state_0[...], state_1
+    forcing_own[0], forcing_own[1] = forcing_0[...], forcing_1
+    edges[0], edges[1] = edges_0[...], edges_1
+    width = first[0].shape[0]
+    for i, value in enumerate(first):
+        first_held[i * width : (i + 1) * width] = first_0[i * width : (i + 1) * width] + value
+    second_held[...] = second_0[...] + second
+    node_grad_held[...] = node_0[...] + node_grad
+    part, block, small = first_held.shape[0] // n, second_held.shape[0] // n, node_grad_held.shape[0] // n
+    wide = node_grad_held.shape[1]
+    for k in range(n):
+        other = lax.axis_index("dst") ^ k
+        into = core_a if k % 2 else kept_a
+        start = (k // 2) * part
+        into[start : start + part] = first_held[pl.ds(pl.multiple_of(other * part, part), part)].astype(into.dtype)
+        into = core_b if k % 2 else kept_b
+        start = (k // 2) * (into.shape[0] // 2)
+        for j in range(2):
+            lanes = slice(j * wide, (j + 1) * wide)
+            size = block // 2
+            spot = pl.ds(pl.multiple_of(other * block + j * size, size), size)
+            into[start : start + size, lanes] = second_held[spot].astype(into.dtype)
+            tiny = small // 2
+            spot = pl.ds(pl.multiple_of(other * small + j * tiny, tiny), tiny)
+            into[start + size : start + size + tiny, lanes] = node_grad_held[spot].astype(into.dtype)
+        start += block // 2 + small // 2
+        put_nodes(into, start, k, (to_src_0[...], to_src_1))
+    put_nodes(target_kept, 0, 2, (to_dst_0[...], to_dst_1))
+    for i, k in enumerate((1, 3)):
+        put_nodes(target_sent, i * target_kept.shape[0], k, (to_dst_0[...], to_dst_1))
+
+
+def put_nodes(into, start, k, values):
+    width = values[0].shape[1]
+    rows = values[0].shape[0] // WAYS
+    half = rows // 2
+    for moment, value in enumerate(values):
+        for j in range(2):
+            lanes = slice((moment * 2 + j) * width, (moment * 2 + j + 1) * width)
+            spot = slice(k * rows + j * half, k * rows + (j + 1) * half)
+            into[start : start + half, lanes] = value[spot].astype(into.dtype)
+
+
+def add_nodes(state, base, value):
+    width, half = state.shape[2], value.shape[0]
+    for moment in range(T_STEPS):
+        for j in range(2):
+            lanes = slice((moment * 2 + j) * width, (moment * 2 + j + 1) * width)
+            spot = slice(j * half, (j + 1) * half)
+            state[moment, spot] = base[moment, spot] + value[:, lanes]
+
+
+def near_kernel(kept, arrived, own, across):
+    wide = own.shape[0]
+    own[...] = kept[:wide] + arrived[:wide].astype(F32)
+    across[...] = (kept[wide:] + arrived[wide:].astype(F32)).astype(BF)
+
+
+def add_kernel(mine, arrived, own, sent):
+    total = mine[...] + arrived[...].astype(F32)
+    own[...] = total
+    sent[...] = total.astype(BF)
+
+
+def last_add_kernel(mine, arrived, sent):
+    sent[...] = (mine[...] + arrived[...].astype(F32)).astype(BF)
+
+
+def middle_kernel(mine, arrived, state_own, target_sent, state, own, sent):
+    total = mine[...] + arrived[...].astype(F32)
+    core = own.shape[0]
+    own[...] = total[:core]
+    sent[:core] = total[:core].astype(BF)
+    sent[core:] = target_sent[...]
+    add_nodes(state, state_own, total[core:])
+
+
+def second_sum_kernel(mine, arrived, target_kept, state_in, state, own, sent):
+    size, half = own.shape[0], target_kept.shape[0]
+    core = mine.shape[0]
+    tiny = core - size
+    total = mine[:size] + arrived[:size].astype(F32)
+    own[...] = total
+    sent[:size] = total.astype(BF)
+    sent[size:core] = mine[size:].astype(BF)
+    sent[core : core + tiny] = arrived[size:core]
+    add_nodes(state, state_in, arrived[core : core + half].astype(F32))
+    sent[core + tiny :] = (target_kept[...] + arrived[core + half :].astype(F32)).astype(BF)
+
+
+def gather_kernel(mine, sent, arrived, state_in, state, share):
+    size, half = mine.shape[0], state.shape[1] // 2
+    tiny = (share.shape[0] - size) // WAYS
+    share[:size] = (mine[...] + arrived[:size].astype(F32)).astype(BF)
+    add_nodes(state, state_in, arrived[size + 2 * tiny :].astype(F32))
+    for k in range(WAYS):
+        start = pl.multiple_of(size + (lax.axis_index("src") ^ k) * tiny, tiny)
+        spot = slice(size + (k % 2) * tiny, size + (k % 2 + 1) * tiny)
+        share[pl.ds(start, tiny)] = (arrived if k // 2 else sent)[spot]
+
+
+def final_first_kernel(*refs):
+    shares, out = refs[:WAYS], refs[WAYS]
+    part = out.shape[0] // WAYS
+    for k in range(WAYS):
+        start = pl.multiple_of((lax.axis_index("dst") ^ k) * part, part)
+        out[pl.ds(start, part)] = shares[k][...].astype(F32)
+
+
+def final_second_kernel(*refs):
+    n = WAYS
+    shares, (second, node) = refs[:n], refs[n:]
+    block = second.shape[0] // n
+    small = block // n
+    size, tiny = block // 2, small // 2
+    wide = second.shape[1]
+    for k in range(n):
+        other = lax.axis_index("dst") ^ k
+        for i in range(2):
+            lanes = slice(i * wide, (i + 1) * wide)
+            start = pl.multiple_of(other * block + i * size, size)
+            second[pl.ds(start, size)] = shares[k][:size, lanes].astype(F32)
+            for j in range(n):
+                start = pl.multiple_of(j * block + other * small + i * tiny, tiny)
+                spot = slice(size + j * tiny, size + (j + 1) * tiny)
+                node[pl.ds(start, tiny)] = shares[k][spot, lanes].astype(F32)
+
+
+def call(kernel, outs, scratch, args, spaces=None):
+    return pl.pallas_call(
+        kernel,
+        out_shape=[jax.ShapeDtypeStruct(shape, dtype) for shape, dtype in outs],
+        in_specs=[pl.BlockSpec(memory_space=space) for space in spaces or [pltpu.VMEM] * len(args)],
+        out_specs=[pl.BlockSpec(memory_space=pltpu.VMEM)] * len(outs),
+        scratch_shapes=[
+            pltpu.VMEM(*entry) if isinstance(entry, tuple) else entry for entry in scratch
+        ],
+        compiler_params=pltpu.CompilerParams(vmem_limit_bytes=32 << 20),
+    )(*args)
+
+
+def in_hbm(value):
+    return pltpu.with_memory_space_constraint(value, pltpu.HBM)
+
+
+def swap(value, axis, k):
+    return lax.ppermute(value, axis, [(i, i ^ k) for i in range(WAYS)])
+
+
+def all_dst(share):
+    across = swap(share, "dst", 2)
+    return [share, swap(share, "dst", 1), across, swap(across, "dst", 1)]
+
+
+def local(
+    node_state,
+    forcing,
+    edge_attr,
+    src_index,
+    dst_index,
+    edge_count,
+    cotangent,
+    edge_w1,
+    edge_w2,
+    node_w1,
+):
+    rows, width = node_state.shape[1:]
+    hid, width_m = edge_w2.shape
+    width_in, width_out = node_w1.shape
+    slots = edge_attr.shape[3]
+    nodes = rows * WAYS
+    steps = T_STEPS
+    attr = edge_attr[:, 0, 0]
+    near = swap(node_state, "dst", 1)
+    across = swap(node_state, "dst", 2)
+    joined = call(
+        join_kernel,
+        [((steps, rows, 2 * width + width_out), BF)],
+        [pltpu.SemaphoreType.DMA((3,))],
+        [near, *(in_hbm(value) for value in (node_state, forcing, cotangent))],
+        [pltpu.VMEM] + [pltpu.HBM] * 3,
+    )[0]
+    targets = {k: swap(joined, "src", k) for k in ORDER}
+    targets = [joined] + [targets[k] for k in range(1, WAYS)]
+    sources = [node_state, near, across, swap(near, "dst", 2)]
+    attr, w1, w2, wn, src_t, dst_t, base, sources[0] = call(
+        stage_kernel,
+        [
+            (attr.shape, BF),
+            (edge_w1.shape, BF),
+            (edge_w2.shape, BF),
+            (node_w1.shape, BF),
+            ((nodes, slots), BF),
+            ((nodes, slots), BF),
+            ((steps, slots, hid), F32),
+            (node_state.shape, BF),
+        ],
+        [((1, slots), jnp.int32), ((1, slots), jnp.int32), pltpu.SemaphoreType.DMA((7,))],
+        [edge_count]
+        + [in_hbm(value) for value in (src_index[0], dst_index[0], attr, edge_w1, edge_w2, node_w1, node_state)],
+        [pltpu.SMEM] + [pltpu.HBM] * 7,
+    )
+    forward, sums = [], []
+    for moment in range(steps):
+        forward.append(
+            call(
+                functools.partial(forward_kernel, moment),
+                [((nodes, width_m), BF), ((nodes, width_m), F32), ((slots, hid), F32), ((nodes, hid), BF)],
+                [],
+                [*sources, *targets, base, src_t, dst_t, w1, w2],
+            )
+        )
+    for message, own, _, _ in forward:
+        total, sent = call(
+            first_sum_kernel,
+            [((nodes, width_m), F32), ((nodes, width_m), BF)],
+            [],
+            [own, swap(message, "src", 1)],
+        )
+        sums.append([total, swap(sent, "src", 2)])
+    args = [
+        [*sources, *targets, *sums[moment], attr, src_t, dst_t, *forward[moment][2:], w1, w2, wn]
+        for moment in range(steps)
+    ]
+    block = width_in // WAYS
+    earlier = call(
+        backward_first_kernel,
+        [
+            ((rows, width), F32),
+            ((rows, width), F32),
+            ((slots, width), F32),
+            ((nodes, width), F32),
+            ((nodes, width), F32),
+            (edge_w1.shape, F32),
+            (edge_w2.shape, F32),
+            ((block, width_out), F32),
+        ],
+        [((nodes, width_in), BF)],
+        args[0],
+    )
+    part, size, tiny, half = edge_w1.shape[0] // WAYS, hid // WAYS // 2, block // WAYS // 2, rows // 2
+    core = size + tiny
+    wide = core + half
+    state_own, grad_forcing, edges, kept_a, core_a, kept_b, core_b, target_kept, target_sent = call(
+        backward_last_kernel,
+        [
+            ((steps, rows, width), F32),
+            ((steps, rows, width), F32),
+            ((steps, slots, width), F32),
+            ((2 * part, hid), F32),
+            ((2 * part, hid), BF),
+            ((2 * wide, hid), F32),
+            ((2 * wide, hid), BF),
+            ((half, hid), F32),
+            ((2 * half, hid), BF),
+        ],
+        [(edge_w1.shape, F32), (edge_w2.shape, F32), ((block, width_out), F32), ((nodes, width_in), BF)],
+        [*args[1], *earlier],
+    )
+
+    def pair(size):
+        return [((size, hid), F32), ((size, hid), BF)]
+
+    state = ((steps, rows, width), F32)
+    mine_a, across_a = call(near_kernel, pair(part), [], [kept_a, swap(core_a, "dst", 1)])
+    mine_b, across_b = call(near_kernel, pair(wide), [], [kept_b, swap(core_b, "dst", 1)])
+    own_a, sent_a = call(add_kernel, pair(part), [], [mine_a, swap(across_a, "dst", 2)])
+    state_sum, own_b, sent_b = call(
+        middle_kernel,
+        [state, ((core, hid), F32), ((core + 2 * half, hid), BF)],
+        [],
+        [mine_b, swap(across_b, "dst", 2), state_own, target_sent],
+    )
+    own_a, sent_a = call(add_kernel, pair(part), [], [own_a, swap(sent_a, "src", 1)])
+    state_sum, own_b, sent_b = call(
+        second_sum_kernel,
+        [state, ((size, hid), F32), ((core + tiny + half, hid), BF)],
+        [],
+        [own_b, swap(sent_b, "src", 1), target_kept, state_sum],
+    )
+    share_a = call(last_add_kernel, [((part, hid), BF)], [], [own_a, swap(sent_a, "src", 2)])[0]
+    grad_state, share_b = call(
+        gather_kernel,
+        [state, ((size + WAYS * tiny, hid), BF)],
+        [],
+        [own_b, sent_b, swap(sent_b, "src", 2), state_sum],
+    )
+    grad_first = call(final_first_kernel, [(edge_w1.shape, F32)], [], all_dst(share_a))[0]
+    grad_second, grad_node = call(
+        final_second_kernel, [(edge_w2.shape, F32), (node_w1.shape, F32)], [], all_dst(share_b)
+    )
+    return grad_state, grad_forcing, edges[:, None, None], grad_first, grad_second, grad_node
 
 
 def silu_slope(value):
@@ -11,7 +487,7 @@
     return sigma * (1.0 + value * (1.0 - sigma))
 
 
-def local(
+def local_any(
     node_state,
     forcing,
     edge_attr,
@@ -122,4 +598,6 @@
         P("groups", None),
         P("groups", None),
     )
-    return jax.shard_map(local, mesh=mesh, in_specs=in_specs, out_specs=out_specs, check_vma=False)
+    square = mesh.shape["src"] == WAYS and mesh.shape["dst"] == WAYS
+    body = local if square else local_any
+    return jax.shard_map(body, mesh=mesh, in_specs=in_specs, out_specs=out_specs, check_vma=False)

time: 242 us -> 62.3 us (0.26)
  blocking collectives: 72.5 us -> 0 us
  waiting for transfers between devices: 92.6 us -> 23 us
  starting transfers between devices: 0.21 us -> 26.4 us
  other arithmetic: 23.3 us -> 0 us
  local copies, waits for them, and re-layouts: 20.2 us -> 0 us
  matrix products: 16 us -> 0 us
  between operations: 16.4 us -> 1.4 us
  Pallas kernels: 0 us -> 11.2 us
    reduce_scatter x4 -> x0, waiting for transfers between devices: 52.2 us -> none  [the longest x2 30.9 us: local(): lax.psum_scatter(source_part, 'dst', scatter_dimension=0, tiled=True)]
    all_gather x4 -> x0, blocking collectives: 47.7 us -> none  [the longest x1 14.2 us: local(): lax.all_gather(cotangent, 'src', axis=1, tiled=True)]
    psum x1 -> x0, waiting for transfers between devices: 40.3 us -> none  [local(): lax.psum((grad_first, grad_second, grad_node), ('src', 'dst'))]
    ppermute x0 -> x24, starting transfers between devices: none -> 26.4 us  [swap(): return lax.ppermute(value, axis, [(i, i ^ k) for i in range(WAYS)])]
    psum x1 -> x0, blocking collectives: 24.8 us -> none  [local(): agg_block = lax.psum(partial_value, 'src')]
    ppermute x0 -> x24, waiting for transfers between devices: none -> 23 us  [swap(): return lax.ppermute(value, axis, [(i, i ^ k) for i in range(WAYS)])]
    scatter-add x6 -> x0, other arithmetic: 18.1 us -> none  [the longest x2 6.68 us: local(): jax.ops.segment_sum(message, dst_local, num_segments=dst_rows)]
    dot_general x18 -> x0, matrix products: 16 us -> none  [the longest x2 3.97 us: local(): jnp.dot(hidden.T, grad_message, preferred_element_type=jnp.float32)]
  transfers between devices with their start and end apart: 5 -> 24, of which waited for: 4 -> 13; matrix products, arithmetic and copies ran while one was open for 11% -> 0% of each run, Pallas kernels for 0% -> 10%
where the time goes in v3:
time: 62.3 us; the launch traced here: 62 us
  starting transfers between devices  26.4 us (42%)
  waiting for transfers between devices  23 us (37%)
  Pallas kernels  11.2 us (18%)
  between operations  1.4 us (2%)
    ppermute x24, starting transfers between devices, swap(): return lax.ppermute(value, axis, [(i, i ^ k) for i in range(WAYS)])  26.4 us
    ppermute x24, waiting for transfers between devices, swap(): return lax.ppermute(value, axis, [(i, i ^ k) for i in range(WAYS)])  23 us
    pallas_call x18, Pallas kernels, call(): pl.pallas_call(kernel, out_shape=[jax.ShapeDtypeStruct(shape, dtype) for...  11.2 us
  transfers between devices with their start and end apart: 24, of which 13 were waited for; matrix products, arithmetic and copies ran while one was open for 0% of the time, Pallas kernels for 10%

profile of v3, /device:TPU:0, one launch (start us, length us, event | category | flops | bytes accessed | tf_op | source)
XLA Modules:
  0.0 62.0 jit_solution(9606647653512384830)
XLA Ops:
  1.1 1.0 %collective-permute-done.near.refs_1_ = bf16[2,32,128]{2,1,0:T(8,128)(2,1)S(1)} collective-permute-done((bf16[2,32,128]{2,1,0:T(8,128)(2,1)}, bf16[2,32,128]{2,1,0:T(8,128)(2,1)S(1)}, u32[]{:S(2)}, u32[]{:S(2)}) %collective-permute-start) | collective-permute-done | bytes 16416 | tf_op jit(solution)/shard_map/ppermute | solution.py:337
  3.0 5.0 %collective-permute-start.5 = (bf16[2,32,512]{2,1,0:T(8,128)(2,1)S(1)}, bf16[2,32,512]{2,1,0:T(8,128)(2,1)S(1)}, u32[]{:S(2)}, u32[]{:S(2)}) collective-permute-start(bf16[2,32,512]{2,1,0:T(8,128)(2,1)S(1)} %shard_map.146.refs_4_), channel_id=1, source_target_pairs={{0,12},{4,8},{8,4},{12,0},{1,13},{5,9},{9,5},{13,1},{2,14},{6,10},... | collective-permute-start | bytes 196616 | tf_op jit(solution)/shard_map/ppermute | solution.py:337
  8.7 1.6 %collective-permute-start.1 = (bf16[2,32,128]{2,1,0:T(8,128)(2,1)}, bf16[2,32,128]{2,1,0:T(8,128)(2,1)S(1)}, u32[]{:S(2)}, u32[]{:S(2)}) collective-permute-start(bf16[2,32,128]{2,1,0:T(8,128)(2,1)} %state.1), channel_id=1, source_target_pairs={{0,2},{1,3},{2,0},{3,1},{4,6},{5,7},{6,4},{7,5},{8,10},{9,11},{10,... | collective-permute-start | bytes 49160 | tf_op jit(solution)/shard_map/ppermute | solution.py:337
  11.4 1.6 %shard_map.145 = (bf16[2,512,128]{2,1,0:T(8,128)(2,1)S(1)}, bf16[384,512]{1,0:T(8,128)(2,1)S(1)}, bf16[512,256]{1,0:T(8,128)(2,1)S(1)}, bf16[512,256]{1,0:T(8,12...) custom-call(s32[1,1]{1,0:T(1,128)S(6)} %copy.17.count, ...), custom_call_target="tpu_custom_call" | custom-call | tf_op jit(solution)/shard_map/pallas_call | solution.py:320
  13.0 1.1 %collective-permute-done.2.refs_3_ = bf16[2,32,128]{2,1,0:T(8,128)(2,1)S(1)} collective-permute-done((bf16[2,32,128]{2,1,0:T(8,128)(2,1)S(1)}, bf16[2,32,128]{2,1,0:T(8,128)(2,1)S(1)}, u32[]{:S(2)}, u32[]{:S(2)}) %collective-permute-start.2) | collective-permute-done | bytes 16416 | tf_op jit(solution)/shard_map/ppermute | solution.py:337
  14.1 1.0 %shard_map.149 = (bf16[128,256]{1,0:T(8,128)(2,1)S(1)}, f32[128,256]{1,0:T(8,128)S(1)}, f32[512,512]{1,0:T(8,128)S(1)}, bf16[128,512]{1,0:T(8,128)(2,1)S(1)}) custom-call(bf16[2,32,128]{2,1,0:T(8,128)(2,1)S(1)} %get-tuple-element.61.refs_0_, bf16[2,32,128]{2,1,0:T(8,128)(2,1)S(1)} %collective-permute-done.near.refs_1_, ...), custom_call_target="tpu_custom_call" | custom-call | tf_op jit(solution)/shard_map/pallas_call | solution.py:320
  15.1 1.3 %collective-permute-start.8 = (bf16[128,256]{1,0:T(8,128)(2,1)S(1)}, bf16[128,256]{1,0:T(8,128)(2,1)S(1)}, u32[]{:S(2)}, u32[]{:S(2)}) collective-permute-start(bf16[128,256]{1,0:T(8,128)(2,1)S(1)} %get-tuple-element.76), channel_id=1, source_target_pairs={{0,4},{4,0},{8,12},{12,8},{1,5},{5,1},{9,13},{13,9},{2,6},{6,2},{1... | collective-permute-start | bytes 196616 | tf_op jit(solution)/shard_map/ppermute | solution.py:337
  16.4 1.0 %shard_map.147 = (bf16[128,256]{1,0:T(8,128)(2,1)S(1)}, f32[128,256]{1,0:T(8,128)S(1)}, f32[512,512]{1,0:T(8,128)S(1)}, bf16[128,512]{1,0:T(8,128)(2,1)S(1)}) custom-call(bf16[2,32,128]{2,1,0:T(8,128)(2,1)S(1)} %get-tuple-element.61.refs_0_, bf16[2,32,128]{2,1,0:T(8,128)(2,1)S(1)} %collective-permute-done.near.refs_1_, ...), custom_call_target="tpu_custom_call" | custom-call | tf_op jit(solution)/shard_map/pallas_call | solution.py:320
  18.3 1.8 %collective-permute-done.8.arrived = bf16[128,256]{1,0:T(8,128)(2,1)S(1)} collective-permute-done((bf16[128,256]{1,0:T(8,128)(2,1)S(1)}, bf16[128,256]{1,0:T(8,128)(2,1)S(1)}, u32[]{:S(2)}, u32[]{:S(2)}) %collective-permute-start.8) | collective-permute-done | bytes 65568 | tf_op jit(solution)/shard_map/ppermute | solution.py:337
  20.1 2.2 %collective-permute-start.9 = (bf16[128,256]{1,0:T(8,128)(2,1)S(1)}, bf16[128,256]{1,0:T(8,128)(2,1)S(1)}, u32[]{:S(2)}, u32[]{:S(2)}) collective-permute-start(bf16[128,256]{1,0:T(8,128)(2,1)S(1)} %get-tuple-element.78), channel_id=1, source_target_pairs={{0,8},{4,12},{8,0},{12,4},{1,9},{5,13},{9,1},{13,5},{2,10},{6,14},... | collective-permute-start | bytes 196616 | tf_op jit(solution)/shard_map/ppermute | solution.py:337
  22.3 2.5 %collective-permute-start.7 = (bf16[128,256]{1,0:T(8,128)(2,1)S(1)}, bf16[128,256]{1,0:T(8,128)(2,1)S(1)}, u32[]{:S(2)}, u32[]{:S(2)}) collective-permute-start(bf16[128,256]{1,0:T(8,128)(2,1)S(1)} %get-tuple-element.70), channel_id=1, source_target_pairs={{0,8},{4,12},{8,0},{12,4},{1,9},{5,13},{9,1},{13,5},{2,10},{6,14},... | collective-permute-start | bytes 196616 | tf_op jit(solution)/shard_map/ppermute | solution.py:337
  24.8 1.7 %collective-permute-done.9.refs_9_ = bf16[128,256]{1,0:T(8,128)(2,1)S(1)} collective-permute-done((bf16[128,256]{1,0:T(8,128)(2,1)S(1)}, bf16[128,256]{1,0:T(8,128)(2,1)S(1)}, u32[]{:S(2)}, u32[]{:S(2)}) %collective-permute-start.9) | collective-permute-done | bytes 65568 | tf_op jit(solution)/shard_map/ppermute | solution.py:337
  26.5 1.5 %shard_map.151 = (f32[32,128]{1,0:T(8,128)S(1)}, f32[32,128]{1,0:T(8,128)S(1)}, f32[512,128]{1,0:T(8,128)S(1)}, f32[128,128]{1,0:T(8,128)S(1)}, f32[128,128]{1,0...) custom-call(bf16[2,32,128]{2,1,0:T(8,128)(2,1)S(1)} %get-tuple-element.61.refs_0_, ...), custom_call_target="tpu_custom_call" | custom-call | tf_op jit(solution)/shard_map/pallas_call | solution.py:320
  28.0 2.4 %shard_map.152 = (f32[2,32,128]{2,1,0:T(8,128)S(1)}, f32[2,32,128]{2,1,0:T(8,128)}, f32[2,512,128]{2,1,0:T(8,128)}, f32[192,512]{1,0:T(8,128)S(1)}, bf16[192,512...) custom-call(bf16[2,32,128]{2,1,0:T(8,128)(2,1)S(1)} %get-tuple-eleme, ...), custom_call_target="tpu_custom_call" | custom-call | tf_op jit(solution)/shard_map/pallas_call | solution.py:320
  31.9 1.3 %collective-permute-start.11 = (bf16[96,512]{1,0:T(8,128)(2,1)S(1)}, bf16[96,512]{1,0:T(8,128)(2,1)S(1)}, u32[]{:S(2)}, u32[]{:S(2)}) collective-permute-start(bf16[96,512]{1,0:T(8,128)(2,1)S(1)} %get-tuple-element.92), channel_id=1, source_target_pairs={{0,2},{1,3},{2,0},{3,1},{4,6},{5,7},{6,4},{7,5},{8,10},{9,11},{10,... | collective-permute-start | bytes 294920 | tf_op jit(solution)/shard_map/ppermute | solution.py:337
  34.1 3.5 %collective-permute-done.11.arrived = bf16[96,512]{1,0:T(8,128)(2,1)S(1)} collective-permute-done((bf16[96,512]{1,0:T(8,128)(2,1)S(1)}, bf16[96,512]{1,0:T(8,128)(2,1)S(1)}, u32[]{:S(2)}, u32[]{:S(2)}) %collective-permute-start.11) | collective-permute-done | bytes 98336 | tf_op jit(solution)/shard_map/ppermute | solution.py:337
  39.9 3.3 %collective-permute-done.12.arrived = bf16[112,512]{1,0:T(8,128)(2,1)S(1)} collective-permute-done((bf16[112,512]{1,0:T(8,128)(2,1)S(1)}, bf16[112,512]{1,0:T(8,128)(2,1)S(1)}, u32[]{:S(2)}, u32[]{:S(2)}) %collective-permute-start.12) | collective-permute-done | bytes 114720 | tf_op jit(solution)/shard_map/ppermute | solution.py:337
  43.2 2.4 %collective-permute-start.13 = (bf16[112,512]{1,0:T(8,128)(2,1)S(1)}, bf16[112,512]{1,0:T(8,128)(2,1)S(1)}, u32[]{:S(2)}, u32[]{:S(2)}) collective-permute-start(bf16[112,512]{1,0:T(8,128)(2,1)S(1)} %get-tuple-element.100.sent), channel_id=1, source_target_pairs={{0,8},{4,12},{8,0},{12,4},{1,9},{5,13},{9,1},{13,5},{2,10},{6,14},... | collective-permute-start | bytes 344072 | tf_op jit(solution)/shard_map/ppermute | solution.py:337
  45.6 1.8 %collective-permute-start.17 = (bf16[96,512]{1,0:T(8,128)(2,1)S(1)}, bf16[96,512]{1,0:T(8,128)(2,1)S(1)}, u32[]{:S(2)}, u32[]{:S(2)}) collective-permute-start(bf16[96,512]{1,0:T(8,128)(2,1)S(1)} %get-tuple-element.112), channel_id=1, source_target_pairs={{0,8},{4,12},{8,0},{12,4},{1,9},{5,13},{9,1},{13,5},{2,10},{6,14},... | collective-permute-start | bytes 294920 | tf_op jit(solution)/shard_map/ppermute | solution.py:337
  47.4 4.6 %collective-permute-done.13.arrived = bf16[112,512]{1,0:T(8,128)(2,1)S(1)} collective-permute-done((bf16[112,512]{1,0:T(8,128)(2,1)S(1)}, bf16[112,512]{1,0:T(8,128)(2,1)S(1)}, u32[]{:S(2)}, u32[]{:S(2)}) %collective-permute-start.13) | collective-permute-done | bytes 114720 | tf_op jit(solution)/shard_map/ppermute | solution.py:337
  52.7 1.0 %collective-permute-start.22 = (bf16[128,512]{1,0:T(8,128)(2,1)S(1)}, bf16[128,512]{1,0:T(8,128)(2,1)S(1)}, u32[]{:S(2)}, u32[]{:S(2)}) collective-permute-start(bf16[128,512]{1,0:T(8,128)(2,1)S(1)} %get-tuple-element.113.refs_0_), channel_id=1, source_target_pairs={{0,2},{1,3},{2,0},{3,1},{4,6},{5,7},{6,4},{7,5},{8,10},{9,11},{10,... | collective-permute-start | bytes 393224 | tf_op jit(solution)/shard_map/ppermute | solution.py:337
  53.7 1.1 %collective-permute-start.19 = (bf16[96,512]{1,0:T(8,128)(2,1)S(1)}, bf16[96,512]{1,0:T(8,128)(2,1)S(1)}, u32[]{:S(2)}, u32[]{:S(2)}) collective-permute-start(bf16[96,512]{1,0:T(8,128)(2,1)S(1)} %shard_map.160.refs_0_), channel_id=1, source_target_pairs={{0,2},{1,3},{2,0},{3,1},{4,6},{5,7},{6,4},{7,5},{8,10},{9,11},{10,... | collective-permute-start | bytes 294920 | tf_op jit(solution)/shard_map/ppermute | solution.py:337
  54.8 2.8 %collective-permute-done.22.refs_2_ = bf16[128,512]{1,0:T(8,128)(2,1)S(1)} collective-permute-done((bf16[128,512]{1,0:T(8,128)(2,1)S(1)}, bf16[128,512]{1,0:T(8,128)(2,1)S(1)}, u32[]{:S(2)}, u32[]{:S(2)}) %collective-permute-start.22) | collective-permute-done | bytes 131104 | tf_op jit(solution)/shard_map/ppermute | solution.py:337
  61.0 1.0 %shard_map.162 = (f32[512,256]{1,0:T(8,128)}, f32[512,256]{1,0:T(8,128)}) custom-call(bf16[128,512]{1,0:T(8,128)(2,1)S(1)} %get-tuple-element.113.refs_0_, bf16[128,512]{1,0:T(8,128)(2,1)S(1)} %collective-permute-done.21.refs_1_, bf16[128,512]{1,0:T(8,128)(2,1)S(1)} %collective-permute-done.22.refs_2_, bf16[128,512]{1,0:T(8,128)(2,1)S(1)} %collective-permute-done.23.refs_3_), custom_call_target="tpu_custom_call" | custom-call | tf_op jit(solution)/shard_map/pallas_call | solution.py:320
  (42 shorter events, 11.9 us)
Async XLA Ops:
  0.6 1.6 %collective-permute-start = (bf16[2,32,128]{2,1,0:T(8,128)(2,1)}, bf16[2,32,128]{2,1,0:T(8,128)(2,1)S(1)}, u32[]{:S(2)}, u32[]{:S(2)}) collective-permute-start(bf16[2,32,128]{2,1,0:T(8,128)(2,1)} %state.1), channel_id=1, source_target_pairs={{0,1},{1,0},{2,3},{3,2},{4,5},{5,4},{6,7},{7,6},{8,9},{9,8},{10,11... | collective-permute-start | bytes 49160 | tf_op jit(solution)/shard_map/ppermute | solution.py:337
  3.0 11.0 %collective-permute-start.5 = (bf16[2,32,512]{2,1,0:T(8,128)(2,1)S(1)}, bf16[2,32,512]{2,1,0:T(8,128)(2,1)S(1)}, u32[]{:S(2)}, u32[]{:S(2)}) collective-permute-start(bf16[2,32,512]{2,1,0:T(8,128)(2,1)S(1)} %shard_map.146.refs_4_), channel_id=1, source_target_pairs={{0,12},{4,8},{8,4},{12,0},{1,13},{5,9},{9,5},{13,1},{2,14},{6,10},... | collective-permute-start | bytes 196616 | tf_op jit(solution)/shard_map/ppermute | solution.py:337
  8.0 6.0 %collective-permute-start.4 = (bf16[2,32,512]{2,1,0:T(8,128)(2,1)S(1)}, bf16[2,32,512]{2,1,0:T(8,128)(2,1)S(1)}, u32[]{:S(2)}, u32[]{:S(2)}) collective-permute-start(bf16[2,32,512]{2,1,0:T(8,128)(2,1)S(1)} %shard_map.146.refs_4_), channel_id=1, source_target_pairs={{0,8},{4,12},{8,0},{12,4},{1,9},{5,13},{9,1},{13,5},{2,10},{6,14},... | collective-permute-start | bytes 196616 | tf_op jit(solution)/shard_map/ppermute | solution.py:337
  8.0 6.0 %collective-permute-start.3 = (bf16[2,32,512]{2,1,0:T(8,128)(2,1)S(1)}, bf16[2,32,512]{2,1,0:T(8,128)(2,1)S(1)}, u32[]{:S(2)}, u32[]{:S(2)}) collective-permute-start(bf16[2,32,512]{2,1,0:T(8,128)(2,1)S(1)} %shard_map.146.refs_4_), channel_id=1, source_target_pairs={{0,4},{4,0},{8,12},{12,8},{1,5},{5,1},{9,13},{13,9},{2,6},{6,2},{1... | collective-permute-start | bytes 196616 | tf_op jit(solution)/shard_map/ppermute | solution.py:337
  8.7 4.3 %collective-permute-start.1 = (bf16[2,32,128]{2,1,0:T(8,128)(2,1)}, bf16[2,32,128]{2,1,0:T(8,128)(2,1)S(1)}, u32[]{:S(2)}, u32[]{:S(2)}) collective-permute-start(bf16[2,32,128]{2,1,0:T(8,128)(2,1)} %state.1), channel_id=1, source_target_pairs={{0,2},{1,3},{2,0},{3,1},{4,6},{5,7},{6,4},{7,5},{8,10},{9,11},{10,... | collective-permute-start | bytes 49160 | tf_op jit(solution)/shard_map/ppermute | solution.py:337
  10.3 3.7 %collective-permute-start.2 = (bf16[2,32,128]{2,1,0:T(8,128)(2,1)S(1)}, bf16[2,32,128]{2,1,0:T(8,128)(2,1)S(1)}, u32[]{:S(2)}, u32[]{:S(2)}) collective-permute-start(bf16[2,32,128]{2,1,0:T(8,128)(2,1)S(1)} %collective-permute-done.near.refs_1_), channel_id=1, source_target_pairs={{0,2},{1,3},{2,0},{3,1},{4,6},{5,7},{6,4},{7,5},{8,10},{9,11},{10,... | collective-permute-start | bytes 49160 | tf_op jit(solution)/shard_map/ppermute | solution.py:337
  15.1 5.0 %collective-permute-start.8 = (bf16[128,256]{1,0:T(8,128)(2,1)S(1)}, bf16[128,256]{1,0:T(8,128)(2,1)S(1)}, u32[]{:S(2)}, u32[]{:S(2)}) collective-permute-start(bf16[128,256]{1,0:T(8,128)(2,1)S(1)} %get-tuple-element.76), channel_id=1, source_target_pairs={{0,4},{4,0},{8,12},{12,8},{1,5},{5,1},{9,13},{13,9},{2,6},{6,2},{1... | collective-permute-start | bytes 196616 | tf_op jit(solution)/shard_map/ppermute | solution.py:337
  17.5 4.8 %collective-permute-start.6 = (bf16[128,256]{1,0:T(8,128)(2,1)S(1)}, bf16[128,256]{1,0:T(8,128)(2,1)S(1)}, u32[]{:S(2)}, u32[]{:S(2)}) collective-permute-start(bf16[128,256]{1,0:T(8,128)(2,1)S(1)} %get-tuple-element.68), channel_id=1, source_target_pairs={{0,4},{4,0},{8,12},{12,8},{1,5},{5,1},{9,13},{13,9},{2,6},{6,2},{1... | collective-permute-start | bytes 196616 | tf_op jit(solution)/shard_map/ppermute | solution.py:337
  20.1 6.4 %collective-permute-start.9 = (bf16[128,256]{1,0:T(8,128)(2,1)S(1)}, bf16[128,256]{1,0:T(8,128)(2,1)S(1)}, u32[]{:S(2)}, u32[]{:S(2)}) collective-permute-start(bf16[128,256]{1,0:T(8,128)(2,1)S(1)} %get-tuple-element.78), channel_id=1, source_target_pairs={{0,8},{4,12},{8,0},{12,4},{1,9},{5,13},{9,1},{13,5},{2,10},{6,14},... | collective-permute-start | bytes 196616 | tf_op jit(solution)/shard_map/ppermute | solution.py:337
  22.3 5.7 %collective-permute-start.7 = (bf16[128,256]{1,0:T(8,128)(2,1)S(1)}, bf16[128,256]{1,0:T(8,128)(2,1)S(1)}, u32[]{:S(2)}, u32[]{:S(2)}) collective-permute-start(bf16[128,256]{1,0:T(8,128)(2,1)S(1)} %get-tuple-element.70), channel_id=1, source_target_pairs={{0,8},{4,12},{8,0},{12,4},{1,9},{5,13},{9,1},{13,5},{2,10},{6,14},... | collective-permute-start | bytes 196616 | tf_op jit(solution)/shard_map/ppermute | solution.py:337
  30.4 1.4 %collective-permute-start.10 = (bf16[192,512]{1,0:T(8,128)(2,1)S(1)}, bf16[192,512]{1,0:T(8,128)(2,1)S(1)}, u32[]{:S(2)}, u32[]{:S(2)}) collective-permute-start(bf16[192,512]{1,0:T(8,128)(2,1)S(1)} %get-tuple-element.90), channel_id=1, source_target_pairs={{0,1},{1,0},{2,3},{3,2},{4,5},{5,4},{6,7},{7,6},{8,9},{9,8},{10,11... | collective-permute-start | bytes 589832 | tf_op jit(solution)/shard_map/ppermute | solution.py:337
  30.4 2.8 %collective-permute-start.14 = (bf16[192,512]{1,0:T(8,128)(2,1)S(1)}, bf16[192,512]{1,0:T(8,128)(2,1)S(1)}, u32[]{:S(2)}, u32[]{:S(2)}) collective-permute-start(bf16[192,512]{1,0:T(8,128)(2,1)S(1)} %get-tuple-element.106), channel_id=1, source_target_pairs={{0,1},{1,0},{2,3},{3,2},{4,5},{5,4},{6,7},{7,6},{8,9},{9,8},{10,11... | collective-permute-start | bytes 589832 | tf_op jit(solution)/shard_map/ppermute | solution.py:337
  31.9 5.7 %collective-permute-start.11 = (bf16[96,512]{1,0:T(8,128)(2,1)S(1)}, bf16[96,512]{1,0:T(8,128)(2,1)S(1)}, u32[]{:S(2)}, u32[]{:S(2)}) collective-permute-start(bf16[96,512]{1,0:T(8,128)(2,1)S(1)} %get-tuple-element.92), channel_id=1, source_target_pairs={{0,2},{1,3},{2,0},{3,1},{4,6},{5,7},{6,4},{7,5},{8,10},{9,11},{10,... | collective-permute-start | bytes 294920 | tf_op jit(solution)/shard_map/ppermute | solution.py:337
  33.2 5.7 %collective-permute-start.15 = (bf16[96,512]{1,0:T(8,128)(2,1)S(1)}, bf16[96,512]{1,0:T(8,128)(2,1)S(1)}, u32[]{:S(2)}, u32[]{:S(2)}) collective-permute-start(bf16[96,512]{1,0:T(8,128)(2,1)S(1)} %get-tuple-element.108), channel_id=1, source_target_pairs={{0,2},{1,3},{2,0},{3,1},{4,6},{5,7},{6,4},{7,5},{8,10},{9,11},{10,... | collective-permute-start | bytes 294920 | tf_op jit(solution)/shard_map/ppermute | solution.py:337
  37.6 5.6 %collective-permute-start.12 = (bf16[112,512]{1,0:T(8,128)(2,1)S(1)}, bf16[112,512]{1,0:T(8,128)(2,1)S(1)}, u32[]{:S(2)}, u32[]{:S(2)}) collective-permute-start(bf16[112,512]{1,0:T(8,128)(2,1)S(1)} %get-tuple-element.96), channel_id=1, source_target_pairs={{0,4},{4,0},{8,12},{12,8},{1,5},{5,1},{9,13},{13,9},{2,6},{6,2},{1... | collective-permute-start | bytes 344072 | tf_op jit(solution)/shard_map/ppermute | solution.py:337
  38.9 6.7 %collective-permute-start.16 = (bf16[96,512]{1,0:T(8,128)(2,1)S(1)}, bf16[96,512]{1,0:T(8,128)(2,1)S(1)}, u32[]{:S(2)}, u32[]{:S(2)}) collective-permute-start(bf16[96,512]{1,0:T(8,128)(2,1)S(1)} %get-tuple-element.110), channel_id=1, source_target_pairs={{0,4},{4,0},{8,12},{12,8},{1,5},{5,1},{9,13},{13,9},{2,6},{6,2},{1... | collective-permute-start | bytes 294920 | tf_op jit(solution)/shard_map/ppermute | solution.py:337
  43.2 8.9 %collective-permute-start.13 = (bf16[112,512]{1,0:T(8,128)(2,1)S(1)}, bf16[112,512]{1,0:T(8,128)(2,1)S(1)}, u32[]{:S(2)}, u32[]{:S(2)}) collective-permute-start(bf16[112,512]{1,0:T(8,128)(2,1)S(1)} %get-tuple-element.100.sent), channel_id=1, source_target_pairs={{0,8},{4,12},{8,0},{12,4},{1,9},{5,13},{9,1},{13,5},{2,10},{6,14},... | collective-permute-start | bytes 344072 | tf_op jit(solution)/shard_map/ppermute | solution.py:337
  45.6 8.1 %collective-permute-start.17 = (bf16[96,512]{1,0:T(8,128)(2,1)S(1)}, bf16[96,512]{1,0:T(8,128)(2,1)S(1)}, u32[]{:S(2)}, u32[]{:S(2)}) collective-permute-start(bf16[96,512]{1,0:T(8,128)(2,1)S(1)} %get-tuple-element.112), channel_id=1, source_target_pairs={{0,8},{4,12},{8,0},{12,4},{1,9},{5,13},{9,1},{13,5},{2,10},{6,14},... | collective-permute-start | bytes 294920 | tf_op jit(solution)/shard_map/ppermute | solution.py:337
  52.7 5.0 %collective-permute-start.22 = (bf16[128,512]{1,0:T(8,128)(2,1)S(1)}, bf16[128,512]{1,0:T(8,128)(2,1)S(1)}, u32[]{:S(2)}, u32[]{:S(2)}) collective-permute-start(bf16[128,512]{1,0:T(8,128)(2,1)S(1)} %get-tuple-element.113.refs_0_), channel_id=1, source_target_pairs={{0,2},{1,3},{2,0},{3,1},{4,6},{5,7},{6,4},{7,5},{8,10},{9,11},{10,... | collective-permute-start | bytes 393224 | tf_op jit(solution)/shard_map/ppermute | solution.py:337
  53.7 5.0 %collective-permute-start.19 = (bf16[96,512]{1,0:T(8,128)(2,1)S(1)}, bf16[96,512]{1,0:T(8,128)(2,1)S(1)}, u32[]{:S(2)}, u32[]{:S(2)}) collective-permute-start(bf16[96,512]{1,0:T(8,128)(2,1)S(1)} %shard_map.160.refs_0_), channel_id=1, source_target_pairs={{0,2},{1,3},{2,0},{3,1},{4,6},{5,7},{6,4},{7,5},{8,10},{9,11},{10,... | collective-permute-start | bytes 294920 | tf_op jit(solution)/shard_map/ppermute | solution.py:337
  54.8 6.1 %collective-permute-start.21 = (bf16[128,512]{1,0:T(8,128)(2,1)S(1)}, bf16[128,512]{1,0:T(8,128)(2,1)S(1)}, u32[]{:S(2)}, u32[]{:S(2)}) collective-permute-start(bf16[128,512]{1,0:T(8,128)(2,1)S(1)} %get-tuple-element.113.refs_0_), channel_id=1, source_target_pairs={{0,1},{1,0},{2,3},{3,2},{4,5},{5,4},{6,7},{7,6},{8,9},{9,8},{10,11... | collective-permute-start | bytes 393224 | tf_op jit(solution)/shard_map/ppermute | solution.py:337
  57.7 3.3 %collective-permute-start.23 = (bf16[128,512]{1,0:T(8,128)(2,1)S(1)}, bf16[128,512]{1,0:T(8,128)(2,1)S(1)}, u32[]{:S(2)}, u32[]{:S(2)}) collective-permute-start(bf16[128,512]{1,0:T(8,128)(2,1)S(1)} %collective-permute-done.22.refs_2_), channel_id=1, source_target_pairs={{0,1},{1,0},{2,3},{3,2},{4,5},{5,4},{6,7},{7,6},{8,9},{9,8},{10,11... | collective-permute-start | bytes 393224 | tf_op jit(solution)/shard_map/ppermute | solution.py:337
  57.7 1.5 %collective-permute-start.18 = (bf16[96,512]{1,0:T(8,128)(2,1)S(1)}, bf16[96,512]{1,0:T(8,128)(2,1)S(1)}, u32[]{:S(2)}, u32[]{:S(2)}) collective-permute-start(bf16[96,512]{1,0:T(8,128)(2,1)S(1)} %shard_map.160.refs_0_), channel_id=1, source_target_pairs={{0,1},{1,0},{2,3},{3,2},{4,5},{5,4},{6,7},{7,6},{8,9},{9,8},{10,11... | collective-permute-start | bytes 294920 | tf_op jit(solution)/shard_map/ppermute | solution.py:337
  58.7 1.3 %collective-permute-start.20 = (bf16[96,512]{1,0:T(8,128)(2,1)S(1)}, bf16[96,512]{1,0:T(8,128)(2,1)S(1)}, u32[]{:S(2)}, u32[]{:S(2)}) collective-permute-start(bf16[96,512]{1,0:T(8,128)(2,1)S(1)} %collective-permute-done.19.refs_2_), channel_id=1, source_target_pairs={{0,1},{1,0},{2,3},{3,2},{4,5},{5,4},{6,7},{7,6},{8,9},{9,8},{10,11... | collective-permute-start | bytes 294920 | tf_op jit(solution)/shard_map/ppermute | solution.py:337

commit v4 on v3

--- a/solution.py
+++ b/solution.py
@@ -42,8 +42,8 @@
     return jnp.where(hit, 1.0, 0.0).astype(BF)
 
 
-def stacked(refs, moment):
-    return jnp.concatenate([ref[moment] for ref in refs], axis=0)
+def stacked(refs, moment, width):
+    return jnp.concatenate([ref[moment, :, :width] for ref in refs], axis=0)
 
 
 def turned(value, k):
@@ -51,7 +51,7 @@
     return jnp.concatenate([value[(j ^ k) * rows : ((j ^ k) + 1) * rows] for j in range(WAYS)], axis=0)
 
 
-def join_kernel(near, state, forcing, cotangent, joined, sems):
+def join_kernel(state, forcing, cotangent, joined, sems):
     width = state.shape[2]
     copies = [
         pltpu.make_async_copy(state, joined.at[:, :, :width], sems.at[0]),
@@ -64,9 +64,11 @@
         copy.wait()
 
 
-def stage_kernel(count, src_hbm, dst_hbm, attr_hbm, w1_hbm, w2_hbm, wn_hbm, state_hbm, *refs):
-    attr, w1, w2, wn, src_t, dst_t, base, state, src_held, dst_held, sems = refs
+def stage_kernel(count, src_hbm, dst_hbm, attr_hbm, w1_hbm, w2_hbm, wn_hbm, *refs):
+    attr, w1, w2, wn, src_t, dst_t, base, src_held, dst_held, sems = refs
     width = attr.shape[2]
+    nodes, slots = src_t.shape
+    rows = nodes // WAYS
     copies = [
         pltpu.make_async_copy(source, target, sems.at[i])
         for i, (source, target) in enumerate(
@@ -77,7 +79,6 @@
                 (w1_hbm, w1),
                 (w2_hbm, w2),
                 (wn_hbm, wn),
-                (state_hbm, state),
             ]
         )
     ]
@@ -85,8 +86,6 @@
         copy.start()
     copies[0].wait()
     copies[1].wait()
-    nodes, slots = src_t.shape
-    rows = nodes // WAYS
     live = lax.broadcasted_iota(jnp.int32, (1, slots), 1) < count[0, 0]
     src_t[...] = one_hot_t(src_held[...] ^ (lax.axis_index("dst") * rows), nodes)
     dst_t[...] = one_hot_t(dst_held[...] ^ (lax.axis_index("src") * rows), nodes, live)
@@ -102,11 +101,11 @@
     n = WAYS
     sources, targets, refs = refs[:n], refs[n : 2 * n], refs[2 * n :]
     base, src_t, dst_t, w1, w2, message, own, slope, sums = refs
-    width = sources[0].shape[2]
+    width = sources[1].shape[2]
     ends = jnp.concatenate(
         [
-            mm_tn(src_t[...], stacked(sources, moment)).astype(BF),
-            mm_tn(dst_t[...], stacked(targets, moment)[:, :width]).astype(BF),
+            mm_tn(src_t[...], stacked(sources, moment, width)).astype(BF),
+            mm_tn(dst_t[...], stacked(targets, moment, width)).astype(BF),
         ],
         axis=1,
     )
@@ -131,9 +130,9 @@
 
 def backward(moment, sources, targets, total, arrived, attr, src_t, dst_t, slope, sums, w1, w2, wn, node_held):
     n = WAYS
-    rows, width = targets[0].shape[1], sources[0].shape[2]
+    rows, width = sources[1].shape[1:]
     width_m = w2.shape[1]
-    joined = stacked(targets, moment)
+    joined = stacked(targets, moment, targets[0].shape[2])
     state, forcing, cotangent = joined[:, :width], joined[:, width : 2 * width], joined[:, 2 * width :]
     agg = total[...] + turned(arrived[...].astype(F32), 2)
     node_in = jnp.concatenate([state, agg.astype(BF), forcing], axis=1)
@@ -149,7 +148,7 @@
     to_src = mm_nt(from_src, w1[:width])
     to_dst = mm_nt(from_dst, w1[width : 2 * width])
     first = [
-        mm_tn(stacked(sources, moment), from_src),
+        mm_tn(stacked(sources, moment, width), from_src),
         mm_tn(state, from_dst),
         mm_tn(attr[moment], grad_pre_edge),
     ]
@@ -289,42 +288,55 @@
         share[pl.ds(start, tiny)] = (arrived if k // 2 else sent)[spot]
 
 
-def final_first_kernel(*refs):
-    shares, out = refs[:WAYS], refs[WAYS]
-    part = out.shape[0] // WAYS
-    for k in range(WAYS):
-        start = pl.multiple_of((lax.axis_index("dst") ^ k) * part, part)
-        out[pl.ds(start, part)] = shares[k][...].astype(F32)
-
-
-def final_second_kernel(*refs):
+def put_shares(places, shares_a, shares_b, outs, scratch):
+    first, second, node = outs
+    first_held, second_held, node_held, sems = scratch
     n = WAYS
-    shares, (second, node) = refs[:n], refs[n:]
-    block = second.shape[0] // n
-    small = block // n
-    size, tiny = block // 2, small // 2
-    wide = second.shape[1]
-    for k in range(n):
+    part, block = first.shape[0] // n, second.shape[0] // n
+    small = node.shape[0] // n // n
+    size, tiny, wide = block // 2, small // 2, second.shape[1]
+    copies = []
+
+    def put(source, target):
+        copies.append(pltpu.make_async_copy(source, target, sems.at[len(copies)]))
+        copies[-1].start()
+
+    for i, k in enumerate(places):
         other = lax.axis_index("dst") ^ k
-        for i in range(2):
-            lanes = slice(i * wide, (i + 1) * wide)
-            start = pl.multiple_of(other * block + i * size, size)
-            second[pl.ds(start, size)] = shares[k][:size, lanes].astype(F32)
+        first_held[i] = shares_a[i][...].astype(F32)
+        put(first_held.at[i], first.at[pl.ds(pl.multiple_of(other * part, part), part)])
+        for h in range(2):
+            lanes = slice(h * wide, (h + 1) * wide)
+            second_held[i, h * size : (h + 1) * size] = shares_b[i][:size, lanes].astype(F32)
             for j in range(n):
-                start = pl.multiple_of(j * block + other * small + i * tiny, tiny)
                 spot = slice(size + j * tiny, size + (j + 1) * tiny)
-                node[pl.ds(start, tiny)] = shares[k][spot, lanes].astype(F32)
-
-
-def call(kernel, outs, scratch, args, spaces=None):
+                node_held[i, j, h * tiny : (h + 1) * tiny] = shares_b[i][spot, lanes].astype(F32)
+        put(second_held.at[i], second.at[pl.ds(pl.multiple_of(other * block, block), block)])
+        for j in range(n):
+            start = pl.multiple_of(j * block + other * small, small)
+            put(node_held.at[i, j], node.at[pl.ds(start, small)])
+    for copy in copies:
+        copy.wait()
+
+
+def first_shares_kernel(own_a, near_a, own_b, near_b, *refs):
+    put_shares((0, 1), (own_a, near_a), (own_b, near_b), refs[:3], refs[3:])
+
+
+def last_shares_kernel(across_a, far_a, across_b, far_b, *refs):
+    put_shares((2, 3), (across_a, far_a), (across_b, far_b), refs[3:6], refs[6:])
+
+
+def call(kernel, outs, scratch, args, spaces=None, out_spaces=None, aliases=None):
     return pl.pallas_call(
         kernel,
         out_shape=[jax.ShapeDtypeStruct(shape, dtype) for shape, dtype in outs],
         in_specs=[pl.BlockSpec(memory_space=space) for space in spaces or [pltpu.VMEM] * len(args)],
-        out_specs=[pl.BlockSpec(memory_space=pltpu.VMEM)] * len(outs),
+        out_specs=[pl.BlockSpec(memory_space=space) for space in out_spaces or [pltpu.VMEM] * len(outs)],
         scratch_shapes=[
             pltpu.VMEM(*entry) if isinstance(entry, tuple) else entry for entry in scratch
         ],
+        input_output_aliases=aliases or {},
         compiler_params=pltpu.CompilerParams(vmem_limit_bytes=32 << 20),
     )(*args)
 
@@ -335,11 +347,6 @@
 
 def swap(value, axis, k):
     return lax.ppermute(value, axis, [(i, i ^ k) for i in range(WAYS)])
-
-
-def all_dst(share):
-    across = swap(share, "dst", 2)
-    return [share, swap(share, "dst", 1), across, swap(across, "dst", 1)]
 
 
 def local(
@@ -361,34 +368,24 @@
     nodes = rows * WAYS
     steps = T_STEPS
     attr = edge_attr[:, 0, 0]
-    near = swap(node_state, "dst", 1)
-    across = swap(node_state, "dst", 2)
     joined = call(
         join_kernel,
         [((steps, rows, 2 * width + width_out), BF)],
         [pltpu.SemaphoreType.DMA((3,))],
-        [near, *(in_hbm(value) for value in (node_state, forcing, cotangent))],
-        [pltpu.VMEM] + [pltpu.HBM] * 3,
+        [in_hbm(value) for value in (node_state, forcing, cotangent)],
+        [pltpu.HBM] * 3,
     )[0]
     targets = {k: swap(joined, "src", k) for k in ORDER}
     targets = [joined] + [targets[k] for k in range(1, WAYS)]
-    sources = [node_state, near, across, swap(near, "dst", 2)]
-    attr, w1, w2, wn, src_t, dst_t, base, sources[0] = call(
+    sources = [joined] + [swap(node_state, "dst", k) for k in range(1, WAYS)]
+    given = (src_index[0], dst_index[0], attr, edge_w1, edge_w2, node_w1)
+    attr, w1, w2, wn, src_t, dst_t, base = call(
         stage_kernel,
-        [
-            (attr.shape, BF),
-            (edge_w1.shape, BF),
-            (edge_w2.shape, BF),
-            (node_w1.shape, BF),
-            ((nodes, slots), BF),
-            ((nodes, slots), BF),
-            ((steps, slots, hid), F32),
-            (node_state.shape, BF),
-        ],
-        [((1, slots), jnp.int32), ((1, slots), jnp.int32), pltpu.SemaphoreType.DMA((7,))],
-        [edge_count]
-        + [in_hbm(value) for value in (src_index[0], dst_index[0], attr, edge_w1, edge_w2, node_w1, node_state)],
-        [pltpu.SMEM] + [pltpu.HBM] * 7,
+        [(value.shape, value.dtype) for value in given[2:]]
+        + [((nodes, slots), BF), ((nodes, slots), BF), ((steps, slots, hid), F32)],
+        [((1, slots), jnp.int32), ((1, slots), jnp.int32), pltpu.SemaphoreType.DMA((len(given),))],
+        [edge_count, *(in_hbm(value) for value in given)],
+        [pltpu.SMEM] + [pltpu.HBM] * len(given),
     )
     forward, sums = [], []
     for moment in range(steps):
@@ -475,9 +472,32 @@
         [],
         [own_b, sent_b, swap(sent_b, "src", 2), state_sum],
     )
-    grad_first = call(final_first_kernel, [(edge_w1.shape, F32)], [], all_dst(share_a))[0]
-    grad_second, grad_node = call(
-        final_second_kernel, [(edge_w2.shape, F32), (node_w1.shape, F32)], [], all_dst(share_b)
+    outs = [(edge_w1.shape, F32), (edge_w2.shape, F32), (node_w1.shape, F32)]
+    held = [
+        ((2, part, hid), F32),
+        ((2, block, width_out), F32),
+        ((2, WAYS, 2 * tiny, width_out), F32),
+        pltpu.SemaphoreType.DMA((2 * (2 + WAYS),)),
+    ]
+    shares = [share_a, share_b]
+    across = [swap(share, "dst", 2) for share in shares]
+    near = [swap(share, "dst", 1) for share in shares]
+    grads = call(
+        first_shares_kernel,
+        outs,
+        held,
+        [share_a, near[0], share_b, near[1]],
+        out_spaces=[pltpu.HBM] * 3,
+    )
+    far = [swap(share, "dst", 1) for share in across]
+    grad_first, grad_second, grad_node = call(
+        last_shares_kernel,
+        outs,
+        held,
+        [across[0], far[0], across[1], far[1], *grads],
+        [pltpu.VMEM] * 4 + [pltpu.HBM] * 3,
+        [pltpu.HBM] * 3,
+        {4: 0, 5: 1, 6: 2},
     )
     return grad_state, grad_forcing, edges[:, None, None], grad_first, grad_second, grad_node
 

time: 62.3 us -> 60.5 us (0.971)
  waiting for transfers between devices: 23 us -> 20.2 us
  starting transfers between devices: 26.4 us -> 27.4 us
    ppermute x24, waiting for transfers between devices: 23 us -> 20.2 us  [swap(): return lax.ppermute(value, axis, [(i, i ^ k) for i in range(WAYS)])]
    ppermute x24, starting transfers between devices: 26.4 us -> 27.4 us  [swap(): return lax.ppermute(value, axis, [(i, i ^ k) for i in range(WAYS)])]
  transfers between devices with their start and end apart: 24 -> 24, of which waited for: 13 -> 11; matrix products, arithmetic and copies ran while one was open for 0% -> 0% of each run, Pallas kernels for 10% -> 10%
where the time goes in v4:
time: 60.5 us; the launch traced here: 60.2 us
  starting transfers between devices  27.4 us (45%)
  waiting for transfers between devices  20.2 us (33%)
  Pallas kernels  11.3 us (19%)
  between operations  1.42 us (2%)
    ppermute x24, starting transfers between devices, swap(): return lax.ppermute(value, axis, [(i, i ^ k) for i in range(WAYS)])  27.4 us
    ppermute x24, waiting for transfers between devices, swap(): return lax.ppermute(value, axis, [(i, i ^ k) for i in range(WAYS)])  20.2 us
    pallas_call x18, Pallas kernels, call(): pl.pallas_call(kernel, out_shape=[jax.ShapeDtypeStruct(shape, dtype) for...  11.3 us
  transfers between devices with their start and end apart: 24, of which 11 were waited for; matrix products, arithmetic and copies ran while one was open for 0% of the time, Pallas kernels for 10%

profile of v4, /device:TPU:0, one launch (start us, length us, event | category | flops | bytes accessed | tf_op | source)
XLA Modules:
  0.0 60.2 jit_solution(11706038900053451992)
XLA Ops:
  1.5 5.1 %collective-permute-start.5 = (bf16[2,32,512]{2,1,0:T(8,128)(2,1)S(1)}, bf16[2,32,512]{2,1,0:T(8,128)(2,1)S(1)}, u32[]{:S(2)}, u32[]{:S(2)}) collective-permute-start(bf16[2,32,512]{2,1,0:T(8,128)(2,1)S(1)} %shard_map.145.refs_0_.refs_4_), channel_id=1, source_target_pairs={{0,12},{4,8},{8,4},{12,0},{1,13},{5,9},{9,5},{13,1},{2,14},{6,10},... | collective-permute-start | bytes 196616 | tf_op jit(solution)/shard_map/ppermute | solution.py:349
  7.2 1.7 %collective-permute-start.2 = (bf16[2,32,128]{2,1,0:T(8,128)(2,1)}, bf16[2,32,128]{2,1,0:T(8,128)(2,1)S(1)}, u32[]{:S(2)}, u32[]{:S(2)}) collective-permute-start(bf16[2,32,128]{2,1,0:T(8,128)(2,1)} %state.1), channel_id=1, source_target_pairs={{0,3},{1,2},{2,1},{3,0},{4,7},{5,6},{6,5},{7,4},{8,11},{9,10},{10,... | collective-permute-start | bytes 49160 | tf_op jit(solution)/shard_map/ppermute | solution.py:349
  9.0 1.3 %collective-permute-start.1 = (bf16[2,32,128]{2,1,0:T(8,128)(2,1)}, bf16[2,32,128]{2,1,0:T(8,128)(2,1)S(1)}, u32[]{:S(2)}, u32[]{:S(2)}) collective-permute-start(bf16[2,32,128]{2,1,0:T(8,128)(2,1)} %state.1), channel_id=1, source_target_pairs={{0,2},{1,3},{2,0},{3,1},{4,6},{5,7},{6,4},{7,5},{8,10},{9,11},{10,... | collective-permute-start | bytes 49160 | tf_op jit(solution)/shard_map/ppermute | solution.py:349
  10.9 1.6 %shard_map.146 = (bf16[2,512,128]{2,1,0:T(8,128)(2,1)S(1)}, bf16[384,512]{1,0:T(8,128)(2,1)S(1)}, bf16[512,256]{1,0:T(8,128)(2,1)S(1)}, bf16[512,256]{1,0:T(8,12...) custom-call(s32[1,1]{1,0:T(1,128)S(6)} %copy.23.count, ...), custom_call_target="tpu_custom_call" | custom-call | tf_op jit(solution)/shard_map/pallas_call | solution.py:331
  12.9 1.0 %shard_map.149 = (bf16[128,256]{1,0:T(8,128)(2,1)S(1)}, f32[128,256]{1,0:T(8,128)S(1)}, f32[512,512]{1,0:T(8,128)S(1)}, bf16[128,512]{1,0:T(8,128)(2,1)S(1)}) custom-call(bf16[2,32,512]{2,1,0:T(8,128)(2,1)S(1)} %shard_map.145.refs_0_.refs_4_, bf16[2,32,128]{2,1,0:T(8,128)(2,1)S(1)} %collective-permute-done.refs_1_, ...), custom_call_target="tpu_custom_call" | custom-call | tf_op jit(solution)/shard_map/pallas_call | solution.py:331
  14.0 1.3 %collective-permute-start.8 = (bf16[128,256]{1,0:T(8,128)(2,1)S(1)}, bf16[128,256]{1,0:T(8,128)(2,1)S(1)}, u32[]{:S(2)}, u32[]{:S(2)}) collective-permute-start(bf16[128,256]{1,0:T(8,128)(2,1)S(1)} %get-tuple-element.78), channel_id=1, source_target_pairs={{0,4},{4,0},{8,12},{12,8},{1,5},{5,1},{9,13},{13,9},{2,6},{6,2},{1... | collective-permute-start | bytes 196616 | tf_op jit(solution)/shard_map/ppermute | solution.py:349
  15.3 1.0 %shard_map.147 = (bf16[128,256]{1,0:T(8,128)(2,1)S(1)}, f32[128,256]{1,0:T(8,128)S(1)}, f32[512,512]{1,0:T(8,128)S(1)}, bf16[128,512]{1,0:T(8,128)(2,1)S(1)}) custom-call(bf16[2,32,512]{2,1,0:T(8,128)(2,1)S(1)} %shard_map.145.refs_0_.refs_4_, bf16[2,32,128]{2,1,0:T(8,128)(2,1)S(1)} %collective-permute-done.refs_1_, ...), custom_call_target="tpu_custom_call" | custom-call | tf_op jit(solution)/shard_map/pallas_call | solution.py:331
  17.2 1.3 %collective-permute-done.8.arrived = bf16[128,256]{1,0:T(8,128)(2,1)S(1)} collective-permute-done((bf16[128,256]{1,0:T(8,128)(2,1)S(1)}, bf16[128,256]{1,0:T(8,128)(2,1)S(1)}, u32[]{:S(2)}, u32[]{:S(2)}) %collective-permute-start.8) | collective-permute-done | bytes 65568 | tf_op jit(solution)/shard_map/ppermute | solution.py:349
  18.5 2.0 %collective-permute-start.9 = (bf16[128,256]{1,0:T(8,128)(2,1)S(1)}, bf16[128,256]{1,0:T(8,128)(2,1)S(1)}, u32[]{:S(2)}, u32[]{:S(2)}) collective-permute-start(bf16[128,256]{1,0:T(8,128)(2,1)S(1)} %get-tuple-element.80), channel_id=1, source_target_pairs={{0,8},{4,12},{8,0},{12,4},{1,9},{5,13},{9,1},{13,5},{2,10},{6,14},... | collective-permute-start | bytes 196616 | tf_op jit(solution)/shard_map/ppermute | solution.py:349
  21.4 2.3 %collective-permute-start.7 = (bf16[128,256]{1,0:T(8,128)(2,1)S(1)}, bf16[128,256]{1,0:T(8,128)(2,1)S(1)}, u32[]{:S(2)}, u32[]{:S(2)}) collective-permute-start(bf16[128,256]{1,0:T(8,128)(2,1)S(1)} %get-tuple-element.72), channel_id=1, source_target_pairs={{0,8},{4,12},{8,0},{12,4},{1,9},{5,13},{9,1},{13,5},{2,10},{6,14},... | collective-permute-start | bytes 196616 | tf_op jit(solution)/shard_map/ppermute | solution.py:349
  23.7 1.7 %collective-permute-done.9.refs_9_ = bf16[128,256]{1,0:T(8,128)(2,1)S(1)} collective-permute-done((bf16[128,256]{1,0:T(8,128)(2,1)S(1)}, bf16[128,256]{1,0:T(8,128)(2,1)S(1)}, u32[]{:S(2)}, u32[]{:S(2)}) %collective-permute-start.9) | collective-permute-done | bytes 65568 | tf_op jit(solution)/shard_map/ppermute | solution.py:349
  25.4 1.5 %shard_map.151 = (f32[32,128]{1,0:T(8,128)S(1)}, f32[32,128]{1,0:T(8,128)S(1)}, f32[512,128]{1,0:T(8,128)S(1)}, f32[128,128]{1,0:T(8,128)S(1)}, f32[128,128]{1,0...) custom-call(bf16[2,32,512]{2,1,0:T(8,128)(2,1)S(1)} %shard_map.145.refs_0_.refs_4_, ...), custom_call_target="tpu_custom_call" | custom-call | tf_op jit(solution)/shard_map/pallas_call | solution.py:331
  26.9 2.4 %shard_map.152 = (f32[2,32,128]{2,1,0:T(8,128)S(1)}, f32[2,32,128]{2,1,0:T(8,128)}, f32[2,512,128]{2,1,0:T(8,128)}, f32[192,512]{1,0:T(8,128)S(1)}, bf16[192,512...) custom-call(bf16[2,32,512]{2,1,0:T(8,128)(2,1)S(1)} %shard_map.145.r, ...), custom_call_target="tpu_custom_call" | custom-call | tf_op jit(solution)/shard_map/pallas_call | solution.py:331
  30.8 1.3 %collective-permute-start.11 = (bf16[96,512]{1,0:T(8,128)(2,1)S(1)}, bf16[96,512]{1,0:T(8,128)(2,1)S(1)}, u32[]{:S(2)}, u32[]{:S(2)}) collective-permute-start(bf16[96,512]{1,0:T(8,128)(2,1)S(1)} %get-tuple-element.94), channel_id=1, source_target_pairs={{0,2},{1,3},{2,0},{3,1},{4,6},{5,7},{6,4},{7,5},{8,10},{9,11},{10,... | collective-permute-start | bytes 294920 | tf_op jit(solution)/shard_map/ppermute | solution.py:349
  33.0 3.5 %collective-permute-done.11.arrived = bf16[96,512]{1,0:T(8,128)(2,1)S(1)} collective-permute-done((bf16[96,512]{1,0:T(8,128)(2,1)S(1)}, bf16[96,512]{1,0:T(8,128)(2,1)S(1)}, u32[]{:S(2)}, u32[]{:S(2)}) %collective-permute-start.11) | collective-permute-done | bytes 98336 | tf_op jit(solution)/shard_map/ppermute | solution.py:349
  36.5 1.3 %collective-permute-start.12 = (bf16[112,512]{1,0:T(8,128)(2,1)S(1)}, bf16[112,512]{1,0:T(8,128)(2,1)S(1)}, u32[]{:S(2)}, u32[]{:S(2)}) collective-permute-start(bf16[112,512]{1,0:T(8,128)(2,1)S(1)} %get-tuple-element.98), channel_id=1, source_target_pairs={{0,4},{4,0},{8,12},{12,8},{1,5},{5,1},{9,13},{13,9},{2,6},{6,2},{1... | collective-permute-start | bytes 344072 | tf_op jit(solution)/shard_map/ppermute | solution.py:349
  37.8 1.3 %collective-permute-start.16 = (bf16[96,512]{1,0:T(8,128)(2,1)S(1)}, bf16[96,512]{1,0:T(8,128)(2,1)S(1)}, u32[]{:S(2)}, u32[]{:S(2)}) collective-permute-start(bf16[96,512]{1,0:T(8,128)(2,1)S(1)} %get-tuple-element.112), channel_id=1, source_target_pairs={{0,4},{4,0},{8,12},{12,8},{1,5},{5,1},{9,13},{13,9},{2,6},{6,2},{1... | collective-permute-start | bytes 294920 | tf_op jit(solution)/shard_map/ppermute | solution.py:349
  39.1 3.0 %collective-permute-done.12.arrived = bf16[112,512]{1,0:T(8,128)(2,1)S(1)} collective-permute-done((bf16[112,512]{1,0:T(8,128)(2,1)S(1)}, bf16[112,512]{1,0:T(8,128)(2,1)S(1)}, u32[]{:S(2)}, u32[]{:S(2)}) %collective-permute-start.12) | collective-permute-done | bytes 114720 | tf_op jit(solution)/shard_map/ppermute | solution.py:349
  42.1 2.5 %collective-permute-start.13 = (bf16[112,512]{1,0:T(8,128)(2,1)S(1)}, bf16[112,512]{1,0:T(8,128)(2,1)S(1)}, u32[]{:S(2)}, u32[]{:S(2)}) collective-permute-start(bf16[112,512]{1,0:T(8,128)(2,1)S(1)} %get-tuple-element.102.sent), channel_id=1, source_target_pairs={{0,8},{4,12},{8,0},{12,4},{1,9},{5,13},{9,1},{13,5},{2,10},{6,14},... | collective-permute-start | bytes 344072 | tf_op jit(solution)/shard_map/ppermute | solution.py:349
  44.6 1.8 %collective-permute-start.17 = (bf16[96,512]{1,0:T(8,128)(2,1)S(1)}, bf16[96,512]{1,0:T(8,128)(2,1)S(1)}, u32[]{:S(2)}, u32[]{:S(2)}) collective-permute-start(bf16[96,512]{1,0:T(8,128)(2,1)S(1)} %get-tuple-element.114), channel_id=1, source_target_pairs={{0,8},{4,12},{8,0},{12,4},{1,9},{5,13},{9,1},{13,5},{2,10},{6,14},... | collective-permute-start | bytes 294920 | tf_op jit(solution)/shard_map/ppermute | solution.py:349
  46.4 4.6 %collective-permute-done.13.arrived = bf16[112,512]{1,0:T(8,128)(2,1)S(1)} collective-permute-done((bf16[112,512]{1,0:T(8,128)(2,1)S(1)}, bf16[112,512]{1,0:T(8,128)(2,1)S(1)}, u32[]{:S(2)}, u32[]{:S(2)}) %collective-permute-start.13) | collective-permute-done | bytes 114720 | tf_op jit(solution)/shard_map/ppermute | solution.py:349
  51.7 1.2 %collective-permute-start.20 = (bf16[128,512]{1,0:T(8,128)(2,1)S(1)}, bf16[128,512]{1,0:T(8,128)(2,1)S(1)}, u32[]{:S(2)}, u32[]{:S(2)}) collective-permute-start(bf16[128,512]{1,0:T(8,128)(2,1)S(1)} %get-tuple-element.115.own_b), channel_id=1, source_target_pairs={{0,2},{1,3},{2,0},{3,1},{4,6},{5,7},{6,4},{7,5},{8,10},{9,11},{10,... | collective-permute-start | bytes 393224 | tf_op jit(solution)/shard_map/ppermute | solution.py:349
  53.8 2.8 %collective-permute-done.20.across_b = bf16[128,512]{1,0:T(8,128)(2,1)S(1)} collective-permute-done((bf16[128,512]{1,0:T(8,128)(2,1)S(1)}, bf16[128,512]{1,0:T(8,128)(2,1)S(1)}, u32[]{:S(2)}, u32[]{:S(2)}) %collective-permute-start.20) | collective-permute-done | bytes 131104 | tf_op jit(solution)/shard_map/ppermute | solution.py:349
  59.2 1.0 %shard_map.162 = (f32[384,512]{1,0:T(8,128)}, f32[512,256]{1,0:T(8,128)}, f32[512,256]{1,0:T(8,128)}) custom-call(bf16[96,512]{1,0:T(8,128)(2,1)S(1)} %collective-permute-done.18.across_a, bf16[96,512]{1,0:T(8,128)(2,1)S(1)} %collective-permute-done.19.far_a, ...), custom_call_target="tpu_custom_call", output_to_operand_aliasing={{0}: (4, {}), {1}: (5, {}), {2}: (6, {})} | custom-call | tf_op jit(solution)/shard_map/pallas_call | solution.py:331
  (42 shorter events, 10.2 us)
Async XLA Ops:
  1.5 11.5 %collective-permute-start.5 = (bf16[2,32,512]{2,1,0:T(8,128)(2,1)S(1)}, bf16[2,32,512]{2,1,0:T(8,128)(2,1)S(1)}, u32[]{:S(2)}, u32[]{:S(2)}) collective-permute-start(bf16[2,32,512]{2,1,0:T(8,128)(2,1)S(1)} %shard_map.145.refs_0_.refs_4_), channel_id=1, source_target_pairs={{0,12},{4,8},{8,4},{12,0},{1,13},{5,9},{9,5},{13,1},{2,14},{6,10},... | collective-permute-start | bytes 196616 | tf_op jit(solution)/shard_map/ppermute | solution.py:349
  6.6 6.4 %collective-permute-start.4 = (bf16[2,32,512]{2,1,0:T(8,128)(2,1)S(1)}, bf16[2,32,512]{2,1,0:T(8,128)(2,1)S(1)}, u32[]{:S(2)}, u32[]{:S(2)}) collective-permute-start(bf16[2,32,512]{2,1,0:T(8,128)(2,1)S(1)} %shard_map.145.refs_0_.refs_4_), channel_id=1, source_target_pairs={{0,8},{4,12},{8,0},{12,4},{1,9},{5,13},{9,1},{13,5},{2,10},{6,14},... | collective-permute-start | bytes 196616 | tf_op jit(solution)/shard_map/ppermute | solution.py:349
  6.6 6.4 %collective-permute-start.3 = (bf16[2,32,512]{2,1,0:T(8,128)(2,1)S(1)}, bf16[2,32,512]{2,1,0:T(8,128)(2,1)S(1)}, u32[]{:S(2)}, u32[]{:S(2)}) collective-permute-start(bf16[2,32,512]{2,1,0:T(8,128)(2,1)S(1)} %shard_map.145.refs_0_.refs_4_), channel_id=1, source_target_pairs={{0,4},{4,0},{8,12},{12,8},{1,5},{5,1},{9,13},{13,9},{2,6},{6,2},{1... | collective-permute-start | bytes 196616 | tf_op jit(solution)/shard_map/ppermute | solution.py:349
  7.2 1.8 %collective-permute-start = (bf16[2,32,128]{2,1,0:T(8,128)(2,1)}, bf16[2,32,128]{2,1,0:T(8,128)(2,1)S(1)}, u32[]{:S(2)}, u32[]{:S(2)}) collective-permute-start(bf16[2,32,128]{2,1,0:T(8,128)(2,1)} %state.1), channel_id=1, source_target_pairs={{0,1},{1,0},{2,3},{3,2},{4,5},{5,4},{6,7},{7,6},{8,9},{9,8},{10,11... | collective-permute-start | bytes 49160 | tf_op jit(solution)/shard_map/ppermute | solution.py:349
  7.2 5.3 %collective-permute-start.2 = (bf16[2,32,128]{2,1,0:T(8,128)(2,1)}, bf16[2,32,128]{2,1,0:T(8,128)(2,1)S(1)}, u32[]{:S(2)}, u32[]{:S(2)}) collective-permute-start(bf16[2,32,128]{2,1,0:T(8,128)(2,1)} %state.1), channel_id=1, source_target_pairs={{0,3},{1,2},{2,1},{3,0},{4,7},{5,6},{6,5},{7,4},{8,11},{9,10},{10,... | collective-permute-start | bytes 49160 | tf_op jit(solution)/shard_map/ppermute | solution.py:349
  9.0 4.0 %collective-permute-start.1 = (bf16[2,32,128]{2,1,0:T(8,128)(2,1)}, bf16[2,32,128]{2,1,0:T(8,128)(2,1)S(1)}, u32[]{:S(2)}, u32[]{:S(2)}) collective-permute-start(bf16[2,32,128]{2,1,0:T(8,128)(2,1)} %state.1), channel_id=1, source_target_pairs={{0,2},{1,3},{2,0},{3,1},{4,6},{5,7},{6,4},{7,5},{8,10},{9,11},{10,... | collective-permute-start | bytes 49160 | tf_op jit(solution)/shard_map/ppermute | solution.py:349
  14.0 4.5 %collective-permute-start.8 = (bf16[128,256]{1,0:T(8,128)(2,1)S(1)}, bf16[128,256]{1,0:T(8,128)(2,1)S(1)}, u32[]{:S(2)}, u32[]{:S(2)}) collective-permute-start(bf16[128,256]{1,0:T(8,128)(2,1)S(1)} %get-tuple-element.78), channel_id=1, source_target_pairs={{0,4},{4,0},{8,12},{12,8},{1,5},{5,1},{9,13},{13,9},{2,6},{6,2},{1... | collective-permute-start | bytes 196616 | tf_op jit(solution)/shard_map/ppermute | solution.py:349
  16.3 5.0 %collective-permute-start.6 = (bf16[128,256]{1,0:T(8,128)(2,1)S(1)}, bf16[128,256]{1,0:T(8,128)(2,1)S(1)}, u32[]{:S(2)}, u32[]{:S(2)}) collective-permute-start(bf16[128,256]{1,0:T(8,128)(2,1)S(1)} %get-tuple-element.70), channel_id=1, source_target_pairs={{0,4},{4,0},{8,12},{12,8},{1,5},{5,1},{9,13},{13,9},{2,6},{6,2},{1... | collective-permute-start | bytes 196616 | tf_op jit(solution)/shard_map/ppermute | solution.py:349
  18.5 6.9 %collective-permute-start.9 = (bf16[128,256]{1,0:T(8,128)(2,1)S(1)}, bf16[128,256]{1,0:T(8,128)(2,1)S(1)}, u32[]{:S(2)}, u32[]{:S(2)}) collective-permute-start(bf16[128,256]{1,0:T(8,128)(2,1)S(1)} %get-tuple-element.80), channel_id=1, source_target_pairs={{0,8},{4,12},{8,0},{12,4},{1,9},{5,13},{9,1},{13,5},{2,10},{6,14},... | collective-permute-start | bytes 196616 | tf_op jit(solution)/shard_map/ppermute | solution.py:349
  21.4 5.5 %collective-permute-start.7 = (bf16[128,256]{1,0:T(8,128)(2,1)S(1)}, bf16[128,256]{1,0:T(8,128)(2,1)S(1)}, u32[]{:S(2)}, u32[]{:S(2)}) collective-permute-start(bf16[128,256]{1,0:T(8,128)(2,1)S(1)} %get-tuple-element.72), channel_id=1, source_target_pairs={{0,8},{4,12},{8,0},{12,4},{1,9},{5,13},{9,1},{13,5},{2,10},{6,14},... | collective-permute-start | bytes 196616 | tf_op jit(solution)/shard_map/ppermute | solution.py:349
  29.3 1.4 %collective-permute-start.10 = (bf16[192,512]{1,0:T(8,128)(2,1)S(1)}, bf16[192,512]{1,0:T(8,128)(2,1)S(1)}, u32[]{:S(2)}, u32[]{:S(2)}) collective-permute-start(bf16[192,512]{1,0:T(8,128)(2,1)S(1)} %get-tuple-element.92), channel_id=1, source_target_pairs={{0,1},{1,0},{2,3},{3,2},{4,5},{5,4},{6,7},{7,6},{8,9},{9,8},{10,11... | collective-permute-start | bytes 589832 | tf_op jit(solution)/shard_map/ppermute | solution.py:349
  29.3 2.7 %collective-permute-start.14 = (bf16[192,512]{1,0:T(8,128)(2,1)S(1)}, bf16[192,512]{1,0:T(8,128)(2,1)S(1)}, u32[]{:S(2)}, u32[]{:S(2)}) collective-permute-start(bf16[192,512]{1,0:T(8,128)(2,1)S(1)} %get-tuple-element.108), channel_id=1, source_target_pairs={{0,1},{1,0},{2,3},{3,2},{4,5},{5,4},{6,7},{7,6},{8,9},{9,8},{10,11... | collective-permute-start | bytes 589832 | tf_op jit(solution)/shard_map/ppermute | solution.py:349
  30.8 5.7 %collective-permute-start.11 = (bf16[96,512]{1,0:T(8,128)(2,1)S(1)}, bf16[96,512]{1,0:T(8,128)(2,1)S(1)}, u32[]{:S(2)}, u32[]{:S(2)}) collective-permute-start(bf16[96,512]{1,0:T(8,128)(2,1)S(1)} %get-tuple-element.94), channel_id=1, source_target_pairs={{0,2},{1,3},{2,0},{3,1},{4,6},{5,7},{6,4},{7,5},{8,10},{9,11},{10,... | collective-permute-start | bytes 294920 | tf_op jit(solution)/shard_map/ppermute | solution.py:349
  32.1 5.7 %collective-permute-start.15 = (bf16[96,512]{1,0:T(8,128)(2,1)S(1)}, bf16[96,512]{1,0:T(8,128)(2,1)S(1)}, u32[]{:S(2)}, u32[]{:S(2)}) collective-permute-start(bf16[96,512]{1,0:T(8,128)(2,1)S(1)} %get-tuple-element.110), channel_id=1, source_target_pairs={{0,2},{1,3},{2,0},{3,1},{4,6},{5,7},{6,4},{7,5},{8,10},{9,11},{10,... | collective-permute-start | bytes 294920 | tf_op jit(solution)/shard_map/ppermute | solution.py:349
  36.5 5.6 %collective-permute-start.12 = (bf16[112,512]{1,0:T(8,128)(2,1)S(1)}, bf16[112,512]{1,0:T(8,128)(2,1)S(1)}, u32[]{:S(2)}, u32[]{:S(2)}) collective-permute-start(bf16[112,512]{1,0:T(8,128)(2,1)S(1)} %get-tuple-element.98), channel_id=1, source_target_pairs={{0,4},{4,0},{8,12},{12,8},{1,5},{5,1},{9,13},{13,9},{2,6},{6,2},{1... | collective-permute-start | bytes 344072 | tf_op jit(solution)/shard_map/ppermute | solution.py:349
  37.8 6.8 %collective-permute-start.16 = (bf16[96,512]{1,0:T(8,128)(2,1)S(1)}, bf16[96,512]{1,0:T(8,128)(2,1)S(1)}, u32[]{:S(2)}, u32[]{:S(2)}) collective-permute-start(bf16[96,512]{1,0:T(8,128)(2,1)S(1)} %get-tuple-element.112), channel_id=1, source_target_pairs={{0,4},{4,0},{8,12},{12,8},{1,5},{5,1},{9,13},{13,9},{2,6},{6,2},{1... | collective-permute-start | bytes 294920 | tf_op jit(solution)/shard_map/ppermute | solution.py:349
  42.1 8.9 %collective-permute-start.13 = (bf16[112,512]{1,0:T(8,128)(2,1)S(1)}, bf16[112,512]{1,0:T(8,128)(2,1)S(1)}, u32[]{:S(2)}, u32[]{:S(2)}) collective-permute-start(bf16[112,512]{1,0:T(8,128)(2,1)S(1)} %get-tuple-element.102.sent), channel_id=1, source_target_pairs={{0,8},{4,12},{8,0},{12,4},{1,9},{5,13},{9,1},{13,5},{2,10},{6,14},... | collective-permute-start | bytes 344072 | tf_op jit(solution)/shard_map/ppermute | solution.py:349
  44.6 8.3 %collective-permute-start.17 = (bf16[96,512]{1,0:T(8,128)(2,1)S(1)}, bf16[96,512]{1,0:T(8,128)(2,1)S(1)}, u32[]{:S(2)}, u32[]{:S(2)}) collective-permute-start(bf16[96,512]{1,0:T(8,128)(2,1)S(1)} %get-tuple-element.114), channel_id=1, source_target_pairs={{0,8},{4,12},{8,0},{12,4},{1,9},{5,13},{9,1},{13,5},{2,10},{6,14},... | collective-permute-start | bytes 294920 | tf_op jit(solution)/shard_map/ppermute | solution.py:349
  51.7 5.0 %collective-permute-start.20 = (bf16[128,512]{1,0:T(8,128)(2,1)S(1)}, bf16[128,512]{1,0:T(8,128)(2,1)S(1)}, u32[]{:S(2)}, u32[]{:S(2)}) collective-permute-start(bf16[128,512]{1,0:T(8,128)(2,1)S(1)} %get-tuple-element.115.own_b), channel_id=1, source_target_pairs={{0,2},{1,3},{2,0},{3,1},{4,6},{5,7},{6,4},{7,5},{8,10},{9,11},{10,... | collective-permute-start | bytes 393224 | tf_op jit(solution)/shard_map/ppermute | solution.py:349
  52.9 4.8 %collective-permute-start.18 = (bf16[96,512]{1,0:T(8,128)(2,1)S(1)}, bf16[96,512]{1,0:T(8,128)(2,1)S(1)}, u32[]{:S(2)}, u32[]{:S(2)}) collective-permute-start(bf16[96,512]{1,0:T(8,128)(2,1)S(1)} %shard_map.160.own_a), channel_id=1, source_target_pairs={{0,2},{1,3},{2,0},{3,1},{4,6},{5,7},{6,4},{7,5},{8,10},{9,11},{10,... | collective-permute-start | bytes 294920 | tf_op jit(solution)/shard_map/ppermute | solution.py:349
  53.8 4.3 %collective-permute-start.23 = (bf16[128,512]{1,0:T(8,128)(2,1)S(1)}, bf16[128,512]{1,0:T(8,128)(2,1)S(1)}, u32[]{:S(2)}, u32[]{:S(2)}) collective-permute-start(bf16[128,512]{1,0:T(8,128)(2,1)S(1)} %get-tuple-element.115.own_b), channel_id=1, source_target_pairs={{0,1},{1,0},{2,3},{3,2},{4,5},{5,4},{6,7},{7,6},{8,9},{9,8},{10,11... | collective-permute-start | bytes 393224 | tf_op jit(solution)/shard_map/ppermute | solution.py:349
  56.6 2.5 %collective-permute-start.21 = (bf16[128,512]{1,0:T(8,128)(2,1)S(1)}, bf16[128,512]{1,0:T(8,128)(2,1)S(1)}, u32[]{:S(2)}, u32[]{:S(2)}) collective-permute-start(bf16[128,512]{1,0:T(8,128)(2,1)S(1)} %collective-permute-done.20.across_b), channel_id=1, source_target_pairs={{0,1},{1,0},{2,3},{3,2},{4,5},{5,4},{6,7},{7,6},{8,9},{9,8},{10,11... | collective-permute-start | bytes 393224 | tf_op jit(solution)/shard_map/ppermute | solution.py:349
  56.6 1.5 %collective-permute-start.22 = (bf16[96,512]{1,0:T(8,128)(2,1)S(1)}, bf16[96,512]{1,0:T(8,128)(2,1)S(1)}, u32[]{:S(2)}, u32[]{:S(2)}) collective-permute-start(bf16[96,512]{1,0:T(8,128)(2,1)S(1)} %shard_map.160.own_a), channel_id=1, source_target_pairs={{0,1},{1,0},{2,3},{3,2},{4,5},{5,4},{6,7},{7,6},{8,9},{9,8},{10,11... | collective-permute-start | bytes 294920 | tf_op jit(solution)/shard_map/ppermute | solution.py:349
  57.7 1.5 %collective-permute-start.19 = (bf16[96,512]{1,0:T(8,128)(2,1)S(1)}, bf16[96,512]{1,0:T(8,128)(2,1)S(1)}, u32[]{:S(2)}, u32[]{:S(2)}) collective-permute-start(bf16[96,512]{1,0:T(8,128)(2,1)S(1)} %collective-permute-done.18.across_a), channel_id=1, source_target_pairs={{0,1},{1,0},{2,3},{3,2},{4,5},{5,4},{6,7},{7,6},{8,9},{9,8},{10,11... | collective-permute-start | bytes 294920 | tf_op jit(solution)/shard_map/ppermute | solution.py:349

commit v5 on v4

--- a/solution.py
+++ b/solution.py
@@ -128,21 +128,19 @@
     sent[...] = value.astype(BF)
 
 
-def backward(moment, sources, targets, total, arrived, attr, src_t, dst_t, slope, sums, w1, w2, wn, node_held):
-    n = WAYS
+def backward(moment, put_edges, sources, targets, total, arrived, attr, src_t, dst_t, slope, sums, w1, w2, wn):
     rows, width = sources[1].shape[1:]
     width_m = w2.shape[1]
     joined = stacked(targets, moment, targets[0].shape[2])
     state, forcing, cotangent = joined[:, :width], joined[:, width : 2 * width], joined[:, 2 * width :]
     agg = total[...] + turned(arrived[...].astype(F32), 2)
     node_in = jnp.concatenate([state, agg.astype(BF), forcing], axis=1)
-    node_held[...] = node_in
     grad_pre = (cotangent.astype(F32) * slope_of(mm(node_in, wn[...]))).astype(BF)
     grad_in = mm_nt(grad_pre, wn[...])
     grad_agg = grad_in[:, width : width + width_m].astype(BF)
     grad_message = mm_tn(dst_t[...], grad_agg).astype(BF)
     grad_pre_edge = (mm_nt(grad_message, w2[...]) * slope[...]).astype(BF)
-    edges = mm_nt(grad_pre_edge, w1[2 * width :])
+    put_edges(mm_nt(grad_pre_edge, w1[2 * width :]), grad_in[:rows, width + width_m :])
     from_src = mm(src_t[...], grad_pre_edge).astype(BF)
     from_dst = mm(dst_t[...], grad_pre_edge).astype(BF)
     to_src = mm_nt(from_src, w1[:width])
@@ -153,11 +151,9 @@
         mm_tn(attr[moment], grad_pre_edge),
     ]
     second = mm_tn(sums[...], grad_agg)
-    block = wn.shape[0] // n
-    spot = pl.multiple_of(lax.axis_index("src") * block, block)
-    node_grad = mm_tn(node_held[:, pl.ds(spot, block)], grad_pre)
+    node_grad = mm_tn(node_in, grad_pre)
     state_own = grad_in[:rows, :width] + to_dst[:rows]
-    return state_own, grad_in[:rows, width + width_m :], edges, to_src, to_dst, first, second, node_grad
+    return state_own, to_src, to_dst, first, second, node_grad
 
 
 def split_refs(refs):
@@ -167,10 +163,13 @@
 
 def backward_first_kernel(*refs):
     sources, targets, args, refs = split_refs(refs)
-    *outs, first_out, second_out, node_out, node_held = refs
-    *values, first, second, node_grad = backward(0, sources, targets, *args, node_held)
-    for ref, value in zip(outs, values, strict=True):
-        ref[...] = value
+    state, forcing, edges, to_src, to_dst, first_out, second_out, node_out = refs
+
+    def put_edges(edge_values, forcing_values):
+        edges[...] = edge_values
+        forcing[...] = forcing_values
+
+    state[...], to_src[...], to_dst[...], first, second, node_grad = backward(0, put_edges, sources, targets, *args)
     width = first[0].shape[0]
     for i, value in enumerate(first):
         first_out[i * width : (i + 1) * width] = value
@@ -183,20 +182,31 @@
     sources, targets, args, refs = split_refs(refs)
     state_0, forcing_0, edges_0, to_src_0, to_dst_0, first_0, second_0, node_0 = refs[:8]
     state_own, forcing_own, edges, kept_a, core_a, kept_b, core_b, target_kept, target_sent = refs[8:17]
-    first_held, second_held, node_grad_held, node_held = refs[17:]
-    state_1, forcing_1, edges_1, to_src_1, to_dst_1, first, second, node_grad = backward(
-        1, sources, targets, *args, node_held
-    )
+    first_held, second_held, node_grad_held, edges_1, forcing_1, sems = refs[17:]
+    copies = [
+        pltpu.make_async_copy(source, target, sems.at[i])
+        for i, (source, target) in enumerate(
+            [(edges_0, edges.at[0]), (forcing_0, forcing_own.at[0]), (edges_1, edges.at[1]), (forcing_1, forcing_own.at[1])]
+        )
+    ]
+    copies[0].start()
+    copies[1].start()
+
+    def put_edges(edge_values, forcing_values):
+        edges_1[...] = edge_values
+        forcing_1[...] = forcing_values
+        copies[2].start()
+        copies[3].start()
+
+    state_1, to_src_1, to_dst_1, first, second, node_grad = backward(1, put_edges, sources, targets, *args)
     state_own[0], state_own[1] = state_0[...], state_1
-    forcing_own[0], forcing_own[1] = forcing_0[...], forcing_1
-    edges[0], edges[1] = edges_0[...], edges_1
     width = first[0].shape[0]
     for i, value in enumerate(first):
         first_held[i * width : (i + 1) * width] = first_0[i * width : (i + 1) * width] + value
     second_held[...] = second_0[...] + second
     node_grad_held[...] = node_0[...] + node_grad
-    part, block, small = first_held.shape[0] // n, second_held.shape[0] // n, node_grad_held.shape[0] // n
-    wide = node_grad_held.shape[1]
+    part, block = first_held.shape[0] // n, second_held.shape[0] // n
+    size, wide = block // 2, second_held.shape[1]
     for k in range(n):
         other = lax.axis_index("dst") ^ k
         into = core_a if k % 2 else kept_a
@@ -204,19 +214,17 @@
         into[start : start + part] = first_held[pl.ds(pl.multiple_of(other * part, part), part)].astype(into.dtype)
         into = core_b if k % 2 else kept_b
         start = (k // 2) * (into.shape[0] // 2)
-        for j in range(2):
-            lanes = slice(j * wide, (j + 1) * wide)
-            size = block // 2
-            spot = pl.ds(pl.multiple_of(other * block + j * size, size), size)
-            into[start : start + size, lanes] = second_held[spot].astype(into.dtype)
-            tiny = small // 2
-            spot = pl.ds(pl.multiple_of(other * small + j * tiny, tiny), tiny)
-            into[start + size : start + size + tiny, lanes] = node_grad_held[spot].astype(into.dtype)
-        start += block // 2 + small // 2
+        for held in (second_held, node_grad_held):
+            for j in range(2):
+                spot = pl.ds(pl.multiple_of(other * block + j * size, size), size)
+                into[start : start + size, j * wide : (j + 1) * wide] = held[spot].astype(into.dtype)
+            start += size
         put_nodes(into, start, k, (to_src_0[...], to_src_1))
     put_nodes(target_kept, 0, 2, (to_dst_0[...], to_dst_1))
     for i, k in enumerate((1, 3)):
         put_nodes(target_sent, i * target_kept.shape[0], k, (to_dst_0[...], to_dst_1))
+    for copy in copies:
+        copy.wait()
 
 
 def put_nodes(into, start, k, values):
@@ -255,46 +263,32 @@
     sent[...] = (mine[...] + arrived[...].astype(F32)).astype(BF)
 
 
-def middle_kernel(mine, arrived, state_own, target_sent, state, own, sent):
+def middle_kernel(mine, arrived, state_own, target_sent, state, own, sent, node_share):
     total = mine[...] + arrived[...].astype(F32)
-    core = own.shape[0]
-    own[...] = total[:core]
-    sent[:core] = total[:core].astype(BF)
-    sent[core:] = target_sent[...]
-    add_nodes(state, state_own, total[core:])
+    size = own.shape[0]
+    own[...] = total[:size]
+    sent[:size] = total[:size].astype(BF)
+    sent[size:] = target_sent[...]
+    node_share[...] = total[size : 2 * size].astype(BF)
+    add_nodes(state, state_own, total[2 * size :])
 
 
 def second_sum_kernel(mine, arrived, target_kept, state_in, state, own, sent):
     size, half = own.shape[0], target_kept.shape[0]
-    core = mine.shape[0]
-    tiny = core - size
-    total = mine[:size] + arrived[:size].astype(F32)
+    total = mine[...] + arrived[:size].astype(F32)
     own[...] = total
     sent[:size] = total.astype(BF)
-    sent[size:core] = mine[size:].astype(BF)
-    sent[core : core + tiny] = arrived[size:core]
-    add_nodes(state, state_in, arrived[core : core + half].astype(F32))
-    sent[core + tiny :] = (target_kept[...] + arrived[core + half :].astype(F32)).astype(BF)
-
-
-def gather_kernel(mine, sent, arrived, state_in, state, share):
-    size, half = mine.shape[0], state.shape[1] // 2
-    tiny = (share.shape[0] - size) // WAYS
-    share[:size] = (mine[...] + arrived[:size].astype(F32)).astype(BF)
-    add_nodes(state, state_in, arrived[size + 2 * tiny :].astype(F32))
-    for k in range(WAYS):
-        start = pl.multiple_of(size + (lax.axis_index("src") ^ k) * tiny, tiny)
-        spot = slice(size + (k % 2) * tiny, size + (k % 2 + 1) * tiny)
-        share[pl.ds(start, tiny)] = (arrived if k // 2 else sent)[spot]
-
-
-def put_shares(places, shares_a, shares_b, outs, scratch):
-    first, second, node = outs
-    first_held, second_held, node_held, sems = scratch
-    n = WAYS
-    part, block = first.shape[0] // n, second.shape[0] // n
-    small = node.shape[0] // n // n
-    size, tiny, wide = block // 2, small // 2, second.shape[1]
+    add_nodes(state, state_in, arrived[size : size + half].astype(F32))
+    sent[size:] = (target_kept[...] + arrived[size + half :].astype(F32)).astype(BF)
+
+
+def gather_kernel(mine, arrived, node_across, share, node_sent):
+    share[...] = (mine[...] + arrived[: mine.shape[0]].astype(F32)).astype(BF)
+    node_sent[...] = node_across[...]
+
+
+def put_shares(places, shares, outs, scratch):
+    *held, sems = scratch
     copies = []
 
     def put(source, target):
@@ -303,28 +297,29 @@
 
     for i, k in enumerate(places):
         other = lax.axis_index("dst") ^ k
-        first_held[i] = shares_a[i][...].astype(F32)
-        put(first_held.at[i], first.at[pl.ds(pl.multiple_of(other * part, part), part)])
-        for h in range(2):
-            lanes = slice(h * wide, (h + 1) * wide)
-            second_held[i, h * size : (h + 1) * size] = shares_b[i][:size, lanes].astype(F32)
-            for j in range(n):
-                spot = slice(size + j * tiny, size + (j + 1) * tiny)
-                node_held[i, j, h * tiny : (h + 1) * tiny] = shares_b[i][spot, lanes].astype(F32)
-        put(second_held.at[i], second.at[pl.ds(pl.multiple_of(other * block, block), block)])
-        for j in range(n):
-            start = pl.multiple_of(j * block + other * small, small)
-            put(node_held.at[i, j], node.at[pl.ds(start, small)])
+        for out, into, share in zip(outs, held, shares[i], strict=True):
+            rows, wide = into.shape[1:]
+            size = share.shape[0]
+            for h in range(rows // size):
+                into[i, h * size : (h + 1) * size] = share[:, h * wide : (h + 1) * wide].astype(F32)
+            put(into.at[i], out.at[pl.ds(pl.multiple_of(other * rows, rows), rows)])
+    return copies
+
+
+def first_shares_kernel(*refs):
+    copies = put_shares((0, 1), (refs[:3], refs[3:6]), refs[6:9], refs[9:])
     for copy in copies:
         copy.wait()
 
 
-def first_shares_kernel(own_a, near_a, own_b, near_b, *refs):
-    put_shares((0, 1), (own_a, near_a), (own_b, near_b), refs[:3], refs[3:])
-
-
-def last_shares_kernel(across_a, far_a, across_b, far_b, *refs):
-    put_shares((2, 3), (across_a, far_a), (across_b, far_b), refs[3:6], refs[6:])
+def last_shares_kernel(state_in, arrived, *refs):
+    state_held, state_sem = refs[17:]
+    copies = put_shares((2, 3), (refs[:3], refs[3:6]), refs[10:13], refs[13:17])
+    add_nodes(state_held, state_in, arrived[arrived.shape[0] - state_in.shape[1] // 2 :].astype(F32))
+    copies.append(pltpu.make_async_copy(state_held, refs[9], state_sem))
+    copies[-1].start()
+    for copy in copies:
+        copy.wait()
 
 
 def call(kernel, outs, scratch, args, spaces=None, out_spaces=None, aliases=None):
@@ -363,7 +358,7 @@
 ):
     rows, width = node_state.shape[1:]
     hid, width_m = edge_w2.shape
-    width_in, width_out = node_w1.shape
+    width_out = node_w1.shape[1]
     slots = edge_attr.shape[3]
     nodes = rows * WAYS
     steps = T_STEPS
@@ -409,7 +404,6 @@
         [*sources, *targets, *sums[moment], attr, src_t, dst_t, *forward[moment][2:], w1, w2, wn]
         for moment in range(steps)
     ]
-    block = width_in // WAYS
     earlier = call(
         backward_first_kernel,
         [
@@ -420,14 +414,14 @@
             ((nodes, width), F32),
             (edge_w1.shape, F32),
             (edge_w2.shape, F32),
-            ((block, width_out), F32),
+            (node_w1.shape, F32),
         ],
-        [((nodes, width_in), BF)],
+        [],
         args[0],
     )
-    part, size, tiny, half = edge_w1.shape[0] // WAYS, hid // WAYS // 2, block // WAYS // 2, rows // 2
-    core = size + tiny
-    wide = core + half
+    part, block, half = edge_w1.shape[0] // WAYS, hid // WAYS, rows // 2
+    size = block // 2
+    wide = 2 * size + half
     state_own, grad_forcing, edges, kept_a, core_a, kept_b, core_b, target_kept, target_sent = call(
         backward_last_kernel,
         [
@@ -441,8 +435,16 @@
             ((half, hid), F32),
             ((2 * half, hid), BF),
         ],
-        [(edge_w1.shape, F32), (edge_w2.shape, F32), ((block, width_out), F32), ((nodes, width_in), BF)],
+        [
+            (edge_w1.shape, F32),
+            (edge_w2.shape, F32),
+            (node_w1.shape, F32),
+            ((slots, width), F32),
+            ((rows, width), F32),
+            pltpu.SemaphoreType.DMA((4,)),
+        ],
         [*args[1], *earlier],
+        out_spaces=[pltpu.VMEM] + [pltpu.HBM] * 2 + [pltpu.VMEM] * 6,
     )
 
     def pair(size):
@@ -452,52 +454,43 @@
     mine_a, across_a = call(near_kernel, pair(part), [], [kept_a, swap(core_a, "dst", 1)])
     mine_b, across_b = call(near_kernel, pair(wide), [], [kept_b, swap(core_b, "dst", 1)])
     own_a, sent_a = call(add_kernel, pair(part), [], [mine_a, swap(across_a, "dst", 2)])
-    state_sum, own_b, sent_b = call(
+    state_sum, own_b, sent_b, node_share = call(
         middle_kernel,
-        [state, ((core, hid), F32), ((core + 2 * half, hid), BF)],
+        [state, ((size, hid), F32), ((size + 2 * half, hid), BF), ((size, hid), BF)],
         [],
         [mine_b, swap(across_b, "dst", 2), state_own, target_sent],
     )
+    node_across = swap(node_share, "dst", 2)
     own_a, sent_a = call(add_kernel, pair(part), [], [own_a, swap(sent_a, "src", 1)])
     state_sum, own_b, sent_b = call(
         second_sum_kernel,
-        [state, ((size, hid), F32), ((core + tiny + half, hid), BF)],
+        [state, ((size, hid), F32), ((size + half, hid), BF)],
         [],
         [own_b, swap(sent_b, "src", 1), target_kept, state_sum],
     )
     share_a = call(last_add_kernel, [((part, hid), BF)], [], [own_a, swap(sent_a, "src", 2)])[0]
-    grad_state, share_b = call(
-        gather_kernel,
-        [state, ((size + WAYS * tiny, hid), BF)],
-        [],
-        [own_b, sent_b, swap(sent_b, "src", 2), state_sum],
-    )
+    arrived = swap(sent_b, "src", 2)
+    share_b, node_across = call(gather_kernel, [((size, hid), BF)] * 2, [], [own_b, arrived, node_across])
+    own = [share_a, share_b, node_share]
+    across = [swap(share_a, "dst", 2), swap(share_b, "dst", 2), node_across]
     outs = [(edge_w1.shape, F32), (edge_w2.shape, F32), (node_w1.shape, F32)]
-    held = [
-        ((2, part, hid), F32),
-        ((2, block, width_out), F32),
-        ((2, WAYS, 2 * tiny, width_out), F32),
-        pltpu.SemaphoreType.DMA((2 * (2 + WAYS),)),
-    ]
-    shares = [share_a, share_b]
-    across = [swap(share, "dst", 2) for share in shares]
-    near = [swap(share, "dst", 1) for share in shares]
+    held = [((2, value.shape[0] // WAYS, value.shape[1]), F32) for value in (edge_w1, edge_w2, node_w1)]
+    held.append(pltpu.SemaphoreType.DMA((6,)))
     grads = call(
         first_shares_kernel,
         outs,
         held,
-        [share_a, near[0], share_b, near[1]],
+        own + [swap(share, "dst", 1) for share in own],
         out_spaces=[pltpu.HBM] * 3,
     )
-    far = [swap(share, "dst", 1) for share in across]
-    grad_first, grad_second, grad_node = call(
+    grad_state, grad_first, grad_second, grad_node = call(
         last_shares_kernel,
-        outs,
-        held,
-        [across[0], far[0], across[1], far[1], *grads],
-        [pltpu.VMEM] * 4 + [pltpu.HBM] * 3,
-        [pltpu.HBM] * 3,
-        {4: 0, 5: 1, 6: 2},
+        [state] + outs,
+        held + [state, pltpu.SemaphoreType.DMA],
+        [state_sum, arrived] + across + [swap(share, "dst", 1) for share in across] + list(grads),
+        [pltpu.VMEM] * 8 + [pltpu.HBM] * 3,
+        [pltpu.HBM] * 4,
+        {8: 1, 9: 2, 10: 3},
     )
     return grad_state, grad_forcing, edges[:, None, None], grad_first, grad_second, grad_node
 

time: 60.5 us -> 58.6 us (0.969)
  waiting for transfers between devices: 20.2 us -> 17.6 us
  starting transfers between devices: 27.4 us -> 28.7 us
  Pallas kernels: 11.3 us -> 10.5 us
    ppermute x24 -> x27, waiting for transfers between devices: 20.2 us -> 17.6 us  [swap(): return lax.ppermute(value, axis, [(i, i ^ k) for i in range(WAYS)])]
    ppermute x24 -> x27, starting transfers between devices: 27.4 us -> 28.7 us  [swap(): return lax.ppermute(value, axis, [(i, i ^ k) for i in range(WAYS)])]
    pallas_call x18, Pallas kernels: 11.3 us -> 10.5 us  [call(): pl.pallas_call(kernel, out_shape=[jax.ShapeDtypeStruct(shape, dtype) for...]
  transfers between devices with their start and end apart: 24 -> 27, of which waited for: 11 -> 14; matrix products, arithmetic and copies ran while one was open for 0% -> 0% of each run, Pallas kernels for 10% -> 9%
where the time goes in v5:
time: 58.6 us; the launch traced here: 58.4 us
  starting transfers between devices  28.7 us (49%)
  waiting for transfers between devices  17.6 us (30%)
  Pallas kernels  10.5 us (18%)
  between operations  1.44 us (2%)
    ppermute x27, starting transfers between devices, swap(): return lax.ppermute(value, axis, [(i, i ^ k) for i in range(WAYS)])  28.7 us
    ppermute x27, waiting for transfers between devices, swap(): return lax.ppermute(value, axis, [(i, i ^ k) for i in range(WAYS)])  17.6 us
    pallas_call x18, Pallas kernels, call(): pl.pallas_call(kernel, out_shape=[jax.ShapeDtypeStruct(shape, dtype) for...  10.5 us
  transfers between devices with their start and end apart: 27, of which 14 were waited for; matrix products, arithmetic and copies ran while one was open for 0% of the time, Pallas kernels for 9%

profile of v5, /device:TPU:0, one launch (start us, length us, event | category | flops | bytes accessed | tf_op | source)
XLA Modules:
  0.0 58.4 jit_solution(8299341198816158799)
XLA Ops:
  1.5 5.1 %collective-permute-start.5 = (bf16[2,32,512]{2,1,0:T(8,128)(2,1)S(1)}, bf16[2,32,512]{2,1,0:T(8,128)(2,1)S(1)}, u32[]{:S(2)}, u32[]{:S(2)}) collective-permute-start(bf16[2,32,512]{2,1,0:T(8,128)(2,1)S(1)} %shard_map.145.refs_0_.refs_4_), channel_id=1, source_target_pairs={{0,12},{4,8},{8,4},{12,0},{1,13},{5,9},{9,5},{13,1},{2,14},{6,10},... | collective-permute-start | bytes 196616 | tf_op jit(solution)/shard_map/ppermute | solution.py:344
  7.2 1.7 %collective-permute-start.2 = (bf16[2,32,128]{2,1,0:T(8,128)(2,1)}, bf16[2,32,128]{2,1,0:T(8,128)(2,1)S(1)}, u32[]{:S(2)}, u32[]{:S(2)}) collective-permute-start(bf16[2,32,128]{2,1,0:T(8,128)(2,1)} %state.1), channel_id=1, source_target_pairs={{0,3},{1,2},{2,1},{3,0},{4,7},{5,6},{6,5},{7,4},{8,11},{9,10},{10,... | collective-permute-start | bytes 49160 | tf_op jit(solution)/shard_map/ppermute | solution.py:344
  9.0 1.3 %collective-permute-start.1 = (bf16[2,32,128]{2,1,0:T(8,128)(2,1)}, bf16[2,32,128]{2,1,0:T(8,128)(2,1)S(1)}, u32[]{:S(2)}, u32[]{:S(2)}) collective-permute-start(bf16[2,32,128]{2,1,0:T(8,128)(2,1)} %state.1), channel_id=1, source_target_pairs={{0,2},{1,3},{2,0},{3,1},{4,6},{5,7},{6,4},{7,5},{8,10},{9,11},{10,... | collective-permute-start | bytes 49160 | tf_op jit(solution)/shard_map/ppermute | solution.py:344
  10.9 1.6 %shard_map.146 = (bf16[2,512,128]{2,1,0:T(8,128)(2,1)S(1)}, bf16[384,512]{1,0:T(8,128)(2,1)S(1)}, bf16[512,256]{1,0:T(8,128)(2,1)S(1)}, bf16[512,256]{1,0:T(8,12...) custom-call(s32[1,1]{1,0:T(1,128)S(6)} %copy.23.count, ...), custom_call_target="tpu_custom_call" | custom-call | tf_op jit(solution)/shard_map/pallas_call | solution.py:326
  14.0 1.3 %collective-permute-start.8 = (bf16[128,256]{1,0:T(8,128)(2,1)S(1)}, bf16[128,256]{1,0:T(8,128)(2,1)S(1)}, u32[]{:S(2)}, u32[]{:S(2)}) collective-permute-start(bf16[128,256]{1,0:T(8,128)(2,1)S(1)} %get-tuple-element.80), channel_id=1, source_target_pairs={{0,4},{4,0},{8,12},{12,8},{1,5},{5,1},{9,13},{13,9},{2,6},{6,2},{1... | collective-permute-start | bytes 196616 | tf_op jit(solution)/shard_map/ppermute | solution.py:344
  17.2 1.3 %collective-permute-done.8.arrived = bf16[128,256]{1,0:T(8,128)(2,1)S(1)} collective-permute-done((bf16[128,256]{1,0:T(8,128)(2,1)S(1)}, bf16[128,256]{1,0:T(8,128)(2,1)S(1)}, u32[]{:S(2)}, u32[]{:S(2)}) %collective-permute-start.8) | collective-permute-done | bytes 65568 | tf_op jit(solution)/shard_map/ppermute | solution.py:344
  18.5 2.0 %collective-permute-start.9 = (bf16[128,256]{1,0:T(8,128)(2,1)S(1)}, bf16[128,256]{1,0:T(8,128)(2,1)S(1)}, u32[]{:S(2)}, u32[]{:S(2)}) collective-permute-start(bf16[128,256]{1,0:T(8,128)(2,1)S(1)} %get-tuple-element.82), channel_id=1, source_target_pairs={{0,8},{4,12},{8,0},{12,4},{1,9},{5,13},{9,1},{13,5},{2,10},{6,14},... | collective-permute-start | bytes 196616 | tf_op jit(solution)/shard_map/ppermute | solution.py:344
  21.4 2.3 %collective-permute-start.7 = (bf16[128,256]{1,0:T(8,128)(2,1)S(1)}, bf16[128,256]{1,0:T(8,128)(2,1)S(1)}, u32[]{:S(2)}, u32[]{:S(2)}) collective-permute-start(bf16[128,256]{1,0:T(8,128)(2,1)S(1)} %get-tuple-element.74), channel_id=1, source_target_pairs={{0,8},{4,12},{8,0},{12,4},{1,9},{5,13},{9,1},{13,5},{2,10},{6,14},... | collective-permute-start | bytes 196616 | tf_op jit(solution)/shard_map/ppermute | solution.py:344
  23.7 1.7 %collective-permute-done.9.refs_9_ = bf16[128,256]{1,0:T(8,128)(2,1)S(1)} collective-permute-done((bf16[128,256]{1,0:T(8,128)(2,1)S(1)}, bf16[128,256]{1,0:T(8,128)(2,1)S(1)}, u32[]{:S(2)}, u32[]{:S(2)}) %collective-permute-start.9) | collective-permute-done | bytes 65568 | tf_op jit(solution)/shard_map/ppermute | solution.py:344
  25.4 1.5 %shard_map.151 = (f32[32,128]{1,0:T(8,128)S(1)}, f32[32,128]{1,0:T(8,128)S(1)}, f32[512,128]{1,0:T(8,128)S(1)}, f32[128,128]{1,0:T(8,128)S(1)}, f32[128,128]{1,0...) custom-call(bf16[2,32,512]{2,1,0:T(8,128)(2,1)S(1)} %shard_map.145.refs_0_.refs_4_, ...), custom_call_target="tpu_custom_call" | custom-call | tf_op jit(solution)/shard_map/pallas_call | solution.py:326
  26.9 2.3 %shard_map.152 = (f32[2,32,128]{2,1,0:T(8,128)S(1)}, f32[2,32,128]{2,1,0:T(8,128)}, f32[2,512,128]{2,1,0:T(8,128)}, f32[192,512]{1,0:T(8,128)S(1)}, bf16[192,512...) custom-call(bf16[2,32,512]{2,1,0:T(8,128)(2,1)S(1)} %shard_map.145.r, ...), custom_call_target="tpu_custom_call" | custom-call | tf_op jit(solution)/shard_map/pallas_call | solution.py:326
  29.8 1.4 %collective-permute-done.14.arrived = bf16[192,512]{1,0:T(8,128)(2,1)S(1)} collective-permute-done((bf16[192,512]{1,0:T(8,128)(2,1)S(1)}, bf16[192,512]{1,0:T(8,128)(2,1)S(1)}, u32[]{:S(2)}, u32[]{:S(2)}) %collective-permute-start.14) | collective-permute-done | bytes 196640 | tf_op jit(solution)/shard_map/ppermute | solution.py:344
  31.2 1.3 %collective-permute-start.15 = (bf16[96,512]{1,0:T(8,128)(2,1)S(1)}, bf16[96,512]{1,0:T(8,128)(2,1)S(1)}, u32[]{:S(2)}, u32[]{:S(2)}) collective-permute-start(bf16[96,512]{1,0:T(8,128)(2,1)S(1)} %get-tuple-element.108), channel_id=1, source_target_pairs={{0,2},{1,3},{2,0},{3,1},{4,6},{5,7},{6,4},{7,5},{8,10},{9,11},{10,... | collective-permute-start | bytes 294920 | tf_op jit(solution)/shard_map/ppermute | solution.py:344
  33.4 3.5 %collective-permute-done.15.arrived = bf16[96,512]{1,0:T(8,128)(2,1)S(1)} collective-permute-done((bf16[96,512]{1,0:T(8,128)(2,1)S(1)}, bf16[96,512]{1,0:T(8,128)(2,1)S(1)}, u32[]{:S(2)}, u32[]{:S(2)}) %collective-permute-start.15) | collective-permute-done | bytes 98336 | tf_op jit(solution)/shard_map/ppermute | solution.py:344
  37.0 1.3 %collective-permute-start.16 = (bf16[96,512]{1,0:T(8,128)(2,1)S(1)}, bf16[96,512]{1,0:T(8,128)(2,1)S(1)}, u32[]{:S(2)}, u32[]{:S(2)}) collective-permute-start(bf16[96,512]{1,0:T(8,128)(2,1)S(1)} %get-tuple-element.110), channel_id=1, source_target_pairs={{0,4},{4,0},{8,12},{12,8},{1,5},{5,1},{9,13},{13,9},{2,6},{6,2},{1... | collective-permute-start | bytes 294920 | tf_op jit(solution)/shard_map/ppermute | solution.py:344
  39.3 1.3 %collective-permute-start.12 = (bf16[96,512]{1,0:T(8,128)(2,1)S(1)}, bf16[96,512]{1,0:T(8,128)(2,1)S(1)}, u32[]{:S(2)}, u32[]{:S(2)}) collective-permute-start(bf16[96,512]{1,0:T(8,128)(2,1)S(1)} %get-tuple-element.100), channel_id=1, source_target_pairs={{0,4},{4,0},{8,12},{12,8},{1,5},{5,1},{9,13},{13,9},{2,6},{6,2},{1... | collective-permute-start | bytes 294920 | tf_op jit(solution)/shard_map/ppermute | solution.py:344
  40.6 1.4 %collective-permute-done.16.arrived = bf16[96,512]{1,0:T(8,128)(2,1)S(1)} collective-permute-done((bf16[96,512]{1,0:T(8,128)(2,1)S(1)}, bf16[96,512]{1,0:T(8,128)(2,1)S(1)}, u32[]{:S(2)}, u32[]{:S(2)}) %collective-permute-start.16) | collective-permute-done | bytes 98336 | tf_op jit(solution)/shard_map/ppermute | solution.py:344
  42.1 2.1 %collective-permute-start.17 = (bf16[96,512]{1,0:T(8,128)(2,1)S(1)}, bf16[96,512]{1,0:T(8,128)(2,1)S(1)}, u32[]{:S(2)}, u32[]{:S(2)}) collective-permute-start(bf16[96,512]{1,0:T(8,128)(2,1)S(1)} %get-tuple-element.112), channel_id=1, source_target_pairs={{0,8},{4,12},{8,0},{12,4},{1,9},{5,13},{9,1},{13,5},{2,10},{6,14},... | collective-permute-start | bytes 294920 | tf_op jit(solution)/shard_map/ppermute | solution.py:344
  45.1 1.8 %collective-permute-start.13 = (bf16[80,512]{1,0:T(8,128)(2,1)S(1)}, bf16[80,512]{1,0:T(8,128)(2,1)S(1)}, u32[]{:S(2)}, u32[]{:S(2)}) collective-permute-start(bf16[80,512]{1,0:T(8,128)(2,1)S(1)} %get-tuple-element.104), channel_id=1, source_target_pairs={{0,8},{4,12},{8,0},{12,4},{1,9},{5,13},{9,1},{13,5},{2,10},{6,14},... | collective-permute-start | bytes 245768 | tf_op jit(solution)/shard_map/ppermute | solution.py:344
  46.9 1.2 %collective-permute-start.19 = (bf16[64,512]{1,0:T(8,128)(2,1)S(1)}, bf16[64,512]{1,0:T(8,128)(2,1)S(1)}, u32[]{:S(2)}, u32[]{:S(2)}) collective-permute-start(bf16[64,512]{1,0:T(8,128)(2,1)S(1)} %get-tuple-element.114.refs_2_), channel_id=1, source_target_pairs={{0,2},{1,3},{2,0},{3,1},{4,6},{5,7},{6,4},{7,5},{8,10},{9,11},{10,... | collective-permute-start | bytes 196616 | tf_op jit(solution)/shard_map/ppermute | solution.py:344
  48.1 1.9 %collective-permute-done.17.arrived = bf16[96,512]{1,0:T(8,128)(2,1)S(1)} collective-permute-done((bf16[96,512]{1,0:T(8,128)(2,1)S(1)}, bf16[96,512]{1,0:T(8,128)(2,1)S(1)}, u32[]{:S(2)}, u32[]{:S(2)}) %collective-permute-start.17) | collective-permute-done | bytes 98336 | tf_op jit(solution)/shard_map/ppermute | solution.py:344
  50.0 1.3 %collective-permute-start.18 = (bf16[96,512]{1,0:T(8,128)(2,1)S(1)}, bf16[96,512]{1,0:T(8,128)(2,1)S(1)}, u32[]{:S(2)}, u32[]{:S(2)}) collective-permute-start(bf16[96,512]{1,0:T(8,128)(2,1)S(1)} %shard_map.159.refs_0_), channel_id=1, source_target_pairs={{0,2},{1,3},{2,0},{3,1},{4,6},{5,7},{6,4},{7,5},{8,10},{9,11},{10,... | collective-permute-start | bytes 294920 | tf_op jit(solution)/shard_map/ppermute | solution.py:344
  51.7 1.3 %collective-permute-start.20 = (bf16[64,512]{1,0:T(8,128)(2,1)S(1)}, bf16[64,512]{1,0:T(8,128)(2,1)S(1)}, u32[]{:S(2)}, u32[]{:S(2)}) collective-permute-start(bf16[64,512]{1,0:T(8,128)(2,1)S(1)} %get-tuple-element.115.refs_1_), channel_id=1, source_target_pairs={{0,2},{1,3},{2,0},{3,1},{4,6},{5,7},{6,4},{7,5},{8,10},{9,11},{10,... | collective-permute-start | bytes 196616 | tf_op jit(solution)/shard_map/ppermute | solution.py:344
  53.0 1.9 %collective-permute-done.18.refs_0_ = bf16[96,512]{1,0:T(8,128)(2,1)S(1)} collective-permute-done((bf16[96,512]{1,0:T(8,128)(2,1)S(1)}, bf16[96,512]{1,0:T(8,128)(2,1)S(1)}, u32[]{:S(2)}, u32[]{:S(2)}) %collective-permute-start.18) | collective-permute-done | bytes 98336 | tf_op jit(solution)/shard_map/ppermute | solution.py:344
  (48 shorter events, 13.2 us)
Async XLA Ops:
  1.5 11.5 %collective-permute-start.5 = (bf16[2,32,512]{2,1,0:T(8,128)(2,1)S(1)}, bf16[2,32,512]{2,1,0:T(8,128)(2,1)S(1)}, u32[]{:S(2)}, u32[]{:S(2)}) collective-permute-start(bf16[2,32,512]{2,1,0:T(8,128)(2,1)S(1)} %shard_map.145.refs_0_.refs_4_), channel_id=1, source_target_pairs={{0,12},{4,8},{8,4},{12,0},{1,13},{5,9},{9,5},{13,1},{2,14},{6,10},... | collective-permute-start | bytes 196616 | tf_op jit(solution)/shard_map/ppermute | solution.py:344
  6.6 6.4 %collective-permute-start.4 = (bf16[2,32,512]{2,1,0:T(8,128)(2,1)S(1)}, bf16[2,32,512]{2,1,0:T(8,128)(2,1)S(1)}, u32[]{:S(2)}, u32[]{:S(2)}) collective-permute-start(bf16[2,32,512]{2,1,0:T(8,128)(2,1)S(1)} %shard_map.145.refs_0_.refs_4_), channel_id=1, source_target_pairs={{0,8},{4,12},{8,0},{12,4},{1,9},{5,13},{9,1},{13,5},{2,10},{6,14},... | collective-permute-start | bytes 196616 | tf_op jit(solution)/shard_map/ppermute | solution.py:344
  6.6 6.4 %collective-permute-start.3 = (bf16[2,32,512]{2,1,0:T(8,128)(2,1)S(1)}, bf16[2,32,512]{2,1,0:T(8,128)(2,1)S(1)}, u32[]{:S(2)}, u32[]{:S(2)}) collective-permute-start(bf16[2,32,512]{2,1,0:T(8,128)(2,1)S(1)} %shard_map.145.refs_0_.refs_4_), channel_id=1, source_target_pairs={{0,4},{4,0},{8,12},{12,8},{1,5},{5,1},{9,13},{13,9},{2,6},{6,2},{1... | collective-permute-start | bytes 196616 | tf_op jit(solution)/shard_map/ppermute | solution.py:344
  7.2 5.3 %collective-permute-start.2 = (bf16[2,32,128]{2,1,0:T(8,128)(2,1)}, bf16[2,32,128]{2,1,0:T(8,128)(2,1)S(1)}, u32[]{:S(2)}, u32[]{:S(2)}) collective-permute-start(bf16[2,32,128]{2,1,0:T(8,128)(2,1)} %state.1), channel_id=1, source_target_pairs={{0,3},{1,2},{2,1},{3,0},{4,7},{5,6},{6,5},{7,4},{8,11},{9,10},{10,... | collective-permute-start | bytes 49160 | tf_op jit(solution)/shard_map/ppermute | solution.py:344
  9.0 4.0 %collective-permute-start.1 = (bf16[2,32,128]{2,1,0:T(8,128)(2,1)}, bf16[2,32,128]{2,1,0:T(8,128)(2,1)S(1)}, u32[]{:S(2)}, u32[]{:S(2)}) collective-permute-start(bf16[2,32,128]{2,1,0:T(8,128)(2,1)} %state.1), channel_id=1, source_target_pairs={{0,2},{1,3},{2,0},{3,1},{4,6},{5,7},{6,4},{7,5},{8,10},{9,11},{10,... | collective-permute-start | bytes 49160 | tf_op jit(solution)/shard_map/ppermute | solution.py:344
  14.0 4.5 %collective-permute-start.8 = (bf16[128,256]{1,0:T(8,128)(2,1)S(1)}, bf16[128,256]{1,0:T(8,128)(2,1)S(1)}, u32[]{:S(2)}, u32[]{:S(2)}) collective-permute-start(bf16[128,256]{1,0:T(8,128)(2,1)S(1)} %get-tuple-element.80), channel_id=1, source_target_pairs={{0,4},{4,0},{8,12},{12,8},{1,5},{5,1},{9,13},{13,9},{2,6},{6,2},{1... | collective-permute-start | bytes 196616 | tf_op jit(solution)/shard_map/ppermute | solution.py:344
  16.3 5.0 %collective-permute-start.6 = (bf16[128,256]{1,0:T(8,128)(2,1)S(1)}, bf16[128,256]{1,0:T(8,128)(2,1)S(1)}, u32[]{:S(2)}, u32[]{:S(2)}) collective-permute-start(bf16[128,256]{1,0:T(8,128)(2,1)S(1)} %get-tuple-element.72), channel_id=1, source_target_pairs={{0,4},{4,0},{8,12},{12,8},{1,5},{5,1},{9,13},{13,9},{2,6},{6,2},{1... | collective-permute-start | bytes 196616 | tf_op jit(solution)/shard_map/ppermute | solution.py:344
  18.5 6.9 %collective-permute-start.9 = (bf16[128,256]{1,0:T(8,128)(2,1)S(1)}, bf16[128,256]{1,0:T(8,128)(2,1)S(1)}, u32[]{:S(2)}, u32[]{:S(2)}) collective-permute-start(bf16[128,256]{1,0:T(8,128)(2,1)S(1)} %get-tuple-element.82), channel_id=1, source_target_pairs={{0,8},{4,12},{8,0},{12,4},{1,9},{5,13},{9,1},{13,5},{2,10},{6,14},... | collective-permute-start | bytes 196616 | tf_op jit(solution)/shard_map/ppermute | solution.py:344
  21.4 5.5 %collective-permute-start.7 = (bf16[128,256]{1,0:T(8,128)(2,1)S(1)}, bf16[128,256]{1,0:T(8,128)(2,1)S(1)}, u32[]{:S(2)}, u32[]{:S(2)}) collective-permute-start(bf16[128,256]{1,0:T(8,128)(2,1)S(1)} %get-tuple-element.74), channel_id=1, source_target_pairs={{0,8},{4,12},{8,0},{12,4},{1,9},{5,13},{9,1},{13,5},{2,10},{6,14},... | collective-permute-start | bytes 196616 | tf_op jit(solution)/shard_map/ppermute | solution.py:344
  29.3 3.2 %collective-permute-start.10 = (bf16[288,512]{1,0:T(8,128)(2,1)S(1)}, bf16[288,512]{1,0:T(8,128)(2,1)S(1)}, u32[]{:S(2)}, u32[]{:S(2)}) collective-permute-start(bf16[288,512]{1,0:T(8,128)(2,1)S(1)} %get-tuple-element.94), channel_id=1, source_target_pairs={{0,1},{1,0},{2,3},{3,2},{4,5},{5,4},{6,7},{7,6},{8,9},{9,8},{10,11... | collective-permute-start | bytes 884744 | tf_op jit(solution)/shard_map/ppermute | solution.py:344
  29.3 1.9 %collective-permute-start.14 = (bf16[192,512]{1,0:T(8,128)(2,1)S(1)}, bf16[192,512]{1,0:T(8,128)(2,1)S(1)}, u32[]{:S(2)}, u32[]{:S(2)}) collective-permute-start(bf16[192,512]{1,0:T(8,128)(2,1)S(1)} %get-tuple-element.106), channel_id=1, source_target_pairs={{0,1},{1,0},{2,3},{3,2},{4,5},{5,4},{6,7},{7,6},{8,9},{9,8},{10,11... | collective-permute-start | bytes 589832 | tf_op jit(solution)/shard_map/ppermute | solution.py:344
  31.2 5.7 %collective-permute-start.15 = (bf16[96,512]{1,0:T(8,128)(2,1)S(1)}, bf16[96,512]{1,0:T(8,128)(2,1)S(1)}, u32[]{:S(2)}, u32[]{:S(2)}) collective-permute-start(bf16[96,512]{1,0:T(8,128)(2,1)S(1)} %get-tuple-element.108), channel_id=1, source_target_pairs={{0,2},{1,3},{2,0},{3,1},{4,6},{5,7},{6,4},{7,5},{8,10},{9,11},{10,... | collective-permute-start | bytes 294920 | tf_op jit(solution)/shard_map/ppermute | solution.py:344
  32.5 6.7 %collective-permute-start.11 = (bf16[144,512]{1,0:T(8,128)(2,1)S(1)}, bf16[144,512]{1,0:T(8,128)(2,1)S(1)}, u32[]{:S(2)}, u32[]{:S(2)}) collective-permute-start(bf16[144,512]{1,0:T(8,128)(2,1)S(1)} %get-tuple-element.96), channel_id=1, source_target_pairs={{0,2},{1,3},{2,0},{3,1},{4,6},{5,7},{6,4},{7,5},{8,10},{9,11},{10,... | collective-permute-start | bytes 442376 | tf_op jit(solution)/shard_map/ppermute | solution.py:344
  37.0 5.1 %collective-permute-start.16 = (bf16[96,512]{1,0:T(8,128)(2,1)S(1)}, bf16[96,512]{1,0:T(8,128)(2,1)S(1)}, u32[]{:S(2)}, u32[]{:S(2)}) collective-permute-start(bf16[96,512]{1,0:T(8,128)(2,1)S(1)} %get-tuple-element.110), channel_id=1, source_target_pairs={{0,4},{4,0},{8,12},{12,8},{1,5},{5,1},{9,13},{13,9},{2,6},{6,2},{1... | collective-permute-start | bytes 294920 | tf_op jit(solution)/shard_map/ppermute | solution.py:344
  39.3 5.7 %collective-permute-start.12 = (bf16[96,512]{1,0:T(8,128)(2,1)S(1)}, bf16[96,512]{1,0:T(8,128)(2,1)S(1)}, u32[]{:S(2)}, u32[]{:S(2)}) collective-permute-start(bf16[96,512]{1,0:T(8,128)(2,1)S(1)} %get-tuple-element.100), channel_id=1, source_target_pairs={{0,4},{4,0},{8,12},{12,8},{1,5},{5,1},{9,13},{13,9},{2,6},{6,2},{1... | collective-permute-start | bytes 294920 | tf_op jit(solution)/shard_map/ppermute | solution.py:344
  42.1 7.9 %collective-permute-start.17 = (bf16[96,512]{1,0:T(8,128)(2,1)S(1)}, bf16[96,512]{1,0:T(8,128)(2,1)S(1)}, u32[]{:S(2)}, u32[]{:S(2)}) collective-permute-start(bf16[96,512]{1,0:T(8,128)(2,1)S(1)} %get-tuple-element.112), channel_id=1, source_target_pairs={{0,8},{4,12},{8,0},{12,4},{1,9},{5,13},{9,1},{13,5},{2,10},{6,14},... | collective-permute-start | bytes 294920 | tf_op jit(solution)/shard_map/ppermute | solution.py:344
  45.1 6.6 %collective-permute-start.13 = (bf16[80,512]{1,0:T(8,128)(2,1)S(1)}, bf16[80,512]{1,0:T(8,128)(2,1)S(1)}, u32[]{:S(2)}, u32[]{:S(2)}) collective-permute-start(bf16[80,512]{1,0:T(8,128)(2,1)S(1)} %get-tuple-element.104), channel_id=1, source_target_pairs={{0,8},{4,12},{8,0},{12,4},{1,9},{5,13},{9,1},{13,5},{2,10},{6,14},... | collective-permute-start | bytes 245768 | tf_op jit(solution)/shard_map/ppermute | solution.py:344
  46.9 4.3 %collective-permute-start.19 = (bf16[64,512]{1,0:T(8,128)(2,1)S(1)}, bf16[64,512]{1,0:T(8,128)(2,1)S(1)}, u32[]{:S(2)}, u32[]{:S(2)}) collective-permute-start(bf16[64,512]{1,0:T(8,128)(2,1)S(1)} %get-tuple-element.114.refs_2_), channel_id=1, source_target_pairs={{0,2},{1,3},{2,0},{3,1},{4,6},{5,7},{6,4},{7,5},{8,10},{9,11},{10,... | collective-permute-start | bytes 196616 | tf_op jit(solution)/shard_map/ppermute | solution.py:344
  50.0 4.9 %collective-permute-start.18 = (bf16[96,512]{1,0:T(8,128)(2,1)S(1)}, bf16[96,512]{1,0:T(8,128)(2,1)S(1)}, u32[]{:S(2)}, u32[]{:S(2)}) collective-permute-start(bf16[96,512]{1,0:T(8,128)(2,1)S(1)} %shard_map.159.refs_0_), channel_id=1, source_target_pairs={{0,2},{1,3},{2,0},{3,1},{4,6},{5,7},{6,4},{7,5},{8,10},{9,11},{10,... | collective-permute-start | bytes 294920 | tf_op jit(solution)/shard_map/ppermute | solution.py:344
  51.2 4.2 %collective-permute-start.26 = (bf16[64,512]{1,0:T(8,128)(2,1)S(1)}, bf16[64,512]{1,0:T(8,128)(2,1)S(1)}, u32[]{:S(2)}, u32[]{:S(2)}) collective-permute-start(bf16[64,512]{1,0:T(8,128)(2,1)S(1)} %get-tuple-element.114.refs_2_), channel_id=1, source_target_pairs={{0,1},{1,0},{2,3},{3,2},{4,5},{5,4},{6,7},{7,6},{8,9},{9,8},{10,11... | collective-permute-start | bytes 196616 | tf_op jit(solution)/shard_map/ppermute | solution.py:344
  51.7 4.3 %collective-permute-start.20 = (bf16[64,512]{1,0:T(8,128)(2,1)S(1)}, bf16[64,512]{1,0:T(8,128)(2,1)S(1)}, u32[]{:S(2)}, u32[]{:S(2)}) collective-permute-start(bf16[64,512]{1,0:T(8,128)(2,1)S(1)} %get-tuple-element.115.refs_1_), channel_id=1, source_target_pairs={{0,2},{1,3},{2,0},{3,1},{4,6},{5,7},{6,4},{7,5},{8,10},{9,11},{10,... | collective-permute-start | bytes 196616 | tf_op jit(solution)/shard_map/ppermute | solution.py:344
  53.0 3.1 %collective-permute-start.24 = (bf16[96,512]{1,0:T(8,128)(2,1)S(1)}, bf16[96,512]{1,0:T(8,128)(2,1)S(1)}, u32[]{:S(2)}, u32[]{:S(2)}) collective-permute-start(bf16[96,512]{1,0:T(8,128)(2,1)S(1)} %shard_map.159.refs_0_), channel_id=1, source_target_pairs={{0,1},{1,0},{2,3},{3,2},{4,5},{5,4},{6,7},{7,6},{8,9},{9,8},{10,11... | collective-permute-start | bytes 294920 | tf_op jit(solution)/shard_map/ppermute | solution.py:344
  54.9 2.4 %collective-permute-start.21 = (bf16[96,512]{1,0:T(8,128)(2,1)S(1)}, bf16[96,512]{1,0:T(8,128)(2,1)S(1)}, u32[]{:S(2)}, u32[]{:S(2)}) collective-permute-start(bf16[96,512]{1,0:T(8,128)(2,1)S(1)} %collective-permute-done.18.refs_0_), channel_id=1, source_target_pairs={{0,1},{1,0},{2,3},{3,2},{4,5},{5,4},{6,7},{7,6},{8,9},{9,8},{10,11... | collective-permute-start | bytes 294920 | tf_op jit(solution)/shard_map/ppermute | solution.py:344
  55.4 1.9 %collective-permute-start.23 = (bf16[64,512]{1,0:T(8,128)(2,1)S(1)}, bf16[64,512]{1,0:T(8,128)(2,1)S(1)}, u32[]{:S(2)}, u32[]{:S(2)}) collective-permute-start(bf16[64,512]{1,0:T(8,128)(2,1)S(1)} %get-tuple-element.116.refs_2_), channel_id=1, source_target_pairs={{0,1},{1,0},{2,3},{3,2},{4,5},{5,4},{6,7},{7,6},{8,9},{9,8},{10,11... | collective-permute-start | bytes 196616 | tf_op jit(solution)/shard_map/ppermute | solution.py:344
  (3 other events, 4.4 us)

commit v6 on v5

--- a/solution.py
+++ b/solution.py
@@ -180,23 +180,13 @@
 def backward_last_kernel(*refs):
     n = WAYS
     sources, targets, args, refs = split_refs(refs)
-    state_0, forcing_0, edges_0, to_src_0, to_dst_0, first_0, second_0, node_0 = refs[:8]
-    state_own, forcing_own, edges, kept_a, core_a, kept_b, core_b, target_kept, target_sent = refs[8:17]
-    first_held, second_held, node_grad_held, edges_1, forcing_1, sems = refs[17:]
-    copies = [
-        pltpu.make_async_copy(source, target, sems.at[i])
-        for i, (source, target) in enumerate(
-            [(edges_0, edges.at[0]), (forcing_0, forcing_own.at[0]), (edges_1, edges.at[1]), (forcing_1, forcing_own.at[1])]
-        )
-    ]
-    copies[0].start()
-    copies[1].start()
+    state_0, to_src_0, to_dst_0, first_0, second_0, node_0 = refs[:6]
+    state_own, forcing, edges, first_held, second_held, node_grad_held, src_kept = refs[6:13]
+    core_a, core_b, target_kept, target_sent = refs[13:]
 
     def put_edges(edge_values, forcing_values):
-        edges_1[...] = edge_values
-        forcing_1[...] = forcing_values
-        copies[2].start()
-        copies[3].start()
+        edges[...] = edge_values
+        forcing[...] = forcing_values
 
     state_1, to_src_1, to_dst_1, first, second, node_grad = backward(1, put_edges, sources, targets, *args)
     state_own[0], state_own[1] = state_0[...], state_1
@@ -207,22 +197,29 @@
     node_grad_held[...] = node_0[...] + node_grad
     part, block = first_held.shape[0] // n, second_held.shape[0] // n
     size, wide = block // 2, second_held.shape[1]
-    for k in range(n):
+    for i, k in enumerate((1, 3)):
         other = lax.axis_index("dst") ^ k
-        into = core_a if k % 2 else kept_a
-        start = (k // 2) * part
-        into[start : start + part] = first_held[pl.ds(pl.multiple_of(other * part, part), part)].astype(into.dtype)
-        into = core_b if k % 2 else kept_b
-        start = (k // 2) * (into.shape[0] // 2)
+        core_a[i * part : (i + 1) * part] = first_held[pl.ds(pl.multiple_of(other * part, part), part)].astype(BF)
+        start = i * (core_b.shape[0] // 2)
         for held in (second_held, node_grad_held):
             for j in range(2):
                 spot = pl.ds(pl.multiple_of(other * block + j * size, size), size)
-                into[start : start + size, j * wide : (j + 1) * wide] = held[spot].astype(into.dtype)
+                core_b[start : start + size, j * wide : (j + 1) * wide] = held[spot].astype(BF)
             start += size
-        put_nodes(into, start, k, (to_src_0[...], to_src_1))
+        put_nodes(core_b, start, k, (to_src_0[...], to_src_1))
+    for i, k in enumerate((0, 2)):
+        put_nodes(src_kept, i * target_kept.shape[0], k, (to_src_0[...], to_src_1))
     put_nodes(target_kept, 0, 2, (to_dst_0[...], to_dst_1))
     for i, k in enumerate((1, 3)):
         put_nodes(target_sent, i * target_kept.shape[0], k, (to_dst_0[...], to_dst_1))
+
+
+def out_kernel(forcing_0, edges_0, forcing_1, edges_1, forcing, edges, token, sems):
+    pairs = [(edges_0, edges.at[0]), (edges_1, edges.at[1]), (forcing_0, forcing.at[0]), (forcing_1, forcing.at[1])]
+    copies = [pltpu.make_async_copy(*ends, sems.at[i]) for i, ends in enumerate(pairs)]
+    for copy in copies:
+        copy.start()
+    token[...] = jnp.zeros_like(token)
     for copy in copies:
         copy.wait()
 
@@ -247,10 +244,29 @@
             state[moment, spot] = base[moment, spot] + value[:, lanes]
 
 
-def near_kernel(kept, arrived, own, across):
-    wide = own.shape[0]
-    own[...] = kept[:wide] + arrived[:wide].astype(F32)
-    across[...] = (kept[wide:] + arrived[wide:].astype(F32)).astype(BF)
+def first_near_kernel(whole, arrived, own, across):
+    part = own.shape[0]
+    for i, (k, into) in enumerate(((0, own), (2, across))):
+        spot = pl.ds(pl.multiple_of((lax.axis_index("dst") ^ k) * part, part), part)
+        into[...] = (whole[spot] + arrived[i * part : (i + 1) * part].astype(F32)).astype(into.dtype)
+
+
+def second_near_kernel(second, node_grad, src_kept, arrived, own, across):
+    wide = second.shape[1]
+    block = second.shape[0] // WAYS
+    size, half = block // 2, src_kept.shape[0] // 2
+    for i, (k, into) in enumerate(((0, own), (2, across))):
+        other = lax.axis_index("dst") ^ k
+        start = 0
+        for whole in (second, node_grad):
+            for j in range(2):
+                lanes = slice(j * wide, (j + 1) * wide)
+                spot = pl.ds(pl.multiple_of(other * block + j * size, size), size)
+                value = arrived[i * into.shape[0] + start : i * into.shape[0] + start + size, lanes]
+                into[start : start + size, lanes] = (whole[spot] + value.astype(F32)).astype(into.dtype)
+            start += size
+        value = arrived[i * into.shape[0] + start : (i + 1) * into.shape[0]]
+        into[start:] = (src_kept[i * half : (i + 1) * half] + value.astype(F32)).astype(into.dtype)
 
 
 def add_kernel(mine, arrived, own, sent):
@@ -259,30 +275,29 @@
     sent[...] = total.astype(BF)
 
 
-def last_add_kernel(mine, arrived, sent):
-    sent[...] = (mine[...] + arrived[...].astype(F32)).astype(BF)
-
-
-def middle_kernel(mine, arrived, state_own, target_sent, state, own, sent, node_share):
+def second_middle_kernel(mine, arrived, target_sent, _, own, sent, node_share, nodes):
     total = mine[...] + arrived[...].astype(F32)
     size = own.shape[0]
     own[...] = total[:size]
     sent[:size] = total[:size].astype(BF)
     sent[size:] = target_sent[...]
     node_share[...] = total[size : 2 * size].astype(BF)
-    add_nodes(state, state_own, total[2 * size :])
-
-
-def second_sum_kernel(mine, arrived, target_kept, state_in, state, own, sent):
+    nodes[...] = total[2 * size :]
+
+
+def second_sum_over_src_kernel(mine, arrived, target_kept, own, sent):
     size, half = own.shape[0], target_kept.shape[0]
     total = mine[...] + arrived[:size].astype(F32)
     own[...] = total
     sent[:size] = total.astype(BF)
-    add_nodes(state, state_in, arrived[size : size + half].astype(F32))
     sent[size:] = (target_kept[...] + arrived[size + half :].astype(F32)).astype(BF)
 
 
-def gather_kernel(mine, arrived, node_across, share, node_sent):
+def first_gather_kernel(mine, arrived, share):
+    share[...] = (mine[...] + arrived[...].astype(F32)).astype(BF)
+
+
+def second_gather_kernel(mine, arrived, node_across, share, node_sent):
     share[...] = (mine[...] + arrived[: mine.shape[0]].astype(F32)).astype(BF)
     node_sent[...] = node_across[...]
 
@@ -312,11 +327,18 @@
         copy.wait()
 
 
-def last_shares_kernel(state_in, arrived, *refs):
-    state_held, state_sem = refs[17:]
-    copies = put_shares((2, 3), (refs[:3], refs[3:6]), refs[10:13], refs[13:17])
-    add_nodes(state_held, state_in, arrived[arrived.shape[0] - state_in.shape[1] // 2 :].astype(F32))
-    copies.append(pltpu.make_async_copy(state_held, refs[9], state_sem))
+def last_shares_kernel(state_own, nodes, arrived_1, arrived_2, *refs):
+    shares, outs, scratch = refs[:6], refs[9:13], refs[13:]
+    *held, state_held, state_sem = scratch
+    copies = put_shares((2, 3), (shares[:3], shares[3:]), outs[1:], held)
+    half = nodes.shape[0]
+    part = arrived_2.shape[0] - half
+    add_nodes(
+        state_held,
+        state_own,
+        nodes[...] + arrived_1[part : part + half].astype(F32) + arrived_2[part:].astype(F32),
+    )
+    copies.append(pltpu.make_async_copy(state_held, outs[0], state_sem))
     copies[-1].start()
     for copy in copies:
         copy.wait()
@@ -404,7 +426,7 @@
         [*sources, *targets, *sums[moment], attr, src_t, dst_t, *forward[moment][2:], w1, w2, wn]
         for moment in range(steps)
     ]
-    earlier = call(
+    state_0, forcing_0, edges_0, *earlier = call(
         backward_first_kernel,
         [
             ((rows, width), F32),
@@ -422,55 +444,58 @@
     part, block, half = edge_w1.shape[0] // WAYS, hid // WAYS, rows // 2
     size = block // 2
     wide = 2 * size + half
-    state_own, grad_forcing, edges, kept_a, core_a, kept_b, core_b, target_kept, target_sent = call(
+    state_own, forcing_1, edges_1, first, second, node_grad, src_kept, core_a, core_b, target_kept, target_sent = call(
         backward_last_kernel,
         [
             ((steps, rows, width), F32),
-            ((steps, rows, width), F32),
-            ((steps, slots, width), F32),
-            ((2 * part, hid), F32),
+            ((rows, width), F32),
+            ((slots, width), F32),
+            (edge_w1.shape, F32),
+            (edge_w2.shape, F32),
+            (node_w1.shape, F32),
+            ((2 * half, hid), F32),
             ((2 * part, hid), BF),
-            ((2 * wide, hid), F32),
             ((2 * wide, hid), BF),
             ((half, hid), F32),
             ((2 * half, hid), BF),
         ],
-        [
-            (edge_w1.shape, F32),
-            (edge_w2.shape, F32),
-            (node_w1.shape, F32),
-            ((slots, width), F32),
-            ((rows, width), F32),
-            pltpu.SemaphoreType.DMA((4,)),
-        ],
-        [*args[1], *earlier],
-        out_spaces=[pltpu.VMEM] + [pltpu.HBM] * 2 + [pltpu.VMEM] * 6,
-    )
-
-    def pair(size):
-        return [((size, hid), F32), ((size, hid), BF)]
-
+        [],
+        [*args[1], state_0, *earlier],
+    )
+    grad_forcing, edges, token = call(
+        out_kernel,
+        [((steps, rows, width), F32), ((steps, slots, width), F32), ((8, 128), F32)],
+        [pltpu.SemaphoreType.DMA((4,))],
+        [forcing_0, edges_0, forcing_1, edges_1],
+        out_spaces=[pltpu.HBM] * 2 + [pltpu.VMEM],
+    )
+
+    def both(count, sent):
+        return [((count, hid), F32), ((sent, hid), BF)]
+
+    mine_a, across_a = call(first_near_kernel, both(part, part), [], [first, swap(core_a, "dst", 1)])
+    mine_b, across_b = call(
+        second_near_kernel, both(wide, wide), [], [second, node_grad, src_kept, swap(core_b, "dst", 1)]
+    )
+    own_a, sent_a = call(add_kernel, both(part, part), [], [mine_a, swap(across_a, "dst", 2)])
+    own_b, sent_b, node_share, nodes_sum = call(
+        second_middle_kernel,
+        both(size, size + 2 * half) + [((size, hid), BF), ((half, hid), F32)],
+        [],
+        [mine_b, swap(across_b, "dst", 2), target_sent, token],
+    )
+    node_across = swap(node_share, "dst", 2)
+    own_a, sent_a = call(add_kernel, both(part, part), [], [own_a, swap(sent_a, "src", 1)])
+    arrived_1 = swap(sent_b, "src", 1)
+    own_b, sent_b = call(
+        second_sum_over_src_kernel, both(size, size + half), [], [own_b, arrived_1, target_kept]
+    )
+    share_a = call(first_gather_kernel, [((part, hid), BF)], [], [own_a, swap(sent_a, "src", 2)])[0]
+    arrived_2 = swap(sent_b, "src", 2)
+    share_b, node_across = call(
+        second_gather_kernel, [((size, hid), BF)] * 2, [], [own_b, arrived_2, node_across]
+    )
     state = ((steps, rows, width), F32)
-    mine_a, across_a = call(near_kernel, pair(part), [], [kept_a, swap(core_a, "dst", 1)])
-    mine_b, across_b = call(near_kernel, pair(wide), [], [kept_b, swap(core_b, "dst", 1)])
-    own_a, sent_a = call(add_kernel, pair(part), [], [mine_a, swap(across_a, "dst", 2)])
-    state_sum, own_b, sent_b, node_share = call(
-        middle_kernel,
-        [state, ((size, hid), F32), ((size + 2 * half, hid), BF), ((size, hid), BF)],
-        [],
-        [mine_b, swap(across_b, "dst", 2), state_own, target_sent],
-    )
-    node_across = swap(node_share, "dst", 2)
-    own_a, sent_a = call(add_kernel, pair(part), [], [own_a, swap(sent_a, "src", 1)])
-    state_sum, own_b, sent_b = call(
-        second_sum_kernel,
-        [state, ((size, hid), F32), ((size + half, hid), BF)],
-        [],
-        [own_b, swap(sent_b, "src", 1), target_kept, state_sum],
-    )
-    share_a = call(last_add_kernel, [((part, hid), BF)], [], [own_a, swap(sent_a, "src", 2)])[0]
-    arrived = swap(sent_b, "src", 2)
-    share_b, node_across = call(gather_kernel, [((size, hid), BF)] * 2, [], [own_b, arrived, node_across])
     own = [share_a, share_b, node_share]
     across = [swap(share_a, "dst", 2), swap(share_b, "dst", 2), node_across]
     outs = [(edge_w1.shape, F32), (edge_w2.shape, F32), (node_w1.shape, F32)]
@@ -487,10 +512,10 @@
         last_shares_kernel,
         [state] + outs,
         held + [state, pltpu.SemaphoreType.DMA],
-        [state_sum, arrived] + across + [swap(share, "dst", 1) for share in across] + list(grads),
-        [pltpu.VMEM] * 8 + [pltpu.HBM] * 3,
+        [state_own, nodes_sum, arrived_1, arrived_2] + across + [swap(share, "dst", 1) for share in across] + list(grads),
+        [pltpu.VMEM] * 10 + [pltpu.HBM] * 3,
         [pltpu.HBM] * 4,
-        {8: 1, 9: 2, 10: 3},
+        {10: 1, 11: 2, 12: 3},
     )
     return grad_state, grad_forcing, edges[:, None, None], grad_first, grad_second, grad_node
 

time: 58.6 us -> 57.8 us (0.986)
  waiting for transfers between devices: 17.6 us -> 16.8 us
    ppermute x27, waiting for transfers between devices: 17.6 us -> 16.8 us  [swap(): return lax.ppermute(value, axis, [(i, i ^ k) for i in range(WAYS)])]
    pallas_call x18 -> x19, Pallas kernels: 10.5 us -> 10.6 us  [call(): pl.pallas_call(kernel, out_shape=[jax.ShapeDtypeStruct(shape, dtype) for...]
  transfers between devices with their start and end apart: 27 -> 27, of which waited for: 14 -> 14; matrix products, arithmetic and copies ran while one was open for 0% -> 0% of each run, Pallas kernels for 9% -> 11%
where the time goes in v6:
time: 57.8 us; the launch traced here: 57.5 us
  starting transfers between devices  28.8 us (50%)
  waiting for transfers between devices  16.8 us (29%)
  Pallas kernels  10.6 us (18%)
  between operations  1.45 us (3%)
    ppermute x27, starting transfers between devices, swap(): return lax.ppermute(value, axis, [(i, i ^ k) for i in range(WAYS)])  28.8 us
    ppermute x27, waiting for transfers between devices, swap(): return lax.ppermute(value, axis, [(i, i ^ k) for i in range(WAYS)])  16.8 us
    pallas_call x19, Pallas kernels, call(): pl.pallas_call(kernel, out_shape=[jax.ShapeDtypeStruct(shape, dtype) for...  10.6 us
  transfers between devices with their start and end apart: 27, of which 14 were waited for; matrix products, arithmetic and copies ran while one was open for 0% of the time, Pallas kernels for 11%

profile of v6, /device:TPU:0, one launch (start us, length us, event | category | flops | bytes accessed | tf_op | source)
XLA Modules:
  0.0 57.5 jit_solution(10743549096701260462)
XLA Ops:
  1.5 5.1 %collective-permute-start.5 = (bf16[2,32,512]{2,1,0:T(8,128)(2,1)S(1)}, bf16[2,32,512]{2,1,0:T(8,128)(2,1)S(1)}, u32[]{:S(2)}, u32[]{:S(2)}) collective-permute-start(bf16[2,32,512]{2,1,0:T(8,128)(2,1)S(1)} %shard_map.145.refs_0_.refs_4_), channel_id=1, source_target_pairs={{0,12},{4,8},{8,4},{12,0},{1,13},{5,9},{9,5},{13,1},{2,14},{6,10},... | collective-permute-start | bytes 196616 | tf_op jit(solution)/shard_map/ppermute | solution.py:366
  7.2 1.7 %collective-permute-start.2 = (bf16[2,32,128]{2,1,0:T(8,128)(2,1)}, bf16[2,32,128]{2,1,0:T(8,128)(2,1)S(1)}, u32[]{:S(2)}, u32[]{:S(2)}) collective-permute-start(bf16[2,32,128]{2,1,0:T(8,128)(2,1)} %state.1), channel_id=1, source_target_pairs={{0,3},{1,2},{2,1},{3,0},{4,7},{5,6},{6,5},{7,4},{8,11},{9,10},{10,... | collective-permute-start | bytes 49160 | tf_op jit(solution)/shard_map/ppermute | solution.py:366
  9.0 1.3 %collective-permute-start.1 = (bf16[2,32,128]{2,1,0:T(8,128)(2,1)}, bf16[2,32,128]{2,1,0:T(8,128)(2,1)S(1)}, u32[]{:S(2)}, u32[]{:S(2)}) collective-permute-start(bf16[2,32,128]{2,1,0:T(8,128)(2,1)} %state.1), channel_id=1, source_target_pairs={{0,2},{1,3},{2,0},{3,1},{4,6},{5,7},{6,4},{7,5},{8,10},{9,11},{10,... | collective-permute-start | bytes 49160 | tf_op jit(solution)/shard_map/ppermute | solution.py:366
  10.9 1.6 %shard_map.146 = (bf16[2,512,128]{2,1,0:T(8,128)(2,1)S(1)}, bf16[384,512]{1,0:T(8,128)(2,1)S(1)}, bf16[512,256]{1,0:T(8,128)(2,1)S(1)}, bf16[512,256]{1,0:T(8,12...) custom-call(s32[1,1]{1,0:T(1,128)S(6)} %copy.23.count, ...), custom_call_target="tpu_custom_call" | custom-call | tf_op jit(solution)/shard_map/pallas_call | solution.py:348
  14.0 1.3 %collective-permute-start.8 = (bf16[128,256]{1,0:T(8,128)(2,1)S(1)}, bf16[128,256]{1,0:T(8,128)(2,1)S(1)}, u32[]{:S(2)}, u32[]{:S(2)}) collective-permute-start(bf16[128,256]{1,0:T(8,128)(2,1)S(1)} %get-tuple-element.84), channel_id=1, source_target_pairs={{0,4},{4,0},{8,12},{12,8},{1,5},{5,1},{9,13},{13,9},{2,6},{6,2},{1... | collective-permute-start | bytes 196616 | tf_op jit(solution)/shard_map/ppermute | solution.py:366
  17.2 1.3 %collective-permute-done.8.arrived = bf16[128,256]{1,0:T(8,128)(2,1)S(1)} collective-permute-done((bf16[128,256]{1,0:T(8,128)(2,1)S(1)}, bf16[128,256]{1,0:T(8,128)(2,1)S(1)}, u32[]{:S(2)}, u32[]{:S(2)}) %collective-permute-start.8) | collective-permute-done | bytes 65568 | tf_op jit(solution)/shard_map/ppermute | solution.py:366
  18.5 2.0 %collective-permute-start.9 = (bf16[128,256]{1,0:T(8,128)(2,1)S(1)}, bf16[128,256]{1,0:T(8,128)(2,1)S(1)}, u32[]{:S(2)}, u32[]{:S(2)}) collective-permute-start(bf16[128,256]{1,0:T(8,128)(2,1)S(1)} %get-tuple-element.86), channel_id=1, source_target_pairs={{0,8},{4,12},{8,0},{12,4},{1,9},{5,13},{9,1},{13,5},{2,10},{6,14},... | collective-permute-start | bytes 196616 | tf_op jit(solution)/shard_map/ppermute | solution.py:366
  21.4 2.3 %collective-permute-start.7 = (bf16[128,256]{1,0:T(8,128)(2,1)S(1)}, bf16[128,256]{1,0:T(8,128)(2,1)S(1)}, u32[]{:S(2)}, u32[]{:S(2)}) collective-permute-start(bf16[128,256]{1,0:T(8,128)(2,1)S(1)} %get-tuple-element.78), channel_id=1, source_target_pairs={{0,8},{4,12},{8,0},{12,4},{1,9},{5,13},{9,1},{13,5},{2,10},{6,14},... | collective-permute-start | bytes 196616 | tf_op jit(solution)/shard_map/ppermute | solution.py:366
  23.7 1.7 %collective-permute-done.9.refs_9_ = bf16[128,256]{1,0:T(8,128)(2,1)S(1)} collective-permute-done((bf16[128,256]{1,0:T(8,128)(2,1)S(1)}, bf16[128,256]{1,0:T(8,128)(2,1)S(1)}, u32[]{:S(2)}, u32[]{:S(2)}) %collective-permute-start.9) | collective-permute-done | bytes 65568 | tf_op jit(solution)/shard_map/ppermute | solution.py:366
  25.4 1.5 %shard_map.151 = (f32[32,128]{1,0:T(8,128)S(1)}, f32[32,128]{1,0:T(8,128)S(1)}, f32[512,128]{1,0:T(8,128)S(1)}, f32[128,128]{1,0:T(8,128)S(1)}, f32[128,128]{1,0...) custom-call(bf16[2,32,512]{2,1,0:T(8,128)(2,1)S(1)} %shard_map.145.refs_0_.refs_4_, ...), custom_call_target="tpu_custom_call" | custom-call | tf_op jit(solution)/shard_map/pallas_call | solution.py:348
  26.9 1.5 %shard_map.152 = (f32[2,32,128]{2,1,0:T(8,128)S(1)}, f32[32,128]{1,0:T(8,128)S(1)}, f32[512,128]{1,0:T(8,128)S(1)}, f32[384,512]{1,0:T(8,128)S(1)}, f32[512,256]...) custom-call(bf16[2,32,512]{2,1,0:T(8,128)(2,1)S(1)} %shard_map.145.r, ...), custom_call_target="tpu_custom_call" | custom-call | tf_op jit(solution)/shard_map/pallas_call | solution.py:348
  29.0 1.4 %collective-permute-done.14.arrived = bf16[192,512]{1,0:T(8,128)(2,1)S(1)} collective-permute-done((bf16[192,512]{1,0:T(8,128)(2,1)S(1)}, bf16[192,512]{1,0:T(8,128)(2,1)S(1)}, u32[]{:S(2)}, u32[]{:S(2)}) %collective-permute-start.14) | collective-permute-done | bytes 196640 | tf_op jit(solution)/shard_map/ppermute | solution.py:366
  30.4 1.3 %collective-permute-start.15 = (bf16[96,512]{1,0:T(8,128)(2,1)S(1)}, bf16[96,512]{1,0:T(8,128)(2,1)S(1)}, u32[]{:S(2)}, u32[]{:S(2)}) collective-permute-start(bf16[96,512]{1,0:T(8,128)(2,1)S(1)} %get-tuple-element.116), channel_id=1, source_target_pairs={{0,2},{1,3},{2,0},{3,1},{4,6},{5,7},{6,4},{7,5},{8,10},{9,11},{10,... | collective-permute-start | bytes 294920 | tf_op jit(solution)/shard_map/ppermute | solution.py:366
  32.6 3.5 %collective-permute-done.15.arrived = bf16[96,512]{1,0:T(8,128)(2,1)S(1)} collective-permute-done((bf16[96,512]{1,0:T(8,128)(2,1)S(1)}, bf16[96,512]{1,0:T(8,128)(2,1)S(1)}, u32[]{:S(2)}, u32[]{:S(2)}) %collective-permute-start.15) | collective-permute-done | bytes 98336 | tf_op jit(solution)/shard_map/ppermute | solution.py:366
  36.1 1.3 %collective-permute-start.16 = (bf16[96,512]{1,0:T(8,128)(2,1)S(1)}, bf16[96,512]{1,0:T(8,128)(2,1)S(1)}, u32[]{:S(2)}, u32[]{:S(2)}) collective-permute-start(bf16[96,512]{1,0:T(8,128)(2,1)S(1)} %get-tuple-element.118), channel_id=1, source_target_pairs={{0,4},{4,0},{8,12},{12,8},{1,5},{5,1},{9,13},{13,9},{2,6},{6,2},{1... | collective-permute-start | bytes 294920 | tf_op jit(solution)/shard_map/ppermute | solution.py:366
  38.5 1.3 %collective-permute-start.12 = (bf16[96,512]{1,0:T(8,128)(2,1)S(1)}, bf16[96,512]{1,0:T(8,128)(2,1)S(1)}, u32[]{:S(2)}, u32[]{:S(2)}) collective-permute-start(bf16[96,512]{1,0:T(8,128)(2,1)S(1)} %get-tuple-element.109), channel_id=1, source_target_pairs={{0,4},{4,0},{8,12},{12,8},{1,5},{5,1},{9,13},{13,9},{2,6},{6,2},{1... | collective-permute-start | bytes 294920 | tf_op jit(solution)/shard_map/ppermute | solution.py:366
  39.8 1.4 %collective-permute-done.16.arrived = bf16[96,512]{1,0:T(8,128)(2,1)S(1)} collective-permute-done((bf16[96,512]{1,0:T(8,128)(2,1)S(1)}, bf16[96,512]{1,0:T(8,128)(2,1)S(1)}, u32[]{:S(2)}, u32[]{:S(2)}) %collective-permute-start.16) | collective-permute-done | bytes 98336 | tf_op jit(solution)/shard_map/ppermute | solution.py:366
  41.2 2.1 %collective-permute-start.17 = (bf16[96,512]{1,0:T(8,128)(2,1)S(1)}, bf16[96,512]{1,0:T(8,128)(2,1)S(1)}, u32[]{:S(2)}, u32[]{:S(2)}) collective-permute-start(bf16[96,512]{1,0:T(8,128)(2,1)S(1)} %get-tuple-element.120), channel_id=1, source_target_pairs={{0,8},{4,12},{8,0},{12,4},{1,9},{5,13},{9,1},{13,5},{2,10},{6,14},... | collective-permute-start | bytes 294920 | tf_op jit(solution)/shard_map/ppermute | solution.py:366
  44.3 1.8 %collective-permute-start.13 = (bf16[80,512]{1,0:T(8,128)(2,1)S(1)}, bf16[80,512]{1,0:T(8,128)(2,1)S(1)}, u32[]{:S(2)}, u32[]{:S(2)}) collective-permute-start(bf16[80,512]{1,0:T(8,128)(2,1)S(1)} %get-tuple-element.112), channel_id=1, source_target_pairs={{0,8},{4,12},{8,0},{12,4},{1,9},{5,13},{9,1},{13,5},{2,10},{6,14},... | collective-permute-start | bytes 245768 | tf_op jit(solution)/shard_map/ppermute | solution.py:366
  46.1 1.2 %collective-permute-start.19 = (bf16[64,512]{1,0:T(8,128)(2,1)S(1)}, bf16[64,512]{1,0:T(8,128)(2,1)S(1)}, u32[]{:S(2)}, u32[]{:S(2)}) collective-permute-start(bf16[64,512]{1,0:T(8,128)(2,1)S(1)} %get-tuple-element.122.refs_2_), channel_id=1, source_target_pairs={{0,2},{1,3},{2,0},{3,1},{4,6},{5,7},{6,4},{7,5},{8,10},{9,11},{10,... | collective-permute-start | bytes 196616 | tf_op jit(solution)/shard_map/ppermute | solution.py:366
  47.3 1.9 %collective-permute-done.17.arrived = bf16[96,512]{1,0:T(8,128)(2,1)S(1)} collective-permute-done((bf16[96,512]{1,0:T(8,128)(2,1)S(1)}, bf16[96,512]{1,0:T(8,128)(2,1)S(1)}, u32[]{:S(2)}, u32[]{:S(2)}) %collective-permute-start.17) | collective-permute-done | bytes 98336 | tf_op jit(solution)/shard_map/ppermute | solution.py:366
  49.2 1.3 %collective-permute-start.18 = (bf16[96,512]{1,0:T(8,128)(2,1)S(1)}, bf16[96,512]{1,0:T(8,128)(2,1)S(1)}, u32[]{:S(2)}, u32[]{:S(2)}) collective-permute-start(bf16[96,512]{1,0:T(8,128)(2,1)S(1)} %shard_map.160.refs_0_), channel_id=1, source_target_pairs={{0,2},{1,3},{2,0},{3,1},{4,6},{5,7},{6,4},{7,5},{8,10},{9,11},{10,... | collective-permute-start | bytes 294920 | tf_op jit(solution)/shard_map/ppermute | solution.py:366
  50.9 1.3 %collective-permute-start.20 = (bf16[64,512]{1,0:T(8,128)(2,1)S(1)}, bf16[64,512]{1,0:T(8,128)(2,1)S(1)}, u32[]{:S(2)}, u32[]{:S(2)}) collective-permute-start(bf16[64,512]{1,0:T(8,128)(2,1)S(1)} %get-tuple-element.123.refs_1_), channel_id=1, source_target_pairs={{0,2},{1,3},{2,0},{3,1},{4,6},{5,7},{6,4},{7,5},{8,10},{9,11},{10,... | collective-permute-start | bytes 196616 | tf_op jit(solution)/shard_map/ppermute | solution.py:366
  52.2 1.9 %collective-permute-done.18.refs_0_ = bf16[96,512]{1,0:T(8,128)(2,1)S(1)} collective-permute-done((bf16[96,512]{1,0:T(8,128)(2,1)S(1)}, bf16[96,512]{1,0:T(8,128)(2,1)S(1)}, u32[]{:S(2)}, u32[]{:S(2)}) %collective-permute-start.18) | collective-permute-done | bytes 98336 | tf_op jit(solution)/shard_map/ppermute | solution.py:366
  (49 shorter events, 13.1 us)
Async XLA Ops:
  1.5 11.5 %collective-permute-start.5 = (bf16[2,32,512]{2,1,0:T(8,128)(2,1)S(1)}, bf16[2,32,512]{2,1,0:T(8,128)(2,1)S(1)}, u32[]{:S(2)}, u32[]{:S(2)}) collective-permute-start(bf16[2,32,512]{2,1,0:T(8,128)(2,1)S(1)} %shard_map.145.refs_0_.refs_4_), channel_id=1, source_target_pairs={{0,12},{4,8},{8,4},{12,0},{1,13},{5,9},{9,5},{13,1},{2,14},{6,10},... | collective-permute-start | bytes 196616 | tf_op jit(solution)/shard_map/ppermute | solution.py:366
  6.6 6.4 %collective-permute-start.4 = (bf16[2,32,512]{2,1,0:T(8,128)(2,1)S(1)}, bf16[2,32,512]{2,1,0:T(8,128)(2,1)S(1)}, u32[]{:S(2)}, u32[]{:S(2)}) collective-permute-start(bf16[2,32,512]{2,1,0:T(8,128)(2,1)S(1)} %shard_map.145.refs_0_.refs_4_), channel_id=1, source_target_pairs={{0,8},{4,12},{8,0},{12,4},{1,9},{5,13},{9,1},{13,5},{2,10},{6,14},... | collective-permute-start | bytes 196616 | tf_op jit(solution)/shard_map/ppermute | solution.py:366
  6.6 6.4 %collective-permute-start.3 = (bf16[2,32,512]{2,1,0:T(8,128)(2,1)S(1)}, bf16[2,32,512]{2,1,0:T(8,128)(2,1)S(1)}, u32[]{:S(2)}, u32[]{:S(2)}) collective-permute-start(bf16[2,32,512]{2,1,0:T(8,128)(2,1)S(1)} %shard_map.145.refs_0_.refs_4_), channel_id=1, source_target_pairs={{0,4},{4,0},{8,12},{12,8},{1,5},{5,1},{9,13},{13,9},{2,6},{6,2},{1... | collective-permute-start | bytes 196616 | tf_op jit(solution)/shard_map/ppermute | solution.py:366
  7.2 5.3 %collective-permute-start.2 = (bf16[2,32,128]{2,1,0:T(8,128)(2,1)}, bf16[2,32,128]{2,1,0:T(8,128)(2,1)S(1)}, u32[]{:S(2)}, u32[]{:S(2)}) collective-permute-start(bf16[2,32,128]{2,1,0:T(8,128)(2,1)} %state.1), channel_id=1, source_target_pairs={{0,3},{1,2},{2,1},{3,0},{4,7},{5,6},{6,5},{7,4},{8,11},{9,10},{10,... | collective-permute-start | bytes 49160 | tf_op jit(solution)/shard_map/ppermute | solution.py:366
  9.0 4.0 %collective-permute-start.1 = (bf16[2,32,128]{2,1,0:T(8,128)(2,1)}, bf16[2,32,128]{2,1,0:T(8,128)(2,1)S(1)}, u32[]{:S(2)}, u32[]{:S(2)}) collective-permute-start(bf16[2,32,128]{2,1,0:T(8,128)(2,1)} %state.1), channel_id=1, source_target_pairs={{0,2},{1,3},{2,0},{3,1},{4,6},{5,7},{6,4},{7,5},{8,10},{9,11},{10,... | collective-permute-start | bytes 49160 | tf_op jit(solution)/shard_map/ppermute | solution.py:366
  14.0 4.5 %collective-permute-start.8 = (bf16[128,256]{1,0:T(8,128)(2,1)S(1)}, bf16[128,256]{1,0:T(8,128)(2,1)S(1)}, u32[]{:S(2)}, u32[]{:S(2)}) collective-permute-start(bf16[128,256]{1,0:T(8,128)(2,1)S(1)} %get-tuple-element.84), channel_id=1, source_target_pairs={{0,4},{4,0},{8,12},{12,8},{1,5},{5,1},{9,13},{13,9},{2,6},{6,2},{1... | collective-permute-start | bytes 196616 | tf_op jit(solution)/shard_map/ppermute | solution.py:366
  16.3 5.0 %collective-permute-start.6 = (bf16[128,256]{1,0:T(8,128)(2,1)S(1)}, bf16[128,256]{1,0:T(8,128)(2,1)S(1)}, u32[]{:S(2)}, u32[]{:S(2)}) collective-permute-start(bf16[128,256]{1,0:T(8,128)(2,1)S(1)} %get-tuple-element.76), channel_id=1, source_target_pairs={{0,4},{4,0},{8,12},{12,8},{1,5},{5,1},{9,13},{13,9},{2,6},{6,2},{1... | collective-permute-start | bytes 196616 | tf_op jit(solution)/shard_map/ppermute | solution.py:366
  18.5 6.9 %collective-permute-start.9 = (bf16[128,256]{1,0:T(8,128)(2,1)S(1)}, bf16[128,256]{1,0:T(8,128)(2,1)S(1)}, u32[]{:S(2)}, u32[]{:S(2)}) collective-permute-start(bf16[128,256]{1,0:T(8,128)(2,1)S(1)} %get-tuple-element.86), channel_id=1, source_target_pairs={{0,8},{4,12},{8,0},{12,4},{1,9},{5,13},{9,1},{13,5},{2,10},{6,14},... | collective-permute-start | bytes 196616 | tf_op jit(solution)/shard_map/ppermute | solution.py:366
  21.4 5.5 %collective-permute-start.7 = (bf16[128,256]{1,0:T(8,128)(2,1)S(1)}, bf16[128,256]{1,0:T(8,128)(2,1)S(1)}, u32[]{:S(2)}, u32[]{:S(2)}) collective-permute-start(bf16[128,256]{1,0:T(8,128)(2,1)S(1)} %get-tuple-element.78), channel_id=1, source_target_pairs={{0,8},{4,12},{8,0},{12,4},{1,9},{5,13},{9,1},{13,5},{2,10},{6,14},... | collective-permute-start | bytes 196616 | tf_op jit(solution)/shard_map/ppermute | solution.py:366
  28.4 3.2 %collective-permute-start.10 = (bf16[288,512]{1,0:T(8,128)(2,1)S(1)}, bf16[288,512]{1,0:T(8,128)(2,1)S(1)}, u32[]{:S(2)}, u32[]{:S(2)}) collective-permute-start(bf16[288,512]{1,0:T(8,128)(2,1)S(1)} %get-tuple-element.99), channel_id=1, source_target_pairs={{0,1},{1,0},{2,3},{3,2},{4,5},{5,4},{6,7},{7,6},{8,9},{9,8},{10,11... | collective-permute-start | bytes 884744 | tf_op jit(solution)/shard_map/ppermute | solution.py:366
  28.5 1.9 %collective-permute-start.14 = (bf16[192,512]{1,0:T(8,128)(2,1)S(1)}, bf16[192,512]{1,0:T(8,128)(2,1)S(1)}, u32[]{:S(2)}, u32[]{:S(2)}) collective-permute-start(bf16[192,512]{1,0:T(8,128)(2,1)S(1)} %get-tuple-element.114), channel_id=1, source_target_pairs={{0,1},{1,0},{2,3},{3,2},{4,5},{5,4},{6,7},{7,6},{8,9},{9,8},{10,11... | collective-permute-start | bytes 589832 | tf_op jit(solution)/shard_map/ppermute | solution.py:366
  30.4 5.7 %collective-permute-start.15 = (bf16[96,512]{1,0:T(8,128)(2,1)S(1)}, bf16[96,512]{1,0:T(8,128)(2,1)S(1)}, u32[]{:S(2)}, u32[]{:S(2)}) collective-permute-start(bf16[96,512]{1,0:T(8,128)(2,1)S(1)} %get-tuple-element.116), channel_id=1, source_target_pairs={{0,2},{1,3},{2,0},{3,1},{4,6},{5,7},{6,4},{7,5},{8,10},{9,11},{10,... | collective-permute-start | bytes 294920 | tf_op jit(solution)/shard_map/ppermute | solution.py:366
  31.7 6.7 %collective-permute-start.11 = (bf16[144,512]{1,0:T(8,128)(2,1)S(1)}, bf16[144,512]{1,0:T(8,128)(2,1)S(1)}, u32[]{:S(2)}, u32[]{:S(2)}) collective-permute-start(bf16[144,512]{1,0:T(8,128)(2,1)S(1)} %get-tuple-element.101), channel_id=1, source_target_pairs={{0,2},{1,3},{2,0},{3,1},{4,6},{5,7},{6,4},{7,5},{8,10},{9,11},{10,... | collective-permute-start | bytes 442376 | tf_op jit(solution)/shard_map/ppermute | solution.py:366
  36.1 5.1 %collective-permute-start.16 = (bf16[96,512]{1,0:T(8,128)(2,1)S(1)}, bf16[96,512]{1,0:T(8,128)(2,1)S(1)}, u32[]{:S(2)}, u32[]{:S(2)}) collective-permute-start(bf16[96,512]{1,0:T(8,128)(2,1)S(1)} %get-tuple-element.118), channel_id=1, source_target_pairs={{0,4},{4,0},{8,12},{12,8},{1,5},{5,1},{9,13},{13,9},{2,6},{6,2},{1... | collective-permute-start | bytes 294920 | tf_op jit(solution)/shard_map/ppermute | solution.py:366
  38.5 5.7 %collective-permute-start.12 = (bf16[96,512]{1,0:T(8,128)(2,1)S(1)}, bf16[96,512]{1,0:T(8,128)(2,1)S(1)}, u32[]{:S(2)}, u32[]{:S(2)}) collective-permute-start(bf16[96,512]{1,0:T(8,128)(2,1)S(1)} %get-tuple-element.109), channel_id=1, source_target_pairs={{0,4},{4,0},{8,12},{12,8},{1,5},{5,1},{9,13},{13,9},{2,6},{6,2},{1... | collective-permute-start | bytes 294920 | tf_op jit(solution)/shard_map/ppermute | solution.py:366
  41.2 7.9 %collective-permute-start.17 = (bf16[96,512]{1,0:T(8,128)(2,1)S(1)}, bf16[96,512]{1,0:T(8,128)(2,1)S(1)}, u32[]{:S(2)}, u32[]{:S(2)}) collective-permute-start(bf16[96,512]{1,0:T(8,128)(2,1)S(1)} %get-tuple-element.120), channel_id=1, source_target_pairs={{0,8},{4,12},{8,0},{12,4},{1,9},{5,13},{9,1},{13,5},{2,10},{6,14},... | collective-permute-start | bytes 294920 | tf_op jit(solution)/shard_map/ppermute | solution.py:366
  44.3 6.6 %collective-permute-start.13 = (bf16[80,512]{1,0:T(8,128)(2,1)S(1)}, bf16[80,512]{1,0:T(8,128)(2,1)S(1)}, u32[]{:S(2)}, u32[]{:S(2)}) collective-permute-start(bf16[80,512]{1,0:T(8,128)(2,1)S(1)} %get-tuple-element.112), channel_id=1, source_target_pairs={{0,8},{4,12},{8,0},{12,4},{1,9},{5,13},{9,1},{13,5},{2,10},{6,14},... | collective-permute-start | bytes 245768 | tf_op jit(solution)/shard_map/ppermute | solution.py:366
  46.1 4.3 %collective-permute-start.19 = (bf16[64,512]{1,0:T(8,128)(2,1)S(1)}, bf16[64,512]{1,0:T(8,128)(2,1)S(1)}, u32[]{:S(2)}, u32[]{:S(2)}) collective-permute-start(bf16[64,512]{1,0:T(8,128)(2,1)S(1)} %get-tuple-element.122.refs_2_), channel_id=1, source_target_pairs={{0,2},{1,3},{2,0},{3,1},{4,6},{5,7},{6,4},{7,5},{8,10},{9,11},{10,... | collective-permute-start | bytes 196616 | tf_op jit(solution)/shard_map/ppermute | solution.py:366
  49.2 4.9 %collective-permute-start.18 = (bf16[96,512]{1,0:T(8,128)(2,1)S(1)}, bf16[96,512]{1,0:T(8,128)(2,1)S(1)}, u32[]{:S(2)}, u32[]{:S(2)}) collective-permute-start(bf16[96,512]{1,0:T(8,128)(2,1)S(1)} %shard_map.160.refs_0_), channel_id=1, source_target_pairs={{0,2},{1,3},{2,0},{3,1},{4,6},{5,7},{6,4},{7,5},{8,10},{9,11},{10,... | collective-permute-start | bytes 294920 | tf_op jit(solution)/shard_map/ppermute | solution.py:366
  50.4 4.2 %collective-permute-start.26 = (bf16[64,512]{1,0:T(8,128)(2,1)S(1)}, bf16[64,512]{1,0:T(8,128)(2,1)S(1)}, u32[]{:S(2)}, u32[]{:S(2)}) collective-permute-start(bf16[64,512]{1,0:T(8,128)(2,1)S(1)} %get-tuple-element.122.refs_2_), channel_id=1, source_target_pairs={{0,1},{1,0},{2,3},{3,2},{4,5},{5,4},{6,7},{7,6},{8,9},{9,8},{10,11... | collective-permute-start | bytes 196616 | tf_op jit(solution)/shard_map/ppermute | solution.py:366
  50.9 4.3 %collective-permute-start.20 = (bf16[64,512]{1,0:T(8,128)(2,1)S(1)}, bf16[64,512]{1,0:T(8,128)(2,1)S(1)}, u32[]{:S(2)}, u32[]{:S(2)}) collective-permute-start(bf16[64,512]{1,0:T(8,128)(2,1)S(1)} %get-tuple-element.123.refs_1_), channel_id=1, source_target_pairs={{0,2},{1,3},{2,0},{3,1},{4,6},{5,7},{6,4},{7,5},{8,10},{9,11},{10,... | collective-permute-start | bytes 196616 | tf_op jit(solution)/shard_map/ppermute | solution.py:366
  52.2 3.1 %collective-permute-start.24 = (bf16[96,512]{1,0:T(8,128)(2,1)S(1)}, bf16[96,512]{1,0:T(8,128)(2,1)S(1)}, u32[]{:S(2)}, u32[]{:S(2)}) collective-permute-start(bf16[96,512]{1,0:T(8,128)(2,1)S(1)} %shard_map.160.refs_0_), channel_id=1, source_target_pairs={{0,1},{1,0},{2,3},{3,2},{4,5},{5,4},{6,7},{7,6},{8,9},{9,8},{10,11... | collective-permute-start | bytes 294920 | tf_op jit(solution)/shard_map/ppermute | solution.py:366
  54.1 2.4 %collective-permute-start.21 = (bf16[96,512]{1,0:T(8,128)(2,1)S(1)}, bf16[96,512]{1,0:T(8,128)(2,1)S(1)}, u32[]{:S(2)}, u32[]{:S(2)}) collective-permute-start(bf16[96,512]{1,0:T(8,128)(2,1)S(1)} %collective-permute-done.18.refs_0_), channel_id=1, source_target_pairs={{0,1},{1,0},{2,3},{3,2},{4,5},{5,4},{6,7},{7,6},{8,9},{9,8},{10,11... | collective-permute-start | bytes 294920 | tf_op jit(solution)/shard_map/ppermute | solution.py:366
  54.6 1.9 %collective-permute-start.23 = (bf16[64,512]{1,0:T(8,128)(2,1)S(1)}, bf16[64,512]{1,0:T(8,128)(2,1)S(1)}, u32[]{:S(2)}, u32[]{:S(2)}) collective-permute-start(bf16[64,512]{1,0:T(8,128)(2,1)S(1)} %get-tuple-element.124.refs_2_), channel_id=1, source_target_pairs={{0,1},{1,0},{2,3},{3,2},{4,5},{5,4},{6,7},{7,6},{8,9},{9,8},{10,11... | collective-permute-start | bytes 196616 | tf_op jit(solution)/shard_map/ppermute | solution.py:366
  (3 other events, 4.4 us)

commit v7 on v6

--- a/solution.py
+++ b/solution.py
@@ -251,7 +251,7 @@
         into[...] = (whole[spot] + arrived[i * part : (i + 1) * part].astype(F32)).astype(into.dtype)
 
 
-def second_near_kernel(second, node_grad, src_kept, arrived, own, across):
+def second_near_kernel(second, node_grad, src_kept, arrived, _, own, across):
     wide = second.shape[1]
     block = second.shape[0] // WAYS
     size, half = block // 2, src_kept.shape[0] // 2
@@ -275,7 +275,7 @@
     sent[...] = total.astype(BF)
 
 
-def second_middle_kernel(mine, arrived, target_sent, _, own, sent, node_share, nodes):
+def second_middle_kernel(mine, arrived, target_sent, own, sent, node_share, nodes):
     total = mine[...] + arrived[...].astype(F32)
     size = own.shape[0]
     own[...] = total[:size]
@@ -475,14 +475,14 @@
 
     mine_a, across_a = call(first_near_kernel, both(part, part), [], [first, swap(core_a, "dst", 1)])
     mine_b, across_b = call(
-        second_near_kernel, both(wide, wide), [], [second, node_grad, src_kept, swap(core_b, "dst", 1)]
+        second_near_kernel, both(wide, wide), [], [second, node_grad, src_kept, swap(core_b, "dst", 1), token]
     )
     own_a, sent_a = call(add_kernel, both(part, part), [], [mine_a, swap(across_a, "dst", 2)])
     own_b, sent_b, node_share, nodes_sum = call(
         second_middle_kernel,
         both(size, size + 2 * half) + [((size, hid), BF), ((half, hid), F32)],
         [],
-        [mine_b, swap(across_b, "dst", 2), target_sent, token],
+        [mine_b, swap(across_b, "dst", 2), target_sent],
     )
     node_across = swap(node_share, "dst", 2)
     own_a, sent_a = call(add_kernel, both(part, part), [], [own_a, swap(sent_a, "src", 1)])

time: 57.8 us -> 57.4 us (level)
  waiting for transfers between devices: 16.8 us -> 14.8 us
  starting transfers between devices: 28.8 us -> 30.3 us
    ppermute x27, waiting for transfers between devices: 16.8 us -> 14.8 us  [swap(): return lax.ppermute(value, axis, [(i, i ^ k) for i in range(WAYS)])]
    ppermute x27, starting transfers between devices: 28.8 us -> 30.3 us  [swap(): return lax.ppermute(value, axis, [(i, i ^ k) for i in range(WAYS)])]
where the time goes in v7:
time: 57.4 us; the launch traced here: 57.1 us
  starting transfers between devices  30.3 us (53%)
  waiting for transfers between devices  14.8 us (26%)
  Pallas kernels  10.6 us (18%)
  between operations  1.45 us (3%)
    ppermute x27, starting transfers between devices, swap(): return lax.ppermute(value, axis, [(i, i ^ k) for i in range(WAYS)])  30.3 us
    ppermute x27, waiting for transfers between devices, swap(): return lax.ppermute(value, axis, [(i, i ^ k) for i in range(WAYS)])  14.8 us
    pallas_call x19, Pallas kernels, call(): pl.pallas_call(kernel, out_shape=[jax.ShapeDtypeStruct(shape, dtype) for...  10.6 us
  transfers between devices with their start and end apart: 27, of which 14 were waited for; matrix products, arithmetic and copies ran while one was open for 0% of the time, Pallas kernels for 11%

profile of v7, /device:TPU:0, one launch (start us, length us, event | category | flops | bytes accessed | tf_op | source)
XLA Modules:
  0.0 57.1 jit_solution(11205425503467692642)
XLA Ops:
  1.5 5.1 %collective-permute-start.5 = (bf16[2,32,512]{2,1,0:T(8,128)(2,1)S(1)}, bf16[2,32,512]{2,1,0:T(8,128)(2,1)S(1)}, u32[]{:S(2)}, u32[]{:S(2)}) collective-permute-start(bf16[2,32,512]{2,1,0:T(8,128)(2,1)S(1)} %shard_map.145.refs_0_.refs_4_), channel_id=1, source_target_pairs={{0,12},{4,8},{8,4},{12,0},{1,13},{5,9},{9,5},{13,1},{2,14},{6,10},... | collective-permute-start | bytes 196616 | tf_op jit(solution)/shard_map/ppermute | solution.py:366
  7.2 1.7 %collective-permute-start.2 = (bf16[2,32,128]{2,1,0:T(8,128)(2,1)}, bf16[2,32,128]{2,1,0:T(8,128)(2,1)S(1)}, u32[]{:S(2)}, u32[]{:S(2)}) collective-permute-start(bf16[2,32,128]{2,1,0:T(8,128)(2,1)} %state.1), channel_id=1, source_target_pairs={{0,3},{1,2},{2,1},{3,0},{4,7},{5,6},{6,5},{7,4},{8,11},{9,10},{10,... | collective-permute-start | bytes 49160 | tf_op jit(solution)/shard_map/ppermute | solution.py:366
  9.0 1.3 %collective-permute-start.1 = (bf16[2,32,128]{2,1,0:T(8,128)(2,1)}, bf16[2,32,128]{2,1,0:T(8,128)(2,1)S(1)}, u32[]{:S(2)}, u32[]{:S(2)}) collective-permute-start(bf16[2,32,128]{2,1,0:T(8,128)(2,1)} %state.1), channel_id=1, source_target_pairs={{0,2},{1,3},{2,0},{3,1},{4,6},{5,7},{6,4},{7,5},{8,10},{9,11},{10,... | collective-permute-start | bytes 49160 | tf_op jit(solution)/shard_map/ppermute | solution.py:366
  10.9 1.6 %shard_map.146 = (bf16[2,512,128]{2,1,0:T(8,128)(2,1)S(1)}, bf16[384,512]{1,0:T(8,128)(2,1)S(1)}, bf16[512,256]{1,0:T(8,128)(2,1)S(1)}, bf16[512,256]{1,0:T(8,12...) custom-call(s32[1,1]{1,0:T(1,128)S(6)} %copy.23.count, ...), custom_call_target="tpu_custom_call" | custom-call | tf_op jit(solution)/shard_map/pallas_call | solution.py:348
  14.0 1.3 %collective-permute-start.8 = (bf16[128,256]{1,0:T(8,128)(2,1)S(1)}, bf16[128,256]{1,0:T(8,128)(2,1)S(1)}, u32[]{:S(2)}, u32[]{:S(2)}) collective-permute-start(bf16[128,256]{1,0:T(8,128)(2,1)S(1)} %get-tuple-element.84), channel_id=1, source_target_pairs={{0,4},{4,0},{8,12},{12,8},{1,5},{5,1},{9,13},{13,9},{2,6},{6,2},{1... | collective-permute-start | bytes 196616 | tf_op jit(solution)/shard_map/ppermute | solution.py:366
  17.2 1.3 %collective-permute-done.8.arrived = bf16[128,256]{1,0:T(8,128)(2,1)S(1)} collective-permute-done((bf16[128,256]{1,0:T(8,128)(2,1)S(1)}, bf16[128,256]{1,0:T(8,128)(2,1)S(1)}, u32[]{:S(2)}, u32[]{:S(2)}) %collective-permute-start.8) | collective-permute-done | bytes 65568 | tf_op jit(solution)/shard_map/ppermute | solution.py:366
  18.5 2.0 %collective-permute-start.9 = (bf16[128,256]{1,0:T(8,128)(2,1)S(1)}, bf16[128,256]{1,0:T(8,128)(2,1)S(1)}, u32[]{:S(2)}, u32[]{:S(2)}) collective-permute-start(bf16[128,256]{1,0:T(8,128)(2,1)S(1)} %get-tuple-element.86), channel_id=1, source_target_pairs={{0,8},{4,12},{8,0},{12,4},{1,9},{5,13},{9,1},{13,5},{2,10},{6,14},... | collective-permute-start | bytes 196616 | tf_op jit(solution)/shard_map/ppermute | solution.py:366
  21.4 2.3 %collective-permute-start.7 = (bf16[128,256]{1,0:T(8,128)(2,1)S(1)}, bf16[128,256]{1,0:T(8,128)(2,1)S(1)}, u32[]{:S(2)}, u32[]{:S(2)}) collective-permute-start(bf16[128,256]{1,0:T(8,128)(2,1)S(1)} %get-tuple-element.78), channel_id=1, source_target_pairs={{0,8},{4,12},{8,0},{12,4},{1,9},{5,13},{9,1},{13,5},{2,10},{6,14},... | collective-permute-start | bytes 196616 | tf_op jit(solution)/shard_map/ppermute | solution.py:366
  23.7 1.7 %collective-permute-done.9.refs_9_ = bf16[128,256]{1,0:T(8,128)(2,1)S(1)} collective-permute-done((bf16[128,256]{1,0:T(8,128)(2,1)S(1)}, bf16[128,256]{1,0:T(8,128)(2,1)S(1)}, u32[]{:S(2)}, u32[]{:S(2)}) %collective-permute-start.9) | collective-permute-done | bytes 65568 | tf_op jit(solution)/shard_map/ppermute | solution.py:366
  25.4 1.5 %shard_map.151 = (f32[32,128]{1,0:T(8,128)S(1)}, f32[32,128]{1,0:T(8,128)S(1)}, f32[512,128]{1,0:T(8,128)S(1)}, f32[128,128]{1,0:T(8,128)S(1)}, f32[128,128]{1,0...) custom-call(bf16[2,32,512]{2,1,0:T(8,128)(2,1)S(1)} %shard_map.145.refs_0_.refs_4_, ...), custom_call_target="tpu_custom_call" | custom-call | tf_op jit(solution)/shard_map/pallas_call | solution.py:348
  26.9 1.5 %shard_map.152 = (f32[2,32,128]{2,1,0:T(8,128)S(1)}, f32[32,128]{1,0:T(8,128)S(1)}, f32[512,128]{1,0:T(8,128)S(1)}, f32[384,512]{1,0:T(8,128)S(1)}, f32[512,256]...) custom-call(bf16[2,32,512]{2,1,0:T(8,128)(2,1)S(1)} %shard_map.145.r, ...), custom_call_target="tpu_custom_call" | custom-call | tf_op jit(solution)/shard_map/pallas_call | solution.py:348
  29.0 1.4 %collective-permute-done.14.arrived = bf16[192,512]{1,0:T(8,128)(2,1)S(1)} collective-permute-done((bf16[192,512]{1,0:T(8,128)(2,1)S(1)}, bf16[192,512]{1,0:T(8,128)(2,1)S(1)}, u32[]{:S(2)}, u32[]{:S(2)}) %collective-permute-start.14) | collective-permute-done | bytes 196640 | tf_op jit(solution)/shard_map/ppermute | solution.py:366
  30.4 1.3 %collective-permute-start.15 = (bf16[96,512]{1,0:T(8,128)(2,1)S(1)}, bf16[96,512]{1,0:T(8,128)(2,1)S(1)}, u32[]{:S(2)}, u32[]{:S(2)}) collective-permute-start(bf16[96,512]{1,0:T(8,128)(2,1)S(1)} %get-tuple-element.116), channel_id=1, source_target_pairs={{0,2},{1,3},{2,0},{3,1},{4,6},{5,7},{6,4},{7,5},{8,10},{9,11},{10,... | collective-permute-start | bytes 294920 | tf_op jit(solution)/shard_map/ppermute | solution.py:366
  33.5 2.0 %collective-permute-done.15.arrived = bf16[96,512]{1,0:T(8,128)(2,1)S(1)} collective-permute-done((bf16[96,512]{1,0:T(8,128)(2,1)S(1)}, bf16[96,512]{1,0:T(8,128)(2,1)S(1)}, u32[]{:S(2)}, u32[]{:S(2)}) %collective-permute-start.15) | collective-permute-done | bytes 98336 | tf_op jit(solution)/shard_map/ppermute | solution.py:366
  35.5 1.6 %collective-permute-start.16 = (bf16[96,512]{1,0:T(8,128)(2,1)S(1)}, bf16[96,512]{1,0:T(8,128)(2,1)S(1)}, u32[]{:S(2)}, u32[]{:S(2)}) collective-permute-start(bf16[96,512]{1,0:T(8,128)(2,1)S(1)} %get-tuple-element.118), channel_id=1, source_target_pairs={{0,4},{4,0},{8,12},{12,8},{1,5},{5,1},{9,13},{13,9},{2,6},{6,2},{1... | collective-permute-start | bytes 294920 | tf_op jit(solution)/shard_map/ppermute | solution.py:366
  37.1 1.4 %collective-permute-done.11.arrived = bf16[144,512]{1,0:T(8,128)(2,1)S(1)} collective-permute-done((bf16[144,512]{1,0:T(8,128)(2,1)S(1)}, bf16[144,512]{1,0:T(8,128)(2,1)S(1)}, u32[]{:S(2)}, u32[]{:S(2)}) %collective-permute-start.11) | collective-permute-done | bytes 147488 | tf_op jit(solution)/shard_map/ppermute | solution.py:366
  38.5 1.3 %collective-permute-start.12 = (bf16[96,512]{1,0:T(8,128)(2,1)S(1)}, bf16[96,512]{1,0:T(8,128)(2,1)S(1)}, u32[]{:S(2)}, u32[]{:S(2)}) collective-permute-start(bf16[96,512]{1,0:T(8,128)(2,1)S(1)} %get-tuple-element.109), channel_id=1, source_target_pairs={{0,4},{4,0},{8,12},{12,8},{1,5},{5,1},{9,13},{13,9},{2,6},{6,2},{1... | collective-permute-start | bytes 294920 | tf_op jit(solution)/shard_map/ppermute | solution.py:366
  40.2 2.2 %collective-permute-start.17 = (bf16[96,512]{1,0:T(8,128)(2,1)S(1)}, bf16[96,512]{1,0:T(8,128)(2,1)S(1)}, u32[]{:S(2)}, u32[]{:S(2)}) collective-permute-start(bf16[96,512]{1,0:T(8,128)(2,1)S(1)} %get-tuple-element.120), channel_id=1, source_target_pairs={{0,8},{4,12},{8,0},{12,4},{1,9},{5,13},{9,1},{13,5},{2,10},{6,14},... | collective-permute-start | bytes 294920 | tf_op jit(solution)/shard_map/ppermute | solution.py:366
  43.7 2.0 %collective-permute-start.13 = (bf16[80,512]{1,0:T(8,128)(2,1)S(1)}, bf16[80,512]{1,0:T(8,128)(2,1)S(1)}, u32[]{:S(2)}, u32[]{:S(2)}) collective-permute-start(bf16[80,512]{1,0:T(8,128)(2,1)S(1)} %get-tuple-element.112), channel_id=1, source_target_pairs={{0,8},{4,12},{8,0},{12,4},{1,9},{5,13},{9,1},{13,5},{2,10},{6,14},... | collective-permute-start | bytes 245768 | tf_op jit(solution)/shard_map/ppermute | solution.py:366
  45.6 1.5 %collective-permute-start.19 = (bf16[64,512]{1,0:T(8,128)(2,1)S(1)}, bf16[64,512]{1,0:T(8,128)(2,1)S(1)}, u32[]{:S(2)}, u32[]{:S(2)}) collective-permute-start(bf16[64,512]{1,0:T(8,128)(2,1)S(1)} %get-tuple-element.122.refs_2_), channel_id=1, source_target_pairs={{0,2},{1,3},{2,0},{3,1},{4,6},{5,7},{6,4},{7,5},{8,10},{9,11},{10,... | collective-permute-start | bytes 196616 | tf_op jit(solution)/shard_map/ppermute | solution.py:366
  47.1 1.5 %collective-permute-done.17.arrived = bf16[96,512]{1,0:T(8,128)(2,1)S(1)} collective-permute-done((bf16[96,512]{1,0:T(8,128)(2,1)S(1)}, bf16[96,512]{1,0:T(8,128)(2,1)S(1)}, u32[]{:S(2)}, u32[]{:S(2)}) %collective-permute-start.17) | collective-permute-done | bytes 98336 | tf_op jit(solution)/shard_map/ppermute | solution.py:366
  48.7 1.6 %collective-permute-start.18 = (bf16[96,512]{1,0:T(8,128)(2,1)S(1)}, bf16[96,512]{1,0:T(8,128)(2,1)S(1)}, u32[]{:S(2)}, u32[]{:S(2)}) collective-permute-start(bf16[96,512]{1,0:T(8,128)(2,1)S(1)} %shard_map.160.refs_0_), channel_id=1, source_target_pairs={{0,2},{1,3},{2,0},{3,1},{4,6},{5,7},{6,4},{7,5},{8,10},{9,11},{10,... | collective-permute-start | bytes 294920 | tf_op jit(solution)/shard_map/ppermute | solution.py:366
  50.4 1.6 %collective-permute-start.20 = (bf16[64,512]{1,0:T(8,128)(2,1)S(1)}, bf16[64,512]{1,0:T(8,128)(2,1)S(1)}, u32[]{:S(2)}, u32[]{:S(2)}) collective-permute-start(bf16[64,512]{1,0:T(8,128)(2,1)S(1)} %get-tuple-element.123.refs_1_), channel_id=1, source_target_pairs={{0,2},{1,3},{2,0},{3,1},{4,6},{5,7},{6,4},{7,5},{8,10},{9,11},{10,... | collective-permute-start | bytes 196616 | tf_op jit(solution)/shard_map/ppermute | solution.py:366
  52.0 1.3 %collective-permute-done.18.refs_0_ = bf16[96,512]{1,0:T(8,128)(2,1)S(1)} collective-permute-done((bf16[96,512]{1,0:T(8,128)(2,1)S(1)}, bf16[96,512]{1,0:T(8,128)(2,1)S(1)}, u32[]{:S(2)}, u32[]{:S(2)}) %collective-permute-start.18) | collective-permute-done | bytes 98336 | tf_op jit(solution)/shard_map/ppermute | solution.py:366
  (49 shorter events, 13.6 us)
Async XLA Ops:
  1.5 11.5 %collective-permute-start.5 = (bf16[2,32,512]{2,1,0:T(8,128)(2,1)S(1)}, bf16[2,32,512]{2,1,0:T(8,128)(2,1)S(1)}, u32[]{:S(2)}, u32[]{:S(2)}) collective-permute-start(bf16[2,32,512]{2,1,0:T(8,128)(2,1)S(1)} %shard_map.145.refs_0_.refs_4_), channel_id=1, source_target_pairs={{0,12},{4,8},{8,4},{12,0},{1,13},{5,9},{9,5},{13,1},{2,14},{6,10},... | collective-permute-start | bytes 196616 | tf_op jit(solution)/shard_map/ppermute | solution.py:366
  6.6 6.4 %collective-permute-start.4 = (bf16[2,32,512]{2,1,0:T(8,128)(2,1)S(1)}, bf16[2,32,512]{2,1,0:T(8,128)(2,1)S(1)}, u32[]{:S(2)}, u32[]{:S(2)}) collective-permute-start(bf16[2,32,512]{2,1,0:T(8,128)(2,1)S(1)} %shard_map.145.refs_0_.refs_4_), channel_id=1, source_target_pairs={{0,8},{4,12},{8,0},{12,4},{1,9},{5,13},{9,1},{13,5},{2,10},{6,14},... | collective-permute-start | bytes 196616 | tf_op jit(solution)/shard_map/ppermute | solution.py:366
  6.6 6.4 %collective-permute-start.3 = (bf16[2,32,512]{2,1,0:T(8,128)(2,1)S(1)}, bf16[2,32,512]{2,1,0:T(8,128)(2,1)S(1)}, u32[]{:S(2)}, u32[]{:S(2)}) collective-permute-start(bf16[2,32,512]{2,1,0:T(8,128)(2,1)S(1)} %shard_map.145.refs_0_.refs_4_), channel_id=1, source_target_pairs={{0,4},{4,0},{8,12},{12,8},{1,5},{5,1},{9,13},{13,9},{2,6},{6,2},{1... | collective-permute-start | bytes 196616 | tf_op jit(solution)/shard_map/ppermute | solution.py:366
  7.2 5.3 %collective-permute-start.2 = (bf16[2,32,128]{2,1,0:T(8,128)(2,1)}, bf16[2,32,128]{2,1,0:T(8,128)(2,1)S(1)}, u32[]{:S(2)}, u32[]{:S(2)}) collective-permute-start(bf16[2,32,128]{2,1,0:T(8,128)(2,1)} %state.1), channel_id=1, source_target_pairs={{0,3},{1,2},{2,1},{3,0},{4,7},{5,6},{6,5},{7,4},{8,11},{9,10},{10,... | collective-permute-start | bytes 49160 | tf_op jit(solution)/shard_map/ppermute | solution.py:366
  9.0 4.0 %collective-permute-start.1 = (bf16[2,32,128]{2,1,0:T(8,128)(2,1)}, bf16[2,32,128]{2,1,0:T(8,128)(2,1)S(1)}, u32[]{:S(2)}, u32[]{:S(2)}) collective-permute-start(bf16[2,32,128]{2,1,0:T(8,128)(2,1)} %state.1), channel_id=1, source_target_pairs={{0,2},{1,3},{2,0},{3,1},{4,6},{5,7},{6,4},{7,5},{8,10},{9,11},{10,... | collective-permute-start | bytes 49160 | tf_op jit(solution)/shard_map/ppermute | solution.py:366
  14.0 4.5 %collective-permute-start.8 = (bf16[128,256]{1,0:T(8,128)(2,1)S(1)}, bf16[128,256]{1,0:T(8,128)(2,1)S(1)}, u32[]{:S(2)}, u32[]{:S(2)}) collective-permute-start(bf16[128,256]{1,0:T(8,128)(2,1)S(1)} %get-tuple-element.84), channel_id=1, source_target_pairs={{0,4},{4,0},{8,12},{12,8},{1,5},{5,1},{9,13},{13,9},{2,6},{6,2},{1... | collective-permute-start | bytes 196616 | tf_op jit(solution)/shard_map/ppermute | solution.py:366
  16.3 5.0 %collective-permute-start.6 = (bf16[128,256]{1,0:T(8,128)(2,1)S(1)}, bf16[128,256]{1,0:T(8,128)(2,1)S(1)}, u32[]{:S(2)}, u32[]{:S(2)}) collective-permute-start(bf16[128,256]{1,0:T(8,128)(2,1)S(1)} %get-tuple-element.76), channel_id=1, source_target_pairs={{0,4},{4,0},{8,12},{12,8},{1,5},{5,1},{9,13},{13,9},{2,6},{6,2},{1... | collective-permute-start | bytes 196616 | tf_op jit(solution)/shard_map/ppermute | solution.py:366
  18.5 6.9 %collective-permute-start.9 = (bf16[128,256]{1,0:T(8,128)(2,1)S(1)}, bf16[128,256]{1,0:T(8,128)(2,1)S(1)}, u32[]{:S(2)}, u32[]{:S(2)}) collective-permute-start(bf16[128,256]{1,0:T(8,128)(2,1)S(1)} %get-tuple-element.86), channel_id=1, source_target_pairs={{0,8},{4,12},{8,0},{12,4},{1,9},{5,13},{9,1},{13,5},{2,10},{6,14},... | collective-permute-start | bytes 196616 | tf_op jit(solution)/shard_map/ppermute | solution.py:366
  21.4 5.5 %collective-permute-start.7 = (bf16[128,256]{1,0:T(8,128)(2,1)S(1)}, bf16[128,256]{1,0:T(8,128)(2,1)S(1)}, u32[]{:S(2)}, u32[]{:S(2)}) collective-permute-start(bf16[128,256]{1,0:T(8,128)(2,1)S(1)} %get-tuple-element.78), channel_id=1, source_target_pairs={{0,8},{4,12},{8,0},{12,4},{1,9},{5,13},{9,1},{13,5},{2,10},{6,14},... | collective-permute-start | bytes 196616 | tf_op jit(solution)/shard_map/ppermute | solution.py:366
  28.4 4.1 %collective-permute-start.10 = (bf16[288,512]{1,0:T(8,128)(2,1)S(1)}, bf16[288,512]{1,0:T(8,128)(2,1)S(1)}, u32[]{:S(2)}, u32[]{:S(2)}) collective-permute-start(bf16[288,512]{1,0:T(8,128)(2,1)S(1)} %get-tuple-element.99), channel_id=1, source_target_pairs={{0,1},{1,0},{2,3},{3,2},{4,5},{5,4},{6,7},{7,6},{8,9},{9,8},{10,11... | collective-permute-start | bytes 884744 | tf_op jit(solution)/shard_map/ppermute | solution.py:366
  28.5 1.9 %collective-permute-start.14 = (bf16[192,512]{1,0:T(8,128)(2,1)S(1)}, bf16[192,512]{1,0:T(8,128)(2,1)S(1)}, u32[]{:S(2)}, u32[]{:S(2)}) collective-permute-start(bf16[192,512]{1,0:T(8,128)(2,1)S(1)} %get-tuple-element.114), channel_id=1, source_target_pairs={{0,1},{1,0},{2,3},{3,2},{4,5},{5,4},{6,7},{7,6},{8,9},{9,8},{10,11... | collective-permute-start | bytes 589832 | tf_op jit(solution)/shard_map/ppermute | solution.py:366
  30.4 5.1 %collective-permute-start.15 = (bf16[96,512]{1,0:T(8,128)(2,1)S(1)}, bf16[96,512]{1,0:T(8,128)(2,1)S(1)}, u32[]{:S(2)}, u32[]{:S(2)}) collective-permute-start(bf16[96,512]{1,0:T(8,128)(2,1)S(1)} %get-tuple-element.116), channel_id=1, source_target_pairs={{0,2},{1,3},{2,0},{3,1},{4,6},{5,7},{6,4},{7,5},{8,10},{9,11},{10,... | collective-permute-start | bytes 294920 | tf_op jit(solution)/shard_map/ppermute | solution.py:366
  32.6 5.9 %collective-permute-start.11 = (bf16[144,512]{1,0:T(8,128)(2,1)S(1)}, bf16[144,512]{1,0:T(8,128)(2,1)S(1)}, u32[]{:S(2)}, u32[]{:S(2)}) collective-permute-start(bf16[144,512]{1,0:T(8,128)(2,1)S(1)} %get-tuple-element.106), channel_id=1, source_target_pairs={{0,2},{1,3},{2,0},{3,1},{4,6},{5,7},{6,4},{7,5},{8,10},{9,11},{10,... | collective-permute-start | bytes 442376 | tf_op jit(solution)/shard_map/ppermute | solution.py:366
  35.5 4.7 %collective-permute-start.16 = (bf16[96,512]{1,0:T(8,128)(2,1)S(1)}, bf16[96,512]{1,0:T(8,128)(2,1)S(1)}, u32[]{:S(2)}, u32[]{:S(2)}) collective-permute-start(bf16[96,512]{1,0:T(8,128)(2,1)S(1)} %get-tuple-element.118), channel_id=1, source_target_pairs={{0,4},{4,0},{8,12},{12,8},{1,5},{5,1},{9,13},{13,9},{2,6},{6,2},{1... | collective-permute-start | bytes 294920 | tf_op jit(solution)/shard_map/ppermute | solution.py:366
  38.5 5.1 %collective-permute-start.12 = (bf16[96,512]{1,0:T(8,128)(2,1)S(1)}, bf16[96,512]{1,0:T(8,128)(2,1)S(1)}, u32[]{:S(2)}, u32[]{:S(2)}) collective-permute-start(bf16[96,512]{1,0:T(8,128)(2,1)S(1)} %get-tuple-element.109), channel_id=1, source_target_pairs={{0,4},{4,0},{8,12},{12,8},{1,5},{5,1},{9,13},{13,9},{2,6},{6,2},{1... | collective-permute-start | bytes 294920 | tf_op jit(solution)/shard_map/ppermute | solution.py:366
  40.2 8.4 %collective-permute-start.17 = (bf16[96,512]{1,0:T(8,128)(2,1)S(1)}, bf16[96,512]{1,0:T(8,128)(2,1)S(1)}, u32[]{:S(2)}, u32[]{:S(2)}) collective-permute-start(bf16[96,512]{1,0:T(8,128)(2,1)S(1)} %get-tuple-element.120), channel_id=1, source_target_pairs={{0,8},{4,12},{8,0},{12,4},{1,9},{5,13},{9,1},{13,5},{2,10},{6,14},... | collective-permute-start | bytes 294920 | tf_op jit(solution)/shard_map/ppermute | solution.py:366
  43.7 6.7 %collective-permute-start.13 = (bf16[80,512]{1,0:T(8,128)(2,1)S(1)}, bf16[80,512]{1,0:T(8,128)(2,1)S(1)}, u32[]{:S(2)}, u32[]{:S(2)}) collective-permute-start(bf16[80,512]{1,0:T(8,128)(2,1)S(1)} %get-tuple-element.112), channel_id=1, source_target_pairs={{0,8},{4,12},{8,0},{12,4},{1,9},{5,13},{9,1},{13,5},{2,10},{6,14},... | collective-permute-start | bytes 245768 | tf_op jit(solution)/shard_map/ppermute | solution.py:366
  45.6 4.6 %collective-permute-start.19 = (bf16[64,512]{1,0:T(8,128)(2,1)S(1)}, bf16[64,512]{1,0:T(8,128)(2,1)S(1)}, u32[]{:S(2)}, u32[]{:S(2)}) collective-permute-start(bf16[64,512]{1,0:T(8,128)(2,1)S(1)} %get-tuple-element.122.refs_2_), channel_id=1, source_target_pairs={{0,2},{1,3},{2,0},{3,1},{4,6},{5,7},{6,4},{7,5},{8,10},{9,11},{10,... | collective-permute-start | bytes 196616 | tf_op jit(solution)/shard_map/ppermute | solution.py:366
  48.7 4.7 %collective-permute-start.18 = (bf16[96,512]{1,0:T(8,128)(2,1)S(1)}, bf16[96,512]{1,0:T(8,128)(2,1)S(1)}, u32[]{:S(2)}, u32[]{:S(2)}) collective-permute-start(bf16[96,512]{1,0:T(8,128)(2,1)S(1)} %shard_map.160.refs_0_), channel_id=1, source_target_pairs={{0,2},{1,3},{2,0},{3,1},{4,6},{5,7},{6,4},{7,5},{8,10},{9,11},{10,... | collective-permute-start | bytes 294920 | tf_op jit(solution)/shard_map/ppermute | solution.py:366
  50.3 3.6 %collective-permute-start.26 = (bf16[64,512]{1,0:T(8,128)(2,1)S(1)}, bf16[64,512]{1,0:T(8,128)(2,1)S(1)}, u32[]{:S(2)}, u32[]{:S(2)}) collective-permute-start(bf16[64,512]{1,0:T(8,128)(2,1)S(1)} %get-tuple-element.122.refs_2_), channel_id=1, source_target_pairs={{0,1},{1,0},{2,3},{3,2},{4,5},{5,4},{6,7},{7,6},{8,9},{9,8},{10,11... | collective-permute-start | bytes 196616 | tf_op jit(solution)/shard_map/ppermute | solution.py:366
  50.4 4.4 %collective-permute-start.20 = (bf16[64,512]{1,0:T(8,128)(2,1)S(1)}, bf16[64,512]{1,0:T(8,128)(2,1)S(1)}, u32[]{:S(2)}, u32[]{:S(2)}) collective-permute-start(bf16[64,512]{1,0:T(8,128)(2,1)S(1)} %get-tuple-element.123.refs_1_), channel_id=1, source_target_pairs={{0,2},{1,3},{2,0},{3,1},{4,6},{5,7},{6,4},{7,5},{8,10},{9,11},{10,... | collective-permute-start | bytes 196616 | tf_op jit(solution)/shard_map/ppermute | solution.py:366
  52.0 2.9 %collective-permute-start.24 = (bf16[96,512]{1,0:T(8,128)(2,1)S(1)}, bf16[96,512]{1,0:T(8,128)(2,1)S(1)}, u32[]{:S(2)}, u32[]{:S(2)}) collective-permute-start(bf16[96,512]{1,0:T(8,128)(2,1)S(1)} %shard_map.160.refs_0_), channel_id=1, source_target_pairs={{0,1},{1,0},{2,3},{3,2},{4,5},{5,4},{6,7},{7,6},{8,9},{9,8},{10,11... | collective-permute-start | bytes 294920 | tf_op jit(solution)/shard_map/ppermute | solution.py:366
  53.3 2.5 %collective-permute-start.21 = (bf16[96,512]{1,0:T(8,128)(2,1)S(1)}, bf16[96,512]{1,0:T(8,128)(2,1)S(1)}, u32[]{:S(2)}, u32[]{:S(2)}) collective-permute-start(bf16[96,512]{1,0:T(8,128)(2,1)S(1)} %collective-permute-done.18.refs_0_), channel_id=1, source_target_pairs={{0,1},{1,0},{2,3},{3,2},{4,5},{5,4},{6,7},{7,6},{8,9},{9,8},{10,11... | collective-permute-start | bytes 294920 | tf_op jit(solution)/shard_map/ppermute | solution.py:366
  53.9 2.0 %collective-permute-start.23 = (bf16[64,512]{1,0:T(8,128)(2,1)S(1)}, bf16[64,512]{1,0:T(8,128)(2,1)S(1)}, u32[]{:S(2)}, u32[]{:S(2)}) collective-permute-start(bf16[64,512]{1,0:T(8,128)(2,1)S(1)} %get-tuple-element.124.refs_2_), channel_id=1, source_target_pairs={{0,1},{1,0},{2,3},{3,2},{4,5},{5,4},{6,7},{7,6},{8,9},{9,8},{10,11... | collective-permute-start | bytes 196616 | tf_op jit(solution)/shard_map/ppermute | solution.py:366
  (3 other events, 4.5 us)

commit v8 on v7

--- a/solution.py
+++ b/solution.py
@@ -322,15 +322,15 @@
 
 
 def first_shares_kernel(*refs):
-    copies = put_shares((0, 1), (refs[:3], refs[3:6]), refs[6:9], refs[9:])
+    copies = put_shares((0, 1, 2), (refs[:3], refs[3:6], refs[6:9]), refs[9:12], refs[12:])
     for copy in copies:
         copy.wait()
 
 
 def last_shares_kernel(state_own, nodes, arrived_1, arrived_2, *refs):
-    shares, outs, scratch = refs[:6], refs[9:13], refs[13:]
+    shares, outs, scratch = refs[:3], refs[6:10], refs[10:]
     *held, state_held, state_sem = scratch
-    copies = put_shares((2, 3), (shares[:3], shares[3:]), outs[1:], held)
+    copies = put_shares((3,), (shares,), outs[1:], held)
     half = nodes.shape[0]
     part = arrived_2.shape[0] - half
     add_nodes(
@@ -499,23 +499,26 @@
     own = [share_a, share_b, node_share]
     across = [swap(share_a, "dst", 2), swap(share_b, "dst", 2), node_across]
     outs = [(edge_w1.shape, F32), (edge_w2.shape, F32), (node_w1.shape, F32)]
-    held = [((2, value.shape[0] // WAYS, value.shape[1]), F32) for value in (edge_w1, edge_w2, node_w1)]
-    held.append(pltpu.SemaphoreType.DMA((6,)))
+
+    def held(count):
+        shapes = [((count, value.shape[0] // WAYS, value.shape[1]), F32) for value in (edge_w1, edge_w2, node_w1)]
+        return shapes + [pltpu.SemaphoreType.DMA((3 * count,))]
+
     grads = call(
         first_shares_kernel,
         outs,
-        held,
-        own + [swap(share, "dst", 1) for share in own],
+        held(WAYS - 1),
+        own + [swap(share, "dst", 1) for share in own] + across,
         out_spaces=[pltpu.HBM] * 3,
     )
     grad_state, grad_first, grad_second, grad_node = call(
         last_shares_kernel,
         [state] + outs,
-        held + [state, pltpu.SemaphoreType.DMA],
-        [state_own, nodes_sum, arrived_1, arrived_2] + across + [swap(share, "dst", 1) for share in across] + list(grads),
-        [pltpu.VMEM] * 10 + [pltpu.HBM] * 3,
+        held(1) + [state, pltpu.SemaphoreType.DMA],
+        [state_own, nodes_sum, arrived_1, arrived_2] + [swap(share, "dst", 1) for share in across] + list(grads),
+        [pltpu.VMEM] * 7 + [pltpu.HBM] * 3,
         [pltpu.HBM] * 4,
-        {10: 1, 11: 2, 12: 3},
+        {7: 1, 8: 2, 9: 3},
     )
     return grad_state, grad_forcing, edges[:, None, None], grad_first, grad_second, grad_node
 

time: 57.4 us -> 57.2 us (level)
  no operation moved by 1% of the time
where the time goes in v8:
time: 57.2 us; the launch traced here: 56.9 us
  starting transfers between devices  30.3 us (53%)
  waiting for transfers between devices  14.6 us (26%)
  Pallas kernels  10.6 us (19%)
  between operations  1.45 us (3%)
    ppermute x27, starting transfers between devices, swap(): return lax.ppermute(value, axis, [(i, i ^ k) for i in range(WAYS)])  30.3 us
    ppermute x27, waiting for transfers between devices, swap(): return lax.ppermute(value, axis, [(i, i ^ k) for i in range(WAYS)])  14.6 us
    pallas_call x19, Pallas kernels, call(): pl.pallas_call(kernel, out_shape=[jax.ShapeDtypeStruct(shape, dtype) for...  10.6 us
  transfers between devices with their start and end apart: 27, of which 14 were waited for; matrix products, arithmetic and copies ran while one was open for 0% of the time, Pallas kernels for 11%

profile of v8, /device:TPU:0, one launch (start us, length us, event | category | flops | bytes accessed | tf_op | source)
XLA Modules:
  0.0 56.9 jit_solution(8019255284609362287)
XLA Ops:
  1.5 5.1 %collective-permute-start.5 = (bf16[2,32,512]{2,1,0:T(8,128)(2,1)S(1)}, bf16[2,32,512]{2,1,0:T(8,128)(2,1)S(1)}, u32[]{:S(2)}, u32[]{:S(2)}) collective-permute-start(bf16[2,32,512]{2,1,0:T(8,128)(2,1)S(1)} %shard_map.145.refs_0_.refs_4_), channel_id=1, source_target_pairs={{0,12},{4,8},{8,4},{12,0},{1,13},{5,9},{9,5},{13,1},{2,14},{6,10},... | collective-permute-start | bytes 196616 | tf_op jit(solution)/shard_map/ppermute | solution.py:366
  7.2 1.7 %collective-permute-start.2 = (bf16[2,32,128]{2,1,0:T(8,128)(2,1)}, bf16[2,32,128]{2,1,0:T(8,128)(2,1)S(1)}, u32[]{:S(2)}, u32[]{:S(2)}) collective-permute-start(bf16[2,32,128]{2,1,0:T(8,128)(2,1)} %state.1), channel_id=1, source_target_pairs={{0,3},{1,2},{2,1},{3,0},{4,7},{5,6},{6,5},{7,4},{8,11},{9,10},{10,... | collective-permute-start | bytes 49160 | tf_op jit(solution)/shard_map/ppermute | solution.py:366
  9.0 1.3 %collective-permute-start.1 = (bf16[2,32,128]{2,1,0:T(8,128)(2,1)}, bf16[2,32,128]{2,1,0:T(8,128)(2,1)S(1)}, u32[]{:S(2)}, u32[]{:S(2)}) collective-permute-start(bf16[2,32,128]{2,1,0:T(8,128)(2,1)} %state.1), channel_id=1, source_target_pairs={{0,2},{1,3},{2,0},{3,1},{4,6},{5,7},{6,4},{7,5},{8,10},{9,11},{10,... | collective-permute-start | bytes 49160 | tf_op jit(solution)/shard_map/ppermute | solution.py:366
  10.9 1.6 %shard_map.146 = (bf16[2,512,128]{2,1,0:T(8,128)(2,1)S(1)}, bf16[384,512]{1,0:T(8,128)(2,1)S(1)}, bf16[512,256]{1,0:T(8,128)(2,1)S(1)}, bf16[512,256]{1,0:T(8,12...) custom-call(s32[1,1]{1,0:T(1,128)S(6)} %copy.23.count, ...), custom_call_target="tpu_custom_call" | custom-call | tf_op jit(solution)/shard_map/pallas_call | solution.py:348
  14.0 1.3 %collective-permute-start.8 = (bf16[128,256]{1,0:T(8,128)(2,1)S(1)}, bf16[128,256]{1,0:T(8,128)(2,1)S(1)}, u32[]{:S(2)}, u32[]{:S(2)}) collective-permute-start(bf16[128,256]{1,0:T(8,128)(2,1)S(1)} %get-tuple-element.84), channel_id=1, source_target_pairs={{0,4},{4,0},{8,12},{12,8},{1,5},{5,1},{9,13},{13,9},{2,6},{6,2},{1... | collective-permute-start | bytes 196616 | tf_op jit(solution)/shard_map/ppermute | solution.py:366
  17.2 1.3 %collective-permute-done.8.arrived = bf16[128,256]{1,0:T(8,128)(2,1)S(1)} collective-permute-done((bf16[128,256]{1,0:T(8,128)(2,1)S(1)}, bf16[128,256]{1,0:T(8,128)(2,1)S(1)}, u32[]{:S(2)}, u32[]{:S(2)}) %collective-permute-start.8) | collective-permute-done | bytes 65568 | tf_op jit(solution)/shard_map/ppermute | solution.py:366
  18.5 2.0 %collective-permute-start.9 = (bf16[128,256]{1,0:T(8,128)(2,1)S(1)}, bf16[128,256]{1,0:T(8,128)(2,1)S(1)}, u32[]{:S(2)}, u32[]{:S(2)}) collective-permute-start(bf16[128,256]{1,0:T(8,128)(2,1)S(1)} %get-tuple-element.86), channel_id=1, source_target_pairs={{0,8},{4,12},{8,0},{12,4},{1,9},{5,13},{9,1},{13,5},{2,10},{6,14},... | collective-permute-start | bytes 196616 | tf_op jit(solution)/shard_map/ppermute | solution.py:366
  21.4 2.3 %collective-permute-start.7 = (bf16[128,256]{1,0:T(8,128)(2,1)S(1)}, bf16[128,256]{1,0:T(8,128)(2,1)S(1)}, u32[]{:S(2)}, u32[]{:S(2)}) collective-permute-start(bf16[128,256]{1,0:T(8,128)(2,1)S(1)} %get-tuple-element.78), channel_id=1, source_target_pairs={{0,8},{4,12},{8,0},{12,4},{1,9},{5,13},{9,1},{13,5},{2,10},{6,14},... | collective-permute-start | bytes 196616 | tf_op jit(solution)/shard_map/ppermute | solution.py:366
  23.7 1.7 %collective-permute-done.9.refs_9_ = bf16[128,256]{1,0:T(8,128)(2,1)S(1)} collective-permute-done((bf16[128,256]{1,0:T(8,128)(2,1)S(1)}, bf16[128,256]{1,0:T(8,128)(2,1)S(1)}, u32[]{:S(2)}, u32[]{:S(2)}) %collective-permute-start.9) | collective-permute-done | bytes 65568 | tf_op jit(solution)/shard_map/ppermute | solution.py:366
  25.4 1.5 %shard_map.151 = (f32[32,128]{1,0:T(8,128)S(1)}, f32[32,128]{1,0:T(8,128)S(1)}, f32[512,128]{1,0:T(8,128)S(1)}, f32[128,128]{1,0:T(8,128)S(1)}, f32[128,128]{1,0...) custom-call(bf16[2,32,512]{2,1,0:T(8,128)(2,1)S(1)} %shard_map.145.refs_0_.refs_4_, ...), custom_call_target="tpu_custom_call" | custom-call | tf_op jit(solution)/shard_map/pallas_call | solution.py:348
  26.9 1.5 %shard_map.152 = (f32[2,32,128]{2,1,0:T(8,128)S(1)}, f32[32,128]{1,0:T(8,128)S(1)}, f32[512,128]{1,0:T(8,128)S(1)}, f32[384,512]{1,0:T(8,128)S(1)}, f32[512,256]...) custom-call(bf16[2,32,512]{2,1,0:T(8,128)(2,1)S(1)} %shard_map.145.r, ...), custom_call_target="tpu_custom_call" | custom-call | tf_op jit(solution)/shard_map/pallas_call | solution.py:348
  29.0 1.4 %collective-permute-done.14.arrived = bf16[192,512]{1,0:T(8,128)(2,1)S(1)} collective-permute-done((bf16[192,512]{1,0:T(8,128)(2,1)S(1)}, bf16[192,512]{1,0:T(8,128)(2,1)S(1)}, u32[]{:S(2)}, u32[]{:S(2)}) %collective-permute-start.14) | collective-permute-done | bytes 196640 | tf_op jit(solution)/shard_map/ppermute | solution.py:366
  30.4 1.3 %collective-permute-start.15 = (bf16[96,512]{1,0:T(8,128)(2,1)S(1)}, bf16[96,512]{1,0:T(8,128)(2,1)S(1)}, u32[]{:S(2)}, u32[]{:S(2)}) collective-permute-start(bf16[96,512]{1,0:T(8,128)(2,1)S(1)} %get-tuple-element.116), channel_id=1, source_target_pairs={{0,2},{1,3},{2,0},{3,1},{4,6},{5,7},{6,4},{7,5},{8,10},{9,11},{10,... | collective-permute-start | bytes 294920 | tf_op jit(solution)/shard_map/ppermute | solution.py:366
  33.5 2.0 %collective-permute-done.15.arrived = bf16[96,512]{1,0:T(8,128)(2,1)S(1)} collective-permute-done((bf16[96,512]{1,0:T(8,128)(2,1)S(1)}, bf16[96,512]{1,0:T(8,128)(2,1)S(1)}, u32[]{:S(2)}, u32[]{:S(2)}) %collective-permute-start.15) | collective-permute-done | bytes 98336 | tf_op jit(solution)/shard_map/ppermute | solution.py:366
  35.5 1.6 %collective-permute-start.16 = (bf16[96,512]{1,0:T(8,128)(2,1)S(1)}, bf16[96,512]{1,0:T(8,128)(2,1)S(1)}, u32[]{:S(2)}, u32[]{:S(2)}) collective-permute-start(bf16[96,512]{1,0:T(8,128)(2,1)S(1)} %get-tuple-element.118), channel_id=1, source_target_pairs={{0,4},{4,0},{8,12},{12,8},{1,5},{5,1},{9,13},{13,9},{2,6},{6,2},{1... | collective-permute-start | bytes 294920 | tf_op jit(solution)/shard_map/ppermute | solution.py:366
  37.1 1.4 %collective-permute-done.11.arrived = bf16[144,512]{1,0:T(8,128)(2,1)S(1)} collective-permute-done((bf16[144,512]{1,0:T(8,128)(2,1)S(1)}, bf16[144,512]{1,0:T(8,128)(2,1)S(1)}, u32[]{:S(2)}, u32[]{:S(2)}) %collective-permute-start.11) | collective-permute-done | bytes 147488 | tf_op jit(solution)/shard_map/ppermute | solution.py:366
  38.5 1.3 %collective-permute-start.12 = (bf16[96,512]{1,0:T(8,128)(2,1)S(1)}, bf16[96,512]{1,0:T(8,128)(2,1)S(1)}, u32[]{:S(2)}, u32[]{:S(2)}) collective-permute-start(bf16[96,512]{1,0:T(8,128)(2,1)S(1)} %get-tuple-element.109), channel_id=1, source_target_pairs={{0,4},{4,0},{8,12},{12,8},{1,5},{5,1},{9,13},{13,9},{2,6},{6,2},{1... | collective-permute-start | bytes 294920 | tf_op jit(solution)/shard_map/ppermute | solution.py:366
  40.2 2.2 %collective-permute-start.17 = (bf16[96,512]{1,0:T(8,128)(2,1)S(1)}, bf16[96,512]{1,0:T(8,128)(2,1)S(1)}, u32[]{:S(2)}, u32[]{:S(2)}) collective-permute-start(bf16[96,512]{1,0:T(8,128)(2,1)S(1)} %get-tuple-element.120), channel_id=1, source_target_pairs={{0,8},{4,12},{8,0},{12,4},{1,9},{5,13},{9,1},{13,5},{2,10},{6,14},... | collective-permute-start | bytes 294920 | tf_op jit(solution)/shard_map/ppermute | solution.py:366
  43.7 2.0 %collective-permute-start.13 = (bf16[80,512]{1,0:T(8,128)(2,1)S(1)}, bf16[80,512]{1,0:T(8,128)(2,1)S(1)}, u32[]{:S(2)}, u32[]{:S(2)}) collective-permute-start(bf16[80,512]{1,0:T(8,128)(2,1)S(1)} %get-tuple-element.112), channel_id=1, source_target_pairs={{0,8},{4,12},{8,0},{12,4},{1,9},{5,13},{9,1},{13,5},{2,10},{6,14},... | collective-permute-start | bytes 245768 | tf_op jit(solution)/shard_map/ppermute | solution.py:366
  45.6 1.5 %collective-permute-start.20 = (bf16[64,512]{1,0:T(8,128)(2,1)S(1)}, bf16[64,512]{1,0:T(8,128)(2,1)S(1)}, u32[]{:S(2)}, u32[]{:S(2)}) collective-permute-start(bf16[64,512]{1,0:T(8,128)(2,1)S(1)} %get-tuple-element.122.refs_2_), channel_id=1, source_target_pairs={{0,2},{1,3},{2,0},{3,1},{4,6},{5,7},{6,4},{7,5},{8,10},{9,11},{10,... | collective-permute-start | bytes 196616 | tf_op jit(solution)/shard_map/ppermute | solution.py:366
  47.1 1.5 %collective-permute-done.17.arrived = bf16[96,512]{1,0:T(8,128)(2,1)S(1)} collective-permute-done((bf16[96,512]{1,0:T(8,128)(2,1)S(1)}, bf16[96,512]{1,0:T(8,128)(2,1)S(1)}, u32[]{:S(2)}, u32[]{:S(2)}) %collective-permute-start.17) | collective-permute-done | bytes 98336 | tf_op jit(solution)/shard_map/ppermute | solution.py:366
  48.7 1.6 %collective-permute-start.18 = (bf16[96,512]{1,0:T(8,128)(2,1)S(1)}, bf16[96,512]{1,0:T(8,128)(2,1)S(1)}, u32[]{:S(2)}, u32[]{:S(2)}) collective-permute-start(bf16[96,512]{1,0:T(8,128)(2,1)S(1)} %shard_map.160.refs_0_), channel_id=1, source_target_pairs={{0,2},{1,3},{2,0},{3,1},{4,6},{5,7},{6,4},{7,5},{8,10},{9,11},{10,... | collective-permute-start | bytes 294920 | tf_op jit(solution)/shard_map/ppermute | solution.py:366
  50.4 1.6 %collective-permute-start.21 = (bf16[64,512]{1,0:T(8,128)(2,1)S(1)}, bf16[64,512]{1,0:T(8,128)(2,1)S(1)}, u32[]{:S(2)}, u32[]{:S(2)}) collective-permute-start(bf16[64,512]{1,0:T(8,128)(2,1)S(1)} %get-tuple-element.123.refs_1_), channel_id=1, source_target_pairs={{0,2},{1,3},{2,0},{3,1},{4,6},{5,7},{6,4},{7,5},{8,10},{9,11},{10,... | collective-permute-start | bytes 196616 | tf_op jit(solution)/shard_map/ppermute | solution.py:366
  52.0 1.3 %collective-permute-done.18.refs_6_ = bf16[96,512]{1,0:T(8,128)(2,1)S(1)} collective-permute-done((bf16[96,512]{1,0:T(8,128)(2,1)S(1)}, bf16[96,512]{1,0:T(8,128)(2,1)S(1)}, u32[]{:S(2)}, u32[]{:S(2)}) %collective-permute-start.18) | collective-permute-done | bytes 98336 | tf_op jit(solution)/shard_map/ppermute | solution.py:366
  (49 shorter events, 13.5 us)
Async XLA Ops:
  1.5 11.5 %collective-permute-start.5 = (bf16[2,32,512]{2,1,0:T(8,128)(2,1)S(1)}, bf16[2,32,512]{2,1,0:T(8,128)(2,1)S(1)}, u32[]{:S(2)}, u32[]{:S(2)}) collective-permute-start(bf16[2,32,512]{2,1,0:T(8,128)(2,1)S(1)} %shard_map.145.refs_0_.refs_4_), channel_id=1, source_target_pairs={{0,12},{4,8},{8,4},{12,0},{1,13},{5,9},{9,5},{13,1},{2,14},{6,10},... | collective-permute-start | bytes 196616 | tf_op jit(solution)/shard_map/ppermute | solution.py:366
  6.6 6.4 %collective-permute-start.4 = (bf16[2,32,512]{2,1,0:T(8,128)(2,1)S(1)}, bf16[2,32,512]{2,1,0:T(8,128)(2,1)S(1)}, u32[]{:S(2)}, u32[]{:S(2)}) collective-permute-start(bf16[2,32,512]{2,1,0:T(8,128)(2,1)S(1)} %shard_map.145.refs_0_.refs_4_), channel_id=1, source_target_pairs={{0,8},{4,12},{8,0},{12,4},{1,9},{5,13},{9,1},{13,5},{2,10},{6,14},... | collective-permute-start | bytes 196616 | tf_op jit(solution)/shard_map/ppermute | solution.py:366
  6.6 6.4 %collective-permute-start.3 = (bf16[2,32,512]{2,1,0:T(8,128)(2,1)S(1)}, bf16[2,32,512]{2,1,0:T(8,128)(2,1)S(1)}, u32[]{:S(2)}, u32[]{:S(2)}) collective-permute-start(bf16[2,32,512]{2,1,0:T(8,128)(2,1)S(1)} %shard_map.145.refs_0_.refs_4_), channel_id=1, source_target_pairs={{0,4},{4,0},{8,12},{12,8},{1,5},{5,1},{9,13},{13,9},{2,6},{6,2},{1... | collective-permute-start | bytes 196616 | tf_op jit(solution)/shard_map/ppermute | solution.py:366
  7.2 5.3 %collective-permute-start.2 = (bf16[2,32,128]{2,1,0:T(8,128)(2,1)}, bf16[2,32,128]{2,1,0:T(8,128)(2,1)S(1)}, u32[]{:S(2)}, u32[]{:S(2)}) collective-permute-start(bf16[2,32,128]{2,1,0:T(8,128)(2,1)} %state.1), channel_id=1, source_target_pairs={{0,3},{1,2},{2,1},{3,0},{4,7},{5,6},{6,5},{7,4},{8,11},{9,10},{10,... | collective-permute-start | bytes 49160 | tf_op jit(solution)/shard_map/ppermute | solution.py:366
  9.0 4.0 %collective-permute-start.1 = (bf16[2,32,128]{2,1,0:T(8,128)(2,1)}, bf16[2,32,128]{2,1,0:T(8,128)(2,1)S(1)}, u32[]{:S(2)}, u32[]{:S(2)}) collective-permute-start(bf16[2,32,128]{2,1,0:T(8,128)(2,1)} %state.1), channel_id=1, source_target_pairs={{0,2},{1,3},{2,0},{3,1},{4,6},{5,7},{6,4},{7,5},{8,10},{9,11},{10,... | collective-permute-start | bytes 49160 | tf_op jit(solution)/shard_map/ppermute | solution.py:366
  14.0 4.5 %collective-permute-start.8 = (bf16[128,256]{1,0:T(8,128)(2,1)S(1)}, bf16[128,256]{1,0:T(8,128)(2,1)S(1)}, u32[]{:S(2)}, u32[]{:S(2)}) collective-permute-start(bf16[128,256]{1,0:T(8,128)(2,1)S(1)} %get-tuple-element.84), channel_id=1, source_target_pairs={{0,4},{4,0},{8,12},{12,8},{1,5},{5,1},{9,13},{13,9},{2,6},{6,2},{1... | collective-permute-start | bytes 196616 | tf_op jit(solution)/shard_map/ppermute | solution.py:366
  16.3 5.0 %collective-permute-start.6 = (bf16[128,256]{1,0:T(8,128)(2,1)S(1)}, bf16[128,256]{1,0:T(8,128)(2,1)S(1)}, u32[]{:S(2)}, u32[]{:S(2)}) collective-permute-start(bf16[128,256]{1,0:T(8,128)(2,1)S(1)} %get-tuple-element.76), channel_id=1, source_target_pairs={{0,4},{4,0},{8,12},{12,8},{1,5},{5,1},{9,13},{13,9},{2,6},{6,2},{1... | collective-permute-start | bytes 196616 | tf_op jit(solution)/shard_map/ppermute | solution.py:366
  18.5 6.9 %collective-permute-start.9 = (bf16[128,256]{1,0:T(8,128)(2,1)S(1)}, bf16[128,256]{1,0:T(8,128)(2,1)S(1)}, u32[]{:S(2)}, u32[]{:S(2)}) collective-permute-start(bf16[128,256]{1,0:T(8,128)(2,1)S(1)} %get-tuple-element.86), channel_id=1, source_target_pairs={{0,8},{4,12},{8,0},{12,4},{1,9},{5,13},{9,1},{13,5},{2,10},{6,14},... | collective-permute-start | bytes 196616 | tf_op jit(solution)/shard_map/ppermute | solution.py:366
  21.4 5.5 %collective-permute-start.7 = (bf16[128,256]{1,0:T(8,128)(2,1)S(1)}, bf16[128,256]{1,0:T(8,128)(2,1)S(1)}, u32[]{:S(2)}, u32[]{:S(2)}) collective-permute-start(bf16[128,256]{1,0:T(8,128)(2,1)S(1)} %get-tuple-element.78), channel_id=1, source_target_pairs={{0,8},{4,12},{8,0},{12,4},{1,9},{5,13},{9,1},{13,5},{2,10},{6,14},... | collective-permute-start | bytes 196616 | tf_op jit(solution)/shard_map/ppermute | solution.py:366
  28.4 4.1 %collective-permute-start.10 = (bf16[288,512]{1,0:T(8,128)(2,1)S(1)}, bf16[288,512]{1,0:T(8,128)(2,1)S(1)}, u32[]{:S(2)}, u32[]{:S(2)}) collective-permute-start(bf16[288,512]{1,0:T(8,128)(2,1)S(1)} %get-tuple-element.99), channel_id=1, source_target_pairs={{0,1},{1,0},{2,3},{3,2},{4,5},{5,4},{6,7},{7,6},{8,9},{9,8},{10,11... | collective-permute-start | bytes 884744 | tf_op jit(solution)/shard_map/ppermute | solution.py:366
  28.5 1.9 %collective-permute-start.14 = (bf16[192,512]{1,0:T(8,128)(2,1)S(1)}, bf16[192,512]{1,0:T(8,128)(2,1)S(1)}, u32[]{:S(2)}, u32[]{:S(2)}) collective-permute-start(bf16[192,512]{1,0:T(8,128)(2,1)S(1)} %get-tuple-element.114), channel_id=1, source_target_pairs={{0,1},{1,0},{2,3},{3,2},{4,5},{5,4},{6,7},{7,6},{8,9},{9,8},{10,11... | collective-permute-start | bytes 589832 | tf_op jit(solution)/shard_map/ppermute | solution.py:366
  30.4 5.1 %collective-permute-start.15 = (bf16[96,512]{1,0:T(8,128)(2,1)S(1)}, bf16[96,512]{1,0:T(8,128)(2,1)S(1)}, u32[]{:S(2)}, u32[]{:S(2)}) collective-permute-start(bf16[96,512]{1,0:T(8,128)(2,1)S(1)} %get-tuple-element.116), channel_id=1, source_target_pairs={{0,2},{1,3},{2,0},{3,1},{4,6},{5,7},{6,4},{7,5},{8,10},{9,11},{10,... | collective-permute-start | bytes 294920 | tf_op jit(solution)/shard_map/ppermute | solution.py:366
  32.6 5.9 %collective-permute-start.11 = (bf16[144,512]{1,0:T(8,128)(2,1)S(1)}, bf16[144,512]{1,0:T(8,128)(2,1)S(1)}, u32[]{:S(2)}, u32[]{:S(2)}) collective-permute-start(bf16[144,512]{1,0:T(8,128)(2,1)S(1)} %get-tuple-element.106), channel_id=1, source_target_pairs={{0,2},{1,3},{2,0},{3,1},{4,6},{5,7},{6,4},{7,5},{8,10},{9,11},{10,... | collective-permute-start | bytes 442376 | tf_op jit(solution)/shard_map/ppermute | solution.py:366
  35.5 4.7 %collective-permute-start.16 = (bf16[96,512]{1,0:T(8,128)(2,1)S(1)}, bf16[96,512]{1,0:T(8,128)(2,1)S(1)}, u32[]{:S(2)}, u32[]{:S(2)}) collective-permute-start(bf16[96,512]{1,0:T(8,128)(2,1)S(1)} %get-tuple-element.118), channel_id=1, source_target_pairs={{0,4},{4,0},{8,12},{12,8},{1,5},{5,1},{9,13},{13,9},{2,6},{6,2},{1... | collective-permute-start | bytes 294920 | tf_op jit(solution)/shard_map/ppermute | solution.py:366
  38.5 5.1 %collective-permute-start.12 = (bf16[96,512]{1,0:T(8,128)(2,1)S(1)}, bf16[96,512]{1,0:T(8,128)(2,1)S(1)}, u32[]{:S(2)}, u32[]{:S(2)}) collective-permute-start(bf16[96,512]{1,0:T(8,128)(2,1)S(1)} %get-tuple-element.109), channel_id=1, source_target_pairs={{0,4},{4,0},{8,12},{12,8},{1,5},{5,1},{9,13},{13,9},{2,6},{6,2},{1... | collective-permute-start | bytes 294920 | tf_op jit(solution)/shard_map/ppermute | solution.py:366
  40.2 8.4 %collective-permute-start.17 = (bf16[96,512]{1,0:T(8,128)(2,1)S(1)}, bf16[96,512]{1,0:T(8,128)(2,1)S(1)}, u32[]{:S(2)}, u32[]{:S(2)}) collective-permute-start(bf16[96,512]{1,0:T(8,128)(2,1)S(1)} %get-tuple-element.120), channel_id=1, source_target_pairs={{0,8},{4,12},{8,0},{12,4},{1,9},{5,13},{9,1},{13,5},{2,10},{6,14},... | collective-permute-start | bytes 294920 | tf_op jit(solution)/shard_map/ppermute | solution.py:366
  43.7 6.7 %collective-permute-start.13 = (bf16[80,512]{1,0:T(8,128)(2,1)S(1)}, bf16[80,512]{1,0:T(8,128)(2,1)S(1)}, u32[]{:S(2)}, u32[]{:S(2)}) collective-permute-start(bf16[80,512]{1,0:T(8,128)(2,1)S(1)} %get-tuple-element.112), channel_id=1, source_target_pairs={{0,8},{4,12},{8,0},{12,4},{1,9},{5,13},{9,1},{13,5},{2,10},{6,14},... | collective-permute-start | bytes 245768 | tf_op jit(solution)/shard_map/ppermute | solution.py:366
  45.6 4.6 %collective-permute-start.20 = (bf16[64,512]{1,0:T(8,128)(2,1)S(1)}, bf16[64,512]{1,0:T(8,128)(2,1)S(1)}, u32[]{:S(2)}, u32[]{:S(2)}) collective-permute-start(bf16[64,512]{1,0:T(8,128)(2,1)S(1)} %get-tuple-element.122.refs_2_), channel_id=1, source_target_pairs={{0,2},{1,3},{2,0},{3,1},{4,6},{5,7},{6,4},{7,5},{8,10},{9,11},{10,... | collective-permute-start | bytes 196616 | tf_op jit(solution)/shard_map/ppermute | solution.py:366
  48.7 4.7 %collective-permute-start.18 = (bf16[96,512]{1,0:T(8,128)(2,1)S(1)}, bf16[96,512]{1,0:T(8,128)(2,1)S(1)}, u32[]{:S(2)}, u32[]{:S(2)}) collective-permute-start(bf16[96,512]{1,0:T(8,128)(2,1)S(1)} %shard_map.160.refs_0_), channel_id=1, source_target_pairs={{0,2},{1,3},{2,0},{3,1},{4,6},{5,7},{6,4},{7,5},{8,10},{9,11},{10,... | collective-permute-start | bytes 294920 | tf_op jit(solution)/shard_map/ppermute | solution.py:366
  50.3 3.6 %collective-permute-start.26 = (bf16[64,512]{1,0:T(8,128)(2,1)S(1)}, bf16[64,512]{1,0:T(8,128)(2,1)S(1)}, u32[]{:S(2)}, u32[]{:S(2)}) collective-permute-start(bf16[64,512]{1,0:T(8,128)(2,1)S(1)} %get-tuple-element.122.refs_2_), channel_id=1, source_target_pairs={{0,1},{1,0},{2,3},{3,2},{4,5},{5,4},{6,7},{7,6},{8,9},{9,8},{10,11... | collective-permute-start | bytes 196616 | tf_op jit(solution)/shard_map/ppermute | solution.py:366
  50.4 4.4 %collective-permute-start.21 = (bf16[64,512]{1,0:T(8,128)(2,1)S(1)}, bf16[64,512]{1,0:T(8,128)(2,1)S(1)}, u32[]{:S(2)}, u32[]{:S(2)}) collective-permute-start(bf16[64,512]{1,0:T(8,128)(2,1)S(1)} %get-tuple-element.123.refs_1_), channel_id=1, source_target_pairs={{0,2},{1,3},{2,0},{3,1},{4,6},{5,7},{6,4},{7,5},{8,10},{9,11},{10,... | collective-permute-start | bytes 196616 | tf_op jit(solution)/shard_map/ppermute | solution.py:366
  52.0 2.9 %collective-permute-start.24 = (bf16[96,512]{1,0:T(8,128)(2,1)S(1)}, bf16[96,512]{1,0:T(8,128)(2,1)S(1)}, u32[]{:S(2)}, u32[]{:S(2)}) collective-permute-start(bf16[96,512]{1,0:T(8,128)(2,1)S(1)} %shard_map.160.refs_0_), channel_id=1, source_target_pairs={{0,1},{1,0},{2,3},{3,2},{4,5},{5,4},{6,7},{7,6},{8,9},{9,8},{10,11... | collective-permute-start | bytes 294920 | tf_op jit(solution)/shard_map/ppermute | solution.py:366
  53.3 2.7 %collective-permute-start.19 = (bf16[96,512]{1,0:T(8,128)(2,1)S(1)}, bf16[96,512]{1,0:T(8,128)(2,1)S(1)}, u32[]{:S(2)}, u32[]{:S(2)}) collective-permute-start(bf16[96,512]{1,0:T(8,128)(2,1)S(1)} %collective-permute-done.18.refs_6_), channel_id=1, source_target_pairs={{0,1},{1,0},{2,3},{3,2},{4,5},{5,4},{6,7},{7,6},{8,9},{9,8},{10,11... | collective-permute-start | bytes 294920 | tf_op jit(solution)/shard_map/ppermute | solution.py:366
  53.9 2.2 %collective-permute-start.23 = (bf16[64,512]{1,0:T(8,128)(2,1)S(1)}, bf16[64,512]{1,0:T(8,128)(2,1)S(1)}, u32[]{:S(2)}, u32[]{:S(2)}) collective-permute-start(bf16[64,512]{1,0:T(8,128)(2,1)S(1)} %get-tuple-element.124.refs_8_), channel_id=1, source_target_pairs={{0,1},{1,0},{2,3},{3,2},{4,5},{5,4},{6,7},{7,6},{8,9},{9,8},{10,11... | collective-permute-start | bytes 196616 | tf_op jit(solution)/shard_map/ppermute | solution.py:366
  (3 other events, 4.5 us)

commit v9 on v8

--- a/solution.py
+++ b/solution.py
@@ -145,15 +145,9 @@
     from_dst = mm(dst_t[...], grad_pre_edge).astype(BF)
     to_src = mm_nt(from_src, w1[:width])
     to_dst = mm_nt(from_dst, w1[width : 2 * width])
-    first = [
-        mm_tn(stacked(sources, moment, width), from_src),
-        mm_tn(state, from_dst),
-        mm_tn(attr[moment], grad_pre_edge),
-    ]
-    second = mm_tn(sums[...], grad_agg)
-    node_grad = mm_tn(node_in, grad_pre)
+    attr_grad = mm_tn(attr[moment], grad_pre_edge)
     state_own = grad_in[:rows, :width] + to_dst[:rows]
-    return state_own, to_src, to_dst, first, second, node_grad
+    return state_own, to_src, to_dst, attr_grad, from_src, from_dst, grad_agg, node_in, grad_pre
 
 
 def split_refs(refs):
@@ -163,38 +157,41 @@
 
 def backward_first_kernel(*refs):
     sources, targets, args, refs = split_refs(refs)
-    state, forcing, edges, to_src, to_dst, first_out, second_out, node_out = refs
+    state, forcing, edges, *outs = refs
 
     def put_edges(edge_values, forcing_values):
         edges[...] = edge_values
         forcing[...] = forcing_values
 
-    state[...], to_src[...], to_dst[...], first, second, node_grad = backward(0, put_edges, sources, targets, *args)
-    width = first[0].shape[0]
-    for i, value in enumerate(first):
-        first_out[i * width : (i + 1) * width] = value
-    second_out[...] = second
-    node_out[...] = node_grad
+    state[...], *values = backward(0, put_edges, sources, targets, *args)
+    for ref, value in zip(outs, values, strict=True):
+        ref[...] = value
 
 
 def backward_last_kernel(*refs):
     n = WAYS
     sources, targets, args, refs = split_refs(refs)
-    state_0, to_src_0, to_dst_0, first_0, second_0, node_0 = refs[:6]
-    state_own, forcing, edges, first_held, second_held, node_grad_held, src_kept = refs[6:13]
-    core_a, core_b, target_kept, target_sent = refs[13:]
+    state_0, to_src_0, to_dst_0, attr_0, *earlier, sums_0 = refs[:10]
+    state_own, forcing, edges, first_held, second_held, node_grad_held, src_kept = refs[10:17]
+    core_a, core_b, target_kept, target_sent = refs[17:]
 
     def put_edges(edge_values, forcing_values):
         edges[...] = edge_values
         forcing[...] = forcing_values
 
-    state_1, to_src_1, to_dst_1, first, second, node_grad = backward(1, put_edges, sources, targets, *args)
+    state_1, to_src_1, to_dst_1, attr_1, *later = backward(1, put_edges, sources, targets, *args)
     state_own[0], state_own[1] = state_0[...], state_1
-    width = first[0].shape[0]
-    for i, value in enumerate(first):
-        first_held[i * width : (i + 1) * width] = first_0[i * width : (i + 1) * width] + value
-    second_held[...] = second_0[...] + second
-    node_grad_held[...] = node_0[...] + node_grad
+    from_src, from_dst, grad_agg, node_in, grad_pre = (
+        jnp.concatenate([ref[...], value], axis=0) for ref, value in zip(earlier, later, strict=True)
+    )
+    width = attr_1.shape[0]
+    states = jnp.concatenate([stacked(sources, moment, width) for moment in range(T_STEPS)], axis=0)
+    first_held[:width] = mm_tn(states, from_src)
+    first_held[width : 2 * width] = mm_tn(node_in[:, :width], from_dst)
+    first_held[2 * width :] = attr_0[...] + attr_1
+    sums = args[6]
+    second_held[...] = mm_tn(jnp.concatenate([sums_0[...], sums[...]], axis=0), grad_agg)
+    node_grad_held[...] = mm_tn(node_in, grad_pre)
     part, block = first_held.shape[0] // n, second_held.shape[0] // n
     size, wide = block // 2, second_held.shape[1]
     for i, k in enumerate((1, 3)):
@@ -434,9 +431,12 @@
             ((slots, width), F32),
             ((nodes, width), F32),
             ((nodes, width), F32),
-            (edge_w1.shape, F32),
-            (edge_w2.shape, F32),
-            (node_w1.shape, F32),
+            ((width, hid), F32),
+            ((nodes, hid), BF),
+            ((nodes, hid), BF),
+            ((nodes, width_m), BF),
+            ((nodes, node_w1.shape[0]), BF),
+            ((nodes, width_out), BF),
         ],
         [],
         args[0],
@@ -460,7 +460,7 @@
             ((2 * half, hid), BF),
         ],
         [],
-        [*args[1], state_0, *earlier],
+        [*args[1], state_0, *earlier, forward[0][3]],
     )
     grad_forcing, edges, token = call(
         out_kernel,

time: 57.2 us -> 57 us (level)
  no operation moved by 1% of the time
where the time goes in v9:
time: 57 us; the launch traced here: 56.7 us
  starting transfers between devices  30.8 us (54%)
  waiting for transfers between devices  14.1 us (25%)
  Pallas kernels  10.4 us (18%)
  between operations  1.45 us (3%)
    ppermute x27, starting transfers between devices, swap(): return lax.ppermute(value, axis, [(i, i ^ k) for i in range(WAYS)])  30.8 us
    ppermute x27, waiting for transfers between devices, swap(): return lax.ppermute(value, axis, [(i, i ^ k) for i in range(WAYS)])  14.1 us
    pallas_call x19, Pallas kernels, call(): pl.pallas_call(kernel, out_shape=[jax.ShapeDtypeStruct(shape, dtype) for...  10.4 us
  transfers between devices with their start and end apart: 27, of which 14 were waited for; matrix products, arithmetic and copies ran while one was open for 0% of the time, Pallas kernels for 11%

profile of v9, /device:TPU:0, one launch (start us, length us, event | category | flops | bytes accessed | tf_op | source)
XLA Modules:
  0.0 56.7 jit_solution(7813889256816539259)
XLA Ops:
  1.5 5.1 %collective-permute-start.5 = (bf16[2,32,512]{2,1,0:T(8,128)(2,1)S(1)}, bf16[2,32,512]{2,1,0:T(8,128)(2,1)S(1)}, u32[]{:S(2)}, u32[]{:S(2)}) collective-permute-start(bf16[2,32,512]{2,1,0:T(8,128)(2,1)S(1)} %shard_map.145.refs_0_.refs_4_), channel_id=1, source_target_pairs={{0,12},{4,8},{8,4},{12,0},{1,13},{5,9},{9,5},{13,1},{2,14},{6,10},... | collective-permute-start | bytes 196616 | tf_op jit(solution)/shard_map/ppermute | solution.py:363
  7.2 1.7 %collective-permute-start.2 = (bf16[2,32,128]{2,1,0:T(8,128)(2,1)}, bf16[2,32,128]{2,1,0:T(8,128)(2,1)S(1)}, u32[]{:S(2)}, u32[]{:S(2)}) collective-permute-start(bf16[2,32,128]{2,1,0:T(8,128)(2,1)} %state.1), channel_id=1, source_target_pairs={{0,3},{1,2},{2,1},{3,0},{4,7},{5,6},{6,5},{7,4},{8,11},{9,10},{10,... | collective-permute-start | bytes 49160 | tf_op jit(solution)/shard_map/ppermute | solution.py:363
  9.0 1.3 %collective-permute-start.1 = (bf16[2,32,128]{2,1,0:T(8,128)(2,1)}, bf16[2,32,128]{2,1,0:T(8,128)(2,1)S(1)}, u32[]{:S(2)}, u32[]{:S(2)}) collective-permute-start(bf16[2,32,128]{2,1,0:T(8,128)(2,1)} %state.1), channel_id=1, source_target_pairs={{0,2},{1,3},{2,0},{3,1},{4,6},{5,7},{6,4},{7,5},{8,10},{9,11},{10,... | collective-permute-start | bytes 49160 | tf_op jit(solution)/shard_map/ppermute | solution.py:363
  10.9 1.6 %shard_map.146 = (bf16[2,512,128]{2,1,0:T(8,128)(2,1)S(1)}, bf16[384,512]{1,0:T(8,128)(2,1)S(1)}, bf16[512,256]{1,0:T(8,128)(2,1)S(1)}, bf16[512,256]{1,0:T(8,12...) custom-call(s32[1,1]{1,0:T(1,128)S(6)} %copy.23.count, ...), custom_call_target="tpu_custom_call" | custom-call | tf_op jit(solution)/shard_map/pallas_call | solution.py:345
  14.0 1.3 %collective-permute-start.8 = (bf16[128,256]{1,0:T(8,128)(2,1)S(1)}, bf16[128,256]{1,0:T(8,128)(2,1)S(1)}, u32[]{:S(2)}, u32[]{:S(2)}) collective-permute-start(bf16[128,256]{1,0:T(8,128)(2,1)S(1)} %get-tuple-element.87), channel_id=1, source_target_pairs={{0,4},{4,0},{8,12},{12,8},{1,5},{5,1},{9,13},{13,9},{2,6},{6,2},{1... | collective-permute-start | bytes 196616 | tf_op jit(solution)/shard_map/ppermute | solution.py:363
  17.2 1.3 %collective-permute-done.8.arrived = bf16[128,256]{1,0:T(8,128)(2,1)S(1)} collective-permute-done((bf16[128,256]{1,0:T(8,128)(2,1)S(1)}, bf16[128,256]{1,0:T(8,128)(2,1)S(1)}, u32[]{:S(2)}, u32[]{:S(2)}) %collective-permute-start.8) | collective-permute-done | bytes 65568 | tf_op jit(solution)/shard_map/ppermute | solution.py:363
  18.5 2.0 %collective-permute-start.9 = (bf16[128,256]{1,0:T(8,128)(2,1)S(1)}, bf16[128,256]{1,0:T(8,128)(2,1)S(1)}, u32[]{:S(2)}, u32[]{:S(2)}) collective-permute-start(bf16[128,256]{1,0:T(8,128)(2,1)S(1)} %get-tuple-element.89), channel_id=1, source_target_pairs={{0,8},{4,12},{8,0},{12,4},{1,9},{5,13},{9,1},{13,5},{2,10},{6,14},... | collective-permute-start | bytes 196616 | tf_op jit(solution)/shard_map/ppermute | solution.py:363
  21.4 2.3 %collective-permute-start.7 = (bf16[128,256]{1,0:T(8,128)(2,1)S(1)}, bf16[128,256]{1,0:T(8,128)(2,1)S(1)}, u32[]{:S(2)}, u32[]{:S(2)}) collective-permute-start(bf16[128,256]{1,0:T(8,128)(2,1)S(1)} %get-tuple-element.81), channel_id=1, source_target_pairs={{0,8},{4,12},{8,0},{12,4},{1,9},{5,13},{9,1},{13,5},{2,10},{6,14},... | collective-permute-start | bytes 196616 | tf_op jit(solution)/shard_map/ppermute | solution.py:363
  23.7 1.7 %collective-permute-done.9.refs_9_ = bf16[128,256]{1,0:T(8,128)(2,1)S(1)} collective-permute-done((bf16[128,256]{1,0:T(8,128)(2,1)S(1)}, bf16[128,256]{1,0:T(8,128)(2,1)S(1)}, u32[]{:S(2)}, u32[]{:S(2)}) %collective-permute-start.9) | collective-permute-done | bytes 65568 | tf_op jit(solution)/shard_map/ppermute | solution.py:363
  25.4 1.3 %shard_map.151 = (f32[32,128]{1,0:T(8,128)S(1)}, f32[32,128]{1,0:T(8,128)S(1)}, f32[512,128]{1,0:T(8,128)S(1)}, f32[128,128]{1,0:T(8,128)S(1)}, f32[128,128]{1,0...) custom-call(bf16[2,32,512]{2,1,0:T(8,128)(2,1)S(1)} %shard_map.145.r, ...), custom_call_target="tpu_custom_call" | custom-call | tf_op jit(solution)/shard_map/pallas_call | solution.py:345
  26.7 1.5 %shard_map.152 = (f32[2,32,128]{2,1,0:T(8,128)S(1)}, f32[32,128]{1,0:T(8,128)S(1)}, f32[512,128]{1,0:T(8,128)S(1)}, f32[384,512]{1,0:T(8,128)S(1)}, f32[512,256]...) custom-call(bf16[2,32,512]{2,1,0:T(8,128)(2,1)S(1)} %shard_map.145.r, ...), custom_call_target="tpu_custom_call" | custom-call | tf_op jit(solution)/shard_map/pallas_call | solution.py:345
  28.8 1.4 %collective-permute-done.14.arrived = bf16[192,512]{1,0:T(8,128)(2,1)S(1)} collective-permute-done((bf16[192,512]{1,0:T(8,128)(2,1)S(1)}, bf16[192,512]{1,0:T(8,128)(2,1)S(1)}, u32[]{:S(2)}, u32[]{:S(2)}) %collective-permute-start.14) | collective-permute-done | bytes 196640 | tf_op jit(solution)/shard_map/ppermute | solution.py:363
  30.2 1.3 %collective-permute-start.15 = (bf16[96,512]{1,0:T(8,128)(2,1)S(1)}, bf16[96,512]{1,0:T(8,128)(2,1)S(1)}, u32[]{:S(2)}, u32[]{:S(2)}) collective-permute-start(bf16[96,512]{1,0:T(8,128)(2,1)S(1)} %get-tuple-element.122), channel_id=1, source_target_pairs={{0,2},{1,3},{2,0},{3,1},{4,6},{5,7},{6,4},{7,5},{8,10},{9,11},{10,... | collective-permute-start | bytes 294920 | tf_op jit(solution)/shard_map/ppermute | solution.py:363
  33.3 2.0 %collective-permute-done.15.arrived = bf16[96,512]{1,0:T(8,128)(2,1)S(1)} collective-permute-done((bf16[96,512]{1,0:T(8,128)(2,1)S(1)}, bf16[96,512]{1,0:T(8,128)(2,1)S(1)}, u32[]{:S(2)}, u32[]{:S(2)}) %collective-permute-start.15) | collective-permute-done | bytes 98336 | tf_op jit(solution)/shard_map/ppermute | solution.py:363
  35.3 1.8 %collective-permute-start.16 = (bf16[96,512]{1,0:T(8,128)(2,1)S(1)}, bf16[96,512]{1,0:T(8,128)(2,1)S(1)}, u32[]{:S(2)}, u32[]{:S(2)}) collective-permute-start(bf16[96,512]{1,0:T(8,128)(2,1)S(1)} %get-tuple-element.124), channel_id=1, source_target_pairs={{0,4},{4,0},{8,12},{12,8},{1,5},{5,1},{9,13},{13,9},{2,6},{6,2},{1... | collective-permute-start | bytes 294920 | tf_op jit(solution)/shard_map/ppermute | solution.py:363
  38.3 1.5 %collective-permute-start.12 = (bf16[96,512]{1,0:T(8,128)(2,1)S(1)}, bf16[96,512]{1,0:T(8,128)(2,1)S(1)}, u32[]{:S(2)}, u32[]{:S(2)}) collective-permute-start(bf16[96,512]{1,0:T(8,128)(2,1)S(1)} %get-tuple-element.115), channel_id=1, source_target_pairs={{0,4},{4,0},{8,12},{12,8},{1,5},{5,1},{9,13},{13,9},{2,6},{6,2},{1... | collective-permute-start | bytes 294920 | tf_op jit(solution)/shard_map/ppermute | solution.py:363
  40.0 2.3 %collective-permute-start.17 = (bf16[96,512]{1,0:T(8,128)(2,1)S(1)}, bf16[96,512]{1,0:T(8,128)(2,1)S(1)}, u32[]{:S(2)}, u32[]{:S(2)}) collective-permute-start(bf16[96,512]{1,0:T(8,128)(2,1)S(1)} %get-tuple-element.126), channel_id=1, source_target_pairs={{0,8},{4,12},{8,0},{12,4},{1,9},{5,13},{9,1},{13,5},{2,10},{6,14},... | collective-permute-start | bytes 294920 | tf_op jit(solution)/shard_map/ppermute | solution.py:363
  43.4 2.2 %collective-permute-start.13 = (bf16[80,512]{1,0:T(8,128)(2,1)S(1)}, bf16[80,512]{1,0:T(8,128)(2,1)S(1)}, u32[]{:S(2)}, u32[]{:S(2)}) collective-permute-start(bf16[80,512]{1,0:T(8,128)(2,1)S(1)} %get-tuple-element.118), channel_id=1, source_target_pairs={{0,8},{4,12},{8,0},{12,4},{1,9},{5,13},{9,1},{13,5},{2,10},{6,14},... | collective-permute-start | bytes 245768 | tf_op jit(solution)/shard_map/ppermute | solution.py:363
  45.6 1.5 %collective-permute-start.20 = (bf16[64,512]{1,0:T(8,128)(2,1)S(1)}, bf16[64,512]{1,0:T(8,128)(2,1)S(1)}, u32[]{:S(2)}, u32[]{:S(2)}) collective-permute-start(bf16[64,512]{1,0:T(8,128)(2,1)S(1)} %get-tuple-element.128.refs_2_), channel_id=1, source_target_pairs={{0,2},{1,3},{2,0},{3,1},{4,6},{5,7},{6,4},{7,5},{8,10},{9,11},{10,... | collective-permute-start | bytes 196616 | tf_op jit(solution)/shard_map/ppermute | solution.py:363
  47.1 1.4 %collective-permute-done.17.arrived = bf16[96,512]{1,0:T(8,128)(2,1)S(1)} collective-permute-done((bf16[96,512]{1,0:T(8,128)(2,1)S(1)}, bf16[96,512]{1,0:T(8,128)(2,1)S(1)}, u32[]{:S(2)}, u32[]{:S(2)}) %collective-permute-start.17) | collective-permute-done | bytes 98336 | tf_op jit(solution)/shard_map/ppermute | solution.py:363
  48.5 1.5 %collective-permute-start.18 = (bf16[96,512]{1,0:T(8,128)(2,1)S(1)}, bf16[96,512]{1,0:T(8,128)(2,1)S(1)}, u32[]{:S(2)}, u32[]{:S(2)}) collective-permute-start(bf16[96,512]{1,0:T(8,128)(2,1)S(1)} %shard_map.160.refs_0_), channel_id=1, source_target_pairs={{0,2},{1,3},{2,0},{3,1},{4,6},{5,7},{6,4},{7,5},{8,10},{9,11},{10,... | collective-permute-start | bytes 294920 | tf_op jit(solution)/shard_map/ppermute | solution.py:363
  50.3 1.5 %collective-permute-start.21 = (bf16[64,512]{1,0:T(8,128)(2,1)S(1)}, bf16[64,512]{1,0:T(8,128)(2,1)S(1)}, u32[]{:S(2)}, u32[]{:S(2)}) collective-permute-start(bf16[64,512]{1,0:T(8,128)(2,1)S(1)} %get-tuple-element.129.refs_1_), channel_id=1, source_target_pairs={{0,2},{1,3},{2,0},{3,1},{4,6},{5,7},{6,4},{7,5},{8,10},{9,11},{10,... | collective-permute-start | bytes 196616 | tf_op jit(solution)/shard_map/ppermute | solution.py:363
  51.8 1.4 %collective-permute-done.18.refs_6_ = bf16[96,512]{1,0:T(8,128)(2,1)S(1)} collective-permute-done((bf16[96,512]{1,0:T(8,128)(2,1)S(1)}, bf16[96,512]{1,0:T(8,128)(2,1)S(1)}, u32[]{:S(2)}, u32[]{:S(2)}) %collective-permute-start.18) | collective-permute-done | bytes 98336 | tf_op jit(solution)/shard_map/ppermute | solution.py:363
  54.7 1.2 %shard_map.162 = (f32[384,512]{1,0:T(8,128)}, f32[512,256]{1,0:T(8,128)}, f32[512,256]{1,0:T(8,128)}) custom-call(bf16[96,512]{1,0:T(8,128)(2,1)S(1)} %shard_map.160.refs_0_, bf16[64,512]{1,0:T(8,128)(2,1)S(1)} %get-tuple-element.129.refs_1_, bf16[64,512]{1,0:T(8,128)(2,1)S(1)} %get-tuple-element.128.refs_2_, ...), custom_call_target="tpu_custom_call" | custom-call | tf_op jit(solution)/shard_map/pallas_call | solution.py:345
  (49 shorter events, 13.2 us)
Async XLA Ops:
  1.5 11.5 %collective-permute-start.5 = (bf16[2,32,512]{2,1,0:T(8,128)(2,1)S(1)}, bf16[2,32,512]{2,1,0:T(8,128)(2,1)S(1)}, u32[]{:S(2)}, u32[]{:S(2)}) collective-permute-start(bf16[2,32,512]{2,1,0:T(8,128)(2,1)S(1)} %shard_map.145.refs_0_.refs_4_), channel_id=1, source_target_pairs={{0,12},{4,8},{8,4},{12,0},{1,13},{5,9},{9,5},{13,1},{2,14},{6,10},... | collective-permute-start | bytes 196616 | tf_op jit(solution)/shard_map/ppermute | solution.py:363
  6.6 6.4 %collective-permute-start.4 = (bf16[2,32,512]{2,1,0:T(8,128)(2,1)S(1)}, bf16[2,32,512]{2,1,0:T(8,128)(2,1)S(1)}, u32[]{:S(2)}, u32[]{:S(2)}) collective-permute-start(bf16[2,32,512]{2,1,0:T(8,128)(2,1)S(1)} %shard_map.145.refs_0_.refs_4_), channel_id=1, source_target_pairs={{0,8},{4,12},{8,0},{12,4},{1,9},{5,13},{9,1},{13,5},{2,10},{6,14},... | collective-permute-start | bytes 196616 | tf_op jit(solution)/shard_map/ppermute | solution.py:363
  6.6 6.4 %collective-permute-start.3 = (bf16[2,32,512]{2,1,0:T(8,128)(2,1)S(1)}, bf16[2,32,512]{2,1,0:T(8,128)(2,1)S(1)}, u32[]{:S(2)}, u32[]{:S(2)}) collective-permute-start(bf16[2,32,512]{2,1,0:T(8,128)(2,1)S(1)} %shard_map.145.refs_0_.refs_4_), channel_id=1, source_target_pairs={{0,4},{4,0},{8,12},{12,8},{1,5},{5,1},{9,13},{13,9},{2,6},{6,2},{1... | collective-permute-start | bytes 196616 | tf_op jit(solution)/shard_map/ppermute | solution.py:363
  7.2 5.3 %collective-permute-start.2 = (bf16[2,32,128]{2,1,0:T(8,128)(2,1)}, bf16[2,32,128]{2,1,0:T(8,128)(2,1)S(1)}, u32[]{:S(2)}, u32[]{:S(2)}) collective-permute-start(bf16[2,32,128]{2,1,0:T(8,128)(2,1)} %state.1), channel_id=1, source_target_pairs={{0,3},{1,2},{2,1},{3,0},{4,7},{5,6},{6,5},{7,4},{8,11},{9,10},{10,... | collective-permute-start | bytes 49160 | tf_op jit(solution)/shard_map/ppermute | solution.py:363
  9.0 4.0 %collective-permute-start.1 = (bf16[2,32,128]{2,1,0:T(8,128)(2,1)}, bf16[2,32,128]{2,1,0:T(8,128)(2,1)S(1)}, u32[]{:S(2)}, u32[]{:S(2)}) collective-permute-start(bf16[2,32,128]{2,1,0:T(8,128)(2,1)} %state.1), channel_id=1, source_target_pairs={{0,2},{1,3},{2,0},{3,1},{4,6},{5,7},{6,4},{7,5},{8,10},{9,11},{10,... | collective-permute-start | bytes 49160 | tf_op jit(solution)/shard_map/ppermute | solution.py:363
  14.0 4.5 %collective-permute-start.8 = (bf16[128,256]{1,0:T(8,128)(2,1)S(1)}, bf16[128,256]{1,0:T(8,128)(2,1)S(1)}, u32[]{:S(2)}, u32[]{:S(2)}) collective-permute-start(bf16[128,256]{1,0:T(8,128)(2,1)S(1)} %get-tuple-element.87), channel_id=1, source_target_pairs={{0,4},{4,0},{8,12},{12,8},{1,5},{5,1},{9,13},{13,9},{2,6},{6,2},{1... | collective-permute-start | bytes 196616 | tf_op jit(solution)/shard_map/ppermute | solution.py:363
  16.3 5.0 %collective-permute-start.6 = (bf16[128,256]{1,0:T(8,128)(2,1)S(1)}, bf16[128,256]{1,0:T(8,128)(2,1)S(1)}, u32[]{:S(2)}, u32[]{:S(2)}) collective-permute-start(bf16[128,256]{1,0:T(8,128)(2,1)S(1)} %get-tuple-element.79), channel_id=1, source_target_pairs={{0,4},{4,0},{8,12},{12,8},{1,5},{5,1},{9,13},{13,9},{2,6},{6,2},{1... | collective-permute-start | bytes 196616 | tf_op jit(solution)/shard_map/ppermute | solution.py:363
  18.5 6.9 %collective-permute-start.9 = (bf16[128,256]{1,0:T(8,128)(2,1)S(1)}, bf16[128,256]{1,0:T(8,128)(2,1)S(1)}, u32[]{:S(2)}, u32[]{:S(2)}) collective-permute-start(bf16[128,256]{1,0:T(8,128)(2,1)S(1)} %get-tuple-element.89), channel_id=1, source_target_pairs={{0,8},{4,12},{8,0},{12,4},{1,9},{5,13},{9,1},{13,5},{2,10},{6,14},... | collective-permute-start | bytes 196616 | tf_op jit(solution)/shard_map/ppermute | solution.py:363
  21.4 5.3 %collective-permute-start.7 = (bf16[128,256]{1,0:T(8,128)(2,1)S(1)}, bf16[128,256]{1,0:T(8,128)(2,1)S(1)}, u32[]{:S(2)}, u32[]{:S(2)}) collective-permute-start(bf16[128,256]{1,0:T(8,128)(2,1)S(1)} %get-tuple-element.81), channel_id=1, source_target_pairs={{0,8},{4,12},{8,0},{12,4},{1,9},{5,13},{9,1},{13,5},{2,10},{6,14},... | collective-permute-start | bytes 196616 | tf_op jit(solution)/shard_map/ppermute | solution.py:363
  28.2 4.1 %collective-permute-start.10 = (bf16[288,512]{1,0:T(8,128)(2,1)S(1)}, bf16[288,512]{1,0:T(8,128)(2,1)S(1)}, u32[]{:S(2)}, u32[]{:S(2)}) collective-permute-start(bf16[288,512]{1,0:T(8,128)(2,1)S(1)} %get-tuple-element.105), channel_id=1, source_target_pairs={{0,1},{1,0},{2,3},{3,2},{4,5},{5,4},{6,7},{7,6},{8,9},{9,8},{10,11... | collective-permute-start | bytes 884744 | tf_op jit(solution)/shard_map/ppermute | solution.py:363
  28.3 1.9 %collective-permute-start.14 = (bf16[192,512]{1,0:T(8,128)(2,1)S(1)}, bf16[192,512]{1,0:T(8,128)(2,1)S(1)}, u32[]{:S(2)}, u32[]{:S(2)}) collective-permute-start(bf16[192,512]{1,0:T(8,128)(2,1)S(1)} %get-tuple-element.120), channel_id=1, source_target_pairs={{0,1},{1,0},{2,3},{3,2},{4,5},{5,4},{6,7},{7,6},{8,9},{9,8},{10,11... | collective-permute-start | bytes 589832 | tf_op jit(solution)/shard_map/ppermute | solution.py:363
  30.2 5.1 %collective-permute-start.15 = (bf16[96,512]{1,0:T(8,128)(2,1)S(1)}, bf16[96,512]{1,0:T(8,128)(2,1)S(1)}, u32[]{:S(2)}, u32[]{:S(2)}) collective-permute-start(bf16[96,512]{1,0:T(8,128)(2,1)S(1)} %get-tuple-element.122), channel_id=1, source_target_pairs={{0,2},{1,3},{2,0},{3,1},{4,6},{5,7},{6,4},{7,5},{8,10},{9,11},{10,... | collective-permute-start | bytes 294920 | tf_op jit(solution)/shard_map/ppermute | solution.py:363
  32.4 5.9 %collective-permute-start.11 = (bf16[144,512]{1,0:T(8,128)(2,1)S(1)}, bf16[144,512]{1,0:T(8,128)(2,1)S(1)}, u32[]{:S(2)}, u32[]{:S(2)}) collective-permute-start(bf16[144,512]{1,0:T(8,128)(2,1)S(1)} %get-tuple-element.112), channel_id=1, source_target_pairs={{0,2},{1,3},{2,0},{3,1},{4,6},{5,7},{6,4},{7,5},{8,10},{9,11},{10,... | collective-permute-start | bytes 442376 | tf_op jit(solution)/shard_map/ppermute | solution.py:363
  35.3 4.7 %collective-permute-start.16 = (bf16[96,512]{1,0:T(8,128)(2,1)S(1)}, bf16[96,512]{1,0:T(8,128)(2,1)S(1)}, u32[]{:S(2)}, u32[]{:S(2)}) collective-permute-start(bf16[96,512]{1,0:T(8,128)(2,1)S(1)} %get-tuple-element.124), channel_id=1, source_target_pairs={{0,4},{4,0},{8,12},{12,8},{1,5},{5,1},{9,13},{13,9},{2,6},{6,2},{1... | collective-permute-start | bytes 294920 | tf_op jit(solution)/shard_map/ppermute | solution.py:363
  38.3 5.1 %collective-permute-start.12 = (bf16[96,512]{1,0:T(8,128)(2,1)S(1)}, bf16[96,512]{1,0:T(8,128)(2,1)S(1)}, u32[]{:S(2)}, u32[]{:S(2)}) collective-permute-start(bf16[96,512]{1,0:T(8,128)(2,1)S(1)} %get-tuple-element.115), channel_id=1, source_target_pairs={{0,4},{4,0},{8,12},{12,8},{1,5},{5,1},{9,13},{13,9},{2,6},{6,2},{1... | collective-permute-start | bytes 294920 | tf_op jit(solution)/shard_map/ppermute | solution.py:363
  40.0 8.5 %collective-permute-start.17 = (bf16[96,512]{1,0:T(8,128)(2,1)S(1)}, bf16[96,512]{1,0:T(8,128)(2,1)S(1)}, u32[]{:S(2)}, u32[]{:S(2)}) collective-permute-start(bf16[96,512]{1,0:T(8,128)(2,1)S(1)} %get-tuple-element.126), channel_id=1, source_target_pairs={{0,8},{4,12},{8,0},{12,4},{1,9},{5,13},{9,1},{13,5},{2,10},{6,14},... | collective-permute-start | bytes 294920 | tf_op jit(solution)/shard_map/ppermute | solution.py:363
  43.4 6.8 %collective-permute-start.13 = (bf16[80,512]{1,0:T(8,128)(2,1)S(1)}, bf16[80,512]{1,0:T(8,128)(2,1)S(1)}, u32[]{:S(2)}, u32[]{:S(2)}) collective-permute-start(bf16[80,512]{1,0:T(8,128)(2,1)S(1)} %get-tuple-element.118), channel_id=1, source_target_pairs={{0,8},{4,12},{8,0},{12,4},{1,9},{5,13},{9,1},{13,5},{2,10},{6,14},... | collective-permute-start | bytes 245768 | tf_op jit(solution)/shard_map/ppermute | solution.py:363
  45.6 4.4 %collective-permute-start.20 = (bf16[64,512]{1,0:T(8,128)(2,1)S(1)}, bf16[64,512]{1,0:T(8,128)(2,1)S(1)}, u32[]{:S(2)}, u32[]{:S(2)}) collective-permute-start(bf16[64,512]{1,0:T(8,128)(2,1)S(1)} %get-tuple-element.128.refs_2_), channel_id=1, source_target_pairs={{0,2},{1,3},{2,0},{3,1},{4,6},{5,7},{6,4},{7,5},{8,10},{9,11},{10,... | collective-permute-start | bytes 196616 | tf_op jit(solution)/shard_map/ppermute | solution.py:363
  48.5 4.7 %collective-permute-start.18 = (bf16[96,512]{1,0:T(8,128)(2,1)S(1)}, bf16[96,512]{1,0:T(8,128)(2,1)S(1)}, u32[]{:S(2)}, u32[]{:S(2)}) collective-permute-start(bf16[96,512]{1,0:T(8,128)(2,1)S(1)} %shard_map.160.refs_0_), channel_id=1, source_target_pairs={{0,2},{1,3},{2,0},{3,1},{4,6},{5,7},{6,4},{7,5},{8,10},{9,11},{10,... | collective-permute-start | bytes 294920 | tf_op jit(solution)/shard_map/ppermute | solution.py:363
  50.0 3.7 %collective-permute-start.26 = (bf16[64,512]{1,0:T(8,128)(2,1)S(1)}, bf16[64,512]{1,0:T(8,128)(2,1)S(1)}, u32[]{:S(2)}, u32[]{:S(2)}) collective-permute-start(bf16[64,512]{1,0:T(8,128)(2,1)S(1)} %get-tuple-element.128.refs_2_), channel_id=1, source_target_pairs={{0,1},{1,0},{2,3},{3,2},{4,5},{5,4},{6,7},{7,6},{8,9},{9,8},{10,11... | collective-permute-start | bytes 196616 | tf_op jit(solution)/shard_map/ppermute | solution.py:363
  50.3 4.4 %collective-permute-start.21 = (bf16[64,512]{1,0:T(8,128)(2,1)S(1)}, bf16[64,512]{1,0:T(8,128)(2,1)S(1)}, u32[]{:S(2)}, u32[]{:S(2)}) collective-permute-start(bf16[64,512]{1,0:T(8,128)(2,1)S(1)} %get-tuple-element.129.refs_1_), channel_id=1, source_target_pairs={{0,2},{1,3},{2,0},{3,1},{4,6},{5,7},{6,4},{7,5},{8,10},{9,11},{10,... | collective-permute-start | bytes 196616 | tf_op jit(solution)/shard_map/ppermute | solution.py:363
  51.8 2.9 %collective-permute-start.24 = (bf16[96,512]{1,0:T(8,128)(2,1)S(1)}, bf16[96,512]{1,0:T(8,128)(2,1)S(1)}, u32[]{:S(2)}, u32[]{:S(2)}) collective-permute-start(bf16[96,512]{1,0:T(8,128)(2,1)S(1)} %shard_map.160.refs_0_), channel_id=1, source_target_pairs={{0,1},{1,0},{2,3},{3,2},{4,5},{5,4},{6,7},{7,6},{8,9},{9,8},{10,11... | collective-permute-start | bytes 294920 | tf_op jit(solution)/shard_map/ppermute | solution.py:363
  53.2 2.6 %collective-permute-start.19 = (bf16[96,512]{1,0:T(8,128)(2,1)S(1)}, bf16[96,512]{1,0:T(8,128)(2,1)S(1)}, u32[]{:S(2)}, u32[]{:S(2)}) collective-permute-start(bf16[96,512]{1,0:T(8,128)(2,1)S(1)} %collective-permute-done.18.refs_6_), channel_id=1, source_target_pairs={{0,1},{1,0},{2,3},{3,2},{4,5},{5,4},{6,7},{7,6},{8,9},{9,8},{10,11... | collective-permute-start | bytes 294920 | tf_op jit(solution)/shard_map/ppermute | solution.py:363
  53.7 2.1 %collective-permute-start.23 = (bf16[64,512]{1,0:T(8,128)(2,1)S(1)}, bf16[64,512]{1,0:T(8,128)(2,1)S(1)}, u32[]{:S(2)}, u32[]{:S(2)}) collective-permute-start(bf16[64,512]{1,0:T(8,128)(2,1)S(1)} %get-tuple-element.130.refs_8_), channel_id=1, source_target_pairs={{0,1},{1,0},{2,3},{3,2},{4,5},{5,4},{6,7},{7,6},{8,9},{9,8},{10,11... | collective-permute-start | bytes 196616 | tf_op jit(solution)/shard_map/ppermute | solution.py:363
  (3 other events, 4.4 us)

commit v10 on v9

--- a/solution.py
+++ b/solution.py
@@ -111,8 +111,9 @@
     )
     pre = base[moment] + mm(ends, w1[: 2 * width])
     sigma = sigmoid(pre)
-    hidden = (pre * sigma).astype(BF)
-    slope[...] = sigma * (1.0 + pre * (1.0 - sigma))
+    value = pre * sigma
+    hidden = value.astype(BF)
+    slope[...] = value + sigma * (1.0 - value)
     total = mm(dst_t[...], hidden)
     high = total.astype(BF)
     low = (total - high.astype(F32)).astype(BF)

time: 57 us -> 57 us (level)
  no operation moved by 1% of the time
where the time goes in v10:
time: 57 us; the launch traced here: 56.7 us
  starting transfers between devices  31.2 us (55%)
  waiting for transfers between devices  13.8 us (24%)
  Pallas kernels  10.3 us (18%)
  between operations  1.45 us (3%)
    ppermute x27, starting transfers between devices, swap(): return lax.ppermute(value, axis, [(i, i ^ k) for i in range(WAYS)])  31.2 us
    ppermute x27, waiting for transfers between devices, swap(): return lax.ppermute(value, axis, [(i, i ^ k) for i in range(WAYS)])  13.8 us
    pallas_call x19, Pallas kernels, call(): pl.pallas_call(kernel, out_shape=[jax.ShapeDtypeStruct(shape, dtype) for...  10.3 us
  transfers between devices with their start and end apart: 27, of which 14 were waited for; matrix products, arithmetic and copies ran while one was open for 0% of the time, Pallas kernels for 11%

profile of v10, /device:TPU:0, one launch (start us, length us, event | category | flops | bytes accessed | tf_op | source)
XLA Modules:
  0.0 56.7 jit_solution(12283482308994312267)
XLA Ops:
  1.5 5.1 %collective-permute-start.5 = (bf16[2,32,512]{2,1,0:T(8,128)(2,1)S(1)}, bf16[2,32,512]{2,1,0:T(8,128)(2,1)S(1)}, u32[]{:S(2)}, u32[]{:S(2)}) collective-permute-start(bf16[2,32,512]{2,1,0:T(8,128)(2,1)S(1)} %shard_map.145.refs_0_.refs_4_), channel_id=1, source_target_pairs={{0,12},{4,8},{8,4},{12,0},{1,13},{5,9},{9,5},{13,1},{2,14},{6,10},... | collective-permute-start | bytes 196616 | tf_op jit(solution)/shard_map/ppermute | solution.py:364
  7.2 1.7 %collective-permute-start.2 = (bf16[2,32,128]{2,1,0:T(8,128)(2,1)}, bf16[2,32,128]{2,1,0:T(8,128)(2,1)S(1)}, u32[]{:S(2)}, u32[]{:S(2)}) collective-permute-start(bf16[2,32,128]{2,1,0:T(8,128)(2,1)} %state.1), channel_id=1, source_target_pairs={{0,3},{1,2},{2,1},{3,0},{4,7},{5,6},{6,5},{7,4},{8,11},{9,10},{10,... | collective-permute-start | bytes 49160 | tf_op jit(solution)/shard_map/ppermute | solution.py:364
  9.0 1.3 %collective-permute-start.1 = (bf16[2,32,128]{2,1,0:T(8,128)(2,1)}, bf16[2,32,128]{2,1,0:T(8,128)(2,1)S(1)}, u32[]{:S(2)}, u32[]{:S(2)}) collective-permute-start(bf16[2,32,128]{2,1,0:T(8,128)(2,1)} %state.1), channel_id=1, source_target_pairs={{0,2},{1,3},{2,0},{3,1},{4,6},{5,7},{6,4},{7,5},{8,10},{9,11},{10,... | collective-permute-start | bytes 49160 | tf_op jit(solution)/shard_map/ppermute | solution.py:364
  10.9 1.6 %shard_map.146 = (bf16[2,512,128]{2,1,0:T(8,128)(2,1)S(1)}, bf16[384,512]{1,0:T(8,128)(2,1)S(1)}, bf16[512,256]{1,0:T(8,128)(2,1)S(1)}, bf16[512,256]{1,0:T(8,12...) custom-call(s32[1,1]{1,0:T(1,128)S(6)} %copy.23.count, ...), custom_call_target="tpu_custom_call" | custom-call | tf_op jit(solution)/shard_map/pallas_call | solution.py:346
  14.0 1.3 %collective-permute-start.8 = (bf16[128,256]{1,0:T(8,128)(2,1)S(1)}, bf16[128,256]{1,0:T(8,128)(2,1)S(1)}, u32[]{:S(2)}, u32[]{:S(2)}) collective-permute-start(bf16[128,256]{1,0:T(8,128)(2,1)S(1)} %get-tuple-element.87), channel_id=1, source_target_pairs={{0,4},{4,0},{8,12},{12,8},{1,5},{5,1},{9,13},{13,9},{2,6},{6,2},{1... | collective-permute-start | bytes 196616 | tf_op jit(solution)/shard_map/ppermute | solution.py:364
  17.1 1.4 %collective-permute-done.8.arrived = bf16[128,256]{1,0:T(8,128)(2,1)S(1)} collective-permute-done((bf16[128,256]{1,0:T(8,128)(2,1)S(1)}, bf16[128,256]{1,0:T(8,128)(2,1)S(1)}, u32[]{:S(2)}, u32[]{:S(2)}) %collective-permute-start.8) | collective-permute-done | bytes 65568 | tf_op jit(solution)/shard_map/ppermute | solution.py:364
  18.5 2.0 %collective-permute-start.9 = (bf16[128,256]{1,0:T(8,128)(2,1)S(1)}, bf16[128,256]{1,0:T(8,128)(2,1)S(1)}, u32[]{:S(2)}, u32[]{:S(2)}) collective-permute-start(bf16[128,256]{1,0:T(8,128)(2,1)S(1)} %get-tuple-element.89), channel_id=1, source_target_pairs={{0,8},{4,12},{8,0},{12,4},{1,9},{5,13},{9,1},{13,5},{2,10},{6,14},... | collective-permute-start | bytes 196616 | tf_op jit(solution)/shard_map/ppermute | solution.py:364
  21.3 2.3 %collective-permute-start.7 = (bf16[128,256]{1,0:T(8,128)(2,1)S(1)}, bf16[128,256]{1,0:T(8,128)(2,1)S(1)}, u32[]{:S(2)}, u32[]{:S(2)}) collective-permute-start(bf16[128,256]{1,0:T(8,128)(2,1)S(1)} %get-tuple-element.81), channel_id=1, source_target_pairs={{0,8},{4,12},{8,0},{12,4},{1,9},{5,13},{9,1},{13,5},{2,10},{6,14},... | collective-permute-start | bytes 196616 | tf_op jit(solution)/shard_map/ppermute | solution.py:364
  23.6 1.7 %collective-permute-done.9.refs_9_ = bf16[128,256]{1,0:T(8,128)(2,1)S(1)} collective-permute-done((bf16[128,256]{1,0:T(8,128)(2,1)S(1)}, bf16[128,256]{1,0:T(8,128)(2,1)S(1)}, u32[]{:S(2)}, u32[]{:S(2)}) %collective-permute-start.9) | collective-permute-done | bytes 65568 | tf_op jit(solution)/shard_map/ppermute | solution.py:364
  25.3 1.3 %shard_map.151 = (f32[32,128]{1,0:T(8,128)S(1)}, f32[32,128]{1,0:T(8,128)S(1)}, f32[512,128]{1,0:T(8,128)S(1)}, f32[128,128]{1,0:T(8,128)S(1)}, f32[128,128]{1,0...) custom-call(bf16[2,32,512]{2,1,0:T(8,128)(2,1)S(1)} %shard_map.145.r, ...), custom_call_target="tpu_custom_call" | custom-call | tf_op jit(solution)/shard_map/pallas_call | solution.py:346
  26.6 1.5 %shard_map.152 = (f32[2,32,128]{2,1,0:T(8,128)S(1)}, f32[32,128]{1,0:T(8,128)S(1)}, f32[512,128]{1,0:T(8,128)S(1)}, f32[384,512]{1,0:T(8,128)S(1)}, f32[512,256]...) custom-call(bf16[2,32,512]{2,1,0:T(8,128)(2,1)S(1)} %shard_map.145.r, ...), custom_call_target="tpu_custom_call" | custom-call | tf_op jit(solution)/shard_map/pallas_call | solution.py:346
  28.7 1.4 %collective-permute-done.14.arrived = bf16[192,512]{1,0:T(8,128)(2,1)S(1)} collective-permute-done((bf16[192,512]{1,0:T(8,128)(2,1)S(1)}, bf16[192,512]{1,0:T(8,128)(2,1)S(1)}, u32[]{:S(2)}, u32[]{:S(2)}) %collective-permute-start.14) | collective-permute-done | bytes 196640 | tf_op jit(solution)/shard_map/ppermute | solution.py:364
  30.1 1.3 %collective-permute-start.15 = (bf16[96,512]{1,0:T(8,128)(2,1)S(1)}, bf16[96,512]{1,0:T(8,128)(2,1)S(1)}, u32[]{:S(2)}, u32[]{:S(2)}) collective-permute-start(bf16[96,512]{1,0:T(8,128)(2,1)S(1)} %get-tuple-element.122), channel_id=1, source_target_pairs={{0,2},{1,3},{2,0},{3,1},{4,6},{5,7},{6,4},{7,5},{8,10},{9,11},{10,... | collective-permute-start | bytes 294920 | tf_op jit(solution)/shard_map/ppermute | solution.py:364
  33.2 2.0 %collective-permute-done.15.arrived = bf16[96,512]{1,0:T(8,128)(2,1)S(1)} collective-permute-done((bf16[96,512]{1,0:T(8,128)(2,1)S(1)}, bf16[96,512]{1,0:T(8,128)(2,1)S(1)}, u32[]{:S(2)}, u32[]{:S(2)}) %collective-permute-start.15) | collective-permute-done | bytes 98336 | tf_op jit(solution)/shard_map/ppermute | solution.py:364
  35.2 1.8 %collective-permute-start.16 = (bf16[96,512]{1,0:T(8,128)(2,1)S(1)}, bf16[96,512]{1,0:T(8,128)(2,1)S(1)}, u32[]{:S(2)}, u32[]{:S(2)}) collective-permute-start(bf16[96,512]{1,0:T(8,128)(2,1)S(1)} %get-tuple-element.124), channel_id=1, source_target_pairs={{0,4},{4,0},{8,12},{12,8},{1,5},{5,1},{9,13},{13,9},{2,6},{6,2},{1... | collective-permute-start | bytes 294920 | tf_op jit(solution)/shard_map/ppermute | solution.py:364
  38.2 1.5 %collective-permute-start.12 = (bf16[96,512]{1,0:T(8,128)(2,1)S(1)}, bf16[96,512]{1,0:T(8,128)(2,1)S(1)}, u32[]{:S(2)}, u32[]{:S(2)}) collective-permute-start(bf16[96,512]{1,0:T(8,128)(2,1)S(1)} %get-tuple-element.115), channel_id=1, source_target_pairs={{0,4},{4,0},{8,12},{12,8},{1,5},{5,1},{9,13},{13,9},{2,6},{6,2},{1... | collective-permute-start | bytes 294920 | tf_op jit(solution)/shard_map/ppermute | solution.py:364
  39.9 2.4 %collective-permute-start.17 = (bf16[96,512]{1,0:T(8,128)(2,1)S(1)}, bf16[96,512]{1,0:T(8,128)(2,1)S(1)}, u32[]{:S(2)}, u32[]{:S(2)}) collective-permute-start(bf16[96,512]{1,0:T(8,128)(2,1)S(1)} %get-tuple-element.126), channel_id=1, source_target_pairs={{0,8},{4,12},{8,0},{12,4},{1,9},{5,13},{9,1},{13,5},{2,10},{6,14},... | collective-permute-start | bytes 294920 | tf_op jit(solution)/shard_map/ppermute | solution.py:364
  43.4 2.2 %collective-permute-start.13 = (bf16[80,512]{1,0:T(8,128)(2,1)S(1)}, bf16[80,512]{1,0:T(8,128)(2,1)S(1)}, u32[]{:S(2)}, u32[]{:S(2)}) collective-permute-start(bf16[80,512]{1,0:T(8,128)(2,1)S(1)} %get-tuple-element.118), channel_id=1, source_target_pairs={{0,8},{4,12},{8,0},{12,4},{1,9},{5,13},{9,1},{13,5},{2,10},{6,14},... | collective-permute-start | bytes 245768 | tf_op jit(solution)/shard_map/ppermute | solution.py:364
  45.6 1.5 %collective-permute-start.20 = (bf16[64,512]{1,0:T(8,128)(2,1)S(1)}, bf16[64,512]{1,0:T(8,128)(2,1)S(1)}, u32[]{:S(2)}, u32[]{:S(2)}) collective-permute-start(bf16[64,512]{1,0:T(8,128)(2,1)S(1)} %get-tuple-element.128.refs_2_), channel_id=1, source_target_pairs={{0,2},{1,3},{2,0},{3,1},{4,6},{5,7},{6,4},{7,5},{8,10},{9,11},{10,... | collective-permute-start | bytes 196616 | tf_op jit(solution)/shard_map/ppermute | solution.py:364
  47.0 1.4 %collective-permute-done.17.arrived = bf16[96,512]{1,0:T(8,128)(2,1)S(1)} collective-permute-done((bf16[96,512]{1,0:T(8,128)(2,1)S(1)}, bf16[96,512]{1,0:T(8,128)(2,1)S(1)}, u32[]{:S(2)}, u32[]{:S(2)}) %collective-permute-start.17) | collective-permute-done | bytes 98336 | tf_op jit(solution)/shard_map/ppermute | solution.py:364
  48.5 1.6 %collective-permute-start.18 = (bf16[96,512]{1,0:T(8,128)(2,1)S(1)}, bf16[96,512]{1,0:T(8,128)(2,1)S(1)}, u32[]{:S(2)}, u32[]{:S(2)}) collective-permute-start(bf16[96,512]{1,0:T(8,128)(2,1)S(1)} %shard_map.160.refs_0_), channel_id=1, source_target_pairs={{0,2},{1,3},{2,0},{3,1},{4,6},{5,7},{6,4},{7,5},{8,10},{9,11},{10,... | collective-permute-start | bytes 294920 | tf_op jit(solution)/shard_map/ppermute | solution.py:364
  50.2 1.6 %collective-permute-start.21 = (bf16[64,512]{1,0:T(8,128)(2,1)S(1)}, bf16[64,512]{1,0:T(8,128)(2,1)S(1)}, u32[]{:S(2)}, u32[]{:S(2)}) collective-permute-start(bf16[64,512]{1,0:T(8,128)(2,1)S(1)} %get-tuple-element.129.refs_1_), channel_id=1, source_target_pairs={{0,2},{1,3},{2,0},{3,1},{4,6},{5,7},{6,4},{7,5},{8,10},{9,11},{10,... | collective-permute-start | bytes 196616 | tf_op jit(solution)/shard_map/ppermute | solution.py:364
  51.8 1.3 %collective-permute-done.18.refs_6_ = bf16[96,512]{1,0:T(8,128)(2,1)S(1)} collective-permute-done((bf16[96,512]{1,0:T(8,128)(2,1)S(1)}, bf16[96,512]{1,0:T(8,128)(2,1)S(1)}, u32[]{:S(2)}, u32[]{:S(2)}) %collective-permute-start.18) | collective-permute-done | bytes 98336 | tf_op jit(solution)/shard_map/ppermute | solution.py:364
  54.7 1.2 %shard_map.162 = (f32[384,512]{1,0:T(8,128)}, f32[512,256]{1,0:T(8,128)}, f32[512,256]{1,0:T(8,128)}) custom-call(bf16[96,512]{1,0:T(8,128)(2,1)S(1)} %shard_map.160.refs_0_, bf16[64,512]{1,0:T(8,128)(2,1)S(1)} %get-tuple-element.129.refs_1_, bf16[64,512]{1,0:T(8,128)(2,1)S(1)} %get-tuple-element.128.refs_2_, ...), custom_call_target="tpu_custom_call" | custom-call | tf_op jit(solution)/shard_map/pallas_call | solution.py:346
  (49 shorter events, 12.9 us)
Async XLA Ops:
  1.5 11.5 %collective-permute-start.5 = (bf16[2,32,512]{2,1,0:T(8,128)(2,1)S(1)}, bf16[2,32,512]{2,1,0:T(8,128)(2,1)S(1)}, u32[]{:S(2)}, u32[]{:S(2)}) collective-permute-start(bf16[2,32,512]{2,1,0:T(8,128)(2,1)S(1)} %shard_map.145.refs_0_.refs_4_), channel_id=1, source_target_pairs={{0,12},{4,8},{8,4},{12,0},{1,13},{5,9},{9,5},{13,1},{2,14},{6,10},... | collective-permute-start | bytes 196616 | tf_op jit(solution)/shard_map/ppermute | solution.py:364
  6.6 6.4 %collective-permute-start.4 = (bf16[2,32,512]{2,1,0:T(8,128)(2,1)S(1)}, bf16[2,32,512]{2,1,0:T(8,128)(2,1)S(1)}, u32[]{:S(2)}, u32[]{:S(2)}) collective-permute-start(bf16[2,32,512]{2,1,0:T(8,128)(2,1)S(1)} %shard_map.145.refs_0_.refs_4_), channel_id=1, source_target_pairs={{0,8},{4,12},{8,0},{12,4},{1,9},{5,13},{9,1},{13,5},{2,10},{6,14},... | collective-permute-start | bytes 196616 | tf_op jit(solution)/shard_map/ppermute | solution.py:364
  6.6 6.4 %collective-permute-start.3 = (bf16[2,32,512]{2,1,0:T(8,128)(2,1)S(1)}, bf16[2,32,512]{2,1,0:T(8,128)(2,1)S(1)}, u32[]{:S(2)}, u32[]{:S(2)}) collective-permute-start(bf16[2,32,512]{2,1,0:T(8,128)(2,1)S(1)} %shard_map.145.refs_0_.refs_4_), channel_id=1, source_target_pairs={{0,4},{4,0},{8,12},{12,8},{1,5},{5,1},{9,13},{13,9},{2,6},{6,2},{1... | collective-permute-start | bytes 196616 | tf_op jit(solution)/shard_map/ppermute | solution.py:364
  7.2 5.3 %collective-permute-start.2 = (bf16[2,32,128]{2,1,0:T(8,128)(2,1)}, bf16[2,32,128]{2,1,0:T(8,128)(2,1)S(1)}, u32[]{:S(2)}, u32[]{:S(2)}) collective-permute-start(bf16[2,32,128]{2,1,0:T(8,128)(2,1)} %state.1), channel_id=1, source_target_pairs={{0,3},{1,2},{2,1},{3,0},{4,7},{5,6},{6,5},{7,4},{8,11},{9,10},{10,... | collective-permute-start | bytes 49160 | tf_op jit(solution)/shard_map/ppermute | solution.py:364
  9.0 4.0 %collective-permute-start.1 = (bf16[2,32,128]{2,1,0:T(8,128)(2,1)}, bf16[2,32,128]{2,1,0:T(8,128)(2,1)S(1)}, u32[]{:S(2)}, u32[]{:S(2)}) collective-permute-start(bf16[2,32,128]{2,1,0:T(8,128)(2,1)} %state.1), channel_id=1, source_target_pairs={{0,2},{1,3},{2,0},{3,1},{4,6},{5,7},{6,4},{7,5},{8,10},{9,11},{10,... | collective-permute-start | bytes 49160 | tf_op jit(solution)/shard_map/ppermute | solution.py:364
  14.0 4.5 %collective-permute-start.8 = (bf16[128,256]{1,0:T(8,128)(2,1)S(1)}, bf16[128,256]{1,0:T(8,128)(2,1)S(1)}, u32[]{:S(2)}, u32[]{:S(2)}) collective-permute-start(bf16[128,256]{1,0:T(8,128)(2,1)S(1)} %get-tuple-element.87), channel_id=1, source_target_pairs={{0,4},{4,0},{8,12},{12,8},{1,5},{5,1},{9,13},{13,9},{2,6},{6,2},{1... | collective-permute-start | bytes 196616 | tf_op jit(solution)/shard_map/ppermute | solution.py:364
  16.3 5.0 %collective-permute-start.6 = (bf16[128,256]{1,0:T(8,128)(2,1)S(1)}, bf16[128,256]{1,0:T(8,128)(2,1)S(1)}, u32[]{:S(2)}, u32[]{:S(2)}) collective-permute-start(bf16[128,256]{1,0:T(8,128)(2,1)S(1)} %get-tuple-element.79), channel_id=1, source_target_pairs={{0,4},{4,0},{8,12},{12,8},{1,5},{5,1},{9,13},{13,9},{2,6},{6,2},{1... | collective-permute-start | bytes 196616 | tf_op jit(solution)/shard_map/ppermute | solution.py:364
  18.5 6.8 %collective-permute-start.9 = (bf16[128,256]{1,0:T(8,128)(2,1)S(1)}, bf16[128,256]{1,0:T(8,128)(2,1)S(1)}, u32[]{:S(2)}, u32[]{:S(2)}) collective-permute-start(bf16[128,256]{1,0:T(8,128)(2,1)S(1)} %get-tuple-element.89), channel_id=1, source_target_pairs={{0,8},{4,12},{8,0},{12,4},{1,9},{5,13},{9,1},{13,5},{2,10},{6,14},... | collective-permute-start | bytes 196616 | tf_op jit(solution)/shard_map/ppermute | solution.py:364
  21.3 5.3 %collective-permute-start.7 = (bf16[128,256]{1,0:T(8,128)(2,1)S(1)}, bf16[128,256]{1,0:T(8,128)(2,1)S(1)}, u32[]{:S(2)}, u32[]{:S(2)}) collective-permute-start(bf16[128,256]{1,0:T(8,128)(2,1)S(1)} %get-tuple-element.81), channel_id=1, source_target_pairs={{0,8},{4,12},{8,0},{12,4},{1,9},{5,13},{9,1},{13,5},{2,10},{6,14},... | collective-permute-start | bytes 196616 | tf_op jit(solution)/shard_map/ppermute | solution.py:364
  28.1 4.1 %collective-permute-start.10 = (bf16[288,512]{1,0:T(8,128)(2,1)S(1)}, bf16[288,512]{1,0:T(8,128)(2,1)S(1)}, u32[]{:S(2)}, u32[]{:S(2)}) collective-permute-start(bf16[288,512]{1,0:T(8,128)(2,1)S(1)} %get-tuple-element.105), channel_id=1, source_target_pairs={{0,1},{1,0},{2,3},{3,2},{4,5},{5,4},{6,7},{7,6},{8,9},{9,8},{10,11... | collective-permute-start | bytes 884744 | tf_op jit(solution)/shard_map/ppermute | solution.py:364
  28.2 1.9 %collective-permute-start.14 = (bf16[192,512]{1,0:T(8,128)(2,1)S(1)}, bf16[192,512]{1,0:T(8,128)(2,1)S(1)}, u32[]{:S(2)}, u32[]{:S(2)}) collective-permute-start(bf16[192,512]{1,0:T(8,128)(2,1)S(1)} %get-tuple-element.120), channel_id=1, source_target_pairs={{0,1},{1,0},{2,3},{3,2},{4,5},{5,4},{6,7},{7,6},{8,9},{9,8},{10,11... | collective-permute-start | bytes 589832 | tf_op jit(solution)/shard_map/ppermute | solution.py:364
  30.1 5.1 %collective-permute-start.15 = (bf16[96,512]{1,0:T(8,128)(2,1)S(1)}, bf16[96,512]{1,0:T(8,128)(2,1)S(1)}, u32[]{:S(2)}, u32[]{:S(2)}) collective-permute-start(bf16[96,512]{1,0:T(8,128)(2,1)S(1)} %get-tuple-element.122), channel_id=1, source_target_pairs={{0,2},{1,3},{2,0},{3,1},{4,6},{5,7},{6,4},{7,5},{8,10},{9,11},{10,... | collective-permute-start | bytes 294920 | tf_op jit(solution)/shard_map/ppermute | solution.py:364
  32.3 5.8 %collective-permute-start.11 = (bf16[144,512]{1,0:T(8,128)(2,1)S(1)}, bf16[144,512]{1,0:T(8,128)(2,1)S(1)}, u32[]{:S(2)}, u32[]{:S(2)}) collective-permute-start(bf16[144,512]{1,0:T(8,128)(2,1)S(1)} %get-tuple-element.112), channel_id=1, source_target_pairs={{0,2},{1,3},{2,0},{3,1},{4,6},{5,7},{6,4},{7,5},{8,10},{9,11},{10,... | collective-permute-start | bytes 442376 | tf_op jit(solution)/shard_map/ppermute | solution.py:364
  35.2 4.7 %collective-permute-start.16 = (bf16[96,512]{1,0:T(8,128)(2,1)S(1)}, bf16[96,512]{1,0:T(8,128)(2,1)S(1)}, u32[]{:S(2)}, u32[]{:S(2)}) collective-permute-start(bf16[96,512]{1,0:T(8,128)(2,1)S(1)} %get-tuple-element.124), channel_id=1, source_target_pairs={{0,4},{4,0},{8,12},{12,8},{1,5},{5,1},{9,13},{13,9},{2,6},{6,2},{1... | collective-permute-start | bytes 294920 | tf_op jit(solution)/shard_map/ppermute | solution.py:364
  38.2 5.1 %collective-permute-start.12 = (bf16[96,512]{1,0:T(8,128)(2,1)S(1)}, bf16[96,512]{1,0:T(8,128)(2,1)S(1)}, u32[]{:S(2)}, u32[]{:S(2)}) collective-permute-start(bf16[96,512]{1,0:T(8,128)(2,1)S(1)} %get-tuple-element.115), channel_id=1, source_target_pairs={{0,4},{4,0},{8,12},{12,8},{1,5},{5,1},{9,13},{13,9},{2,6},{6,2},{1... | collective-permute-start | bytes 294920 | tf_op jit(solution)/shard_map/ppermute | solution.py:364
  39.9 8.5 %collective-permute-start.17 = (bf16[96,512]{1,0:T(8,128)(2,1)S(1)}, bf16[96,512]{1,0:T(8,128)(2,1)S(1)}, u32[]{:S(2)}, u32[]{:S(2)}) collective-permute-start(bf16[96,512]{1,0:T(8,128)(2,1)S(1)} %get-tuple-element.126), channel_id=1, source_target_pairs={{0,8},{4,12},{8,0},{12,4},{1,9},{5,13},{9,1},{13,5},{2,10},{6,14},... | collective-permute-start | bytes 294920 | tf_op jit(solution)/shard_map/ppermute | solution.py:364
  43.4 6.8 %collective-permute-start.13 = (bf16[80,512]{1,0:T(8,128)(2,1)S(1)}, bf16[80,512]{1,0:T(8,128)(2,1)S(1)}, u32[]{:S(2)}, u32[]{:S(2)}) collective-permute-start(bf16[80,512]{1,0:T(8,128)(2,1)S(1)} %get-tuple-element.118), channel_id=1, source_target_pairs={{0,8},{4,12},{8,0},{12,4},{1,9},{5,13},{9,1},{13,5},{2,10},{6,14},... | collective-permute-start | bytes 245768 | tf_op jit(solution)/shard_map/ppermute | solution.py:364
  45.6 4.5 %collective-permute-start.20 = (bf16[64,512]{1,0:T(8,128)(2,1)S(1)}, bf16[64,512]{1,0:T(8,128)(2,1)S(1)}, u32[]{:S(2)}, u32[]{:S(2)}) collective-permute-start(bf16[64,512]{1,0:T(8,128)(2,1)S(1)} %get-tuple-element.128.refs_2_), channel_id=1, source_target_pairs={{0,2},{1,3},{2,0},{3,1},{4,6},{5,7},{6,4},{7,5},{8,10},{9,11},{10,... | collective-permute-start | bytes 196616 | tf_op jit(solution)/shard_map/ppermute | solution.py:364
  48.5 4.7 %collective-permute-start.18 = (bf16[96,512]{1,0:T(8,128)(2,1)S(1)}, bf16[96,512]{1,0:T(8,128)(2,1)S(1)}, u32[]{:S(2)}, u32[]{:S(2)}) collective-permute-start(bf16[96,512]{1,0:T(8,128)(2,1)S(1)} %shard_map.160.refs_0_), channel_id=1, source_target_pairs={{0,2},{1,3},{2,0},{3,1},{4,6},{5,7},{6,4},{7,5},{8,10},{9,11},{10,... | collective-permute-start | bytes 294920 | tf_op jit(solution)/shard_map/ppermute | solution.py:364
  50.1 3.6 %collective-permute-start.26 = (bf16[64,512]{1,0:T(8,128)(2,1)S(1)}, bf16[64,512]{1,0:T(8,128)(2,1)S(1)}, u32[]{:S(2)}, u32[]{:S(2)}) collective-permute-start(bf16[64,512]{1,0:T(8,128)(2,1)S(1)} %get-tuple-element.128.refs_2_), channel_id=1, source_target_pairs={{0,1},{1,0},{2,3},{3,2},{4,5},{5,4},{6,7},{7,6},{8,9},{9,8},{10,11... | collective-permute-start | bytes 196616 | tf_op jit(solution)/shard_map/ppermute | solution.py:364
  50.2 4.5 %collective-permute-start.21 = (bf16[64,512]{1,0:T(8,128)(2,1)S(1)}, bf16[64,512]{1,0:T(8,128)(2,1)S(1)}, u32[]{:S(2)}, u32[]{:S(2)}) collective-permute-start(bf16[64,512]{1,0:T(8,128)(2,1)S(1)} %get-tuple-element.129.refs_1_), channel_id=1, source_target_pairs={{0,2},{1,3},{2,0},{3,1},{4,6},{5,7},{6,4},{7,5},{8,10},{9,11},{10,... | collective-permute-start | bytes 196616 | tf_op jit(solution)/shard_map/ppermute | solution.py:364
  51.8 2.9 %collective-permute-start.24 = (bf16[96,512]{1,0:T(8,128)(2,1)S(1)}, bf16[96,512]{1,0:T(8,128)(2,1)S(1)}, u32[]{:S(2)}, u32[]{:S(2)}) collective-permute-start(bf16[96,512]{1,0:T(8,128)(2,1)S(1)} %shard_map.160.refs_0_), channel_id=1, source_target_pairs={{0,1},{1,0},{2,3},{3,2},{4,5},{5,4},{6,7},{7,6},{8,9},{9,8},{10,11... | collective-permute-start | bytes 294920 | tf_op jit(solution)/shard_map/ppermute | solution.py:364
  53.1 2.7 %collective-permute-start.19 = (bf16[96,512]{1,0:T(8,128)(2,1)S(1)}, bf16[96,512]{1,0:T(8,128)(2,1)S(1)}, u32[]{:S(2)}, u32[]{:S(2)}) collective-permute-start(bf16[96,512]{1,0:T(8,128)(2,1)S(1)} %collective-permute-done.18.refs_6_), channel_id=1, source_target_pairs={{0,1},{1,0},{2,3},{3,2},{4,5},{5,4},{6,7},{7,6},{8,9},{9,8},{10,11... | collective-permute-start | bytes 294920 | tf_op jit(solution)/shard_map/ppermute | solution.py:364
  53.7 2.2 %collective-permute-start.23 = (bf16[64,512]{1,0:T(8,128)(2,1)S(1)}, bf16[64,512]{1,0:T(8,128)(2,1)S(1)}, u32[]{:S(2)}, u32[]{:S(2)}) collective-permute-start(bf16[64,512]{1,0:T(8,128)(2,1)S(1)} %get-tuple-element.130.refs_8_), channel_id=1, source_target_pairs={{0,1},{1,0},{2,3},{3,2},{4,5},{5,4},{6,7},{7,6},{8,9},{9,8},{10,11... | collective-permute-start | bytes 196616 | tf_op jit(solution)/shard_map/ppermute | solution.py:364
  (3 other events, 4.5 us)
